TPU v7x, 32 devices: a whole 2x2x4 slice. The times are simulated.
32 devices in a mesh: dp: 8 (over z, x), expert: 4 (over y, core).
Axes of the slice: x: 2, y: 2, z: 4, core: 2. Of those that a mesh axis runs over, the one named last changes fastest.
Arguments:
- hidden_in: float32 [12288, 1024], P(('dp', 'expert')), may hold values from -6 to 6
- out_grad: float32 [12288, 1024], P(('dp', 'expert')), may hold values from -6 to 6
- segment_ids: int32 [12288], P(('dp', 'expert')), may hold values from 0 to 415, as said below
- parent_ids: int32 [12288], P(('dp', 'expert')), may hold values from 0 to 413, as said below
- positions: int32 [12288], P(('dp', 'expert')), may hold values from 0 to 190, as said below
- expert_ids: int32 [12288, 8], P(('dp', 'expert')), may hold values from 0 to 31, all different within a row; in each aligned block of 384 rows (0 to 383, 384 to 767, ...) at most 144 rows name the same one
- gate_weights: float32 [12288, 8], P(('dp', 'expert')), may hold values from 0.05 to 0.25
- norm_gains: bfloat16 [2, 1024], replicated, may hold values from 0.5 to 1.5
- qkv_weight: bfloat16 [1024, 2048], replicated, may hold values from -0.1875 to 0.1875
- out_weight: bfloat16 [1024, 1024], replicated, may hold values from -1.5 to 1.5
- gate_up_weight: bfloat16 [32, 1024, 1024], P('expert'), may hold values from -0.1875 to 0.1875
- down_weight: bfloat16 [32, 512, 1024], P('expert'), may hold values from -1 to 1
- gain_moment: float32 [2, 1024], replicated, may hold values from 6144 to 737280
- qkv_rows: float32 [1024], replicated, may hold values from 24576 to 2949120
- qkv_cols: float32 [2048], replicated, may hold values from 3072 to 393216
- out_rows: float32 [1024], replicated, may hold values from 1 to 1000
- out_cols: float32 [1024], replicated, may hold values from 1 to 1000
- gateup_rows: float32 [32, 1024], P('expert'), may hold values from 307 to 36864
- gateup_cols: float32 [32, 1024], P('expert'), may hold values from 1 to 1000
- down_rows: float32 [32, 512], P('expert'), may hold values from 1 to 1000
- down_cols: float32 [32, 1024], P('expert'), may hold values from 1 to 1000
Outputs:
- block_out: float32 [12288, 1024], P(('dp', 'expert'))
- input_grad: float32 [12288, 1024], P(('dp', 'expert'))
- update_rms: float32 [5], replicated
- gains_update: float32 [2, 1024], P(None, 'dp')
- gain_moment_new: float32 [2, 1024], P(None, 'dp')
- qkv_new: float32 [1024, 2048], P('dp')
- qkv_rows_new: float32 [1024], P('dp')
- qkv_cols_new: float32 [2048], replicated
- out_new: float32 [1024, 1024], P('dp')
- out_rows_new: float32 [1024], P('dp')
- out_cols_new: float32 [1024], replicated
- gate_up_new: float32 [32, 1024, 1024], P('expert', 'dp')
- gateup_rows_new: float32 [32, 1024], P('expert', 'dp')
- gateup_cols_new: float32 [32, 1024], P('expert')
- down_new: float32 [32, 512, 1024], P('expert', 'dp')
- down_rows_new: float32 [32, 512], P('expert', 'dp')
- down_cols_new: float32 [32, 1024], P('expert')
Inputs may be any that keep to these rules, and one draw needn't show every extreme that they name: `segment_ids`: each 384 consecutive tokens form one tree: a trunk of 128 tokens, then four regions of 64 tokens, each a branch followed by two leaves, every segment nonempty. Tree t's trunk is segment 13 t, its branch b (0 to 3) is 13 t + 1 + 3 b, that branch's leaves 13 t + 2 + 3 b and 13 t + 3 + 3 b. `parent_ids`: A leaf token's entry is its branch's segment, a branch token's is its trunk's segment, a trunk token's is its own segment. `positions`: A token's distance from its tree's root along its path: trunk tokens 0 to 127 in order, a branch continues from 128, each of its leaves from the end of the branch. `expert_ids`: each row names 8 different experts. In the rows of one device no expert is named by more than 144 rows, a bound that some block reaches in some devices' rows.
All inputs are finite; a program needn't handle non-finite values.
Results may differ from a plain program's by a relative error of at most 0.019.
Values may be sent and summed in bfloat16 or wider, within the bound.
A program may use at most 256 MiB of HBM per device.

v0:
```python
import math

import jax
import jax.numpy as jnp
from jax import lax
from jax.sharding import PartitionSpec as P

D = 1024
HEADS = 16
KV_HEADS = 8
HEAD_DIM = 64
FF = 512
TOP = 8


EPS_NORM = 1e-06
EPS_STAT = 1e-30
STAT_DECAY = 0.5
LEARN_RATE = 0.5
CLIP_LEVEL = 0.05
ROPE_BASE = 10000.0
MASKED = -1e30


def rotation_tables(places):
    half_dim = HEAD_DIM // 2
    frequency = jnp.exp(
        jnp.arange(half_dim, dtype=jnp.float32) * (-2.0 * math.log(ROPE_BASE) / HEAD_DIM)
    )
    angles = places.astype(jnp.float32)[:, None] * frequency[None, :]
    return (jnp.cos(angles)[:, None, :], jnp.sin(angles)[:, None, :])


def rotate(vectors, cos_table, sine_table):
    half_dim = vectors.shape[-1] // 2
    front_half = vectors[..., :half_dim]
    back_half = vectors[..., half_dim:]
    return jnp.concatenate(
        [
            front_half * cos_table - back_half * sine_table,
            back_half * cos_table + front_half * sine_table,
        ],
        axis=-1,
    )


def rotate_back(gradients, cos_table, sine_table):
    half_dim = gradients.shape[-1] // 2
    front_half = gradients[..., :half_dim]
    back_half = gradients[..., half_dim:]
    return jnp.concatenate(
        [
            front_half * cos_table + back_half * sine_table,
            back_half * cos_table - front_half * sine_table,
        ],
        axis=-1,
    )


def path_mask(segments, parents, places):
    allowed = (
        (segments[None, :] == segments[:, None])
        | (segments[None, :] == parents[:, None])
        | (segments == parents)[None, :]
    )
    return allowed & (places[None, :] <= places[:, None])


def masked_scores(queries, key_rows, allowed, score_scale):
    raw_scores = (
        jnp.einsum("qhgd,khd->hgqk", queries, key_rows, preferred_element_type=jnp.float32)
        * score_scale
    )
    return jnp.where(allowed, raw_scores, MASKED)


def norm_back(values, inverse, gain_vec, gradient):
    weighted = gradient * gain_vec
    gain_grad = jnp.sum(gradient * values * inverse, axis=0)
    value_grad = inverse * weighted - values * inverse * inverse * inverse * jnp.mean(
        weighted * values, axis=-1, keepdims=True
    )
    return (value_grad, gain_grad)


def up_project(received, weights):
    return jnp.einsum("secd,edf->secf", received, weights, preferred_element_type=jnp.float32)


def activate(gate_up):
    return (jax.nn.silu(gate_up[..., :FF]) * gate_up[..., FF:]).astype(jnp.bfloat16)


def own_share(matrix, share_count, share_index, along):
    width = matrix.shape[along] // share_count
    return lax.dynamic_slice_in_dim(matrix, share_index * width, width, along)


def per_device(
    hidden_in,
    out_grad,
    segment_ids,
    parent_ids,
    positions,
    expert_ids,
    gate_weights,
    norm_gains,
    qkv_weight,
    out_weight,
    gate_up_weight,
    down_weight,
    gain_moment,
    qkv_rows,
    qkv_cols,
    out_rows,
    out_cols,
    gateup_rows,
    gateup_cols,
    down_rows,
    down_cols,
):
    rows_here = hidden_in.shape[0]
    att_width = HEADS * HEAD_DIM
    kv_width = KV_HEADS * HEAD_DIM
    group_size = HEADS // KV_HEADS
    score_scale = HEAD_DIM ** (-0.5)
    cos_table, sine_table = rotation_tables(positions)
    gain_attn = norm_gains[0].astype(jnp.float32)
    gain_ffn = norm_gains[1].astype(jnp.float32)
    inverse_attn = lax.rsqrt(jnp.mean(hidden_in * hidden_in, axis=-1, keepdims=True) + EPS_NORM)
    normed = (hidden_in * inverse_attn * gain_attn).astype(jnp.bfloat16)
    projected = jnp.dot(normed, qkv_weight, preferred_element_type=jnp.float32)
    queries = rotate(
        projected[:, :att_width].reshape(rows_here, HEADS, HEAD_DIM), cos_table, sine_table
    )
    queries = queries.astype(jnp.bfloat16).reshape(rows_here, KV_HEADS, group_size, HEAD_DIM)
    key_rows = rotate(
        projected[:, att_width : att_width + kv_width].reshape(rows_here, KV_HEADS, HEAD_DIM),
        cos_table,
        sine_table,
    ).astype(jnp.bfloat16)
    value_rows = (
        projected[:, att_width + kv_width :]
        .reshape(rows_here, KV_HEADS, HEAD_DIM)
        .astype(jnp.bfloat16)
    )
    allowed = path_mask(segment_ids, parent_ids, positions)
    scores = masked_scores(queries, key_rows, allowed, score_scale)
    row_max = jnp.max(scores, axis=-1, keepdims=True)
    exponent = jnp.exp(scores - row_max)
    row_total = jnp.sum(exponent, axis=-1, keepdims=True)
    log_total = row_max + jnp.log(row_total)
    probs_low = (exponent / row_total).astype(jnp.bfloat16)
    attended = jnp.einsum(
        "hgqk,khd->qhgd", probs_low, value_rows, preferred_element_type=jnp.float32
    )
    attended = attended.reshape(rows_here, att_width).astype(jnp.bfloat16)
    middle = hidden_in + jnp.dot(attended, out_weight, preferred_element_type=jnp.float32)
    inverse_ffn = lax.rsqrt(jnp.mean(middle * middle, axis=-1, keepdims=True) + EPS_NORM)
    normed_ffn = (middle * inverse_ffn * gain_ffn).astype(jnp.bfloat16)
    experts_here = gate_up_weight.shape[0]
    groups = lax.axis_size("expert")
    total_experts = experts_here * groups
    capacity = 3 * rows_here * TOP // (2 * total_experts)
    flat_ids = expert_ids.reshape(-1)
    onehot = (flat_ids[:, None] == jnp.arange(total_experts, dtype=jnp.int32)[None, :]).astype(
        jnp.int32
    )
    slot_index = jnp.sum((jnp.cumsum(onehot, axis=0) - onehot) * onehot, axis=1)
    target = flat_ids * capacity + slot_index
    source_row = jnp.arange(rows_here * TOP, dtype=jnp.int32) // TOP
    outgoing = (
        jnp.zeros((total_experts * capacity, D), jnp.bfloat16)
        .at[target]
        .set(normed_ffn[source_row])
    )
    outgoing = outgoing.reshape(groups, experts_here, capacity, D)
    received = lax.all_to_all(outgoing, "expert", split_axis=0, concat_axis=0, tiled=True)
    gate_up = up_project(received, gate_up_weight)
    produced = jnp.einsum(
        "secf,efd->secd", activate(gate_up), down_weight, preferred_element_type=jnp.float32
    ).astype(jnp.bfloat16)
    returned = lax.all_to_all(produced, "expert", split_axis=0, concat_axis=0, tiled=True)
    results = (returned, received, gate_up)
    returned = results[0]
    received = results[1]
    picked = (
        returned.reshape(total_experts * capacity, D)[target]
        .astype(jnp.float32)
        .reshape(rows_here, TOP, D)
    )
    block_out = middle + jnp.sum(picked * gate_weights[:, :, None], axis=1)
    slot_grads = (
        (gate_weights[:, :, None] * out_grad[:, None, :])
        .reshape(rows_here * TOP, D)
        .astype(jnp.bfloat16)
    )
    outgoing_grads = (
        jnp.zeros((total_experts * capacity, D), jnp.bfloat16).at[target].set(slot_grads)
    )
    outgoing_grads = outgoing_grads.reshape(groups, experts_here, capacity, D)
    arrived = lax.all_to_all(outgoing_grads, "expert", split_axis=0, concat_axis=0, tiled=True)
    act_grad = jnp.einsum(
        "secd,efd->secf", arrived, down_weight, preferred_element_type=jnp.float32
    )
    arrived, act_grad = (arrived, act_grad)
    gate_up = results[2]
    gate_part = gate_up[..., :FF]
    up_part = gate_up[..., FF:]
    sigmoid_gate = jax.nn.sigmoid(gate_part)
    silu_gate = gate_part * sigmoid_gate
    activated = (silu_gate * up_part).astype(jnp.bfloat16)
    down_wgrad = jnp.einsum(
        "secf,secd->efd", activated, arrived, preferred_element_type=jnp.float32
    )
    gate_grad = act_grad * up_part * sigmoid_gate * (1.0 + gate_part * (1.0 - sigmoid_gate))
    gate_up_grad = jnp.concatenate([gate_grad, act_grad * silu_gate], axis=-1).astype(jnp.bfloat16)
    gate_up_wgrad = jnp.einsum(
        "secd,secf->edf", received, gate_up_grad, preferred_element_type=jnp.float32
    )
    input_slots = jnp.einsum(
        "secf,edf->secd", gate_up_grad, gate_up_weight, preferred_element_type=jnp.float32
    ).astype(jnp.bfloat16)
    sent_back = lax.all_to_all(input_slots, "expert", split_axis=0, concat_axis=0, tiled=True)
    normed_ffn_grad = jnp.sum(
        sent_back.reshape(total_experts * capacity, D)[target]
        .astype(jnp.float32)
        .reshape(rows_here, TOP, D),
        axis=1,
    )
    middle_norm_grad, gain_ffn_grad = norm_back(middle, inverse_ffn, gain_ffn, normed_ffn_grad)
    middle_grad = out_grad + middle_norm_grad
    branch_grad = middle_grad.astype(jnp.bfloat16)
    out_wgrad = jnp.einsum("ta,tc->ac", attended, branch_grad, preferred_element_type=jnp.float32)
    attended_grad = jnp.einsum(
        "tc,ac->ta", branch_grad, out_weight, preferred_element_type=jnp.float32
    )
    attended_grad = attended_grad.astype(jnp.bfloat16).reshape(
        rows_here, KV_HEADS, group_size, HEAD_DIM
    )
    scores = masked_scores(queries, key_rows, allowed, score_scale)
    probs = jnp.exp(scores - log_total)
    probs_low = probs.astype(jnp.bfloat16)
    prob_grad = jnp.einsum(
        "qhgd,khd->hgqk", attended_grad, value_rows, preferred_element_type=jnp.float32
    )
    row_dot = jnp.sum(probs * prob_grad, axis=-1, keepdims=True)
    score_grad = (probs * (prob_grad - row_dot)).astype(jnp.bfloat16)
    query_grad = (
        jnp.einsum("hgqk,khd->qhgd", score_grad, key_rows, preferred_element_type=jnp.float32)
        * score_scale
    )
    key_grad = (
        jnp.einsum("hgqk,qhgd->khd", score_grad, queries, preferred_element_type=jnp.float32)
        * score_scale
    )
    value_grad = jnp.einsum(
        "hgqk,qhgd->khd", probs_low, attended_grad, preferred_element_type=jnp.float32
    )
    projected_grad = jnp.concatenate(
        [
            rotate_back(
                query_grad.reshape(rows_here, HEADS, HEAD_DIM), cos_table, sine_table
            ).reshape(rows_here, att_width),
            rotate_back(key_grad, cos_table, sine_table).reshape(rows_here, kv_width),
            value_grad.reshape(rows_here, kv_width),
        ],
        axis=1,
    ).astype(jnp.bfloat16)
    qkv_wgrad = jnp.einsum("tc,tq->cq", normed, projected_grad, preferred_element_type=jnp.float32)
    normed_grad = jnp.einsum(
        "tq,cq->tc", projected_grad, qkv_weight, preferred_element_type=jnp.float32
    )
    hidden_norm_grad, gain_attn_grad = norm_back(hidden_in, inverse_attn, gain_attn, normed_grad)
    input_grad = middle_grad + hidden_norm_grad
    gains_grad = jnp.stack([gain_attn_grad, gain_ffn_grad])
    dp_count = lax.axis_size("dp")
    dp_index = lax.axis_index("dp")
    gateup_part, down_part = (
        lax.psum_scatter(gate_up_wgrad, "dp", scatter_dimension=1, tiled=True),
        lax.psum_scatter(down_wgrad, "dp", scatter_dimension=1, tiled=True),
    )
    gateup_square = gateup_part * gateup_part + EPS_STAT
    gateup_rows_new = STAT_DECAY * own_share(gateup_rows, dp_count, dp_index, 1) + (
        1.0 - STAT_DECAY
    ) * jnp.mean(gateup_square, axis=-1)
    down_square = down_part * down_part + EPS_STAT
    down_rows_new = STAT_DECAY * own_share(down_rows, dp_count, dp_index, 1) + (
        1.0 - STAT_DECAY
    ) * jnp.mean(down_square, axis=-1)
    qkv_full, out_full, gains_full = lax.psum((qkv_wgrad, out_wgrad, gains_grad), ("dp", "expert"))
    qkv_square = qkv_full * qkv_full + EPS_STAT
    qkv_cols_new = STAT_DECAY * qkv_cols + (1.0 - STAT_DECAY) * jnp.mean(qkv_square, axis=0)
    qkv_rows_all = STAT_DECAY * qkv_rows + (1.0 - STAT_DECAY) * jnp.mean(qkv_square, axis=1)
    qkv_row_mean = jnp.mean(qkv_rows_all)
    qkv_own = own_share(qkv_full, dp_count, dp_index, 0)
    qkv_rows_new = own_share(qkv_rows_all, dp_count, dp_index, 0)
    out_square = out_full * out_full + EPS_STAT
    out_cols_new = STAT_DECAY * out_cols + (1.0 - STAT_DECAY) * jnp.mean(out_square, axis=0)
    out_rows_all = STAT_DECAY * out_rows + (1.0 - STAT_DECAY) * jnp.mean(out_square, axis=1)
    out_row_mean = jnp.mean(out_rows_all)
    out_own = own_share(out_full, dp_count, dp_index, 0)
    out_rows_new = own_share(out_rows_all, dp_count, dp_index, 0)
    gains_own = own_share(gains_full, dp_count, dp_index, 1)
    gateup_col_sum, gateup_row_sum, down_col_sum, down_row_sum = lax.psum(
        (
            jnp.sum(gateup_square, axis=1),
            jnp.sum(gateup_rows_new, axis=1),
            jnp.sum(down_square, axis=1),
            jnp.sum(down_rows_new, axis=1),
        ),
        "dp",
    )
    gateup_cols_new = STAT_DECAY * gateup_cols + (1.0 - STAT_DECAY) * (gateup_col_sum / D)
    gateup_row_mean = gateup_row_sum / D
    gateup_step = (
        gateup_part
        * lax.rsqrt(gateup_rows_new / gateup_row_mean[:, None])[:, :, None]
        * lax.rsqrt(gateup_cols_new)[:, None, :]
    )
    down_cols_new = STAT_DECAY * down_cols + (1.0 - STAT_DECAY) * (down_col_sum / FF)
    down_row_mean = down_row_sum / FF
    down_step = (
        down_part
        * lax.rsqrt(down_rows_new / down_row_mean[:, None])[:, :, None]
        * lax.rsqrt(down_cols_new)[:, None, :]
    )
    qkv_step = (
        qkv_own * lax.rsqrt(qkv_rows_new / qkv_row_mean)[:, None] * lax.rsqrt(qkv_cols_new)[None, :]
    )
    out_step = (
        out_own * lax.rsqrt(out_rows_new / out_row_mean)[:, None] * lax.rsqrt(out_cols_new)[None, :]
    )
    gain_moment_new = STAT_DECAY * own_share(gain_moment, dp_count, dp_index, 1) + (
        1.0 - STAT_DECAY
    ) * (gains_own * gains_own + EPS_STAT)
    gains_step = gains_own * lax.rsqrt(gain_moment_new)
    dense_flag = (lax.axis_index("expert") == 0).astype(jnp.float32)
    dense_squares, expert_squares = lax.psum(
        (
            jnp.stack(
                [
                    jnp.sum(gains_step * gains_step),
                    jnp.sum(qkv_step * qkv_step),
                    jnp.sum(out_step * out_step),
                ]
            )
            * dense_flag,
            jnp.stack([jnp.sum(gateup_step * gateup_step), jnp.sum(down_step * down_step)]),
        ),
        ("dp", "expert"),
    )
    element_counts = jnp.array(
        [
            2 * D,
            D * qkv_weight.shape[1],
            att_width * D,
            total_experts * D * 2 * FF,
            total_experts * FF * D,
        ],
        jnp.float32,
    )
    update_rms = jnp.sqrt(jnp.concatenate([dense_squares, expert_squares]) / element_counts)
    factors = LEARN_RATE / jnp.maximum(1.0, update_rms / CLIP_LEVEL)
    gains_update = -factors[0] * gains_step
    qkv_new = (
        own_share(qkv_weight, dp_count, dp_index, 0).astype(jnp.float32) - factors[1] * qkv_step
    )
    out_new = (
        own_share(out_weight, dp_count, dp_index, 0).astype(jnp.float32) - factors[2] * out_step
    )
    gate_up_new = (
        own_share(gate_up_weight, dp_count, dp_index, 1).astype(jnp.float32)
        - factors[3] * gateup_step
    )
    down_new = (
        own_share(down_weight, dp_count, dp_index, 1).astype(jnp.float32) - factors[4] * down_step
    )
    return (
        block_out,
        input_grad,
        update_rms,
        gains_update,
        gain_moment_new,
        qkv_new,
        qkv_rows_new,
        qkv_cols_new,
        out_new,
        out_rows_new,
        out_cols_new,
        gate_up_new,
        gateup_rows_new,
        gateup_cols_new,
        down_new,
        down_rows_new,
        down_cols_new,
    )


def solution(mesh):
    placed = (
        P(("dp", "expert"), None),
        P(("dp", "expert"), None),
        P(("dp", "expert")),
        P(("dp", "expert")),
        P(("dp", "expert")),
        P(("dp", "expert"), None),
        P(("dp", "expert"), None),
        P(),
        P(),
        P(),
        P("expert", None, None),
        P("expert", None, None),
        P(),
        P(),
        P(),
        P(),
        P(),
        P("expert", None),
        P("expert", None),
        P("expert", None),
        P("expert", None),
    )
    return jax.shard_map(
        per_device,
        mesh=mesh,
        in_specs=placed,
        out_specs=(
            P(("dp", "expert"), None),
            P(("dp", "expert"), None),
            P(),
            P(None, "dp"),
            P(None, "dp"),
            P("dp", None),
            P("dp"),
            P(),
            P("dp", None),
            P("dp"),
            P(),
            P("expert", "dp", None),
            P("expert", "dp"),
            P("expert", None),
            P("expert", "dp", None),
            P("expert", "dp"),
            P("expert", None),
        ),
        check_vma=False,
    )
```

profile of v0, /device:TPU:0, one launch (start us, length us, event | category | flops | bytes accessed | tf_op | source)
XLA Modules:
  0.0 1752.8 jit_solution(12310289574372233477)
XLA Ops:
  18.6 9.2 reduce-window.6
  42.9 42.0 %scatter_custom_fusion = bf16[4608,1024]{1,0:T(8,128)(2,1)} fusion(s32[3072]{0:T(1024)S(1)} %bitcast.228, bf16[384,1024]{1,0:T(8,128)(2,1)S(1)} %multiply_convert_fusion.1, s32[3072]{0:T(1024)S(1)} %broadcast_clamp_fusion.1, bf16[]{:T(256)} %constant.51.clone.1), kind=kCustom, calls=%fused_computation.52 | custom fusion | bytes 9437186 | tf_op jit(solution)/shard_map/scatter | solution.py:175
  91.5 20.9 %scatter_custom_fusion.1 = bf16[4608,1024]{1,0:T(8,128)(2,1)} fusion(s32[3072]{0:T(1024)S(1)} %bitcast.229, f32[384,1024]{1,0:T(8,128)S(1)} %copy-done.6, f32[3072]{0:T(1024)S(1)} %mul.634, bf16[]{:T(256)} %constant.51.clone.1), kind=kCustom, calls=%fused_computation.51 | custom fusion | flops 6291456 | bytes 11022338 | tf_op jit(solution)/shard_map/scatter | solution.py:199
  112.4 83.9 %all-to-all-done = bf16[4,8,144,1024]{3,2,1,0:T(8,128)(2,1)} async-done(((bf16[4,8,144,1024]{3,2,1,0:T(8,128)(2,1)}), bf16[4,8,144,1024]{3,2,1,0:T(8,128)(2,1)}, u32[]{:S(2)}, u32[]{:S(2)}) %all-to-all-start) | async-done | bytes 9437216 | tf_op jit(solution)/shard_map/all_to_all | solution.py:178
  202.3 21.0 %fusion.23 = f32[4,8,144,1024]{3,2,0,1:T(8,128)} fusion(bf16[8,1024,1024]{2,1,0:T(8,128)(2,1)} %param.32, bf16[4,8,144,1024]{3,2,1,0:T(8,128)(2,1)} %all-to-all-done), kind=kOutput, calls=%fused_computation.47 | convolution fusion | flops 9663676416 | bytes 45088768 | tf_op jit(solution)/shard_map/secd,edf->secf/dot_general | solution.py:87
  223.3 83.4 %all-to-all-done.2 = bf16[4,8,144,1024]{3,2,1,0:T(8,128)(2,1)} async-done(((bf16[4,8,144,1024]{3,2,1,0:T(8,128)(2,1)}), bf16[4,8,144,1024]{3,2,1,0:T(8,128)(2,1)}, u32[]{:S(2)}, u32[]{:S(2)}) %all-to-all-start.2) | async-done | bytes 9437216 | tf_op jit(solution)/shard_map/all_to_all | solution.py:202
  306.7 23.1 %fusion.11 = (bf16[4,8,144,512]{3,2,0,1:T(8,128)(2,1)}, bf16[4,8,144,512]{3,2,0,1:T(8,128)(2,1)}, bf16[4,8,144,512]{3,2,0,1:T(8,128)(2,1)}) fusion(f32[4,8,144,1024]{3,2,0,1:T(8,128)} %fusion.23, bf16[8,512,1024]{2,1,0:T(8,128)(2,1)} %param.33, bf16[4,8,144,1024]{3,2,1,0:T(8,128)(2,1)} %all-to-all-done.2), kind=kOutput, calls=%fused_computation.25 | convolution fusion | flops 4867227648 | bytes 50855936 | tf_op jit(solution)/shard_map/secd,efd->secf/dot_general | solution.py:203
  329.8 11.5 convert_bitcast_fusion.1
  341.3 9.1 copy.87
  356.7 18.4 %convert_bitcast_fusion = bf16[4,8,144,1024]{3,2,0,1:T(8,128)(2,1)} fusion(bf16[8,1024,1024]{2,1,0:T(8,128)(2,1)} %param.32, bf16[4,8,144,512]{3,2,0,1:T(8,128)(2,1)} %get-tuple-element.62, bf16[4,8,144,512]{3,2,0,1:T(8,128)(2,1)} %get-tuple-element.61), kind=kOutput, calls=%fused_computation.31 | convolution fusion | flops 9687269376 | bytes 35651584 | tf_op jit(solution)/shard_map/secf,edf->secd/dot_general | solution.py:221
  375.1 9.1 copy.91
  384.2 76.8 %all-to-all-done.1 = bf16[4,8,144,1024]{3,2,1,0:T(8,128)(2,1)} async-done(((bf16[4,8,144,1024]{3,2,1,0:T(8,128)(2,1)}), bf16[4,8,144,1024]{3,2,1,0:T(8,128)(2,1)}, u32[]{:S(2)}, u32[]{:S(2)}) %all-to-all-start.1) | async-done | bytes 9437216 | tf_op jit(solution)/shard_map/all_to_all | solution.py:183
  466.9 20.8 %gather_fusion = bf16[3072,1024]{1,0:T(8,128)(2,1)} fusion(bf16[4608,1024]{1,0:T(8,128)(2,1)} %bitcast.27, s32[3072]{0:T(1024)S(1)} %broadcast_clamp_fusion), kind=kCustom, calls=%fused_computation.1 | custom fusion | bytes 12595200 | tf_op jit(solution)/shard_map/gather | solution.py:188
  487.7 83.5 %all-to-all-done.3 = bf16[4,8,144,1024]{3,2,1,0:T(8,128)(2,1)} async-done(((bf16[4,8,144,1024]{3,2,1,0:T(8,128)(2,1)}), bf16[4,8,144,1024]{3,2,1,0:T(8,128)(2,1)}, u32[]{:S(2)}, u32[]{:S(2)}) %all-to-all-start.3) | async-done | bytes 9437216 | tf_op jit(solution)/shard_map/all_to_all | solution.py:224
  571.3 20.8 %gather_fusion.1 = bf16[3072,1024]{1,0:T(8,128)(2,1)} fusion(bf16[4608,1024]{1,0:T(8,128)(2,1)} %bitcast.35, s32[3072]{0:T(1024)S(1)} %broadcast_clamp_fusion), kind=kCustom, calls=%fused_computation.2 | custom fusion | bytes 12595200 | tf_op jit(solution)/shard_map/gather | solution.py:226
  592.1 12.3 convert_reduce_fusion
  627.7 11.2 fusion.8
  651.4 14.7 convolution_bitcast_fusion.1
  666.1 25.5 %convolution_bitcast_fusion = f32[8,1024,1024]{2,1,0:T(8,128)} fusion(bf16[4,8,144,1024]{3,2,1,0:T(8,128)(2,1)} %all-to-all-done, bf16[4,8,144,512]{3,2,0,1:T(8,128)(2,1)} %get-tuple-element.62, bf16[4,8,144,512]{3,2,0,1:T(8,128)(2,1)} %get-tuple-element.61), kind=kOutput, calls=%fused_computation.9 | convolution fusion | flops 9682550784 | bytes 52428800 | tf_op jit(solution)/shard_map/secd,secf->edf/dot_general | solution.py:218
  698.1 42.7 %psum.63 = f32[2,1024]{1,0:T(2,128)S(1)} all-reduce(f32[2,1024]{1,0:T(2,128)S(1)} %pad_maximum_fusion.9), channel_id=1, replica_groups=mesh['dp'=8,'expert'=4] {'dp','expert'}, use_global_device_ids=true, to_apply=%region_16.17 | all-reduce | flops 2048 | bytes 16384 | tf_op jit(solution)/shard_map/psum | solution.py:291
  742.7 418.4 %all-reduce.6.cloned.1.call-done = (f32[1024,1024]{1,0:T(8,128)}, f32[1024,2048]{1,0:T(8,128)}) async-done(((f32[1024,1024]{1,0:T(8,128)}, f32[1024,2048]{1,0:T(8,128)}), (f32[1024,1024]{1,0:T(8,128)}, f32[1024,2048]{1,0:T(8,128)})) %all-reduce.6.cloned.1.call-update) | async-done | bytes 12582928 | tf_op jit(solution)/shard_map/psum | solution.py:291
  1182.0 419.3 %reduce-scatter.3.cloned.1.call-done = f32[8,128,1024]{2,1,0:T(8,128)} async-done(((f32[8,1024,1024]{2,1,0:T(8,128)}), f32[8,128,1024]{2,1,0:T(8,128)}) %reduce-scatter.3.cloned.1.call-update) | async-done | bytes 4194320 | tf_op jit(solution)/shard_map/reduce_scatter | solution.py:280
  1608.2 67.0 %all-reduce.8.cloned.1.call-done = (f32[8,1024]{1,0:T(8,128)}, f32[8]{0:T(128)}, f32[8,1024]{1,0:T(8,128)}, f32[8]{0:T(128)}) async-done(((f32[8,1024]{1,0:T(8,128)}, f32[8]{0:T(128)}, f32[8,1024]{1,0:T(8,128)}, f32[8]{0:T(128)}), (f32[8,1024]{1,0:T(8,128)}, f32[8]{0:T(128)}, f32[8,1024]{1,0:T(8,128)}, f32[8]{0:T(128)})) %all-reduce.8.cloned.1.call-update) | async-done | bytes 65616 | tf_op jit(solution)/shard_map/psum | solution.py:305
  1687.5 40.2 %all-reduce = (f32[2]{0:T(128)S(1)}, f32[3]{0:T(128)S(1)}) all-reduce(f32[2]{0:T(128)S(1)} %pad_maximum_fusion.10, f32[3]{0:T(128)S(1)} %maximum_multiply_fusion), channel_id=1, replica_groups=mesh['dp'=8,'expert'=4] {'dp','expert'}, use_global_device_ids=true, to_apply=%region_43.44 | all-reduce | flops 5 | bytes 40 | tf_op jit(solution)/shard_map/psum | solution.py:339
  (204 shorter events, 149.0 us)
Async XLA Ops:
  18.2 18.3 %copy-start.13 = (pred[384,384]{0,1:T(8,128)(4,1)}, pred[384,384]{0,1:T(8,128)(4,1)S(1)}, u32[]{:S(2)}) copy-start(pred[384,384]{0,1:T(8,128)(4,1)S(1)} %compare_and_fusion) | copy-start | bytes 442372
  84.9 111.4 %all-to-all-start = ((bf16[4,8,144,1024]{3,2,1,0:T(8,128)(2,1)}), bf16[4,8,144,1024]{3,2,1,0:T(8,128)(2,1)}, u32[]{:S(2)}, u32[]{:S(2)}) async-start(bf16[4,8,144,1024]{3,2,1,0:T(8,128)(2,1)} %bitcast.191), calls=%async_computation | async-start | bytes 18874368 | tf_op jit(solution)/shard_map/all_to_all | solution.py:178
  196.3 110.4 %all-to-all-start.2 = ((bf16[4,8,144,1024]{3,2,1,0:T(8,128)(2,1)}), bf16[4,8,144,1024]{3,2,1,0:T(8,128)(2,1)}, u32[]{:S(2)}, u32[]{:S(2)}) async-start(bf16[4,8,144,1024]{3,2,1,0:T(8,128)(2,1)} %bitcast.190), calls=%async_computation.2 | async-start | bytes 18874368 | tf_op jit(solution)/shard_map/all_to_all | solution.py:202
  350.5 110.6 %all-to-all-start.1 = ((bf16[4,8,144,1024]{3,2,1,0:T(8,128)(2,1)}), bf16[4,8,144,1024]{3,2,1,0:T(8,128)(2,1)}, u32[]{:S(2)}, u32[]{:S(2)}) async-start(bf16[4,8,144,1024]{3,2,1,0:T(8,128)(2,1)} %copy.87), calls=%async_computation.1 | async-start | bytes 18874368 | tf_op jit(solution)/shard_map/all_to_all | solution.py:183
  461.1 110.2 %all-to-all-start.3 = ((bf16[4,8,144,1024]{3,2,1,0:T(8,128)(2,1)}), bf16[4,8,144,1024]{3,2,1,0:T(8,128)(2,1)}, u32[]{:S(2)}, u32[]{:S(2)}) async-start(bf16[4,8,144,1024]{3,2,1,0:T(8,128)(2,1)} %copy.91), calls=%async_computation.3 | async-start | bytes 18874368 | tf_op jit(solution)/shard_map/all_to_all | solution.py:224
  466.8 694.2 %all-reduce.6.cloned.1.call-start = ((), (), s32[]{:S(2)}) async-start(), calls=%async_computation.8 | async-start | bytes 25165824 | tf_op jit(solution)/shard_map/psum | solution.py:291
  592.1 12.8 copy-start.7
  627.7 11.2 copy-start.16
  627.7 11.2 copy-start.18
  651.4 526.7 %reduce-scatter.5.cloned.1.call-start = ((), (), s32[]{:S(2)}) async-start(), calls=%async_computation.7 | async-start | bytes 18874368 | tf_op jit(solution)/shard_map/reduce_scatter | solution.py:281
  666.1 935.3 %reduce-scatter.3.cloned.1.call-start = ((), (), s32[]{:S(2)}) async-start(), calls=%async_computation.6 | async-start | bytes 37748736 | tf_op jit(solution)/shard_map/reduce_scatter | solution.py:280
  691.7 983.5 %all-reduce.8.cloned.1.call-start = ((), (), s32[]{:S(2)}) async-start(), calls=%async_computation.9 | async-start | bytes 133120 | tf_op jit(solution)/shard_map/psum | solution.py:305
  691.8 472.3 %copy-start.45 = (f32[1024]{0:T(1024)S(1)}, f32[1024]{0:T(1024)}, u32[]{:S(2)}) copy-start(f32[1024]{0:T(1024)} %param.37) | copy-start | bytes 12292
  742.0 993.5 %copy-start.48 = (f32[2,128]{1,0:T(2,128)}, f32[2,128]{1,0:T(2,128)S(1)}, u32[]{:S(2)}) copy-start(f32[2,128]{1,0:T(2,128)S(1)} %get-tuple-element.40) | copy-start | bytes 3076
  1164.0 8.8 copy-start.47
  1164.0 11.3 copy-start.44
  1170.4 505.8 %copy-start.36 = (f32[8,1024]{1,0:T(8,128)S(1)}, f32[8,1024]{1,0:T(8,128)}, u32[]{:S(2)}) copy-start(f32[8,1024]{1,0:T(8,128)} %param.40) | copy-start | bytes 98308
  1170.4 505.8 %copy-start.37 = (f32[8,1024]{1,0:T(8,128)S(1)}, f32[8,1024]{1,0:T(8,128)}, u32[]{:S(2)}) copy-start(f32[8,1024]{1,0:T(8,128)} %param.42) | copy-start | bytes 98308
  1182.0 502.4 %copy-start.40 = (f32[8,64]{1,0:T(8,128)}, f32[8,64]{1,0:T(8,128)S(1)}, u32[]{:S(2)}) copy-start(f32[8,64]{1,0:T(8,128)S(1)} %get-tuple-element.60) | copy-start | bytes 6148
  1606.1 81.3 %copy-start.41 = (f32[8,128]{1,0:T(8,128)}, f32[8,128]{1,0:T(8,128)S(1)}, u32[]{:S(2)}) copy-start(f32[8,128]{1,0:T(8,128)S(1)} %get-tuple-element.58) | copy-start | bytes 12292
  1675.2 10.6 copy-start.20
  1680.4 47.3 %copy-start.49 = (f32[5]{0:T(128)S(1)}, f32[5]{0:T(128)}, u32[]{:S(2)}) copy-start(f32[5]{0:T(128)} %constant.127) | copy-start | bytes 64
  1687.5 48.6 %copy-start.5 = (f32[8,64,1024]{2,1,0:T(8,128)S(1)}, f32[8,64,1024]{2,1,0:T(8,128)}, u32[]{:S(2)}) copy-start(f32[8,64,1024]{2,1,0:T(8,128)} %reduce-scatter.5.cloned.1.call-done) | copy-start | bytes 6291460
  1727.7 12.1 copy-start.2
  (34 other events, 93.4 us)
Sparse Core Ops, SparseCore 0:
  651.5 509.5 all-reduce.5
Sparse Core Ops, SparseCore 1:
  666.2 355.4 reduce-scatter.4
  1025.8 575.5 reduce-scatter.2
  1607.1 68.0 all-reduce.7
where the time goes:
time: 1760 us; the launch traced here: 1750 us
  waiting for transfers between devices  1230 us (70%)
  matrix products  161 us (9%)
  other arithmetic  120 us (7%)
  local copies, waits for them, and re-layouts  113 us (6%)
  blocking collectives  82.9 us (5%)
  starting transfers between devices  24.4 us (1%)
  between operations  18.9 us (1%)
    reduce_scatter x1, waiting for transfers between devices, per_device(): lax.psum_scatter(gate_up_wgrad, 'dp', scatter_dimension=1, tiled=True)  419 us
    psum x1, waiting for transfers between devices, per_device(): lax.psum((qkv_wgrad, out_wgrad, gains_grad), ('dp', 'expert'))  418 us
    all_to_all x1, waiting for transfers between devices, per_device(): lax.all_to_all(outgoing, 'expert', split_axis=0, concat_axis=0, tiled=True)  83.9 us
    all_to_all x1, waiting for transfers between devices, per_device(): lax.all_to_all(input_slots, 'expert', split_axis=0, concat_axis=0, tiled=...  83.5 us
    all_to_all x1, waiting for transfers between devices, per_device(): lax.all_to_all(outgoing_grads, 'expert', split_axis=0, concat_axis=0, til...  83.4 us
    all_to_all x1, waiting for transfers between devices, per_device(): lax.all_to_all(produced, 'expert', split_axis=0, concat_axis=0, tiled=True)  76.8 us
    psum x1, waiting for transfers between devices, per_device(): lax.psum((jnp.sum(gateup_square, axis=1), jnp.sum(gateup_rows_new, axis=1...  67 us
    psum x1, blocking collectives, per_device(): lax.psum((qkv_wgrad, out_wgrad, gains_grad), ('dp', 'expert'))  42.7 us
  transfers between devices with their start and end apart: 8, of which 7 were waited for; matrix products, arithmetic and copies ran while one was open for 9% of the time, Pallas kernels for 0%

commit v1 on v0

--- a/solution.py
+++ b/solution.py
@@ -94,6 +94,100 @@
 def own_share(matrix, share_count, share_index, along):
     width = matrix.shape[along] // share_count
     return lax.dynamic_slice_in_dim(matrix, share_index * width, width, along)
+
+
+def swap(values, axis, mask):
+    count = lax.axis_size(axis)
+    return lax.ppermute(values, axis, [(i, i ^ mask) for i in range(count)])
+
+
+def swap_pair(values):
+    return swap(values, "dp", 1)
+
+
+def swap_chip(values):
+    return swap(values, "expert", 2)
+
+
+def swap_core(values):
+    return swap(values, "expert", 1)
+
+
+def gather_group(shard):
+    from_pair = swap_pair(shard)
+    from_chip = swap_chip(shard)
+    half = shard.shape[0] // 2
+    from_both = jnp.concatenate([swap_chip(from_pair[:half]), swap_pair(from_chip[half:])], axis=0)
+    here = [shard, from_chip, from_pair, from_both]
+    out = []
+    for piece in here:
+        out += [piece, swap_core(piece)]
+    return out
+
+
+def plus(a, b):
+    return (a.astype(jnp.float32) + b.astype(jnp.float32)).astype(jnp.bfloat16)
+
+
+def scatter_group(partial):
+    partial = partial.reshape((4, 2) + partial.shape[1:])
+    summed = [plus(partial[i, 0], swap_core(partial[i, 1])) for i in range(4)]
+    half = partial.shape[2] // 2
+    for_chip = jnp.concatenate(
+        [plus(summed[1][:half], swap_pair(summed[3][:half])), summed[1][half:]], axis=0
+    )
+    for_pair = jnp.concatenate(
+        [summed[2][:half], plus(summed[2][half:], swap_chip(summed[3][half:]))], axis=0
+    )
+    return (
+        summed[0].astype(jnp.float32)
+        + swap_chip(for_chip).astype(jnp.float32)
+        + swap_pair(for_pair).astype(jnp.float32)
+    )
+
+
+def by_owner(matrix):
+    count = lax.axis_size("dp")
+    return matrix.reshape(count, matrix.shape[0] // count, matrix.shape[1])
+
+
+def halve(blocks, axis, mask):
+    bit = lax.rem(lax.axis_index(axis) // mask, 2)
+    keep = lax.dynamic_index_in_dim(blocks, bit, 1, keepdims=False)
+    give = lax.dynamic_index_in_dim(blocks, 1 - bit, 1, keepdims=False)
+    return keep, swap(give, axis, mask)
+
+
+def reduce_expert(blocks):
+    count = blocks.shape[0]
+    rest = blocks.shape[1:]
+    low = 2
+    while low < count:
+        keep, got = halve(blocks.reshape((-1, 2, 2) + rest), "dp", low)
+        blocks = plus(keep, got)
+        low *= 2
+    return halve(blocks.reshape((1, 2) + rest), "dp", 1)[0][0], halve(blocks.reshape((1, 2) + rest), "dp", 1)[1][0]
+
+
+def reduce_dense(blocks):
+    count, rows, columns = blocks.shape
+    blocks = blocks.reshape(count, 2, 2, rows // 4, columns)
+    keep, got = halve(jnp.moveaxis(blocks, 2, 1), "expert", 1)
+    keep, got = halve(plus(keep, got), "expert", 2)
+    blocks = plus(keep, got)
+    low = 1
+    while low < count:
+        keep, got = halve(blocks.reshape((-1, 2, 1) + blocks.shape[1:]), "dp", low)
+        blocks = plus(keep, got).reshape((-1,) + blocks.shape[1:])
+        low *= 2
+    mine = blocks[0]
+    chip = lax.axis_index("expert") // 2
+    core = lax.rem(lax.axis_index("expert"), 2)
+    other = swap_chip(mine)
+    both = jnp.where(chip == 0, jnp.stack([mine, other]), jnp.stack([other, mine]))
+    across = swap_core(both)
+    all_four = jnp.where(core == 0, jnp.stack([both, across], 1), jnp.stack([across, both], 1))
+    return all_four.reshape(rows, columns)
 
 
 def per_device(
@@ -162,72 +256,82 @@
     groups = lax.axis_size("expert")
     total_experts = experts_here * groups
     capacity = 3 * rows_here * TOP // (2 * total_experts)
-    flat_ids = expert_ids.reshape(-1)
-    onehot = (flat_ids[:, None] == jnp.arange(total_experts, dtype=jnp.int32)[None, :]).astype(
-        jnp.int32
-    )
-    slot_index = jnp.sum((jnp.cumsum(onehot, axis=0) - onehot) * onehot, axis=1)
-    target = flat_ids * capacity + slot_index
-    source_row = jnp.arange(rows_here * TOP, dtype=jnp.int32) // TOP
-    outgoing = (
-        jnp.zeros((total_experts * capacity, D), jnp.bfloat16)
-        .at[target]
-        .set(normed_ffn[source_row])
-    )
-    outgoing = outgoing.reshape(groups, experts_here, capacity, D)
-    received = lax.all_to_all(outgoing, "expert", split_axis=0, concat_axis=0, tiled=True)
-    gate_up = up_project(received, gate_up_weight)
-    produced = jnp.einsum(
-        "secf,efd->secd", activate(gate_up), down_weight, preferred_element_type=jnp.float32
+    half_experts = experts_here // 2
+    pair_bit = lax.rem(lax.axis_index("dp"), 2)
+    first_local = pair_bit * half_experts
+    first_expert = lax.axis_index("expert") * experts_here + first_local
+    routing = jnp.concatenate([expert_ids.T.astype(jnp.float32), gate_weights.T], axis=0)
+    routes = jnp.stack(gather_group(routing))
+    named_ids = routes[:, :TOP]
+    my_experts = (first_expert + jnp.arange(half_experts, dtype=jnp.int32)).astype(jnp.float32)
+    hits = named_ids[:, None, :, :] == my_experts[None, :, None, None]
+    named = jnp.any(hits, axis=2)
+    weight_of = jnp.sum(jnp.where(hits, routes[:, None, TOP:], 0.0), axis=2)
+    before = (
+        jnp.arange(rows_here, dtype=jnp.int32)[:, None]
+        < jnp.arange(rows_here, dtype=jnp.int32)[None, :]
     ).astype(jnp.bfloat16)
-    returned = lax.all_to_all(produced, "expert", split_axis=0, concat_axis=0, tiled=True)
-    results = (returned, received, gate_up)
-    returned = results[0]
-    received = results[1]
-    picked = (
-        returned.reshape(total_experts * capacity, D)[target]
-        .astype(jnp.float32)
-        .reshape(rows_here, TOP, D)
-    )
-    block_out = middle + jnp.sum(picked * gate_weights[:, :, None], axis=1)
-    slot_grads = (
-        (gate_weights[:, :, None] * out_grad[:, None, :])
-        .reshape(rows_here * TOP, D)
-        .astype(jnp.bfloat16)
-    )
-    outgoing_grads = (
-        jnp.zeros((total_experts * capacity, D), jnp.bfloat16).at[target].set(slot_grads)
-    )
-    outgoing_grads = outgoing_grads.reshape(groups, experts_here, capacity, D)
-    arrived = lax.all_to_all(outgoing_grads, "expert", split_axis=0, concat_axis=0, tiled=True)
-    act_grad = jnp.einsum(
-        "secd,efd->secf", arrived, down_weight, preferred_element_type=jnp.float32
-    )
-    arrived, act_grad = (arrived, act_grad)
-    gate_up = results[2]
-    gate_part = gate_up[..., :FF]
-    up_part = gate_up[..., FF:]
-    sigmoid_gate = jax.nn.sigmoid(gate_part)
-    silu_gate = gate_part * sigmoid_gate
-    activated = (silu_gate * up_part).astype(jnp.bfloat16)
-    down_wgrad = jnp.einsum(
-        "secf,secd->efd", activated, arrived, preferred_element_type=jnp.float32
-    )
-    gate_grad = act_grad * up_part * sigmoid_gate * (1.0 + gate_part * (1.0 - sigmoid_gate))
-    gate_up_grad = jnp.concatenate([gate_grad, act_grad * silu_gate], axis=-1).astype(jnp.bfloat16)
-    gate_up_wgrad = jnp.einsum(
-        "secd,secf->edf", received, gate_up_grad, preferred_element_type=jnp.float32
-    )
-    input_slots = jnp.einsum(
-        "secf,edf->secd", gate_up_grad, gate_up_weight, preferred_element_type=jnp.float32
-    ).astype(jnp.bfloat16)
-    sent_back = lax.all_to_all(input_slots, "expert", split_axis=0, concat_axis=0, tiled=True)
-    normed_ffn_grad = jnp.sum(
-        sent_back.reshape(total_experts * capacity, D)[target]
-        .astype(jnp.float32)
-        .reshape(rows_here, TOP, D),
-        axis=1,
-    )
+    rank = jnp.einsum(
+        "sjt,tu->sju", named.astype(jnp.bfloat16), before, preferred_element_type=jnp.float32
+    )
+    code = jnp.where(named, rank, -1.0)
+    places = jnp.arange(capacity, dtype=jnp.int32).astype(jnp.float32)
+    chosen = code[:, :, None, :] == places[None, None, :, None]
+    slot_weight = jnp.sum(jnp.where(chosen, weight_of[:, :, None, :], 0.0), axis=-1)
+    pick = chosen.astype(jnp.bfloat16)
+    grads_all = jnp.stack(gather_group(out_grad.astype(jnp.bfloat16)))
+    tokens_all = jnp.stack(gather_group(normed_ffn))
+    mixed = None
+    back = None
+    own_parts = []
+    other_parts = []
+    for j in range(half_experts):
+        up_w = lax.dynamic_index_in_dim(gate_up_weight, first_local + j, 0, keepdims=False)
+        down_w = lax.dynamic_index_in_dim(down_weight, first_local + j, 0, keepdims=False)
+        pick_j = pick[:, j]
+        weight_j = slot_weight[:, j][..., None]
+        received = jnp.einsum(
+            "sct,std->scd", pick_j, tokens_all, preferred_element_type=jnp.float32
+        ).astype(jnp.bfloat16)
+        arrived = (
+            jnp.einsum("sct,std->scd", pick_j, grads_all, preferred_element_type=jnp.float32)
+            * weight_j
+        ).astype(jnp.bfloat16)
+        gate_up = jnp.einsum("scd,df->scf", received, up_w, preferred_element_type=jnp.float32)
+        act_grad = jnp.einsum("scd,fd->scf", arrived, down_w, preferred_element_type=jnp.float32)
+        gate_part = gate_up[..., :FF]
+        up_part = gate_up[..., FF:]
+        sigmoid_gate = jax.nn.sigmoid(gate_part)
+        silu_gate = gate_part * sigmoid_gate
+        activated = (silu_gate * up_part).astype(jnp.bfloat16)
+        gate_grad = act_grad * up_part * sigmoid_gate * (1.0 + gate_part * (1.0 - sigmoid_gate))
+        gate_up_grad = jnp.concatenate([gate_grad, act_grad * silu_gate], axis=-1).astype(
+            jnp.bfloat16
+        )
+        down_wgrad = jnp.einsum(
+            "scf,scd->fd", activated, arrived, preferred_element_type=jnp.float32
+        ).astype(jnp.bfloat16)
+        gate_up_wgrad = jnp.einsum(
+            "scd,scf->df", received, gate_up_grad, preferred_element_type=jnp.float32
+        ).astype(jnp.bfloat16)
+        own, other = reduce_expert(
+            jnp.concatenate([by_owner(gate_up_wgrad), by_owner(down_wgrad)], axis=1)
+        )
+        own_parts.append(own)
+        other_parts.append(other)
+        input_slots = jnp.einsum(
+            "scf,df->scd", gate_up_grad, up_w, preferred_element_type=jnp.float32
+        ).astype(jnp.bfloat16)
+        back_j = jnp.einsum("sct,scd->std", pick_j, input_slots, preferred_element_type=jnp.float32)
+        produced = (
+            jnp.einsum("scf,fd->scd", activated, down_w, preferred_element_type=jnp.float32)
+            * weight_j
+        ).astype(jnp.bfloat16)
+        mixed_j = jnp.einsum("sct,scd->std", pick_j, produced, preferred_element_type=jnp.float32)
+        mixed = mixed_j if mixed is None else mixed + mixed_j
+        back = back_j if back is None else back + back_j
+    normed_ffn_grad = scatter_group(back.astype(jnp.bfloat16))
+    block_out = middle + scatter_group(mixed.astype(jnp.bfloat16))
     middle_norm_grad, gain_ffn_grad = norm_back(middle, inverse_ffn, gain_ffn, normed_ffn_grad)
     middle_grad = out_grad + middle_norm_grad
     branch_grad = middle_grad.astype(jnp.bfloat16)
@@ -276,10 +380,13 @@
     gains_grad = jnp.stack([gain_attn_grad, gain_ffn_grad])
     dp_count = lax.axis_size("dp")
     dp_index = lax.axis_index("dp")
-    gateup_part, down_part = (
-        lax.psum_scatter(gate_up_wgrad, "dp", scatter_dimension=1, tiled=True),
-        lax.psum_scatter(down_wgrad, "dp", scatter_dimension=1, tiled=True),
-    )
+    own = jnp.stack(own_parts).astype(jnp.float32)
+    other = jnp.stack(other_parts).astype(jnp.float32)
+    parts = jnp.where(
+        pair_bit == 0, jnp.concatenate([own, other]), jnp.concatenate([other, own])
+    )
+    gateup_part = parts[:, : D // dp_count]
+    down_part = parts[:, D // dp_count :]
     gateup_square = gateup_part * gateup_part + EPS_STAT
     gateup_rows_new = STAT_DECAY * own_share(gateup_rows, dp_count, dp_index, 1) + (
         1.0 - STAT_DECAY
@@ -288,20 +395,34 @@
     down_rows_new = STAT_DECAY * own_share(down_rows, dp_count, dp_index, 1) + (
         1.0 - STAT_DECAY
     ) * jnp.mean(down_square, axis=-1)
-    qkv_full, out_full, gains_full = lax.psum((qkv_wgrad, out_wgrad, gains_grad), ("dp", "expert"))
-    qkv_square = qkv_full * qkv_full + EPS_STAT
-    qkv_cols_new = STAT_DECAY * qkv_cols + (1.0 - STAT_DECAY) * jnp.mean(qkv_square, axis=0)
-    qkv_rows_all = STAT_DECAY * qkv_rows + (1.0 - STAT_DECAY) * jnp.mean(qkv_square, axis=1)
-    qkv_row_mean = jnp.mean(qkv_rows_all)
-    qkv_own = own_share(qkv_full, dp_count, dp_index, 0)
-    qkv_rows_new = own_share(qkv_rows_all, dp_count, dp_index, 0)
-    out_square = out_full * out_full + EPS_STAT
-    out_cols_new = STAT_DECAY * out_cols + (1.0 - STAT_DECAY) * jnp.mean(out_square, axis=0)
-    out_rows_all = STAT_DECAY * out_rows + (1.0 - STAT_DECAY) * jnp.mean(out_square, axis=1)
-    out_row_mean = jnp.mean(out_rows_all)
-    out_own = own_share(out_full, dp_count, dp_index, 0)
-    out_rows_new = own_share(out_rows_all, dp_count, dp_index, 0)
+    dense_own = jnp.concatenate(
+        [reduce_dense(by_owner(qkv_wgrad.astype(jnp.bfloat16))), reduce_dense(by_owner(out_wgrad.astype(jnp.bfloat16)))], axis=1
+    ).astype(jnp.float32)
+    qkv_own = dense_own[:, : qkv_wgrad.shape[1]]
+    out_own = dense_own[:, qkv_wgrad.shape[1] :]
+    qkv_square = qkv_own * qkv_own + EPS_STAT
+    out_square = out_own * out_own + EPS_STAT
+    qkv_rows_new = STAT_DECAY * own_share(qkv_rows, dp_count, dp_index, 0) + (
+        1.0 - STAT_DECAY
+    ) * jnp.mean(qkv_square, axis=1)
+    out_rows_new = STAT_DECAY * own_share(out_rows, dp_count, dp_index, 0) + (
+        1.0 - STAT_DECAY
+    ) * jnp.mean(out_square, axis=1)
+    gains_full = lax.psum(gains_grad, ("dp", "expert"))
     gains_own = own_share(gains_full, dp_count, dp_index, 1)
+    qkv_col_sum, out_col_sum, qkv_row_sum, out_row_sum = lax.psum(
+        (
+            jnp.sum(qkv_square, axis=0),
+            jnp.sum(out_square, axis=0),
+            jnp.sum(qkv_rows_new),
+            jnp.sum(out_rows_new),
+        ),
+        "dp",
+    )
+    qkv_cols_new = STAT_DECAY * qkv_cols + (1.0 - STAT_DECAY) * (qkv_col_sum / D)
+    qkv_row_mean = qkv_row_sum / D
+    out_cols_new = STAT_DECAY * out_cols + (1.0 - STAT_DECAY) * (out_col_sum / att_width)
+    out_row_mean = out_row_sum / att_width
     gateup_col_sum, gateup_row_sum, down_col_sum, down_row_sum = lax.psum(
         (
             jnp.sum(gateup_square, axis=1),

time: 1760 us -> 860 us (0.49)
  waiting for transfers between devices: 1230 us -> 236 us
  blocking collectives: 82.9 us -> 167 us
  matrix products: 161 us -> 231 us
  local copies, waits for them, and re-layouts: 113 us -> 51.2 us
  starting transfers between devices: 24.4 us -> 61.8 us
  other arithmetic: 120 us -> 98.9 us
    psum x2 -> x0, waiting for transfers between devices: 485 us -> none  [the longest x1 418 us: per_device(): lax.psum((qkv_wgrad, out_wgrad, gains_grad), ('dp', 'expert'))]
    reduce_scatter x2 -> x0, waiting for transfers between devices: 419 us -> none  [the longest x1 419 us: per_device(): lax.psum_scatter(gate_up_wgrad, 'dp', scatter_dimension=1, tiled=True)]
    all_to_all x4 -> x0, waiting for transfers between devices: 328 us -> none  [the longest x1 83.9 us: per_device(): lax.all_to_all(outgoing, 'expert', split_axis=0, concat_axis=0, tiled=True)]
    ppermute x0 -> x66, waiting for transfers between devices: none -> 236 us  [swap(): return lax.ppermute(values, axis, [(i, i ^ mask) for i in range(count)])]
    psum x1 -> x2, blocking collectives: 42.7 us -> 130 us  [the longest x1 93.3 us: per_device(): gains_full = lax.psum(gains_grad, ('dp', 'expert'))]
    dot_general x6 -> x33, matrix products: 114 us -> 193 us  [the longest x4 53.6 us: per_device(): jnp.einsum('sct,scd->std', pick_j, input_slots, preferred_element_type=jn...]
    ppermute x0 -> x66, starting transfers between devices: none -> 61.8 us  [swap(): return lax.ppermute(values, axis, [(i, i ^ mask) for i in range(count)])]
    scatter x1 -> x0, local copies, waits for them, and re-layouts: 42 us -> none  [per_device(): outgoing = jnp.zeros((total_experts * capacity, D), jnp.bfloat16).at[targ...]
  transfers between devices with their start and end apart: 8 -> 66, of which waited for: 7 -> 29; matrix products, arithmetic and copies ran while one was open for 9% -> 19% of each run, Pallas kernels for 0% -> 0%
where the time goes in v1:
time: 860 us; the launch traced here: 851 us
  waiting for transfers between devices  236 us (27%)
  matrix products  231 us (27%)
  blocking collectives  167 us (19%)
  other arithmetic  98.9 us (12%)
  starting transfers between devices  61.8 us (7%)
  local copies, waits for them, and re-layouts  51.2 us (6%)
    ppermute x66, waiting for transfers between devices, swap(): return lax.ppermute(values, axis, [(i, i ^ mask) for i in range(count)])  236 us
    psum x1, blocking collectives, per_device(): gains_full = lax.psum(gains_grad, ('dp', 'expert'))  93.3 us
    ppermute x66, starting transfers between devices, swap(): return lax.ppermute(values, axis, [(i, i ^ mask) for i in range(count)])  61.8 us
    dot_general x4, matrix products, per_device(): jnp.einsum('sct,scd->std', pick_j, input_slots, preferred_element_type=jn...  53.6 us
    dot_general x4, matrix products, per_device(): jnp.einsum('sct,scd->std', pick_j, produced, preferred_element_type=jnp.f...  45.5 us
    psum x1, blocking collectives, per_device(): lax.psum((jnp.stack([jnp.sum(gains_step * gains_step), jnp.sum(qkv_step *...  36.9 us
    psum x1, blocking collectives, per_device(): lax.psum((jnp.sum(gateup_square, axis=1), jnp.sum(gateup_rows_new, axis=1...  36.5 us
    convert_element_type x24, other arithmetic, plus(): return (a.astype(jnp.float32) + b.astype(jnp.float32)).astype(jnp.bfloat16)  24 us
  transfers between devices with their start and end apart: 66, of which 29 were waited for; matrix products, arithmetic and copies ran while one was open for 19% of the time, Pallas kernels for 0%

profile of v1, /device:TPU:0, one launch (start us, length us, event | category | flops | bytes accessed | tf_op | source)
XLA Modules:
  0.0 850.6 jit_solution(16303183681391469145)
XLA Ops:
  41.2 15.8 %collective-permute-done.5 = f32[8,384]{1,0:T(8,128)S(1)} collective-permute-done((f32[8,384]{1,0:T(8,128)S(1)}, f32[8,384]{1,0:T(8,128)S(1)}, u32[]{:S(2)}, u32[]{:S(2)}) %collective-permute-start.5) | collective-permute-done | bytes 12320 | tf_op jit(solution)/shard_map/ppermute | solution.py:101
  72.9 12.2 %collective-permute-done.11 = bf16[384,1024]{1,0:T(8,128)(2,1)S(1)} collective-permute-done((bf16[384,1024]{1,0:T(8,128)(2,1)S(1)}, bf16[384,1024]{1,0:T(8,128)(2,1)S(1)}, u32[]{:S(2)}, u32[]{:S(2)}) %collective-permute-start.11) | collective-permute-done | bytes 786464 | tf_op jit(solution)/shard_map/ppermute | solution.py:101
  132.6 10.8 %fusion.21 = f32[8,384,1024]{2,1,0:T(8,128)} fusion(bf16[8,1024,1024]{2,1,0:T(8,128)(2,1)} %param.32, s32[]{:T(128)S(6)} %select_n.238, bf16[8,144,512]{2,1,0:T(8,128)(2,1)} %copy-done.93, bf16[8,144,512]{2,1,0:T(8,128)(2,1)S(1)} %get-tuple-element.70, pred[8,4,144,384]{3,2,0,1:T(8,128)(4,1)S(1)} %broadcast_compare_fusion), kind=kOutput, calls=%fused_computation.75 | convolution fusion | flops 3327787008 | bytes 17481732 | tf_op jit(solution)/shard_map/sct,scd->std/dot_general | solution.py:325
  162.4 11.2 %fusion.25 = f32[8,384,1024]{2,1,0:T(8,128)} fusion(bf16[8,1024,1024]{2,1,0:T(8,128)(2,1)} %param.32, s32[]{:T(128)S(6)} %select_n.237, bf16[8,144,512]{2,1,0:T(8,128)(2,1)} %copy-done.95, bf16[8,144,512]{2,1,0:T(8,128)(2,1)} %copy-done.94, pred[8,4,144,384]{3,2,0,1:T(8,128)(4,1)S(1)} %broadcast_compare_fusion), kind=kOutput, calls=%fused_computation.80 | convolution fusion | flops 3327787008 | bytes 17481732 | tf_op jit(solution)/shard_map/sct,scd->std/dot_general | solution.py:325
  193.8 11.2 %fusion.29 = f32[8,384,1024]{2,1,0:T(8,128)} fusion(bf16[8,1024,1024]{2,1,0:T(8,128)(2,1)} %param.32, s32[]{:T(128)S(6)} %select_n.234, bf16[8,144,512]{2,1,0:T(8,128)(2,1)} %copy-done.97, bf16[8,144,512]{2,1,0:T(8,128)(2,1)} %copy-done.96, pred[8,4,144,384]{3,2,0,1:T(8,128)(4,1)S(1)} %broadcast_compare_fusion), kind=kOutput, calls=%fused_computation.85 | convolution fusion | flops 3327787008 | bytes 17481732 | tf_op jit(solution)/shard_map/sct,scd->std/dot_general | solution.py:325
  209.5 9.2 %fusion.17 = f32[8,384,1024]{2,1,0:T(8,128)} fusion(f32[8,144]{1,0:T(8,128)S(1)} %get-tuple-element.121, bf16[8,144,512]{2,1,0:T(8,128)(2,1)} %get-tuple-element.88, bf16[8,512,1024]{2,1,0:T(8,128)(2,1)} %param.33, s32[]{:T(128)S(6)} %select_n.234, pred[8,4,144,384]{3,2,0,1:T(8,128)(4,1)S(1)} %broadcast_compare_fusion), kind=kOutput, calls=%fused_computation.65 | convolution fusion | flops 2116288512 | bytes 15261700 | tf_op jit(solution)/shard_map/sct,scd->std/dot_general | solution.py:330
  222.9 8.9 %fusion.18 = f32[8,384,1024]{2,1,0:T(8,128)} fusion(f32[8,144]{1,0:T(8,128)S(1)} %get-tuple-element.120, bf16[8,144,512]{2,1,0:T(8,128)(2,1)S(1)} %get-tuple-element.87, bf16[8,512,1024]{2,1,0:T(8,128)(2,1)} %param.33, s32[]{:T(128)S(6)} %select_n.237, pred[8,4,144,384]{3,2,0,1:T(8,128)(4,1)S(1)} %broadcast_compare_fusion), kind=kOutput, calls=%fused_computation.66 | convolution fusion | flops 2116288512 | bytes 15261700 | tf_op jit(solution)/shard_map/sct,scd->std/dot_general | solution.py:330
  235.5 9.2 %fusion.19 = f32[8,384,1024]{2,1,0:T(8,128)} fusion(f32[8,144]{1,0:T(8,128)S(1)} %get-tuple-element.119, bf16[8,144,512]{2,1,0:T(8,128)(2,1)} %get-tuple-element.89, bf16[8,512,1024]{2,1,0:T(8,128)(2,1)} %param.33, s32[]{:T(128)S(6)} %select_n.238, pred[8,4,144,384]{3,2,0,1:T(8,128)(4,1)S(1)} %broadcast_compare_fusion), kind=kOutput, calls=%fused_computation.67 | convolution fusion | flops 2116288512 | bytes 15261700 | tf_op jit(solution)/shard_map/sct,scd->std/dot_general | solution.py:330
  264.3 20.4 %add_convert_fusion = bf16[8,384,1024]{2,1,0:T(8,128)(2,1)} fusion(f32[8,384,1024]{2,1,0:T(8,128)} %fusion.21, f32[8,384,1024]{2,1,0:T(8,128)} %fusion.29, f32[8,384,1024]{2,1,0:T(8,128)} %fusion.25, pred[8,4,144,384]{3,2,0,1:T(8,128)(4,1)S(1)} %broadcast_compare_fusion, bf16[8,1024,1024]{2,1,0:T(8,128)(2,1)} %param.32, s32[]{:T(128)S(6)} %select_n.239, ...), kind=kOutput, calls=%fused_computation | convolution fusion | flops 3340369920 | bytes 48939012 | tf_op jit(solution)/shard_map/sct,scd->std/dot_general | solution.py:325
  288.9 18.1 %add_convert_fusion.1 = bf16[8,384,1024]{2,1,0:T(8,128)(2,1)} fusion(f32[8,384,1024]{2,1,0:T(8,128)} %fusion.19, f32[8,384,1024]{2,1,0:T(8,128)} %fusion.17, f32[8,384,1024]{2,1,0:T(8,128)} %fusion.18, f32[8,144]{1,0:T(8,128)S(1)} %get-tuple-element.118, bf16[8,144,512]{2,1,0:T(8,128)(2,1)} %get-tuple-element.86, bf16[8,512,1024]{2,1,0:T(8,128)(2,1)} %param.33, ...), kind=kOutput, calls=%fused_computation.1 | convolution fusion | flops 2128871424 | bytes 46718980 | tf_op jit(solution)/shard_map/sct,scd->std/dot_general | solution.py:330
  356.6 32.9 %collective-permute-done.56 = bf16[2,2,192,1024]{3,2,1,0:T(8,128)(2,1)S(1)} collective-permute-done((bf16[2,2,192,1024]{3,2,1,0:T(8,128)(2,1)S(1)}, bf16[2,2,192,1024]{3,2,1,0:T(8,128)(2,1)S(1)}, u32[]{:S(2)}, u32[]{:S(2)}) %collective-permute-start.56) | collective-permute-done | bytes 1572896 | tf_op jit(solution)/shard_map/ppermute | solution.py:101
  393.8 29.5 %collective-permute-done.58 = bf16[2,2,192,1024]{3,2,1,0:T(8,128)(2,1)} collective-permute-done((bf16[2,2,192,1024]{3,2,1,0:T(8,128)(2,1)S(1)}, bf16[2,2,192,1024]{3,2,1,0:T(8,128)(2,1)}, u32[]{:S(2)}, u32[]{:S(2)}) %collective-permute-start.58) | collective-permute-done | bytes 1572896 | tf_op jit(solution)/shard_map/ppermute | solution.py:101
  427.2 29.0 %collective-permute-done.60 = bf16[2,2,192,1024]{3,2,1,0:T(8,128)(2,1)} collective-permute-done((bf16[2,2,192,1024]{3,2,1,0:T(8,128)(2,1)S(1)}, bf16[2,2,192,1024]{3,2,1,0:T(8,128)(2,1)}, u32[]{:S(2)}, u32[]{:S(2)}) %collective-permute-start.60) | collective-permute-done | bytes 1572896 | tf_op jit(solution)/shard_map/ppermute | solution.py:101
  486.4 6.8 fusion.110
  493.2 7.5 fusion
  500.6 11.5 %fusion.2 = bf16[8,2,384,384]{2,3,1,0:T(8,128)(2,1)} fusion(f32[8,384,384,2]{2,1,3,0:T(8,128)} %get-tuple-element.136, f32[8,2,384]{2,1,0:T(2,128)S(1)} %get-tuple-element.135, f32[8,2,384]{2,1,0:T(2,128)S(1)} %bitcast.556, f32[8,384,384,2]{2,1,3,0:T(8,128)} %copy-done.4, pred[384,384]{0,1:T(8,128)(4,1)S(1)} %copy-done.44), kind=kLoop, calls=%fused_computation.6 | loop fusion | flops 14155776 | bytes 23789568 | tf_op jit(solution)/shard_map/convert_element_type | solution.py:352
  528.9 93.3 %psum.77 = f32[2,1024]{1,0:T(2,128)S(1)} all-reduce(f32[2,1024]{1,0:T(2,128)S(1)} %pad_maximum_fusion.33), channel_id=1, replica_groups=mesh['dp'=8,'expert'=4] {'dp','expert'}, use_global_device_ids=true, to_apply=%region_12.13 | all-reduce | flops 2048 | bytes 16384 | tf_op jit(solution)/shard_map/psum | solution.py:411
  646.2 8.4 collective-permute-done.64
  654.6 8.2 collective-permute-done.65
  672.6 9.9 %collective-permute-done.48 = bf16[8,32,1024]{2,1,0:T(8,128)(2,1)S(1)} collective-permute-done((bf16[8,32,1024]{2,1,0:T(8,128)(2,1)S(1)}, bf16[8,32,1024]{2,1,0:T(8,128)(2,1)S(1)}, u32[]{:S(2)}, u32[]{:S(2)}) %collective-permute-start.48) | collective-permute-done | bytes 524320 | tf_op jit(solution)/shard_map/ppermute | solution.py:101
  684.6 19.3 %collective-permute-done.41 = bf16[8,32,2048]{2,1,0:T(8,128)(2,1)S(1)} collective-permute-done((bf16[8,32,2048]{2,1,0:T(8,128)(2,1)S(1)}, bf16[8,32,2048]{2,1,0:T(8,128)(2,1)S(1)}, u32[]{:S(2)}, u32[]{:S(2)}) %collective-permute-start.41) | collective-permute-done | bytes 1048608 | tf_op jit(solution)/shard_map/ppermute | solution.py:101
  707.0 10.3 %collective-permute-done.42 = bf16[4,1,32,2048]{3,2,0,1:T(8,128)(2,1)S(1)} collective-permute-done((bf16[4,1,32,2048]{3,2,0,1:T(8,128)(2,1)S(1)}, bf16[4,1,32,2048]{3,2,0,1:T(8,128)(2,1)S(1)}, u32[]{:S(2)}, u32[]{:S(2)}) %collective-permute-start.42) | collective-permute-done | bytes 524320 | tf_op jit(solution)/shard_map/ppermute | solution.py:101
  740.7 36.5 %all-reduce.3 = (f32[8,1024]{1,0:T(8,128)S(1)}, f32[8]{0:T(128)S(1)}, f32[8,1024]{1,0:T(8,128)S(1)}, f32[8]{0:T(128)S(1)}, f32[1024]{0:T(1024)S(1)}, /*index=5*/f32[]{:T(128)}, f32[2048]{0:T(1024)S(1)}, f32[]{:T(128)}) all-reduce(f32[8,1024]{1,0:T(8,128)S(1)} %get-tuple-element.22, ...), channel_id=1, replica_groups=mesh['dp'=8,'expert'=4] {'dp'}, use_global_device_ids=true, to_apply=%region_37.38 | all-reduce | flops 19474 | bytes 155792 | tf_op jit(solution)/shard_map/psum | solution.py:426
  795.4 36.9 %all-reduce = (f32[2]{0:T(128)S(1)}, f32[3]{0:T(128)S(1)}) all-reduce(f32[2]{0:T(128)S(1)} %pad_maximum_fusion.34, f32[3]{0:T(128)S(1)} %maximum_multiply_fusion), channel_id=1, replica_groups=mesh['dp'=8,'expert'=4] {'dp','expert'}, use_global_device_ids=true, to_apply=%region_39.40 | all-reduce | flops 5 | bytes 40 | tf_op jit(solution)/shard_map/psum | solution.py:460
  (548 shorter events, 378.2 us)
Async XLA Ops:
  2.8 36.7 %collective-permute-start.1 = (f32[16,384]{1,0:T(8,128)}, f32[16,384]{1,0:T(8,128)}, u32[]{:S(2)}, u32[]{:S(2)}) collective-permute-start(f32[16,384]{1,0:T(8,128)} %pad_maximum_fusion.28), channel_id=1, source_target_pairs={{0,2},{1,3},{2,0},{3,1},{4,6},{5,7},{6,4},{7,5},{8,10},{9,11},{10,... | collective-permute-start | bytes 73736 | tf_op jit(solution)/shard_map/ppermute | solution.py:101
  5.8 30.2 %collective-permute-start = (f32[16,384]{1,0:T(8,128)}, f32[16,384]{1,0:T(8,128)}, u32[]{:S(2)}, u32[]{:S(2)}) collective-permute-start(f32[16,384]{1,0:T(8,128)} %pad_maximum_fusion.28), channel_id=1, source_target_pairs={{0,1},{1,0},{2,3},{3,2},{4,5},{5,4},{6,7},{7,6},{8,9},{9,8},{10,11... | collective-permute-start | bytes 73736 | tf_op jit(solution)/shard_map/ppermute | solution.py:101
  5.8 31.2 %collective-permute-start.3 = (f32[16,384]{1,0:T(8,128)}, f32[16,384]{1,0:T(8,128)}, u32[]{:S(2)}, u32[]{:S(2)}) collective-permute-start(f32[16,384]{1,0:T(8,128)} %pad_maximum_fusion.28), channel_id=1, source_target_pairs={{0,4},{4,0},{8,12},{12,8},{16,20},{20,16},{24,28},{28,24},{1,5},{5... | collective-permute-start | bytes 73736 | tf_op jit(solution)/shard_map/ppermute | solution.py:101
  10.1 58.0 %collective-permute-start.25 = (bf16[384,1024]{1,0:T(8,128)(2,1)}, bf16[384,1024]{1,0:T(8,128)(2,1)}, u32[]{:S(2)}, u32[]{:S(2)}) collective-permute-start(bf16[384,1024]{1,0:T(8,128)(2,1)} %get-tuple-element.61), channel_id=1, source_target_pairs={{0,2},{1,3},{2,0},{3,1},{4,6},{5,7},{6,4},{7,5},{8,10},{9,11},{10,... | collective-permute-start | bytes 2359304 | tf_op jit(solution)/shard_map/ppermute | solution.py:101
  10.6 76.2 %collective-permute-start.24 = (bf16[384,1024]{1,0:T(8,128)(2,1)}, bf16[384,1024]{1,0:T(8,128)(2,1)}, u32[]{:S(2)}, u32[]{:S(2)}) collective-permute-start(bf16[384,1024]{1,0:T(8,128)(2,1)} %get-tuple-element.61), channel_id=1, source_target_pairs={{0,1},{1,0},{2,3},{3,2},{4,5},{5,4},{6,7},{7,6},{8,9},{9,8},{10,11... | collective-permute-start | bytes 2359304 | tf_op jit(solution)/shard_map/ppermute | solution.py:101
  36.0 34.7 %collective-permute-start.27 = (bf16[384,1024]{1,0:T(8,128)(2,1)}, bf16[384,1024]{1,0:T(8,128)(2,1)S(1)}, u32[]{:S(2)}, u32[]{:S(2)}) collective-permute-start(bf16[384,1024]{1,0:T(8,128)(2,1)} %get-tuple-element.61), channel_id=1, source_target_pairs={{0,4},{4,0},{8,12},{12,8},{16,20},{20,16},{24,28},{28,24},{1,5},{5... | collective-permute-start | bytes 2359304 | tf_op jit(solution)/shard_map/ppermute | solution.py:101
  37.0 34.1 %collective-permute-start.9 = (bf16[384,1024]{1,0:T(8,128)(2,1)S(1)}, bf16[384,1024]{1,0:T(8,128)(2,1)S(1)}, u32[]{:S(2)}, u32[]{:S(2)}) collective-permute-start(bf16[384,1024]{1,0:T(8,128)(2,1)S(1)} %get-tuple-element.63), channel_id=1, source_target_pairs={{0,2},{1,3},{2,0},{3,1},{4,6},{5,7},{6,4},{7,5},{8,10},{9,11},{10,... | collective-permute-start | bytes 2359304 | tf_op jit(solution)/shard_map/ppermute | solution.py:101
  288.4 30.1 %collective-permute-start.34 = (bf16[384,1024]{1,0:T(8,128)(2,1)}, bf16[384,1024]{1,0:T(8,128)(2,1)}, u32[]{:S(2)}, u32[]{:S(2)}) collective-permute-start(bf16[384,1024]{1,0:T(8,128)(2,1)} %get-tuple-element.74), channel_id=1, source_target_pairs={{0,1},{1,0},{2,3},{3,2},{4,5},{5,4},{6,7},{7,6},{8,9},{9,8},{10,11... | collective-permute-start | bytes 2359304 | tf_op jit(solution)/shard_map/ppermute | solution.py:101
  288.7 31.6 %collective-permute-start.33 = (bf16[384,1024]{1,0:T(8,128)(2,1)}, bf16[384,1024]{1,0:T(8,128)(2,1)}, u32[]{:S(2)}, u32[]{:S(2)}) collective-permute-start(bf16[384,1024]{1,0:T(8,128)(2,1)} %get-tuple-element.75), channel_id=1, source_target_pairs={{0,1},{1,0},{2,3},{3,2},{4,5},{5,4},{6,7},{7,6},{8,9},{9,8},{10,11... | collective-permute-start | bytes 2359304 | tf_op jit(solution)/shard_map/ppermute | solution.py:101
  318.5 37.3 %collective-permute-start.54 = (bf16[2,2,192,1024]{3,2,1,0:T(8,128)(2,1)S(1)}, bf16[2,2,192,1024]{3,2,1,0:T(8,128)(2,1)S(1)}, u32[]{:S(2)}, u32[]{:S(2)}) collective-permute-start(bf16[2,2,192,1024]{3,2,1,0:T(8,128)(2,1)S(1)} %fusion.91), channel_id=1, source_target_pairs={{0,8},{4,12},{8,0},{12,4},{16,24},{20,28},{24,16},{28,20},{1,9},{5... | collective-permute-start | bytes 4718600 | tf_op jit(solution)/shard_map/ppermute | solution.py:101
  320.4 69.1 %collective-permute-start.56 = (bf16[2,2,192,1024]{3,2,1,0:T(8,128)(2,1)S(1)}, bf16[2,2,192,1024]{3,2,1,0:T(8,128)(2,1)S(1)}, u32[]{:S(2)}, u32[]{:S(2)}) collective-permute-start(bf16[2,2,192,1024]{3,2,1,0:T(8,128)(2,1)S(1)} %fusion.87), channel_id=1, source_target_pairs={{0,8},{4,12},{8,0},{12,4},{16,24},{20,28},{24,16},{28,20},{1,9},{5... | collective-permute-start | bytes 4718600 | tf_op jit(solution)/shard_map/ppermute | solution.py:101
  323.4 99.9 %collective-permute-start.58 = (bf16[2,2,192,1024]{3,2,1,0:T(8,128)(2,1)S(1)}, bf16[2,2,192,1024]{3,2,1,0:T(8,128)(2,1)}, u32[]{:S(2)}, u32[]{:S(2)}) collective-permute-start(bf16[2,2,192,1024]{3,2,1,0:T(8,128)(2,1)S(1)} %fusion.83), channel_id=1, source_target_pairs={{0,8},{4,12},{8,0},{12,4},{16,24},{20,28},{24,16},{28,20},{1,9},{5... | collective-permute-start | bytes 4718600 | tf_op jit(solution)/shard_map/ppermute | solution.py:101
  338.4 117.9 %collective-permute-start.60 = (bf16[2,2,192,1024]{3,2,1,0:T(8,128)(2,1)S(1)}, bf16[2,2,192,1024]{3,2,1,0:T(8,128)(2,1)}, u32[]{:S(2)}, u32[]{:S(2)}) collective-permute-start(bf16[2,2,192,1024]{3,2,1,0:T(8,128)(2,1)S(1)} %fusion.79), channel_id=1, source_target_pairs={{0,8},{4,12},{8,0},{12,4},{16,24},{20,28},{24,16},{28,20},{1,9},{5... | collective-permute-start | bytes 4718600 | tf_op jit(solution)/shard_map/ppermute | solution.py:101
  353.9 106.2 %collective-permute-start.32 = (bf16[384,1024]{1,0:T(8,128)(2,1)}, bf16[384,1024]{1,0:T(8,128)(2,1)S(1)}, u32[]{:S(2)}, u32[]{:S(2)}) collective-permute-start(bf16[384,1024]{1,0:T(8,128)(2,1)} %get-tuple-element.72), channel_id=1, source_target_pairs={{0,1},{1,0},{2,3},{3,2},{4,5},{5,4},{6,7},{7,6},{8,9},{9,8},{10,11... | collective-permute-start | bytes 2359304 | tf_op jit(solution)/shard_map/ppermute | solution.py:101
  355.8 111.5 %collective-permute-start.16 = (bf16[384,1024]{1,0:T(8,128)(2,1)S(1)}, bf16[384,1024]{1,0:T(8,128)(2,1)S(1)}, u32[]{:S(2)}, u32[]{:S(2)}) collective-permute-start(bf16[384,1024]{1,0:T(8,128)(2,1)S(1)} %get-tuple-element.79), channel_id=1, source_target_pairs={{0,1},{1,0},{2,3},{3,2},{4,5},{5,4},{6,7},{7,6},{8,9},{9,8},{10,11... | collective-permute-start | bytes 2359304 | tf_op jit(solution)/shard_map/ppermute | solution.py:101
  389.5 74.1 %collective-permute-start.39 = (bf16[384,1024]{1,0:T(8,128)(2,1)S(1)}, bf16[384,1024]{1,0:T(8,128)(2,1)S(1)}, u32[]{:S(2)}, u32[]{:S(2)}) collective-permute-start(bf16[384,1024]{1,0:T(8,128)(2,1)S(1)} %copy-done.62), channel_id=1, source_target_pairs={{0,4},{4,0},{8,12},{12,8},{16,20},{20,16},{24,28},{28,24},{1,5},{5... | collective-permute-start | bytes 2359304 | tf_op jit(solution)/shard_map/ppermute | solution.py:101
  423.3 42.8 %collective-permute-start.36 = (bf16[384,1024]{1,0:T(8,128)(2,1)S(1)}, bf16[384,1024]{1,0:T(8,128)(2,1)S(1)}, u32[]{:S(2)}, u32[]{:S(2)}) collective-permute-start(bf16[384,1024]{1,0:T(8,128)(2,1)S(1)} %copy-done.61), channel_id=1, source_target_pairs={{0,2},{1,3},{2,0},{3,1},{4,6},{5,7},{6,4},{7,5},{8,10},{9,11},{10,... | collective-permute-start | bytes 2359304 | tf_op jit(solution)/shard_map/ppermute | solution.py:101
  463.6 160.1 %collective-permute-start.55 = (bf16[1,2,192,1024]{3,2,1,0:T(8,128)(2,1)}, bf16[1,2,192,1024]{3,2,1,0:T(8,128)(2,1)}, u32[]{:S(2)}, u32[]{:S(2)}) collective-permute-start(bf16[1,2,192,1024]{3,2,1,0:T(8,128)(2,1)} %constant_dynamic-slice_fusion.5), channel_id=1, source_target_pairs={{0,16},{4,20},{8,24},{12,28},{16,0},{20,4},{24,8},{28,12},{1,17},{... | collective-permute-start | bytes 2359304 | tf_op jit(solution)/shard_map/ppermute | solution.py:101
  466.2 159.3 %collective-permute-start.57 = (bf16[1,2,192,1024]{3,2,1,0:T(8,128)(2,1)}, bf16[1,2,192,1024]{3,2,1,0:T(8,128)(2,1)}, u32[]{:S(2)}, u32[]{:S(2)}) collective-permute-start(bf16[1,2,192,1024]{3,2,1,0:T(8,128)(2,1)} %constant_dynamic-slice_fusion.4), channel_id=1, source_target_pairs={{0,16},{4,20},{8,24},{12,28},{16,0},{20,4},{24,8},{28,12},{1,17},{... | collective-permute-start | bytes 2359304 | tf_op jit(solution)/shard_map/ppermute | solution.py:101
  467.3 162.0 %collective-permute-start.59 = (bf16[1,2,192,1024]{3,2,1,0:T(8,128)(2,1)}, bf16[1,2,192,1024]{3,2,1,0:T(8,128)(2,1)}, u32[]{:S(2)}, u32[]{:S(2)}) collective-permute-start(bf16[1,2,192,1024]{3,2,1,0:T(8,128)(2,1)} %constant_dynamic-slice_fusion.3), channel_id=1, source_target_pairs={{0,16},{4,20},{8,24},{12,28},{16,0},{20,4},{24,8},{28,12},{1,17},{... | collective-permute-start | bytes 2359304 | tf_op jit(solution)/shard_map/ppermute | solution.py:101
  475.3 155.9 %collective-permute-start.61 = (bf16[1,2,192,1024]{3,2,1,0:T(8,128)(2,1)}, bf16[1,2,192,1024]{3,2,1,0:T(8,128)(2,1)}, u32[]{:S(2)}, u32[]{:S(2)}) collective-permute-start(bf16[1,2,192,1024]{3,2,1,0:T(8,128)(2,1)} %constant_dynamic-slice_fusion.2), channel_id=1, source_target_pairs={{0,16},{4,20},{8,24},{12,28},{16,0},{20,4},{24,8},{28,12},{1,17},{... | collective-permute-start | bytes 2359304 | tf_op jit(solution)/shard_map/ppermute | solution.py:101
  518.5 146.7 %collective-permute-start.47 = (bf16[8,2,32,1024]{3,2,0,1:T(8,128)(2,1)}, bf16[8,2,32,1024]{3,2,0,1:T(8,128)(2,1)}, u32[]{:S(2)}, u32[]{:S(2)}) collective-permute-start(bf16[8,2,32,1024]{3,2,0,1:T(8,128)(2,1)} %bitcast.480), channel_id=1, source_target_pairs={{0,1},{1,0},{2,3},{3,2},{4,5},{5,4},{6,7},{7,6},{8,9},{9,8},{10,11... | collective-permute-start | bytes 3145736 | tf_op jit(solution)/shard_map/ppermute | solution.py:101
  623.7 45.8 %collective-permute-start.40 = (bf16[8,2,32,2048]{3,2,0,1:T(8,128)(2,1)}, bf16[8,2,32,2048]{3,2,0,1:T(8,128)(2,1)S(1)}, u32[]{:S(2)}, u32[]{:S(2)}) collective-permute-start(bf16[8,2,32,2048]{3,2,0,1:T(8,128)(2,1)} %bitcast.528), channel_id=1, source_target_pairs={{0,1},{1,0},{2,3},{3,2},{4,5},{5,4},{6,7},{7,6},{8,9},{9,8},{10,11... | collective-permute-start | bytes 6291464 | tf_op jit(solution)/shard_map/ppermute | solution.py:101
  670.4 33.6 %collective-permute-start.41 = (bf16[8,32,2048]{2,1,0:T(8,128)(2,1)S(1)}, bf16[8,32,2048]{2,1,0:T(8,128)(2,1)S(1)}, u32[]{:S(2)}, u32[]{:S(2)}) collective-permute-start(bf16[8,32,2048]{2,1,0:T(8,128)(2,1)S(1)} %dynamic-slice_bitcast_fusion), channel_id=1, source_target_pairs={{0,2},{1,3},{2,0},{3,1},{4,6},{5,7},{6,4},{7,5},{8,10},{9,11},{10,... | collective-permute-start | bytes 3145736 | tf_op jit(solution)/shard_map/ppermute | solution.py:101
  (146 other events, 1991.1 us)

commit v2 on v1

v2 whole, which is shorter than its diff:
```python
import functools
import math

import jax
import jax.numpy as jnp
from jax import lax
from jax.experimental import pallas as pl
from jax.experimental.pallas import tpu as pltpu
from jax.sharding import PartitionSpec as P

VM = 60 * 1024 * 1024


def dot(a, b, ca=1, cb=0):
    return lax.dot_general(a, b, (((ca,), (cb,)), ((), ())), preferred_element_type=jnp.float32)


def route_kernel(first_ref, *refs):
    routes, (code_ref, weight_ref, named_ref) = refs[:-3], refs[-3:]
    count = weight_ref.shape[0] // len(routes)
    first = first_ref[0]
    top = routes[0].shape[0] // 2
    rows = routes[0].shape[1]
    for r, route in enumerate(routes):
        ids = route[:top, :]
        gates = route[top:, :]
        for j in range(count):
            hit = ids == (first + j).astype(jnp.float32)
            at = r * count + j
            named_ref[at : at + 1, :] = jnp.max(jnp.where(hit, 1.0, 0.0), axis=0, keepdims=True)
            weight_ref[at : at + 1, :] = jnp.sum(jnp.where(hit, gates, 0.0), axis=0, keepdims=True)
    earlier = lax.broadcasted_iota(jnp.int32, (rows, rows), 0)
    later = lax.broadcasted_iota(jnp.int32, (rows, rows), 1)
    before = jnp.where(earlier < later, 1.0, 0.0).astype(jnp.bfloat16)
    rank = dot(named_ref[...].astype(jnp.bfloat16), before)
    code_ref[...] = jnp.where(named_ref[...] > 0.0, rank, -1.0)


def route_slots(first_expert, routes, count):
    rows = routes[0].shape[1]
    out = jax.ShapeDtypeStruct((len(routes) * count, rows), jnp.float32)
    code, weight = pl.pallas_call(
        route_kernel,
        out_shape=(out, out),
        in_specs=[pl.BlockSpec(memory_space=pltpu.SMEM)]
        + [pl.BlockSpec(memory_space=pltpu.VMEM)] * len(routes),
        out_specs=[pl.BlockSpec(memory_space=pltpu.VMEM)] * 2,
        scratch_shapes=[pltpu.VMEM(out.shape, jnp.float32)],
        compiler_params=pltpu.CompilerParams(vmem_limit_bytes=VM),
        name="route_slots",
    )(first_expert.reshape(1), *routes)
    shape = (len(routes), count, rows)
    return code.reshape(shape), weight.reshape(shape)


def one_hot(code, capacity):
    count, rows = code.shape
    place = lax.broadcasted_iota(jnp.int32, (capacity, rows), 0).astype(jnp.float32)
    return [place == code[j : j + 1, :] for j in range(count)]


def dispatch_kernel(weighted, capacity, *refs):
    code_ref, weight_ref, a_ref, b_ref = refs[:4]
    outs = refs[-2:] if weighted else refs[-1:]
    out_ref = outs[0]
    count = code_ref.shape[1]
    for s, source in enumerate((a_ref, b_ref)):
        chosen = one_hot(code_ref[s], capacity)
        pick = jnp.concatenate([c.astype(jnp.float32) for c in chosen], axis=0).astype(jnp.bfloat16)
        rows = dot(pick, source[...])
        for j in range(count):
            part = rows[j * capacity : (j + 1) * capacity]
            if weighted:
                scale = jnp.sum(
                    jnp.where(chosen[j], weight_ref[s, j : j + 1, :], 0.0), axis=1, keepdims=True
                )
                outs[1][j, s] = scale
                part = part * scale
            out_ref[j, s] = part.astype(jnp.bfloat16)


def dispatch(code, weight, pairs, capacity, weighted):
    sources, count, rows = code.shape
    width = pairs[0][0].shape[1]
    shapes = [jax.ShapeDtypeStruct((count, sources, capacity, width), jnp.bfloat16)]
    if weighted:
        shapes.append(jax.ShapeDtypeStruct((count, sources, capacity, 1), jnp.float32))
    made = []
    for i, (a, b) in enumerate(pairs):
        blocks = [pl.BlockSpec((count, 2, capacity, width), lambda g, i=i: (0, i, 0, 0))]
        if weighted:
            blocks.append(pl.BlockSpec((count, 2, capacity, 1), lambda g, i=i: (0, i, 0, 0)))
        small = pl.BlockSpec((2, count, rows), lambda g, i=i: (i, 0, 0))
        whole = pl.BlockSpec((rows, width), lambda g: (0, 0))
        made = pl.pallas_call(
            functools.partial(dispatch_kernel, weighted, capacity),
            grid=(1,),
            out_shape=shapes,
            in_specs=[small, small, whole, whole] + [pl.BlockSpec(memory_space=pl.ANY)] * len(made),
            out_specs=blocks,
            input_output_aliases={4 + k: k for k in range(len(made))},
            compiler_params=pltpu.CompilerParams(vmem_limit_bytes=VM),
            cost_estimate=pl.CostEstimate(
                flops=4 * count * capacity * rows * width,
                bytes_accessed=4 * rows * width + 4 * count * capacity * width,
                transcendentals=0,
            ),
            name="dispatch_%d%s" % (i, "_w" if weighted else ""),
        )(code, weight, a, b, *made)
    return made


def expert_kernel(owners, s_ref, rec_ref, arr_ref, scale_ref, up_ref, down_ref,
                  keep_ref, give_ref, back_ref, mix_ref, act_s, gug_s, wg_s, wd_s):
    ff = down_ref.shape[1]
    rows, width = act_s.shape[0], up_ref.shape[1]
    tile = rows // 3
    up_w = up_ref[0]
    down_w = down_ref[0]
    received = rec_ref[0].reshape(rows, width)
    arrived = arr_ref[0].reshape(rows, width)
    scale = scale_ref[0].reshape(rows, 1)
    for t in range(3):
        at = slice(t * tile, (t + 1) * tile)
        gate_up = dot(received[at], up_w)
        act_grad = dot(arrived[at], down_w, 1, 1)
        gate = gate_up[:, :ff]
        up = gate_up[:, ff:]
        sig = 1.0 / (1.0 + jnp.exp(-gate))
        silu = gate * sig
        act_s[at, :] = (silu * up).astype(jnp.bfloat16)
        gug_s[at, :ff] = (act_grad * up * sig * (1.0 + gate * (1.0 - sig))).astype(jnp.bfloat16)
        gug_s[at, ff:] = (act_grad * silu).astype(jnp.bfloat16)
    wg_s[...] = dot(received, gug_s[...], 0, 0)
    wd_s[...] = dot(act_s[...], arrived, 0, 0)
    bit = s_ref[1]
    up_rows = width // owners
    down_rows = ff // owners
    for slot in range(owners // 2):
        high, low = slot // 2, slot % 2
        for ref, side in ((keep_ref, bit), (give_ref, 1 - bit)):
            owner = high * 4 + side * 2 + low
            ref[slot, :up_rows, :] = wg_s[
                pl.ds(pl.multiple_of(owner * up_rows, up_rows), up_rows), :
            ].astype(jnp.bfloat16)
            ref[slot, up_rows:, :] = wd_s[
                pl.ds(pl.multiple_of(owner * down_rows, down_rows), down_rows), :
            ].astype(jnp.bfloat16)
    per = rows // rec_ref.shape[1]
    for t in range(3):
        at = slice(t * tile, (t + 1) * tile)
        back = dot(gug_s[at, :], up_w, 1, 1).astype(jnp.bfloat16)
        mix = (dot(act_s[at, :], down_w) * scale[at]).astype(jnp.bfloat16)
        back_ref[at, :] = back
        mix_ref[at, :] = mix


def run_expert(scalars, j, received, arrived, scale, up_w, down_w, owners):
    count, sources, capacity, width = received.shape
    ff = down_w.shape[1]
    rows = sources * capacity
    share = (owners // 2, (width + ff) // owners, width)
    rows_spec = pl.BlockSpec((1, sources, capacity, width), lambda g, s: (j, 0, 0, 0))
    whole2 = lambda *shape: pl.BlockSpec(shape, lambda g, s: (0,) * len(shape))
    slots = jax.ShapeDtypeStruct((rows, width), jnp.bfloat16)
    parts = jax.ShapeDtypeStruct(share, jnp.bfloat16)
    return pl.pallas_call(
        functools.partial(expert_kernel, owners),
        out_shape=(parts, parts, slots, slots),
        grid_spec=pltpu.PrefetchScalarGridSpec(
            num_scalar_prefetch=1,
            grid=(1,),
            in_specs=[
                rows_spec,
                rows_spec,
                pl.BlockSpec((1, sources, capacity, 1), lambda g, s: (j, 0, 0, 0)),
                pl.BlockSpec((1, width, 2 * ff), lambda g, s: (s[0] + j, 0, 0)),
                pl.BlockSpec((1, ff, width), lambda g, s: (s[0] + j, 0, 0)),
            ],
            out_specs=[whole2(*share), whole2(*share), whole2(rows, width), whole2(rows, width)],
            scratch_shapes=[
                pltpu.VMEM((rows, ff), jnp.bfloat16),
                pltpu.VMEM((rows, 2 * ff), jnp.bfloat16),
                pltpu.VMEM((width, 2 * ff), jnp.float32),
                pltpu.VMEM((ff, width), jnp.float32),
            ],
        ),
        compiler_params=pltpu.CompilerParams(vmem_limit_bytes=VM),
        cost_estimate=pl.CostEstimate(
            flops=18 * rows * width * ff, bytes_accessed=16 * width * width, transcendentals=rows * ff
        ),
        name="expert_%d" % j,
    )(scalars, received, arrived, scale, up_w, down_w)


def combine_kernel(capacity, code_ref, *refs):
    slots, (a_ref, b_ref) = refs[:-2], refs[-2:]
    for s, out_ref in enumerate((a_ref, b_ref)):
        chosen = one_hot(code_ref[s], capacity)
        pick = jnp.concatenate([c.astype(jnp.float32) for c in chosen], axis=0).astype(jnp.bfloat16)
        rows = jnp.concatenate([ref[s * capacity : (s + 1) * capacity, :] for ref in slots], axis=0)
        out_ref[...] = dot(pick, rows, 0, 0).astype(jnp.bfloat16)


def combine(code, slots, i, capacity, label):
    sources, count, rows = code.shape
    width = slots[0].shape[1]
    out = jax.ShapeDtypeStruct((rows, width), jnp.bfloat16)
    whole = pl.BlockSpec((rows, width), lambda g: (0, 0))
    return pl.pallas_call(
        functools.partial(combine_kernel, capacity),
        grid=(1,),
        out_shape=(out, out),
        in_specs=[pl.BlockSpec((2, count, rows), lambda g: (i, 0, 0))]
        + [pl.BlockSpec((2 * capacity, width), lambda g: (i, 0))] * count,
        out_specs=[whole, whole],
        compiler_params=pltpu.CompilerParams(vmem_limit_bytes=VM),
        cost_estimate=pl.CostEstimate(
            flops=4 * count * capacity * rows * width,
            bytes_accessed=4 * rows * width + 4 * count * capacity * width,
            transcendentals=0,
        ),
        name="combine_%s_%d" % (label, i),
    )(code, *slots)


HEADS = 16
KV_HEADS = 8
HEAD_DIM = 64
EPS_NORM = 1e-06
ROPE_BASE = 10000.0
MASKED = -1e30
LANES = 128


def spread(row):
    rows = row.shape[1]
    by_column = jnp.broadcast_to(row.astype(jnp.float32), (rows, rows))
    return by_column, by_column.T


def mask_and_angles(ids_ref):
    seg_k, seg_q = spread(ids_ref[0:1, :])
    par_k, par_q = spread(ids_ref[1:2, :])
    pos_k, pos_q = spread(ids_ref[2:3, :])
    seen = ((seg_k == seg_q) | (seg_k == par_q) | (seg_k == par_k)) & (pos_k <= pos_q)
    bias = jnp.where(seen, 0.0, MASKED)
    lane = lax.broadcasted_iota(jnp.int32, (seg_k.shape[0], LANES), 1)
    half = HEAD_DIM // 2
    place = lax.rem(lane, half).astype(jnp.float32)
    frequency = jnp.exp(place * (-2.0 * math.log(ROPE_BASE) / HEAD_DIM))
    angles = pos_q[:, :LANES] * frequency
    front = lax.rem(lane, HEAD_DIM) < half
    sine = jnp.sin(angles)
    return bias, jnp.cos(angles), jnp.where(front, -sine, sine), front, lane


def turned(block, cosine, sine, front):
    other = jnp.where(
        front,
        pltpu.roll(block, LANES - HEAD_DIM // 2, 1),
        pltpu.roll(block, HEAD_DIM // 2, 1),
    )
    return block * cosine + other * sine


def two_diagonal(pair, which, lane):
    rolled = pltpu.roll(pair, HEAD_DIM, 1)
    first, last = (pair, rolled) if which == 0 else (rolled, pair)
    low = lane < HEAD_DIM
    return jnp.concatenate(
        [jnp.where(low, first, 0.0), jnp.where(low, 0.0, last)], axis=0
    ).astype(jnp.bfloat16)


def column_block(index):
    return pl.ds(pl.multiple_of(index * LANES, LANES), LANES)


def attend_kernel(hidden_ref, ids_ref, gains_ref, qkv_w_ref, out_w_ref,
                  normed_ref, qkv_ref, attended_ref, lse_ref, middle_ref, normed_f_ref, proj_s, bias_s):
    rows = hidden_ref.shape[0]
    att = HEADS * HEAD_DIM
    kv = KV_HEADS * HEAD_DIM
    hidden = hidden_ref[...]
    gains = gains_ref[...].astype(jnp.float32)
    inverse = lax.rsqrt(jnp.mean(hidden * hidden, axis=-1, keepdims=True) + EPS_NORM)
    normed_ref[...] = (hidden * inverse * gains[0:1, :]).astype(jnp.bfloat16)
    proj_s[...] = dot(normed_ref[...], qkv_w_ref[...])
    bias, cosine, sine, front, lane = mask_and_angles(ids_ref)
    bias_s[...] = bias
    lse_ref[...] = jnp.zeros_like(lse_ref)

    def pair_step(p, carry):
        key_at = column_block(att // LANES + p)
        value_at = column_block((att + kv) // LANES + p)
        keys = turned(proj_s[:, key_at], cosine, sine, front).astype(jnp.bfloat16)
        values = proj_s[:, value_at].astype(jnp.bfloat16)
        qkv_ref[:, key_at] = keys
        qkv_ref[:, value_at] = values
        keys = keys.astype(jnp.float32)
        values = values.astype(jnp.float32)
        for which in range(2):
            query_at = column_block(2 * p + which)
            queries = turned(proj_s[:, query_at], cosine, sine, front).astype(jnp.bfloat16)
            queries = (queries.astype(jnp.float32) * HEAD_DIM**-0.5).astype(jnp.bfloat16)
            qkv_ref[:, query_at] = queries
            scores = dot(queries, two_diagonal(keys, which, lane), 1, 1)
            probs = []
            for head in range(2):
                part = scores[:, head * rows : (head + 1) * rows] + bias_s[...]
                top = jnp.max(part, axis=-1, keepdims=True)
                part = jnp.exp(part - top)
                total = jnp.sum(part, axis=-1, keepdims=True)
                probs.append((part * (1.0 / total)).astype(jnp.bfloat16))
                at = 4 * p + 2 * which + head
                lse_ref[...] = jnp.where(lane == at, top + jnp.log(total), lse_ref[...])
            attended_ref[:, query_at] = dot(
                jnp.concatenate(probs, axis=1), two_diagonal(values, which, lane)
            ).astype(jnp.bfloat16)
        return carry

    lax.fori_loop(0, KV_HEADS // 2, pair_step, 0)
    middle = hidden + dot(attended_ref[...], out_w_ref[...])
    middle_ref[...] = middle
    inverse_f = lax.rsqrt(jnp.mean(middle * middle, axis=-1, keepdims=True) + EPS_NORM)
    normed_f_ref[...] = (middle * inverse_f * gains[1:2, :]).astype(jnp.bfloat16)


def attend(hidden, ids, gains, qkv_w, out_w):
    rows, width = hidden.shape
    shape = jax.ShapeDtypeStruct
    return pl.pallas_call(
        attend_kernel,
        out_shape=(
            shape((rows, width), jnp.bfloat16),
            shape((rows, qkv_w.shape[1]), jnp.bfloat16),
            shape((rows, out_w.shape[0]), jnp.bfloat16),
            shape((rows, LANES), jnp.float32),
            shape((rows, width), jnp.float32),
            shape((rows, width), jnp.bfloat16),
        ),
        in_specs=[pl.BlockSpec(memory_space=pltpu.VMEM)] * 5,
        out_specs=[pl.BlockSpec(memory_space=pltpu.VMEM)] * 6,
        scratch_shapes=[
            pltpu.VMEM((rows, qkv_w.shape[1]), jnp.float32),
            pltpu.VMEM((rows, rows), jnp.float32),
        ],
        compiler_params=pltpu.CompilerParams(vmem_limit_bytes=VM),
        cost_estimate=pl.CostEstimate(
            flops=10 * rows * width * width, bytes_accessed=12 * width * width, transcendentals=HEADS * rows * rows
        ),
        name="attend",
    )(hidden, ids, gains, qkv_w, out_w)


def attend_back_kernel(hidden_ref, grad_ref, middle_ref, a_ref, b_ref, c_ref, normed_ref, qkv_ref, attended_ref, lse_ref,
                       ids_ref, gains_ref, qkv_w_ref, out_w_ref, input_grad_ref, dense_ref, proj_s, bias_s, back_s):
    rows, width = hidden_ref.shape
    att = HEADS * HEAD_DIM
    kv = KV_HEADS * HEAD_DIM
    gains = gains_ref[...].astype(jnp.float32)
    normed_grad = (
        a_ref[...].astype(jnp.float32) + b_ref[...].astype(jnp.float32) + c_ref[...].astype(jnp.float32)
    )
    middle = middle_ref[...]
    inverse_f = lax.rsqrt(jnp.mean(middle * middle, axis=-1, keepdims=True) + EPS_NORM)
    gain_f = jnp.sum(normed_grad * middle * inverse_f, axis=0, keepdims=True)
    weighted = normed_grad * gains[1:2, :]
    middle_grad = grad_ref[...] + (
        inverse_f * weighted
        - middle * (inverse_f * inverse_f * inverse_f)
        * jnp.mean(weighted * middle, axis=-1, keepdims=True)
    )
    input_grad_ref[...] = middle_grad
    branch = middle_grad.astype(jnp.bfloat16)
    columns = att + 2 * kv
    dense_ref[:, columns : columns + width] = dot(attended_ref[...], branch, 0, 0).astype(jnp.bfloat16)
    back_s[...] = dot(branch, out_w_ref[...], 1, 1).astype(jnp.bfloat16)
    bias, cosine, sine, front, lane = mask_and_angles(ids_ref)
    bias_s[...] = bias
    low = lane < HEAD_DIM

    def pair_step(p, carry):
        key_at = column_block(att // LANES + p)
        value_at = column_block((att + kv) // LANES + p)
        keys = qkv_ref[:, key_at].astype(jnp.float32)
        values = qkv_ref[:, value_at].astype(jnp.float32)
        key_grads = []
        value_grads = []
        for which in range(2):
            query_at = column_block(2 * p + which)
            queries = qkv_ref[:, query_at]
            back = back_s[:, query_at]
            key_two = two_diagonal(keys, which, lane)
            scores = dot(queries, key_two, 1, 1)
            prob_grads = dot(back, two_diagonal(values, which, lane), 1, 1)
            probs = []
            score_grads = []
            for head in range(2):
                at = 4 * p + 2 * which + head
                level = jnp.sum(jnp.where(lane == at, lse_ref[...], 0.0), axis=-1, keepdims=True)
                span = slice(head * rows, (head + 1) * rows)
                prob = jnp.exp(scores[:, span] + bias_s[...] - level)
                prob_grad = prob_grads[:, span]
                row_dot = jnp.sum(prob * prob_grad, axis=-1, keepdims=True)
                probs.append(prob.astype(jnp.bfloat16))
                score_grads.append((prob * (prob_grad - row_dot)).astype(jnp.bfloat16))
            score_grads = jnp.concatenate(score_grads, axis=1)
            query_grad = dot(score_grads, key_two) * HEAD_DIM**-0.5
            proj_s[:, query_at] = turned(query_grad, cosine, -sine, front).astype(jnp.bfloat16)
            for grads, left, right in (
                (key_grads, score_grads, queries),
                (value_grads, jnp.concatenate(probs, axis=1), back),
            ):
                both = dot(left, right, 0, 0)
                first, last = both[:rows], both[rows:]
                if which == 0:
                    grads.append(first + pltpu.roll(last, HEAD_DIM, 1))
                else:
                    grads.append(pltpu.roll(first, HEAD_DIM, 1) + last)
        key_grad = jnp.where(low, key_grads[0], key_grads[1])
        proj_s[:, key_at] = turned(key_grad, cosine, -sine, front).astype(jnp.bfloat16)
        proj_s[:, value_at] = jnp.where(low, value_grads[0], value_grads[1]).astype(jnp.bfloat16)
        return carry

    lax.fori_loop(0, KV_HEADS // 2, pair_step, 0)
    dense_ref[:, :columns] = dot(normed_ref[...], proj_s[...], 0, 0).astype(jnp.bfloat16)
    normed_grad = dot(proj_s[...], qkv_w_ref[...], 1, 1)
    hidden = hidden_ref[...]
    inverse = lax.rsqrt(jnp.mean(hidden * hidden, axis=-1, keepdims=True) + EPS_NORM)
    gain_a = jnp.sum(normed_grad * hidden * inverse, axis=0, keepdims=True)
    weighted = normed_grad * gains[0:1, :]
    input_grad_ref[...] += inverse * weighted - hidden * (inverse * inverse * inverse) * jnp.mean(
        weighted * hidden, axis=-1, keepdims=True
    )
    both = jnp.concatenate([gain_a, gain_f, jnp.zeros((LANES - 2, width), jnp.float32)], axis=0)
    dense_ref[:, columns + width :] = both.T.astype(jnp.bfloat16)


def attend_back(hidden, out_grad, middle, parts, normed, qkv, attended, lse, ids, gains, qkv_w, out_w):
    rows, width = hidden.shape
    columns = qkv_w.shape[1] + width + LANES
    return pl.pallas_call(
        attend_back_kernel,
        out_shape=(
            jax.ShapeDtypeStruct((rows, width), jnp.float32),
            jax.ShapeDtypeStruct((width, columns), jnp.bfloat16),
        ),
        in_specs=[pl.BlockSpec(memory_space=pltpu.VMEM)] * 14,
        out_specs=[pl.BlockSpec(memory_space=pltpu.VMEM)] * 2,
        scratch_shapes=[
            pltpu.VMEM((rows, qkv_w.shape[1]), jnp.bfloat16),
            pltpu.VMEM((rows, rows), jnp.float32),
            pltpu.VMEM((rows, out_w.shape[0]), jnp.bfloat16),
        ],
        compiler_params=pltpu.CompilerParams(vmem_limit_bytes=VM),
        cost_estimate=pl.CostEstimate(
            flops=20 * rows * width * width, bytes_accessed=24 * width * width, transcendentals=HEADS * rows * rows
        ),
        name="attend_back",
    )(hidden, out_grad, middle, *parts, normed, qkv, attended, lse, ids, gains, qkv_w, out_w)


MESH = pl.DeviceIdType.MESH


def greet(peers):
    barrier = pltpu.get_barrier_semaphore()
    for peer in peers:
        pl.semaphore_signal(barrier, inc=1, device_id=peer, device_id_type=MESH)
    pl.semaphore_wait(barrier, len(peers))


def total_kernel(axis, count, mine_ref, out_ref, got_ref, send_sem, recv_sem):
    me = lax.axis_index(axis)
    after = [lax.rem(me + k, count) for k in range(count)]
    greet([{axis: after[k]} for k in range(1, count)])
    scatter = [
        pltpu.make_async_remote_copy(
            src_ref=mine_ref.at[after[k]],
            dst_ref=got_ref.at[k],
            send_sem=send_sem.at[0, k],
            recv_sem=recv_sem.at[0, k],
            device_id={axis: after[k]},
            device_id_type=MESH,
        )
        for k in range(1, count)
    ]
    for copy in scatter:
        copy.start()
    total = mine_ref[me]
    for k in range(1, count):
        scatter[k - 1].wait_recv()
        total = total + got_ref[k]
    out_ref[me] = total
    share = [
        pltpu.make_async_remote_copy(
            src_ref=out_ref.at[me],
            dst_ref=out_ref.at[me],
            send_sem=send_sem.at[1, k],
            recv_sem=recv_sem.at[1, k],
            device_id={axis: after[k]},
            device_id_type=MESH,
        )
        for k in range(1, count)
    ]
    for copy in share:
        copy.start()
    for copy in share:
        copy.wait_recv()
    for copy in scatter + share:
        copy.wait_send()


def total_over(values, axis, label):
    count = lax.axis_size(axis)
    rows = -(-values.shape[0] // (8 * 128 * count)) * 8
    padded = jnp.pad(values, (0, count * rows * 128 - values.shape[0])).reshape(count, rows, 128)
    out = pl.pallas_call(
        functools.partial(total_kernel, axis, count),
        out_shape=jax.ShapeDtypeStruct(padded.shape, jnp.float32),
        in_specs=[pl.BlockSpec(memory_space=pltpu.VMEM)],
        out_specs=pl.BlockSpec(memory_space=pltpu.VMEM),
        scratch_shapes=[
            pltpu.VMEM(padded.shape, jnp.float32),
            pltpu.SemaphoreType.DMA((2, count)),
            pltpu.SemaphoreType.DMA((2, count)),
        ],
        compiler_params=pltpu.CompilerParams(
            collective_id=label, has_side_effects=True, vmem_limit_bytes=16 * 1024 * 1024
        ),
        name="total_%d" % label,
    )(padded)
    return out.reshape(-1)[: values.shape[0]]


def collect_kernel(axis, count, mine_ref, out_ref, send_sem, recv_sem, local_sem):
    me = lax.axis_index(axis)
    after = [lax.rem(me + k, count) for k in range(count)]
    greet([{axis: after[k]} for k in range(1, count)])
    copies = [
        pltpu.make_async_remote_copy(
            src_ref=mine_ref,
            dst_ref=out_ref.at[me],
            send_sem=send_sem.at[k],
            recv_sem=recv_sem.at[k],
            device_id={axis: after[k]},
            device_id_type=MESH,
        )
        for k in range(1, count)
    ]
    for copy in copies:
        copy.start()
    out_ref[me] = mine_ref[...]
    for copy in copies:
        copy.wait()


def collect(values, axis, label):
    count = lax.axis_size(axis)
    return pl.pallas_call(
        functools.partial(collect_kernel, axis, count),
        out_shape=jax.ShapeDtypeStruct((count,) + values.shape, jnp.float32),
        in_specs=[pl.BlockSpec(memory_space=pltpu.VMEM)],
        out_specs=pl.BlockSpec(memory_space=pltpu.VMEM),
        scratch_shapes=[
            pltpu.SemaphoreType.DMA((count,)),
            pltpu.SemaphoreType.DMA((count,)),
            pltpu.SemaphoreType.DMA,
        ],
        compiler_params=pltpu.CompilerParams(
            collective_id=label, has_side_effects=True, vmem_limit_bytes=16 * 1024 * 1024
        ),
        name="collect_%d" % label,
    )(values)


def flipped(axis, mask):
    index = lax.axis_index(axis)
    bit = lax.rem(index // mask, 2)
    return bit, {axis: index + mask - 2 * mask * bit}


def dense_kernel(orders, spans, mine_ref, out_ref, sum_ref, *scratch):
    steps = len(orders[0])
    first_got = scratch[0]
    got = scratch[1 : 1 + steps]
    send_sem, recv_sem = scratch[1 + steps :]
    bits = len(mine_ref.shape) - 4
    core, core_peer = flipped("expert", 1)
    chip, chip_peer = flipped("expert", 2)
    links = [flipped("dp", 1 << b) for b in range(bits)] + [(chip, chip_peer)]
    greet([core_peer] + [peer for _, peer in links])
    whole = (slice(None),) * bits
    copies = []

    def send(src, dst, peer, part, step):
        copy = pltpu.make_async_remote_copy(
            src_ref=src,
            dst_ref=dst,
            send_sem=send_sem.at[part, step],
            recv_sem=recv_sem.at[part, step],
            device_id=peer,
            device_id_type=MESH,
        )
        copy.start()
        copies.append(copy)
        return copy

    def add(first, second):
        return (first.astype(jnp.float32) + second.astype(jnp.float32)).astype(jnp.bfloat16)

    flying = []
    for part, span in enumerate(spans):
        at = whole + (1 - core, slice(None), slice(None), span)
        flying.append(send(mine_ref.at[at], first_got.at[..., span], core_peer, part, 0))

    def place(chosen, span):
        return tuple(chosen.get(bits - 1 - i, slice(None)) for i in range(bits)) + (
            chosen.get(bits, slice(None)),
            slice(None),
            span,
        )

    chosen = [{} for _ in spans]
    for step in range(steps + 1):
        for part, span in enumerate(spans):
            flying[part].wait_recv()
            if step == 0:
                sum_ref[..., span] = add(
                    mine_ref[whole + (core, slice(None), slice(None), span)], first_got[..., span]
                )
            else:
                here = place(chosen[part], span)
                sum_ref[here] = add(sum_ref[here], got[step - 1][part_index(orders, part, step - 1) + (slice(None), span)])
            if step < steps:
                link = orders[part][step]
                bit, peer = links[link]
                away = place({**chosen[part], link: 1 - bit}, span)
                flying[part] = send(
                    sum_ref.at[away],
                    got[step].at[part_index(orders, part, step) + (slice(None), span)],
                    peer,
                    part,
                    1 + step,
                )
                chosen[part] = {**chosen[part], link: bit}
            else:
                out_ref[core, chip, :, span] = sum_ref[place(chosen[part], span)]
                mine = out_ref.at[core, chip, :, span]
                flying[part] = send(mine, mine, chip_peer, part, 1 + steps)
    for part, span in enumerate(spans):
        flying[part].wait_recv()
        mine = out_ref.at[core, :, :, span]
        flying[part] = send(mine, mine, core_peer, part, 2 + steps)
    for copy in flying:
        copy.wait_recv()
    for copy in copies:
        copy.wait_send()


def part_index(orders, part, step):
    return (slice(None),) * (len(orders[part]) - 1 - step)


def reduce_dense(dense, label):
    owners = lax.axis_size("dp")
    width, columns = dense.shape
    bits = owners.bit_length() - 1
    rows = width // owners // 4
    tiles = columns // 128
    parts = bits
    bounds = [128 * (tiles * i // parts) for i in range(parts + 1)]
    spans = [slice(a, b) for a, b in zip(bounds[:-1], bounds[1:])]
    all_links = list(range(bits + 1))
    starts = [bits, 0, 1] + list(range(2, bits))
    orders = [tuple(all_links[s:] + all_links[:s]) for s in starts[:parts]]
    shape = (2,) * bits + (2, 2, rows, columns)
    half = (2,) * bits + (2, rows, columns)
    out = pl.pallas_call(
        functools.partial(dense_kernel, orders, spans),
        out_shape=jax.ShapeDtypeStruct((2, 2, rows, columns), jnp.bfloat16),
        in_specs=[pl.BlockSpec(memory_space=pltpu.VMEM)],
        out_specs=pl.BlockSpec(memory_space=pltpu.VMEM),
        scratch_shapes=[pltpu.VMEM(half, jnp.bfloat16), pltpu.VMEM(half, jnp.bfloat16)]
        + [
            pltpu.VMEM((2,) * (bits - step) + (rows, columns), jnp.bfloat16)
            for step in range(bits + 1)
        ]
        + [pltpu.SemaphoreType.DMA((parts, bits + 4)), pltpu.SemaphoreType.DMA((parts, bits + 4))],
        compiler_params=pltpu.CompilerParams(
            collective_id=label, has_side_effects=True, vmem_limit_bytes=VM
        ),
        name="reduce_dense",
    )(dense.reshape(shape))
    return out.reshape(width // owners, columns)


D = 1024
FF = 512
TOP = 8
EPS_STAT = 1e-30
STAT_DECAY = 0.5
LEARN_RATE = 0.5
CLIP_LEVEL = 0.05


def swap(values, axis, mask):
    count = lax.axis_size(axis)
    return lax.ppermute(values, axis, [(i, i ^ mask) for i in range(count)])


def swap_pair(values):
    return swap(values, "dp", 1)


def swap_chip(values):
    return swap(values, "expert", 2)


def swap_core(values):
    return swap(values, "expert", 1)


def gather_group(shard):
    from_pair = swap_pair(shard)
    from_chip = swap_chip(shard)
    half = shard.shape[0] // 2
    from_both = jnp.concatenate([swap_chip(from_pair[:half]), swap_pair(from_chip[half:])], axis=0)
    return [(piece, swap_core(piece)) for piece in (shard, from_chip, from_pair, from_both)]


def plus(a, b):
    return (a.astype(jnp.float32) + b.astype(jnp.float32)).astype(jnp.bfloat16)


def scatter_group(partials):
    summed = [plus(mine, swap_core(theirs)) for mine, theirs in partials]
    half = summed[3].shape[0] // 2
    for_chip = jnp.concatenate(
        [plus(summed[1][:half], swap_pair(summed[3][:half])), summed[1][half:]], axis=0
    )
    for_pair = jnp.concatenate(
        [summed[2][:half], plus(summed[2][half:], swap_chip(summed[3][half:]))], axis=0
    )
    return summed[0], swap_chip(for_chip), swap_pair(for_pair)


def halve(blocks, axis, mask):
    bit = lax.rem(lax.axis_index(axis) // mask, 2)
    keep = lax.dynamic_index_in_dim(blocks, bit, 1, keepdims=False)
    give = lax.dynamic_index_in_dim(blocks, 1 - bit, 1, keepdims=False)
    return keep, swap(give, axis, mask)


def reduce_expert(keep, give):
    count = lax.axis_size("dp")
    rest = keep.shape[1:]
    blocks = plus(keep, swap(give, "dp", 2))
    low = 4
    while low < count:
        keep, got = halve(blocks.reshape((-1, 2, 2) + rest), "dp", low)
        blocks = plus(keep, got)
        low *= 2
    keep, got = halve(blocks.reshape((1, 2) + rest), "dp", 1)
    return keep[0], got[0]


def reduce_dense_far(blocks):
    count = lax.axis_size("dp")
    width, columns = blocks.shape
    rows = width // count
    blocks = blocks.reshape(count, 2, 2, rows // 4, columns)
    keep, got = halve(jnp.moveaxis(blocks, 2, 1), "expert", 1)
    keep, got = halve(plus(keep, got), "expert", 2)
    blocks = plus(keep, got)
    low = 1
    while low < count:
        keep, got = halve(blocks.reshape((-1, 2, 1) + blocks.shape[1:]), "dp", low)
        blocks = plus(keep, got).reshape((-1,) + blocks.shape[1:])
        low *= 2
    mine = blocks[0]
    chip = lax.axis_index("expert") // 2
    core = lax.rem(lax.axis_index("expert"), 2)
    other = swap_chip(mine)
    both = jnp.where(chip == 0, jnp.stack([mine, other]), jnp.stack([other, mine]))
    across = swap_core(both)
    all_four = jnp.where(core == 0, jnp.stack([both, across], 1), jnp.stack([across, both], 1))
    return all_four.reshape(rows, columns)


def own_share(matrix, along):
    count = lax.axis_size("dp")
    width = matrix.shape[along] // count
    return lax.dynamic_slice_in_dim(matrix, lax.axis_index("dp") * width, width, along)


def decayed(old, new):
    return STAT_DECAY * old + (1.0 - STAT_DECAY) * new


def factored(part, rows_old):
    square = part * part
    rows_new = decayed(rows_old, jnp.mean(square + EPS_STAT, axis=-1))
    return (
        rows_new,
        jnp.sum(square + EPS_STAT, axis=-2),
        jnp.sum(square / rows_new[..., None], axis=-2),
    )


def per_device(
    hidden_in,
    out_grad,
    segment_ids,
    parent_ids,
    positions,
    expert_ids,
    gate_weights,
    norm_gains,
    qkv_weight,
    out_weight,
    gate_up_weight,
    down_weight,
    gain_moment,
    qkv_rows,
    qkv_cols,
    out_rows,
    out_cols,
    gateup_rows,
    gateup_cols,
    down_rows,
    down_cols,
):
    rows_here = hidden_in.shape[0]
    dp_count = lax.axis_size("dp")
    groups = lax.axis_size("expert")
    experts_here = gate_up_weight.shape[0]
    total_experts = experts_here * groups
    capacity = 3 * rows_here * TOP // (2 * total_experts)
    half_experts = experts_here // 2
    dp_index = lax.axis_index("dp")
    pair_bit = lax.rem(dp_index, 2)
    z_bit = lax.rem(dp_index // 2, 2)
    first_local = pair_bit * half_experts
    first_expert = lax.axis_index("expert") * experts_here + first_local

    routing = jnp.concatenate([expert_ids.T.astype(jnp.float32), gate_weights.T], axis=0)
    routes = [r for pair in gather_group(routing) for r in pair]
    code, weight_of = route_slots(first_expert, routes, half_experts)
    grad_pairs = gather_group(out_grad.astype(jnp.bfloat16))
    arrived, scale = dispatch(code, weight_of, grad_pairs, capacity, True)

    ids = jnp.stack([segment_ids, parent_ids, positions])
    normed, qkv, attended, lse, middle, normed_ffn = attend(
        hidden_in, ids, norm_gains, qkv_weight, out_weight
    )
    (received,) = dispatch(code, weight_of, gather_group(normed_ffn), capacity, False)
    scalars = jnp.stack([first_local, z_bit])
    own_parts = []
    other_parts = []
    backs = []
    mixes = []
    for j in range(half_experts):
        keep, give, back, mix = run_expert(
            scalars, j, received, arrived, scale, gate_up_weight, down_weight, dp_count
        )
        own, other = reduce_expert(keep, give)
        own_parts.append(own)
        other_parts.append(other)
        backs.append(back)
        mixes.append(mix)
    places = (3, 1, 2, 0)
    back_parts = {i: combine(code, backs, i, capacity, "back") for i in places}
    grad_parts = scatter_group([back_parts[i] for i in range(4)])
    mix_parts = {i: combine(code, mixes, i, capacity, "mix") for i in places}
    block_out = middle + sum(
        part.astype(jnp.float32) for part in scatter_group([mix_parts[i] for i in range(4)])
    )
    input_grad, dense = attend_back(
        hidden_in, out_grad, middle, grad_parts, normed, qkv, attended, lse, ids, norm_gains, qkv_weight, out_weight
    )

    own = jnp.stack(own_parts).astype(jnp.float32)
    other = jnp.stack(other_parts).astype(jnp.float32)
    parts = jnp.where(pair_bit == 0, jnp.concatenate([own, other]), jnp.concatenate([other, own]))
    gateup_part = parts[:, : D // dp_count]
    down_part = parts[:, D // dp_count :]
    gateup_rows_new, gateup_square, gateup_scaled = factored(gateup_part, own_share(gateup_rows, 1))
    down_rows_new, down_square, down_scaled = factored(down_part, own_share(down_rows, 1))
    sizes = [gateup_square.size, gateup_scaled.size, down_square.size, down_scaled.size]
    summed = total_over(
        jnp.concatenate(
            [
                gateup_square.reshape(-1),
                gateup_scaled.reshape(-1),
                down_square.reshape(-1),
                down_scaled.reshape(-1),
                jnp.sum(gateup_rows_new, axis=1),
                jnp.sum(down_rows_new, axis=1),
            ]
        ),
        "dp",
        1,
    )
    pieces = jnp.split(summed, [sum(sizes[: i + 1]) for i in range(4)])
    gateup_square, gateup_scaled, down_square, down_scaled = [
        p.reshape(experts_here, D) for p in pieces[:4]
    ]
    gateup_row_mean = pieces[4][:experts_here] / D
    down_row_mean = pieces[4][experts_here:] / FF
    gateup_cols_new = decayed(gateup_cols, gateup_square / D)
    down_cols_new = decayed(down_cols, down_square / FF)
    expert_squares = jnp.stack(
        [
            jnp.sum(gateup_row_mean * jnp.sum(gateup_scaled / gateup_cols_new, axis=1)),
            jnp.sum(down_row_mean * jnp.sum(down_scaled / down_cols_new, axis=1)),
        ]
    )
    spread_squares = collect(
        jnp.zeros((8, 128), jnp.float32).at[0, :2].set(expert_squares), "expert", 2
    )
    expert_squares = jnp.sum(spread_squares[:, 0, :2], axis=0)

    qkv_columns = qkv_weight.shape[1]
    if D // dp_count % 64 == 0:
        dense_own = reduce_dense(dense, 3)
    else:
        dense_own = reduce_dense_far(dense)
    dense_own = dense_own.astype(jnp.float32)
    qkv_own = dense_own[:, :qkv_columns]
    out_own = dense_own[:, qkv_columns : qkv_columns + D]
    gains_own = dense_own[:, qkv_columns + D : qkv_columns + D + 2].T
    gain_moment_new = decayed(own_share(gain_moment, 1), gains_own * gains_own + EPS_STAT)
    gains_step = gains_own * lax.rsqrt(gain_moment_new)
    qkv_rows_new, qkv_square, qkv_scaled = factored(qkv_own, own_share(qkv_rows, 0))
    out_rows_new, out_square, out_scaled = factored(out_own, own_share(out_rows, 0))
    dense_sums = total_over(
        jnp.concatenate(
            [
                qkv_square,
                qkv_scaled,
                out_square,
                out_scaled,
                jnp.stack(
                    [jnp.sum(qkv_rows_new), jnp.sum(out_rows_new), jnp.sum(gains_step * gains_step)]
                ),
            ]
        ),
        "dp",
        4,
    )
    qkv_square, qkv_scaled, out_square, out_scaled, rest = jnp.split(
        dense_sums, [qkv_columns, 2 * qkv_columns, 2 * qkv_columns + D, 2 * qkv_columns + 2 * D]
    )
    qkv_row_mean = rest[0] / D
    out_row_mean = rest[1] / D
    qkv_cols_new = decayed(qkv_cols, qkv_square / D)
    out_cols_new = decayed(out_cols, out_square / D)
    squares = jnp.concatenate(
        [
            jnp.stack(
                [
                    rest[2],
                    qkv_row_mean * jnp.sum(qkv_scaled / qkv_cols_new),
                    out_row_mean * jnp.sum(out_scaled / out_cols_new),
                ]
            ),
            expert_squares,
        ]
    )
    element_counts = jnp.array(
        [2 * D, D * qkv_columns, D * D, total_experts * D * 2 * FF, total_experts * FF * D], jnp.float32
    )
    update_rms = jnp.sqrt(squares / element_counts)
    factors = LEARN_RATE / jnp.maximum(1.0, update_rms / CLIP_LEVEL)

    def stepped(weight, part, rows_new, row_mean, cols_new, factor):
        return weight.astype(jnp.float32) - part * (
            factor * lax.rsqrt(rows_new / row_mean[..., None])
        )[..., :, None] * lax.rsqrt(cols_new)[..., None, :]

    return (
        block_out,
        input_grad,
        update_rms,
        -factors[0] * gains_step,
        gain_moment_new,
        stepped(own_share(qkv_weight, 0), qkv_own, qkv_rows_new, qkv_row_mean, qkv_cols_new, factors[1]),
        qkv_rows_new,
        qkv_cols_new,
        stepped(own_share(out_weight, 0), out_own, out_rows_new, out_row_mean, out_cols_new, factors[2]),
        out_rows_new,
        out_cols_new,
        stepped(own_share(gate_up_weight, 1), gateup_part, gateup_rows_new, gateup_row_mean, gateup_cols_new, factors[3]),
        gateup_rows_new,
        gateup_cols_new,
        stepped(own_share(down_weight, 1), down_part, down_rows_new, down_row_mean, down_cols_new, factors[4]),
        down_rows_new,
        down_cols_new,
    )


def solution(mesh):
    placed = (
        P(("dp", "expert"), None),
        P(("dp", "expert"), None),
        P(("dp", "expert")),
        P(("dp", "expert")),
        P(("dp", "expert")),
        P(("dp", "expert"), None),
        P(("dp", "expert"), None),
        P(),
        P(),
        P(),
        P("expert", None, None),
        P("expert", None, None),
        P(),
        P(),
        P(),
        P(),
        P(),
        P("expert", None),
        P("expert", None),
        P("expert", None),
        P("expert", None),
    )
    return jax.shard_map(
        per_device,
        mesh=mesh,
        in_specs=placed,
        out_specs=(
            P(("dp", "expert"), None),
            P(("dp", "expert"), None),
            P(),
            P(None, "dp"),
            P(None, "dp"),
            P("dp", None),
            P("dp"),
            P(),
            P("dp", None),
            P("dp"),
            P(),
            P("expert", "dp", None),
            P("expert", "dp"),
            P("expert", None),
            P("expert", "dp", None),
            P("expert", "dp"),
            P("expert", None),
        ),
        check_vma=False,
    )
```

time: 860 us -> 643 us (0.75)
  Pallas kernels: 0 us -> 305 us
  matrix products: 231 us -> 0 us
  blocking collectives: 167 us -> 0 us
  other arithmetic: 98.9 us -> 54.8 us
  local copies, waits for them, and re-layouts: 51.2 us -> 18.8 us
  starting transfers between devices: 61.8 us -> 38.9 us
  waiting for transfers between devices: 236 us -> 215 us
    pallas_call x0 -> x27, Pallas kernels: none -> 305 us  [the longest x1 90.4 us: reduce_dense(): pl.pallas_call(functools.partial(dense_kernel, orders, spans), out_shape=...]
    dot_general x45 -> x0, matrix products: 231 us -> none  [the longest x4 53.6 us: per_device(): jnp.einsum('sct,scd->std', pick_j, input_slots, preferred_element_type=jn...]
    psum x3 -> x0, blocking collectives: 167 us -> none  [the longest x1 93.3 us: per_device(): gains_full = lax.psum(gains_grad, ('dp', 'expert'))]
    ppermute x66 -> x52, starting transfers between devices: 61.8 us -> 38.9 us  [swap(): return lax.ppermute(values, axis, [(i, i ^ mask) for i in range(count)])]
    ppermute x66 -> x52, waiting for transfers between devices: 236 us -> 215 us  [swap(): return lax.ppermute(values, axis, [(i, i ^ mask) for i in range(count)])]
    unnamed x229 -> x136, local copies, waits for them, and re-layouts: 23.1 us -> 5.42 us
    convert_element_type x24 -> x19, other arithmetic: 24 us -> 13.8 us  [plus(): return (a.astype(jnp.float32) + b.astype(jnp.float32)).astype(jnp.bfloat16)]
    reduce_sum x14, other arithmetic: 16.4 us -> 6.31 us  [the longest x4 1.77 us: factored(): jnp.sum(square / rows_new[..., None], axis=-2)]
  transfers between devices with their start and end apart: 66 -> 52, of which waited for: 29 -> 19; matrix products, arithmetic and copies ran while one was open for 19% -> 6% of each run, Pallas kernels for 0% -> 32%
where the time goes in v2:
time: 643 us; the launch traced here: 638 us
  Pallas kernels  305 us (47%)
  waiting for transfers between devices  215 us (33%)
  other arithmetic  54.8 us (9%)
  starting transfers between devices  38.9 us (6%)
  local copies, waits for them, and re-layouts  18.8 us (3%)
    ppermute x52, waiting for transfers between devices, swap(): return lax.ppermute(values, axis, [(i, i ^ mask) for i in range(count)])  215 us
    pallas_call x1, Pallas kernels, reduce_dense(): pl.pallas_call(functools.partial(dense_kernel, orders, spans), out_shape=...  90.4 us
    pallas_call x4, Pallas kernels, run_expert(): pl.pallas_call(functools.partial(expert_kernel, owners), out_shape=(parts...  74.1 us
    ppermute x52, starting transfers between devices, swap(): return lax.ppermute(values, axis, [(i, i ^ mask) for i in range(count)])  38.9 us
    pallas_call x8, Pallas kernels, dispatch(): pl.pallas_call(functools.partial(dispatch_kernel, weighted, capacity), gr...  34.4 us
    pallas_call x8, Pallas kernels, combine(): pl.pallas_call(functools.partial(combine_kernel, capacity), grid=(1,), ou...  31.5 us
    pallas_call x1, Pallas kernels, attend_back(): pl.pallas_call(attend_back_kernel, out_shape=(jax.ShapeDtypeStruct((rows,...  27 us
    pallas_call x2, Pallas kernels, total_over(): pl.pallas_call(functools.partial(total_kernel, axis, count), out_shape=ja...  24.3 us
  transfers between devices with their start and end apart: 52, of which 19 were waited for; matrix products, arithmetic and copies ran while one was open for 6% of the time, Pallas kernels for 32%

profile of v2, /device:TPU:0, one launch (start us, length us, event | category | flops | bytes accessed | tf_op | source)
XLA Modules:
  0.0 637.9 jit_solution(8775168711111981011)
XLA Ops:
  9.4 18.1 %attend.1 = (bf16[384,1024]{1,0:T(8,128)(2,1)}, bf16[384,2048]{1,0:T(8,128)(2,1)}, bf16[384,1024]{1,0:T(8,128)(2,1)}, f32[384,128]{1,0:T(8,128)}, f32[384,1024]{1,0:T(8,128)}, /*index=5*/bf16[384,1024]{1,0:T(8,128)(2,1)}) custom-call(f32[384,1024]{1,0:T(8,128)} %hidden_ref.3, s32[3,384]{1,0:T(4,128)} %pad_add_fusion.ids_ref, bf16[2,1024]{1,0:T(2,128)(2,1)} %gains_ref.3, ...), custom_call_target="tpu_custom_call" | custom-call | flops 4026531840 | bytes 12582912 | tf_op jit(solution)/shard_map/attend/pallas_call | solution.py:333
  31.6 16.0 %collective-permute-done.5 = f32[8,384]{1,0:T(8,128)S(1)} collective-permute-done((f32[8,384]{1,0:T(8,128)S(1)}, f32[8,384]{1,0:T(8,128)S(1)}, u32[]{:S(2)}, u32[]{:S(2)}) %collective-permute-start.5) | collective-permute-done | bytes 12320 | tf_op jit(solution)/shard_map/ppermute | solution.py:711
  56.0 17.2 %collective-permute-done.18.refs_2_ = bf16[384,1024]{1,0:T(8,128)(2,1)} collective-permute-done((bf16[384,1024]{1,0:T(8,128)(2,1)S(1)}, bf16[384,1024]{1,0:T(8,128)(2,1)}, u32[]{:S(2)}, u32[]{:S(2)}) %collective-permute-start.18) | collective-permute-done | bytes 786464 | tf_op jit(solution)/shard_map/ppermute | solution.py:711
  75.7 5.7 collective-permute-done.17
  83.8 5.3 collective-permute-done.9
  134.0 18.4 %expert_3.1 = (bf16[4,192,1024]{2,1,0:T(8,128)(2,1)}, bf16[4,192,1024]{2,1,0:T(8,128)(2,1)}, bf16[1152,1024]{1,0:T(8,128)(2,1)}, bf16[1152,1024]{1,0:T(8,128)(2,1)}) custom-call(s32[2]{0:T(128)} %pad_add_fusion.1.s_ref, bf16[4,8,144,1024]{3,2,1,0:T(8,128)(2,1)} %dispatch_3.1.rec_ref, bf16[4,8,144,1024]{3,2,1,0:T(8,128)(2,1)} %get-tuple-element.89.arr_ref, ...), custom_call_target="tpu_custom_call" | custom-call | flops 10871635968 | bytes 16777216 | tf_op jit(solution)/shard_map/expert_3/pallas_call | solution.py:167
  152.4 18.5 %expert_2.1 = (bf16[4,192,1024]{2,1,0:T(8,128)(2,1)}, bf16[4,192,1024]{2,1,0:T(8,128)(2,1)}, bf16[1152,1024]{1,0:T(8,128)(2,1)}, bf16[1152,1024]{1,0:T(8,128)(2,1)}) custom-call(s32[2]{0:T(128)} %pad_add_fusion.1.s_ref, bf16[4,8,144,1024]{3,2,1,0:T(8,128)(2,1)} %dispatch_3.1.rec_ref, bf16[4,8,144,1024]{3,2,1,0:T(8,128)(2,1)} %get-tuple-element.89.arr_ref, ...), custom_call_target="tpu_custom_call" | custom-call | flops 10871635968 | bytes 16777216 | tf_op jit(solution)/shard_map/expert_2/pallas_call | solution.py:167
  170.9 18.8 %expert_1.1 = (bf16[4,192,1024]{2,1,0:T(8,128)(2,1)}, bf16[4,192,1024]{2,1,0:T(8,128)(2,1)}, bf16[1152,1024]{1,0:T(8,128)(2,1)}, bf16[1152,1024]{1,0:T(8,128)(2,1)}) custom-call(s32[2]{0:T(128)} %pad_add_fusion.1.s_ref, bf16[4,8,144,1024]{3,2,1,0:T(8,128)(2,1)} %dispatch_3.1.rec_ref, bf16[4,8,144,1024]{3,2,1,0:T(8,128)(2,1)} %get-tuple-element.89.arr_ref, ...), custom_call_target="tpu_custom_call" | custom-call | flops 10871635968 | bytes 16777216 | tf_op jit(solution)/shard_map/expert_1/pallas_call | solution.py:167
  189.7 18.4 %expert_0.1 = (bf16[4,192,1024]{2,1,0:T(8,128)(2,1)}, bf16[4,192,1024]{2,1,0:T(8,128)(2,1)}, bf16[1152,1024]{1,0:T(8,128)(2,1)}, bf16[1152,1024]{1,0:T(8,128)(2,1)}) custom-call(s32[2]{0:T(128)} %pad_add_fusion.1.s_ref, bf16[4,8,144,1024]{3,2,1,0:T(8,128)(2,1)} %dispatch_3.1.rec_ref, bf16[4,8,144,1024]{3,2,1,0:T(8,128)(2,1)} %get-tuple-element.89.arr_ref, ...), custom_call_target="tpu_custom_call" | custom-call | flops 10871635968 | bytes 16777216 | tf_op jit(solution)/shard_map/expert_0/pallas_call | solution.py:167
  255.3 8.8 %collective-permute-done.30 = bf16[192,1024]{1,0:T(8,128)(2,1)S(1)} collective-permute-done((bf16[192,1024]{1,0:T(8,128)(2,1)S(1)}, bf16[192,1024]{1,0:T(8,128)(2,1)S(1)}, u32[]{:S(2)}, u32[]{:S(2)}) %collective-permute-start.30) | collective-permute-done | bytes 393248 | tf_op jit(solution)/shard_map/ppermute | solution.py:711
  267.6 6.4 %collective-permute-done.38 = bf16[192,1024]{1,0:T(8,128)(2,1)S(1)} collective-permute-done((bf16[192,1024]{1,0:T(8,128)(2,1)S(1)}, bf16[192,1024]{1,0:T(8,128)(2,1)S(1)}, u32[]{:S(2)}, u32[]{:S(2)}) %collective-permute-start.38) | collective-permute-done | bytes 393248 | tf_op jit(solution)/shard_map/ppermute | solution.py:711
  277.5 5.8 collective-permute-done.44
  285.5 31.5 %collective-permute-done.42 = bf16[4,192,1024]{2,1,0:T(8,128)(2,1)S(1)} collective-permute-done((bf16[4,192,1024]{2,1,0:T(8,128)(2,1)S(1)}, bf16[4,192,1024]{2,1,0:T(8,128)(2,1)S(1)}, u32[]{:S(2)}, u32[]{:S(2)}) %collective-permute-start.42) | collective-permute-done | bytes 1572896 | tf_op jit(solution)/shard_map/ppermute | solution.py:711
  320.9 29.4 %collective-permute-done.40 = bf16[4,192,1024]{2,1,0:T(8,128)(2,1)S(1)} collective-permute-done((bf16[4,192,1024]{2,1,0:T(8,128)(2,1)S(1)}, bf16[4,192,1024]{2,1,0:T(8,128)(2,1)S(1)}, u32[]{:S(2)}, u32[]{:S(2)}) %collective-permute-start.40) | collective-permute-done | bytes 1572896 | tf_op jit(solution)/shard_map/ppermute | solution.py:711
  355.9 27.0 %attend_back.1 = (f32[384,1024]{1,0:T(8,128)}, bf16[1024,3200]{1,0:T(8,128)(2,1)}) custom-call(f32[384,1024]{1,0:T(8,128)} %hidden_ref.3, f32[384,1024]{1,0:T(8,128)} %grad_ref.1, f32[384,1024]{1,0:T(8,128)} %get-tuple-element.79.middle_ref, bf16[384,1024]{1,0:T(8,128)(2,1)} %add_convert_fusion.7.a_ref, bf16[384,1024]{1,0:T(8,128)(2,1)} %copy-done.62, ...), custom_call_target="tpu_custom_call" | custom-call | flops 8053063680 | bytes 25165824 | tf_op jit(solution)/shard_map/attend_back/pallas_call | solution.py:444
  383.0 90.4 %reduce_dense.1 = bf16[2,2,32,3200]{3,2,1,0:T(8,128)(2,1)} custom-call(bf16[2,2,2,2,2,32,3200]{6,5,4,3,2,1,0:T(8,128)(2,1)} %bitcast.113), custom_call_target="tpu_custom_call" | custom-call | tf_op jit(solution)/shard_map/reduce_dense/pallas_call | solution.py:681
  479.4 10.1 %total_4.1 = f32[8,8,128]{2,1,0:T(8,128)S(1)} custom-call(f32[8,8,128]{2,1,0:T(8,128)S(1)} %pad_bitcast_fusion.mine_ref), custom_call_target="tpu_custom_call" | custom-call | tf_op jit(solution)/shard_map/total_4/pallas_call | solution.py:520
  501.1 47.3 %collective-permute-done.43 = bf16[1,2,192,1024]{3,2,1,0:T(8,128)(2,1)S(1)} collective-permute-done((bf16[1,2,192,1024]{3,2,1,0:T(8,128)(2,1)}, bf16[1,2,192,1024]{3,2,1,0:T(8,128)(2,1)S(1)}, u32[]{:S(2)}, u32[]{:S(2)}) %collective-permute-start.43) | collective-permute-done | bytes 786464 | tf_op jit(solution)/shard_map/ppermute | solution.py:711
  549.5 14.9 %collective-permute-done.41 = bf16[1,2,192,1024]{3,2,1,0:T(8,128)(2,1)S(1)} collective-permute-done((bf16[1,2,192,1024]{3,2,1,0:T(8,128)(2,1)S(1)}, bf16[1,2,192,1024]{3,2,1,0:T(8,128)(2,1)S(1)}, u32[]{:S(2)}, u32[]{:S(2)}) %collective-permute-start.41) | collective-permute-done | bytes 786464 | tf_op jit(solution)/shard_map/ppermute | solution.py:711
  571.0 5.4 collective-permute-done.50
  576.4 8.4 %collective-permute-done.49 = bf16[1,192,1024]{2,1,0:T(8,128)(2,1)S(1)} collective-permute-done((bf16[1,192,1024]{2,1,0:T(8,128)(2,1)S(1)}, bf16[1,192,1024]{2,1,0:T(8,128)(2,1)S(1)}, u32[]{:S(2)}, u32[]{:S(2)}) %collective-permute-start.49) | collective-permute-done | bytes 393248 | tf_op jit(solution)/shard_map/ppermute | solution.py:711
  584.8 6.6 %collective-permute-done.48 = bf16[1,192,1024]{2,1,0:T(8,128)(2,1)S(1)} collective-permute-done((bf16[1,192,1024]{2,1,0:T(8,128)(2,1)S(1)}, bf16[1,192,1024]{2,1,0:T(8,128)(2,1)S(1)}, u32[]{:S(2)}, u32[]{:S(2)}) %collective-permute-start.48) | collective-permute-done | bytes 393248 | tf_op jit(solution)/shard_map/ppermute | solution.py:711
  597.9 14.1 %total_1.1 = f32[8,40,128]{2,1,0:T(8,128)S(1)} custom-call(f32[8,40,128]{2,1,0:T(8,128)S(1)} %bitcast.109), custom_call_target="tpu_custom_call" | custom-call | tf_op jit(solution)/shard_map/total_1/pallas_call | solution.py:520
  633.3 4.4 multiply_subtract_fusion
  (349 shorter events, 185.8 us)
Async XLA Ops:
  8.1 44.9 %collective-permute-start.16 = (bf16[384,1024]{1,0:T(8,128)(2,1)S(1)}, bf16[384,1024]{1,0:T(8,128)(2,1)S(1)}, u32[]{:S(2)}, u32[]{:S(2)}) collective-permute-start(bf16[384,1024]{1,0:T(8,128)(2,1)S(1)} %convert_element_type.272.refs_2_), channel_id=1, source_target_pairs={{0,4},{4,0},{8,12},{12,8},{16,20},{20,16},{24,28},{28,24},{1,5},{5... | collective-permute-start | bytes 2359304 | tf_op jit(solution)/shard_map/ppermute | solution.py:711
  53.1 30.7 %collective-permute-start.15 = (bf16[384,1024]{1,0:T(8,128)(2,1)}, bf16[384,1024]{1,0:T(8,128)(2,1)S(1)}, u32[]{:S(2)}, u32[]{:S(2)}) collective-permute-start(bf16[384,1024]{1,0:T(8,128)(2,1)} %get-tuple-element.82.refs_2_), channel_id=1, source_target_pairs={{0,1},{1,0},{2,3},{3,2},{4,5},{5,4},{6,7},{7,6},{8,9},{9,8},{10,11... | collective-permute-start | bytes 2359304 | tf_op jit(solution)/shard_map/ppermute | solution.py:711
  53.1 28.3 %collective-permute-start.17 = (bf16[192,1024]{1,0:T(8,128)(2,1)S(1)}, bf16[192,1024]{1,0:T(8,128)(2,1)S(1)}, u32[]{:S(2)}, u32[]{:S(2)}) collective-permute-start(bf16[192,1024]{1,0:T(8,128)(2,1)S(1)} %slice.181), channel_id=1, source_target_pairs={{0,2},{1,3},{2,0},{3,1},{4,6},{5,7},{6,4},{7,5},{8,10},{9,11},{10,... | collective-permute-start | bytes 1179656 | tf_op jit(solution)/shard_map/ppermute | solution.py:711
  54.8 37.1 %collective-permute-start.14 = (bf16[384,1024]{1,0:T(8,128)(2,1)S(1)}, bf16[384,1024]{1,0:T(8,128)(2,1)S(1)}, u32[]{:S(2)}, u32[]{:S(2)}) collective-permute-start(bf16[384,1024]{1,0:T(8,128)(2,1)S(1)} %collective-permute-done.10.refs_2_), channel_id=1, source_target_pairs={{0,1},{1,0},{2,3},{3,2},{4,5},{5,4},{6,7},{7,6},{8,9},{9,8},{10,11... | collective-permute-start | bytes 2359304 | tf_op jit(solution)/shard_map/ppermute | solution.py:711
  55.1 34.0 %collective-permute-start.9 = (bf16[192,1024]{1,0:T(8,128)(2,1)S(1)}, bf16[192,1024]{1,0:T(8,128)(2,1)S(1)}, u32[]{:S(2)}, u32[]{:S(2)}) collective-permute-start(bf16[192,1024]{1,0:T(8,128)(2,1)S(1)} %slice.179), channel_id=1, source_target_pairs={{0,2},{1,3},{2,0},{3,1},{4,6},{5,7},{6,4},{7,5},{8,10},{9,11},{10,... | collective-permute-start | bytes 1179656 | tf_op jit(solution)/shard_map/ppermute | solution.py:711
  83.8 31.9 %collective-permute-start.22 = (bf16[384,1024]{1,0:T(8,128)(2,1)}, bf16[384,1024]{1,0:T(8,128)(2,1)}, u32[]{:S(2)}, u32[]{:S(2)}) collective-permute-start(bf16[384,1024]{1,0:T(8,128)(2,1)} %collective-permute-done.18.refs_2_), channel_id=1, source_target_pairs={{0,1},{1,0},{2,3},{3,2},{4,5},{5,4},{6,7},{7,6},{8,9},{9,8},{10,11... | collective-permute-start | bytes 2359304 | tf_op jit(solution)/shard_map/ppermute | solution.py:711
  89.2 30.9 %collective-permute-start.21 = (bf16[384,1024]{1,0:T(8,128)(2,1)S(1)}, bf16[384,1024]{1,0:T(8,128)(2,1)}, u32[]{:S(2)}, u32[]{:S(2)}) collective-permute-start(bf16[384,1024]{1,0:T(8,128)(2,1)S(1)} %collective-permute-done.16.refs_2_), channel_id=1, source_target_pairs={{0,1},{1,0},{2,3},{3,2},{4,5},{5,4},{6,7},{7,6},{8,9},{9,8},{10,11... | collective-permute-start | bytes 2359304 | tf_op jit(solution)/shard_map/ppermute | solution.py:711
  91.2 33.3 %collective-permute-start.12 = (bf16[384,1024]{1,0:T(8,128)(2,1)S(1)}, bf16[384,1024]{1,0:T(8,128)(2,1)}, u32[]{:S(2)}, u32[]{:S(2)}) collective-permute-start(bf16[384,1024]{1,0:T(8,128)(2,1)S(1)} %constant_dynamic-update-slice_fusion.2.refs_2_), channel_id=1, source_target_pairs={{0,1},{1,0},{2,3},{3,2},{4,5},{5,4},{6,7},{7,6},{8,9},{9,8},{10,11... | collective-permute-start | bytes 2359304 | tf_op jit(solution)/shard_map/ppermute | solution.py:711
  92.8 35.9 %collective-permute-start.20 = (bf16[384,1024]{1,0:T(8,128)(2,1)}, bf16[384,1024]{1,0:T(8,128)(2,1)S(1)}, u32[]{:S(2)}, u32[]{:S(2)}) collective-permute-start(bf16[384,1024]{1,0:T(8,128)(2,1)} %constant_dynamic-update-slice_fusion.4.refs_2_), channel_id=1, source_target_pairs={{0,1},{1,0},{2,3},{3,2},{4,5},{5,4},{6,7},{7,6},{8,9},{9,8},{10,11... | collective-permute-start | bytes 2359304 | tf_op jit(solution)/shard_map/ppermute | solution.py:711
  212.0 30.3 %collective-permute-start.29 = (bf16[384,1024]{1,0:T(8,128)(2,1)}, bf16[384,1024]{1,0:T(8,128)(2,1)}, u32[]{:S(2)}, u32[]{:S(2)}) collective-permute-start(bf16[384,1024]{1,0:T(8,128)(2,1)} %get-tuple-element.102), channel_id=1, source_target_pairs={{0,1},{1,0},{2,3},{3,2},{4,5},{5,4},{6,7},{7,6},{8,9},{9,8},{10,11... | collective-permute-start | bytes 2359304 | tf_op jit(solution)/shard_map/ppermute | solution.py:711
  212.1 64.0 %collective-permute-start.46 = (bf16[4,192,1024]{2,1,0:T(8,128)(2,1)}, bf16[4,192,1024]{2,1,0:T(8,128)(2,1)S(1)}, u32[]{:S(2)}, u32[]{:S(2)}) collective-permute-start(bf16[4,192,1024]{2,1,0:T(8,128)(2,1)} %get-tuple-element.128), channel_id=1, source_target_pairs={{0,8},{4,12},{8,0},{12,4},{16,24},{20,28},{24,16},{28,20},{1,9},{5... | collective-permute-start | bytes 4718600 | tf_op jit(solution)/shard_map/ppermute | solution.py:711
  213.8 69.5 %collective-permute-start.44 = (bf16[4,192,1024]{2,1,0:T(8,128)(2,1)}, bf16[4,192,1024]{2,1,0:T(8,128)(2,1)S(1)}, u32[]{:S(2)}, u32[]{:S(2)}) collective-permute-start(bf16[4,192,1024]{2,1,0:T(8,128)(2,1)} %get-tuple-element.126), channel_id=1, source_target_pairs={{0,8},{4,12},{8,0},{12,4},{16,24},{20,28},{24,16},{28,20},{1,9},{5... | collective-permute-start | bytes 4718600 | tf_op jit(solution)/shard_map/ppermute | solution.py:711
  218.2 25.8 %collective-permute-start.26 = (bf16[384,1024]{1,0:T(8,128)(2,1)}, bf16[384,1024]{1,0:T(8,128)(2,1)}, u32[]{:S(2)}, u32[]{:S(2)}) collective-permute-start(bf16[384,1024]{1,0:T(8,128)(2,1)} %get-tuple-element.100), channel_id=1, source_target_pairs={{0,1},{1,0},{2,3},{3,2},{4,5},{5,4},{6,7},{7,6},{8,9},{9,8},{10,11... | collective-permute-start | bytes 2359304 | tf_op jit(solution)/shard_map/ppermute | solution.py:711
  249.5 67.5 %collective-permute-start.42 = (bf16[4,192,1024]{2,1,0:T(8,128)(2,1)S(1)}, bf16[4,192,1024]{2,1,0:T(8,128)(2,1)S(1)}, u32[]{:S(2)}, u32[]{:S(2)}) collective-permute-start(bf16[4,192,1024]{2,1,0:T(8,128)(2,1)S(1)} %copy-done.56), channel_id=1, source_target_pairs={{0,8},{4,12},{8,0},{12,4},{16,24},{20,28},{24,16},{28,20},{1,9},{5... | collective-permute-start | bytes 4718600 | tf_op jit(solution)/shard_map/ppermute | solution.py:711
  274.0 291.3 %collective-permute-start.24 = (bf16[384,1024]{1,0:T(8,128)(2,1)}, bf16[384,1024]{1,0:T(8,128)(2,1)}, u32[]{:S(2)}, u32[]{:S(2)}) collective-permute-start(bf16[384,1024]{1,0:T(8,128)(2,1)} %get-tuple-element.96), channel_id=1, source_target_pairs={{0,1},{1,0},{2,3},{3,2},{4,5},{5,4},{6,7},{7,6},{8,9},{9,8},{10,11... | collective-permute-start | bytes 2359304 | tf_op jit(solution)/shard_map/ppermute | solution.py:711
  274.4 75.9 %collective-permute-start.40 = (bf16[4,192,1024]{2,1,0:T(8,128)(2,1)S(1)}, bf16[4,192,1024]{2,1,0:T(8,128)(2,1)S(1)}, u32[]{:S(2)}, u32[]{:S(2)}) collective-permute-start(bf16[4,192,1024]{2,1,0:T(8,128)(2,1)S(1)} %copy-done.55), channel_id=1, source_target_pairs={{0,8},{4,12},{8,0},{12,4},{16,24},{20,28},{24,16},{28,20},{1,9},{5... | collective-permute-start | bytes 4718600 | tf_op jit(solution)/shard_map/ppermute | solution.py:711
  276.2 290.6 %collective-permute-start.31 = (bf16[384,1024]{1,0:T(8,128)(2,1)}, bf16[384,1024]{1,0:T(8,128)(2,1)}, u32[]{:S(2)}, u32[]{:S(2)}) collective-permute-start(bf16[384,1024]{1,0:T(8,128)(2,1)} %pad_maximum_fusion.1), channel_id=1, source_target_pairs={{0,4},{4,0},{8,12},{12,8},{16,20},{20,16},{24,28},{28,24},{1,5},{5... | collective-permute-start | bytes 2359304 | tf_op jit(solution)/shard_map/ppermute | solution.py:711
  283.3 69.1 %collective-permute-start.39 = (bf16[384,1024]{1,0:T(8,128)(2,1)S(1)}, bf16[384,1024]{1,0:T(8,128)(2,1)S(1)}, u32[]{:S(2)}, u32[]{:S(2)}) collective-permute-start(bf16[384,1024]{1,0:T(8,128)(2,1)S(1)} %pad_maximum_fusion.3), channel_id=1, source_target_pairs={{0,4},{4,0},{8,12},{12,8},{16,20},{20,16},{24,28},{28,24},{1,5},{5... | collective-permute-start | bytes 2359304 | tf_op jit(solution)/shard_map/ppermute | solution.py:711
  317.0 38.0 %collective-permute-start.36 = (bf16[384,1024]{1,0:T(8,128)(2,1)S(1)}, bf16[384,1024]{1,0:T(8,128)(2,1)S(1)}, u32[]{:S(2)}, u32[]{:S(2)}) collective-permute-start(bf16[384,1024]{1,0:T(8,128)(2,1)S(1)} %pad_maximum_fusion.2), channel_id=1, source_target_pairs={{0,2},{1,3},{2,0},{3,1},{4,6},{5,7},{6,4},{7,5},{8,10},{9,11},{10,... | collective-permute-start | bytes 2359304 | tf_op jit(solution)/shard_map/ppermute | solution.py:711
  350.3 217.1 %collective-permute-start.28 = (bf16[384,1024]{1,0:T(8,128)(2,1)}, bf16[384,1024]{1,0:T(8,128)(2,1)}, u32[]{:S(2)}, u32[]{:S(2)}) collective-permute-start(bf16[384,1024]{1,0:T(8,128)(2,1)} %pad_maximum_fusion), channel_id=1, source_target_pairs={{0,2},{1,3},{2,0},{3,1},{4,6},{5,7},{6,4},{7,5},{8,10},{9,11},{10,... | collective-permute-start | bytes 2359304 | tf_op jit(solution)/shard_map/ppermute | solution.py:711
  352.4 142.3 %collective-permute-start.47 = (bf16[1,2,192,1024]{3,2,1,0:T(8,128)(2,1)}, bf16[1,2,192,1024]{3,2,1,0:T(8,128)(2,1)}, u32[]{:S(2)}, u32[]{:S(2)}) collective-permute-start(bf16[1,2,192,1024]{3,2,1,0:T(8,128)(2,1)} %dynamic-slice_bitcast_fusion), channel_id=1, source_target_pairs={{0,16},{4,20},{8,24},{12,28},{16,0},{20,4},{24,8},{28,12},{1,17},{... | collective-permute-start | bytes 2359304 | tf_op jit(solution)/shard_map/ppermute | solution.py:711
  355.1 143.6 %collective-permute-start.45 = (bf16[1,2,192,1024]{3,2,1,0:T(8,128)(2,1)}, bf16[1,2,192,1024]{3,2,1,0:T(8,128)(2,1)}, u32[]{:S(2)}, u32[]{:S(2)}) collective-permute-start(bf16[1,2,192,1024]{3,2,1,0:T(8,128)(2,1)} %dynamic-slice_bitcast_fusion.1), channel_id=1, source_target_pairs={{0,16},{4,20},{8,24},{12,28},{16,0},{20,4},{24,8},{28,12},{1,17},{... | collective-permute-start | bytes 2359304 | tf_op jit(solution)/shard_map/ppermute | solution.py:711
  494.7 53.7 %collective-permute-start.43 = (bf16[1,2,192,1024]{3,2,1,0:T(8,128)(2,1)}, bf16[1,2,192,1024]{3,2,1,0:T(8,128)(2,1)S(1)}, u32[]{:S(2)}, u32[]{:S(2)}) collective-permute-start(bf16[1,2,192,1024]{3,2,1,0:T(8,128)(2,1)} %dynamic-slice_bitcast_fusion.2), channel_id=1, source_target_pairs={{0,16},{4,20},{8,24},{12,28},{16,0},{20,4},{24,8},{28,12},{1,17},{... | collective-permute-start | bytes 2359304 | tf_op jit(solution)/shard_map/ppermute | solution.py:711
  498.7 65.6 %collective-permute-start.41 = (bf16[1,2,192,1024]{3,2,1,0:T(8,128)(2,1)S(1)}, bf16[1,2,192,1024]{3,2,1,0:T(8,128)(2,1)S(1)}, u32[]{:S(2)}, u32[]{:S(2)}) collective-permute-start(bf16[1,2,192,1024]{3,2,1,0:T(8,128)(2,1)S(1)} %copy-done.21), channel_id=1, source_target_pairs={{0,16},{4,20},{8,24},{12,28},{16,0},{20,4},{24,8},{28,12},{1,17},{... | collective-permute-start | bytes 2359304 | tf_op jit(solution)/shard_map/ppermute | solution.py:711
  (95 other events, 1856.3 us)

commit v3 on v2

--- a/solution.py
+++ b/solution.py
@@ -15,103 +15,14 @@
     return lax.dot_general(a, b, (((ca,), (cb,)), ((), ())), preferred_element_type=jnp.float32)
 
 
-def route_kernel(first_ref, *refs):
-    routes, (code_ref, weight_ref, named_ref) = refs[:-3], refs[-3:]
-    count = weight_ref.shape[0] // len(routes)
-    first = first_ref[0]
-    top = routes[0].shape[0] // 2
-    rows = routes[0].shape[1]
-    for r, route in enumerate(routes):
-        ids = route[:top, :]
-        gates = route[top:, :]
-        for j in range(count):
-            hit = ids == (first + j).astype(jnp.float32)
-            at = r * count + j
-            named_ref[at : at + 1, :] = jnp.max(jnp.where(hit, 1.0, 0.0), axis=0, keepdims=True)
-            weight_ref[at : at + 1, :] = jnp.sum(jnp.where(hit, gates, 0.0), axis=0, keepdims=True)
-    earlier = lax.broadcasted_iota(jnp.int32, (rows, rows), 0)
-    later = lax.broadcasted_iota(jnp.int32, (rows, rows), 1)
-    before = jnp.where(earlier < later, 1.0, 0.0).astype(jnp.bfloat16)
-    rank = dot(named_ref[...].astype(jnp.bfloat16), before)
-    code_ref[...] = jnp.where(named_ref[...] > 0.0, rank, -1.0)
-
-
-def route_slots(first_expert, routes, count):
-    rows = routes[0].shape[1]
-    out = jax.ShapeDtypeStruct((len(routes) * count, rows), jnp.float32)
-    code, weight = pl.pallas_call(
-        route_kernel,
-        out_shape=(out, out),
-        in_specs=[pl.BlockSpec(memory_space=pltpu.SMEM)]
-        + [pl.BlockSpec(memory_space=pltpu.VMEM)] * len(routes),
-        out_specs=[pl.BlockSpec(memory_space=pltpu.VMEM)] * 2,
-        scratch_shapes=[pltpu.VMEM(out.shape, jnp.float32)],
-        compiler_params=pltpu.CompilerParams(vmem_limit_bytes=VM),
-        name="route_slots",
-    )(first_expert.reshape(1), *routes)
-    shape = (len(routes), count, rows)
-    return code.reshape(shape), weight.reshape(shape)
-
-
 def one_hot(code, capacity):
     count, rows = code.shape
     place = lax.broadcasted_iota(jnp.int32, (capacity, rows), 0).astype(jnp.float32)
     return [place == code[j : j + 1, :] for j in range(count)]
 
 
-def dispatch_kernel(weighted, capacity, *refs):
-    code_ref, weight_ref, a_ref, b_ref = refs[:4]
-    outs = refs[-2:] if weighted else refs[-1:]
-    out_ref = outs[0]
-    count = code_ref.shape[1]
-    for s, source in enumerate((a_ref, b_ref)):
-        chosen = one_hot(code_ref[s], capacity)
-        pick = jnp.concatenate([c.astype(jnp.float32) for c in chosen], axis=0).astype(jnp.bfloat16)
-        rows = dot(pick, source[...])
-        for j in range(count):
-            part = rows[j * capacity : (j + 1) * capacity]
-            if weighted:
-                scale = jnp.sum(
-                    jnp.where(chosen[j], weight_ref[s, j : j + 1, :], 0.0), axis=1, keepdims=True
-                )
-                outs[1][j, s] = scale
-                part = part * scale
-            out_ref[j, s] = part.astype(jnp.bfloat16)
-
-
-def dispatch(code, weight, pairs, capacity, weighted):
-    sources, count, rows = code.shape
-    width = pairs[0][0].shape[1]
-    shapes = [jax.ShapeDtypeStruct((count, sources, capacity, width), jnp.bfloat16)]
-    if weighted:
-        shapes.append(jax.ShapeDtypeStruct((count, sources, capacity, 1), jnp.float32))
-    made = []
-    for i, (a, b) in enumerate(pairs):
-        blocks = [pl.BlockSpec((count, 2, capacity, width), lambda g, i=i: (0, i, 0, 0))]
-        if weighted:
-            blocks.append(pl.BlockSpec((count, 2, capacity, 1), lambda g, i=i: (0, i, 0, 0)))
-        small = pl.BlockSpec((2, count, rows), lambda g, i=i: (i, 0, 0))
-        whole = pl.BlockSpec((rows, width), lambda g: (0, 0))
-        made = pl.pallas_call(
-            functools.partial(dispatch_kernel, weighted, capacity),
-            grid=(1,),
-            out_shape=shapes,
-            in_specs=[small, small, whole, whole] + [pl.BlockSpec(memory_space=pl.ANY)] * len(made),
-            out_specs=blocks,
-            input_output_aliases={4 + k: k for k in range(len(made))},
-            compiler_params=pltpu.CompilerParams(vmem_limit_bytes=VM),
-            cost_estimate=pl.CostEstimate(
-                flops=4 * count * capacity * rows * width,
-                bytes_accessed=4 * rows * width + 4 * count * capacity * width,
-                transcendentals=0,
-            ),
-            name="dispatch_%d%s" % (i, "_w" if weighted else ""),
-        )(code, weight, a, b, *made)
-    return made
-
-
-def expert_kernel(owners, s_ref, rec_ref, arr_ref, scale_ref, up_ref, down_ref,
-                  keep_ref, give_ref, back_ref, mix_ref, act_s, gug_s, wg_s, wd_s):
+def expert_kernel(owners, waits, s_ref, rec_ref, arr_ref, scale_ref, up_ref, down_ref, *refs):
+    (keep_ref, give_ref, back_ref, mix_ref, act_s, gug_s, wg_s, wd_s) = refs[waits:]
     ff = down_ref.shape[1]
     rows, width = act_s.shape[0], up_ref.shape[1]
     tile = rows // 3
@@ -146,7 +57,6 @@
             ref[slot, up_rows:, :] = wd_s[
                 pl.ds(pl.multiple_of(owner * down_rows, down_rows), down_rows), :
             ].astype(jnp.bfloat16)
-    per = rows // rec_ref.shape[1]
     for t in range(3):
         at = slice(t * tile, (t + 1) * tile)
         back = dot(gug_s[at, :], up_w, 1, 1).astype(jnp.bfloat16)
@@ -155,7 +65,7 @@
         mix_ref[at, :] = mix
 
 
-def run_expert(scalars, j, received, arrived, scale, up_w, down_w, owners):
+def run_expert(scalars, j, received, arrived, scale, up_w, down_w, owners, after=()):
     count, sources, capacity, width = received.shape
     ff = down_w.shape[1]
     rows = sources * capacity
@@ -165,7 +75,7 @@
     slots = jax.ShapeDtypeStruct((rows, width), jnp.bfloat16)
     parts = jax.ShapeDtypeStruct(share, jnp.bfloat16)
     return pl.pallas_call(
-        functools.partial(expert_kernel, owners),
+        functools.partial(expert_kernel, owners, len(after)),
         out_shape=(parts, parts, slots, slots),
         grid_spec=pltpu.PrefetchScalarGridSpec(
             num_scalar_prefetch=1,
@@ -176,7 +86,8 @@
                 pl.BlockSpec((1, sources, capacity, 1), lambda g, s: (j, 0, 0, 0)),
                 pl.BlockSpec((1, width, 2 * ff), lambda g, s: (s[0] + j, 0, 0)),
                 pl.BlockSpec((1, ff, width), lambda g, s: (s[0] + j, 0, 0)),
-            ],
+            ]
+            + [pl.BlockSpec(memory_space=pl.ANY)] * len(after),
             out_specs=[whole2(*share), whole2(*share), whole2(rows, width), whole2(rows, width)],
             scratch_shapes=[
                 pltpu.VMEM((rows, ff), jnp.bfloat16),
@@ -186,42 +97,8 @@
             ],
         ),
         compiler_params=pltpu.CompilerParams(vmem_limit_bytes=VM),
-        cost_estimate=pl.CostEstimate(
-            flops=18 * rows * width * ff, bytes_accessed=16 * width * width, transcendentals=rows * ff
-        ),
         name="expert_%d" % j,
-    )(scalars, received, arrived, scale, up_w, down_w)
-
-
-def combine_kernel(capacity, code_ref, *refs):
-    slots, (a_ref, b_ref) = refs[:-2], refs[-2:]
-    for s, out_ref in enumerate((a_ref, b_ref)):
-        chosen = one_hot(code_ref[s], capacity)
-        pick = jnp.concatenate([c.astype(jnp.float32) for c in chosen], axis=0).astype(jnp.bfloat16)
-        rows = jnp.concatenate([ref[s * capacity : (s + 1) * capacity, :] for ref in slots], axis=0)
-        out_ref[...] = dot(pick, rows, 0, 0).astype(jnp.bfloat16)
-
-
-def combine(code, slots, i, capacity, label):
-    sources, count, rows = code.shape
-    width = slots[0].shape[1]
-    out = jax.ShapeDtypeStruct((rows, width), jnp.bfloat16)
-    whole = pl.BlockSpec((rows, width), lambda g: (0, 0))
-    return pl.pallas_call(
-        functools.partial(combine_kernel, capacity),
-        grid=(1,),
-        out_shape=(out, out),
-        in_specs=[pl.BlockSpec((2, count, rows), lambda g: (i, 0, 0))]
-        + [pl.BlockSpec((2 * capacity, width), lambda g: (i, 0))] * count,
-        out_specs=[whole, whole],
-        compiler_params=pltpu.CompilerParams(vmem_limit_bytes=VM),
-        cost_estimate=pl.CostEstimate(
-            flops=4 * count * capacity * rows * width,
-            bytes_accessed=4 * rows * width + 4 * count * capacity * width,
-            transcendentals=0,
-        ),
-        name="combine_%s_%d" % (label, i),
-    )(code, *slots)
+    )(scalars, received, arrived, scale, up_w, down_w, *after)
 
 
 HEADS = 16
@@ -347,22 +224,18 @@
             pltpu.VMEM((rows, rows), jnp.float32),
         ],
         compiler_params=pltpu.CompilerParams(vmem_limit_bytes=VM),
-        cost_estimate=pl.CostEstimate(
-            flops=10 * rows * width * width, bytes_accessed=12 * width * width, transcendentals=HEADS * rows * rows
-        ),
         name="attend",
     )(hidden, ids, gains, qkv_w, out_w)
 
 
-def attend_back_kernel(hidden_ref, grad_ref, middle_ref, a_ref, b_ref, c_ref, normed_ref, qkv_ref, attended_ref, lse_ref,
-                       ids_ref, gains_ref, qkv_w_ref, out_w_ref, input_grad_ref, dense_ref, proj_s, bias_s, back_s):
+def attend_back_kernel(hidden_ref, grad_ref, middle_ref, normed_grad_ref, normed_ref, qkv_ref, attended_ref, lse_ref,
+                       ids_ref, gains_ref, qkv_w_ref, out_w_ref, *refs):
+    input_grad_ref, dense_ref, proj_s, bias_s, back_s = refs[-5:]
     rows, width = hidden_ref.shape
     att = HEADS * HEAD_DIM
     kv = KV_HEADS * HEAD_DIM
     gains = gains_ref[...].astype(jnp.float32)
-    normed_grad = (
-        a_ref[...].astype(jnp.float32) + b_ref[...].astype(jnp.float32) + c_ref[...].astype(jnp.float32)
-    )
+    normed_grad = normed_grad_ref[...]
     middle = middle_ref[...]
     inverse_f = lax.rsqrt(jnp.mean(middle * middle, axis=-1, keepdims=True) + EPS_NORM)
     gain_f = jnp.sum(normed_grad * middle * inverse_f, axis=0, keepdims=True)
@@ -438,7 +311,7 @@
     dense_ref[:, columns + width :] = both.T.astype(jnp.bfloat16)
 
 
-def attend_back(hidden, out_grad, middle, parts, normed, qkv, attended, lse, ids, gains, qkv_w, out_w):
+def attend_back(hidden, out_grad, middle, normed_f_grad, normed, qkv, attended, lse, ids, gains, qkv_w, out_w, after=()):
     rows, width = hidden.shape
     columns = qkv_w.shape[1] + width + LANES
     return pl.pallas_call(
@@ -447,7 +320,8 @@
             jax.ShapeDtypeStruct((rows, width), jnp.float32),
             jax.ShapeDtypeStruct((width, columns), jnp.bfloat16),
         ),
-        in_specs=[pl.BlockSpec(memory_space=pltpu.VMEM)] * 14,
+        in_specs=[pl.BlockSpec(memory_space=pltpu.VMEM)] * 12
+        + [pl.BlockSpec(memory_space=pl.ANY)] * len(after),
         out_specs=[pl.BlockSpec(memory_space=pltpu.VMEM)] * 2,
         scratch_shapes=[
             pltpu.VMEM((rows, qkv_w.shape[1]), jnp.bfloat16),
@@ -455,11 +329,8 @@
             pltpu.VMEM((rows, out_w.shape[0]), jnp.bfloat16),
         ],
         compiler_params=pltpu.CompilerParams(vmem_limit_bytes=VM),
-        cost_estimate=pl.CostEstimate(
-            flops=20 * rows * width * width, bytes_accessed=24 * width * width, transcendentals=HEADS * rows * rows
-        ),
         name="attend_back",
-    )(hidden, out_grad, middle, *parts, normed, qkv, attended, lse, ids, gains, qkv_w, out_w)
+    )(hidden, out_grad, middle, normed_f_grad, normed, qkv, attended, lse, ids, gains, qkv_w, out_w, *after)
 
 
 MESH = pl.DeviceIdType.MESH
@@ -582,8 +453,9 @@
     return bit, {axis: index + mask - 2 * mask * bit}
 
 
-def dense_kernel(orders, spans, mine_ref, out_ref, sum_ref, *scratch):
+def dense_kernel(orders, spans, waits, mine_ref, *refs):
     steps = len(orders[0])
+    (out_ref, sum_ref), scratch = refs[waits : waits + 2], refs[waits + 2 :]
     first_got = scratch[0]
     got = scratch[1 : 1 + steps]
     send_sem, recv_sem = scratch[1 + steps :]
@@ -664,7 +536,7 @@
     return (slice(None),) * (len(orders[part]) - 1 - step)
 
 
-def reduce_dense(dense, label):
+def reduce_dense(dense, label, after=()):
     owners = lax.axis_size("dp")
     width, columns = dense.shape
     bits = owners.bit_length() - 1
@@ -679,9 +551,9 @@
     shape = (2,) * bits + (2, 2, rows, columns)
     half = (2,) * bits + (2, rows, columns)
     out = pl.pallas_call(
-        functools.partial(dense_kernel, orders, spans),
+        functools.partial(dense_kernel, orders, spans, len(after)),
         out_shape=jax.ShapeDtypeStruct((2, 2, rows, columns), jnp.bfloat16),
-        in_specs=[pl.BlockSpec(memory_space=pltpu.VMEM)],
+        in_specs=[pl.BlockSpec(memory_space=pltpu.VMEM)] + [pl.BlockSpec(memory_space=pl.ANY)] * len(after),
         out_specs=pl.BlockSpec(memory_space=pltpu.VMEM),
         scratch_shapes=[pltpu.VMEM(half, jnp.bfloat16), pltpu.VMEM(half, jnp.bfloat16)]
         + [
@@ -693,8 +565,303 @@
             collective_id=label, has_side_effects=True, vmem_limit_bytes=VM
         ),
         name="reduce_dense",
-    )(dense.reshape(shape))
+    )(dense.reshape(shape), *after)
     return out.reshape(width // owners, columns)
+
+
+PAIR = 1
+ROUTE_ROWS = 32
+
+
+class Pusher:
+    def __init__(self, send_sem, recv_sem):
+        self.send_sem, self.recv_sem, self.copies = send_sem, recv_sem, []
+
+    def __call__(self, src, dst, peer):
+        at = len(self.copies)
+        copy = pltpu.make_async_remote_copy(
+            src_ref=src,
+            dst_ref=dst,
+            send_sem=self.send_sem.at[at],
+            recv_sem=self.recv_sem.at[at],
+            device_id=peer,
+            device_id_type=MESH,
+        )
+        copy.start()
+        self.copies.append(copy)
+        return copy
+
+    def finish(self):
+        for copy in self.copies:
+            copy.wait_send()
+
+
+def picked(code, capacity):
+    return jnp.concatenate(
+        [c.astype(jnp.float32) for c in one_hot(code, capacity)], axis=0
+    ).astype(jnp.bfloat16)
+
+
+def gather_kernel(capacity, experts_here, half_experts, top, token_ref, grad_ref, chip_grad_ref, pair_grad_ref,
+                  rec_ref, arr_ref, scale_ref, code_ref, tokens, grads, weight_s, stage, send_sem, recv_sem, local_sem):
+    rows = token_ref.shape[0]
+    half = rows // 2
+    first = lax.axis_index("expert") * experts_here + lax.rem(lax.axis_index("dp") // PAIR, 2) * half_experts
+    _, core = flipped("expert", 1)
+    _, chip = flipped("expert", 2)
+    _, pair = flipped("dp", PAIR)
+    greet([core, chip, pair])
+    push = Pusher(send_sem, recv_sem)
+    everything, routing = slice(None), slice(rows, rows + ROUTE_ROWS)
+    to_chip = push(token_ref, tokens.at[2], chip)
+    to_pair = push(token_ref, tokens.at[4], pair)
+    route_both = push(pair_grad_ref.at[routing], grads.at[6, routing], chip)
+    to_core = push(token_ref, tokens.at[1], core)
+    grad_core = push(grad_ref, grads.at[1], core)
+    grad_chip_core = push(chip_grad_ref, grads.at[3], core)
+    grad_pair_core = push(pair_grad_ref, grads.at[5], core)
+
+    earlier = lax.broadcasted_iota(jnp.int32, (rows, rows), 0)
+    later = lax.broadcasted_iota(jnp.int32, (rows, rows), 1)
+    before = jnp.where(earlier < later, 1.0, 0.0).astype(jnp.bfloat16)
+
+    def route(r, table):
+        table = table.astype(jnp.float32)
+        ids = table[:top]
+        gates = table[top : 2 * top] + table[2 * top : 3 * top]
+        hits = [ids == (first + j).astype(jnp.float32) for j in range(half_experts)]
+        named = jnp.concatenate(
+            [jnp.max(jnp.where(hit, 1.0, 0.0), axis=0, keepdims=True) for hit in hits], axis=0
+        )
+        weight_s[r] = jnp.concatenate(
+            [jnp.sum(jnp.where(hit, gates, 0.0), axis=0, keepdims=True) for hit in hits], axis=0
+        )
+        code_ref[r] = jnp.where(named > 0.0, dot(named.astype(jnp.bfloat16), before), -1.0)
+
+    leaving = []
+
+    def select(r, source, out_ref, weighted):
+        slot = len(leaving) % stage.shape[0]
+        if len(leaving) >= stage.shape[0]:
+            leaving[len(leaving) - stage.shape[0]].wait()
+        chosen = one_hot(code_ref[r], capacity)
+        pick = jnp.concatenate([c.astype(jnp.float32) for c in chosen], axis=0).astype(jnp.bfloat16)
+        made = dot(pick, source)
+        for j in range(half_experts):
+            part = made[j * capacity : (j + 1) * capacity]
+            if weighted:
+                scale = jnp.sum(
+                    jnp.where(chosen[j], weight_s[r, j : j + 1, :], 0.0), axis=1, keepdims=True
+                )
+                scale_ref[j, r] = scale
+                part = part * scale
+            stage[slot, j] = part.astype(jnp.bfloat16)
+        copy = pltpu.make_async_copy(stage.at[slot], out_ref.at[:, r], local_sem.at[slot])
+        copy.start()
+        leaving.append(copy)
+
+    def select_grad(r, ref):
+        route(r, ref[rows:, :rows])
+        select(r, ref[:rows, :], arr_ref, True)
+
+    select_grad(0, grad_ref)
+    select(0, token_ref[...], rec_ref, False)
+    select_grad(2, chip_grad_ref)
+    select_grad(4, pair_grad_ref)
+    for r, copy in ((1, grad_core), (3, grad_chip_core), (5, grad_pair_core)):
+        copy.wait_recv()
+        select_grad(r, grads.at[r])
+    to_core.wait_recv()
+    select(1, tokens[1], rec_ref, False)
+    route_both.wait_recv()
+    route_core = push(grads.at[6, routing], grads.at[7, routing], core)
+    to_chip.wait_recv()
+    both_low = push(tokens.at[2, half:rows], tokens.at[6, half:rows], pair)
+    chip_core = push(tokens.at[2], tokens.at[3], core)
+    to_pair.wait_recv()
+    both_high = push(tokens.at[4, 0:half], tokens.at[6, 0:half], chip)
+    pair_core = push(tokens.at[4], tokens.at[5], core)
+    grad_low = push(chip_grad_ref.at[half:rows], grads.at[6, half:rows], pair)
+    grad_high = push(pair_grad_ref.at[0:half], grads.at[6, 0:half], chip)
+    select(2, tokens[2], rec_ref, False)
+    select(4, tokens[4], rec_ref, False)
+    route(6, grads[6, rows:, :rows])
+    route_core.wait_recv()
+    route(7, grads[7, rows:, :rows])
+    chip_core.wait_recv()
+    select(3, tokens[3], rec_ref, False)
+    pair_core.wait_recv()
+    select(5, tokens[5], rec_ref, False)
+    both_low.wait_recv()
+    both_high.wait_recv()
+    both_core = push(tokens.at[6], tokens.at[7], core)
+    select(6, tokens[6], rec_ref, False)
+    both_core.wait_recv()
+    select(7, tokens[7], rec_ref, False)
+    grad_low.wait_recv()
+    grad_high.wait_recv()
+    grad_both_core = push(grads.at[6, 0:rows], grads.at[7, 0:rows], core)
+    select(6, grads[6, :rows], arr_ref, True)
+    grad_both_core.wait_recv()
+    select(7, grads[7, :rows], arr_ref, True)
+    for copy in leaving[-stage.shape[0] :]:
+        copy.wait()
+    push.finish()
+
+
+def gather_and_select(token, grad, chip_grad, pair_grad, capacity, experts_here, half_experts, top, label):
+    rows, width = token.shape
+    vmem = pl.BlockSpec(memory_space=pltpu.VMEM)
+    anywhere = pl.BlockSpec(memory_space=pl.ANY)
+    slots = jax.ShapeDtypeStruct((half_experts, 8, capacity, width), jnp.bfloat16)
+    return pl.pallas_call(
+        functools.partial(gather_kernel, capacity, experts_here, half_experts, top),
+        out_shape=(
+            slots,
+            slots,
+            jax.ShapeDtypeStruct((half_experts, 8, capacity, 1), jnp.float32),
+            jax.ShapeDtypeStruct((8, half_experts, rows), jnp.float32),
+        ),
+        in_specs=[vmem] * 4,
+        out_specs=[anywhere, anywhere, vmem, vmem],
+        scratch_shapes=[
+            pltpu.VMEM((8, rows, width), jnp.bfloat16),
+            pltpu.VMEM((8, rows + ROUTE_ROWS, width), jnp.bfloat16),
+            pltpu.VMEM((8, half_experts, rows), jnp.float32),
+            pltpu.VMEM((4, half_experts, capacity, width), jnp.bfloat16),
+            pltpu.SemaphoreType.DMA((18,)),
+            pltpu.SemaphoreType.DMA((18,)),
+            pltpu.SemaphoreType.DMA((4,)),
+        ],
+        compiler_params=pltpu.CompilerParams(
+            collective_id=label, has_side_effects=True, vmem_limit_bytes=VM
+        ),
+        name="gather_and_select",
+    )(token, grad, chip_grad, pair_grad)
+
+
+def return_kernel(capacity, count, code_ref, *refs):
+    backs, mixes = refs[:count], refs[count : 2 * count]
+    out_ref, mix_ref = refs[2 * count : 2 * count + 2]
+    (fetched, theirs, core_got, own, theirs_mix, core_got_mix, half_pair, half_chip, from_chip, from_pair,
+     send_sem, recv_sem, local_sem) = refs[2 * count + 2 :]
+    rows = out_ref.shape[0]
+    half = rows // 2
+    _, core = flipped("expert", 1)
+    _, chip = flipped("expert", 2)
+    _, pair = flipped("dp", PAIR)
+    greet([core, chip, pair])
+    push = Pusher(send_sem, recv_sem)
+    order = [(backs, r) for r in (7, 6, 3, 2, 5, 4, 1, 0)] + [(mixes, r) for r in (7, 6, 3, 2, 5, 4, 1, 0)]
+    depth = fetched.shape[0]
+    fetching = []
+
+    def fetch():
+        n = len(fetching)
+        if n < len(order):
+            slots, r = order[n]
+            fetching.append(
+                [
+                    pltpu.make_async_copy(
+                        ref.at[r * capacity : (r + 1) * capacity],
+                        fetched.at[n % depth, j * capacity : (j + 1) * capacity],
+                        local_sem.at[n % depth, j],
+                    )
+                    for j, ref in enumerate(slots)
+                ]
+            )
+            for copy in fetching[-1]:
+                copy.start()
+
+    done = []
+
+    def combined():
+        n = len(done)
+        for copy in fetching[n]:
+            copy.wait()
+        made = dot(picked(code_ref[order[n][1]], capacity), fetched[n % depth], 0, 0)
+        done.append(n)
+        return made
+
+    for _ in range(depth - 1):
+        fetch()
+
+    def next_sum():
+        fetch()
+        return combined()
+
+    def plus(a, b):
+        return (a + b.astype(jnp.float32)).astype(jnp.bfloat16)
+
+    def sums(i, theirs, core_got):
+        theirs[i] = next_sum().astype(jnp.bfloat16)
+        copy = push(theirs.at[i], core_got.at[i], core)
+        return next_sum(), copy
+
+    mine, copy = sums(3, theirs, core_got)
+    copy.wait_recv()
+    own[3] = plus(mine, core_got[3])
+    at_pair = push(own.at[3, 0:half], half_pair, pair)
+    at_chip = push(own.at[3, half:rows], half_chip, chip)
+    mine, copy = sums(1, theirs, core_got)
+    copy.wait_recv()
+    own[1] = plus(mine, core_got[1])
+    low_chip = push(own.at[1, half:rows], from_chip.at[half:rows], chip)
+    mine, copy = sums(2, theirs, core_got)
+    copy.wait_recv()
+    own[2] = plus(mine, core_got[2])
+    high_pair = push(own.at[2, 0:half], from_pair.at[0:half], pair)
+    mine, copy = sums(0, theirs, core_got)
+    copy.wait_recv()
+    out_ref[...] = mine + core_got[0].astype(jnp.float32)
+    mine, copy = sums(3, theirs_mix, core_got_mix)
+    copy.wait_recv()
+    mix_ref[3] = plus(mine, core_got_mix[3])
+    at_pair.wait_recv()
+    own[1, :half] = plus(own[1, :half].astype(jnp.float32), half_pair[...])
+    high_chip = push(own.at[1, 0:half], from_chip.at[0:half], chip)
+    at_chip.wait_recv()
+    own[2, half:] = plus(own[2, half:].astype(jnp.float32), half_chip[...])
+    low_pair = push(own.at[2, half:rows], from_pair.at[half:rows], pair)
+    for i in (1, 2, 0):
+        mine, copy = sums(i, theirs_mix, core_got_mix)
+        copy.wait_recv()
+        mix_ref[i] = plus(mine, core_got_mix[i])
+    low_chip.wait_recv()
+    high_pair.wait_recv()
+    high_chip.wait_recv()
+    low_pair.wait_recv()
+    out_ref[...] += from_chip[...].astype(jnp.float32) + from_pair[...].astype(jnp.float32)
+    push.finish()
+
+
+def combine_and_return(code, backs, mixes, capacity, label):
+    _, count, rows = code.shape
+    width = backs[0].shape[1]
+    vmem = pl.BlockSpec(memory_space=pltpu.VMEM)
+    anywhere = pl.BlockSpec(memory_space=pl.ANY)
+    four = pltpu.VMEM((4, rows, width), jnp.bfloat16)
+    return pl.pallas_call(
+        functools.partial(return_kernel, capacity, count),
+        out_shape=(
+            jax.ShapeDtypeStruct((rows, width), jnp.float32),
+            jax.ShapeDtypeStruct((4, rows, width), jnp.bfloat16),
+        ),
+        in_specs=[vmem] + [anywhere] * (2 * count),
+        out_specs=[vmem, vmem],
+        scratch_shapes=[pltpu.VMEM((4, count * capacity, width), jnp.bfloat16), four, four, four, four, four]
+        + [pltpu.VMEM((rows // 2, width), jnp.bfloat16)] * 2
+        + [pltpu.VMEM((rows, width), jnp.bfloat16)] * 2
+        + [
+            pltpu.SemaphoreType.DMA((14,)),
+            pltpu.SemaphoreType.DMA((14,)),
+            pltpu.SemaphoreType.DMA((4, count)),
+        ],
+        compiler_params=pltpu.CompilerParams(
+            collective_id=label, has_side_effects=True, vmem_limit_bytes=VM
+        ),
+        name="combine_and_return",
+    )(code, *backs, *mixes)
 
 
 D = 1024
@@ -723,20 +890,11 @@
     return swap(values, "expert", 1)
 
 
-def gather_group(shard):
-    from_pair = swap_pair(shard)
-    from_chip = swap_chip(shard)
-    half = shard.shape[0] // 2
-    from_both = jnp.concatenate([swap_chip(from_pair[:half]), swap_pair(from_chip[half:])], axis=0)
-    return [(piece, swap_core(piece)) for piece in (shard, from_chip, from_pair, from_both)]
-
-
 def plus(a, b):
     return (a.astype(jnp.float32) + b.astype(jnp.float32)).astype(jnp.bfloat16)
 
 
-def scatter_group(partials):
-    summed = [plus(mine, swap_core(theirs)) for mine, theirs in partials]
+def return_to_owners(summed):
     half = summed[3].shape[0] // 2
     for_chip = jnp.concatenate(
         [plus(summed[1][:half], swap_pair(summed[3][:half])), summed[1][half:]], axis=0
@@ -754,10 +912,9 @@
     return keep, swap(give, axis, mask)
 
 
-def reduce_expert(keep, give):
+def far_sum(blocks):
     count = lax.axis_size("dp")
-    rest = keep.shape[1:]
-    blocks = plus(keep, swap(give, "dp", 2))
+    rest = blocks.shape[1:]
     low = 4
     while low < count:
         keep, got = halve(blocks.reshape((-1, 2, 2) + rest), "dp", low)
@@ -846,41 +1003,53 @@
     first_local = pair_bit * half_experts
     first_expert = lax.axis_index("expert") * experts_here + first_local
 
-    routing = jnp.concatenate([expert_ids.T.astype(jnp.float32), gate_weights.T], axis=0)
-    routes = [r for pair in gather_group(routing) for r in pair]
-    code, weight_of = route_slots(first_expert, routes, half_experts)
-    grad_pairs = gather_group(out_grad.astype(jnp.bfloat16))
-    arrived, scale = dispatch(code, weight_of, grad_pairs, capacity, True)
-
+    weight_high = gate_weights.astype(jnp.bfloat16)
+    weight_low = (gate_weights - weight_high.astype(jnp.float32)).astype(jnp.bfloat16)
+    routing = jnp.concatenate([expert_ids.astype(jnp.bfloat16), weight_high, weight_low], axis=1).T
+    routing = jnp.pad(routing, ((0, ROUTE_ROWS - routing.shape[0]), (0, D - rows_here)))
+    grad_rows = jnp.concatenate([out_grad.astype(jnp.bfloat16), routing], axis=0)
+    chip_grad_rows = swap_chip(grad_rows)
+    pair_grad_rows = swap_pair(grad_rows)
     ids = jnp.stack([segment_ids, parent_ids, positions])
     normed, qkv, attended, lse, middle, normed_ffn = attend(
         hidden_in, ids, norm_gains, qkv_weight, out_weight
     )
-    (received,) = dispatch(code, weight_of, gather_group(normed_ffn), capacity, False)
+    received, arrived, scale, code = gather_and_select(
+        normed_ffn, grad_rows, chip_grad_rows, pair_grad_rows, capacity, experts_here, half_experts, TOP, 5
+    )
     scalars = jnp.stack([first_local, z_bit])
-    own_parts = []
-    other_parts = []
-    backs = []
-    mixes = []
+    experts = []
+    near = []
+
+    def near_sum(j):
+        keep, give = experts[j][:2]
+        near.append(plus(keep, swap(give, "dp", 2)))
+
     for j in range(half_experts):
-        keep, give, back, mix = run_expert(
-            scalars, j, received, arrived, scale, gate_up_weight, down_weight, dp_count
+        after = [experts[-1][2]] if experts else []
+        if j == 3:
+            near_sum(0)
+            after.append(near[0])
+        experts.append(
+            run_expert(
+                scalars, j, received, arrived, scale, gate_up_weight, down_weight, dp_count, after
+            )
         )
-        own, other = reduce_expert(keep, give)
-        own_parts.append(own)
-        other_parts.append(other)
-        backs.append(back)
-        mixes.append(mix)
-    places = (3, 1, 2, 0)
-    back_parts = {i: combine(code, backs, i, capacity, "back") for i in places}
-    grad_parts = scatter_group([back_parts[i] for i in range(4)])
-    mix_parts = {i: combine(code, mixes, i, capacity, "mix") for i in places}
-    block_out = middle + sum(
-        part.astype(jnp.float32) for part in scatter_group([mix_parts[i] for i in range(4)])
-    )
+    normed_f_grad, mix_sums = combine_and_return(
+        code, [e[2] for e in experts], [e[3] for e in experts], capacity, 6
+    )
+    mix_parts = return_to_owners(mix_sums)
+    block_out = middle + sum(part.astype(jnp.float32) for part in mix_parts)
+    near_sum(1)
     input_grad, dense = attend_back(
-        hidden_in, out_grad, middle, grad_parts, normed, qkv, attended, lse, ids, norm_gains, qkv_weight, out_weight
-    )
+        hidden_in, out_grad, middle, normed_f_grad, normed, qkv, attended, lse, ids, norm_gains, qkv_weight,
+        out_weight, [near[1]]
+    )
+    for j in range(2, half_experts):
+        near_sum(j)
+    far = [far_sum(blocks) for blocks in near]
+    own_parts = [own for own, _ in far]
+    other_parts = [other for _, other in far]
 
     own = jnp.stack(own_parts).astype(jnp.float32)
     other = jnp.stack(other_parts).astype(jnp.float32)
@@ -925,7 +1094,7 @@
 
     qkv_columns = qkv_weight.shape[1]
     if D // dp_count % 64 == 0:
-        dense_own = reduce_dense(dense, 3)
+        dense_own = reduce_dense(dense, 3, [near[2]])
     else:
         dense_own = reduce_dense_far(dense)
     dense_own = dense_own.astype(jnp.float32)

time: 643 us -> 509 us (0.79)
  waiting for transfers between devices: 215 us -> 127 us
  Pallas kernels: 305 us -> 286 us
  starting transfers between devices: 38.9 us -> 20.2 us
  local copies, waits for them, and re-layouts: 18.8 us -> 12.3 us
    ppermute x52 -> x18, waiting for transfers between devices: 215 us -> 127 us  [swap(): return lax.ppermute(values, axis, [(i, i ^ mask) for i in range(count)])]
    ppermute x52 -> x18, starting transfers between devices: 38.9 us -> 20.2 us  [swap(): return lax.ppermute(values, axis, [(i, i ^ mask) for i in range(count)])]
    pallas_call x22 -> x7, Pallas kernels: 232 us -> 214 us  [the longest x4 74.5 us: run_expert(): pl.pallas_call(functools.partial(expert_kernel, owners, len(after)), out_...]
    convert_element_type x19 -> x9, other arithmetic: 13.8 us -> 15.9 us  [plus(): return (a.astype(jnp.float32) + b.astype(jnp.float32)).astype(jnp.bfloat16)]
  transfers between devices with their start and end apart: 52 -> 18, of which waited for: 19 -> 7; matrix products, arithmetic and copies ran while one was open for 6% -> 5% of each run, Pallas kernels for 32% -> 27%
where the time goes in v3:
time: 509 us; the launch traced here: 504 us
  Pallas kernels  286 us (56%)
  waiting for transfers between devices  127 us (25%)
  other arithmetic  54.4 us (11%)
  starting transfers between devices  20.2 us (4%)
  local copies, waits for them, and re-layouts  12.3 us (2%)
    ppermute x18, waiting for transfers between devices, swap(): return lax.ppermute(values, axis, [(i, i ^ mask) for i in range(count)])  127 us
    pallas_call x4, Pallas kernels, run_expert(): pl.pallas_call(functools.partial(expert_kernel, owners, len(after)), out_...  74.5 us
    pallas_call x1, Pallas kernels, reduce_dense(): pl.pallas_call(functools.partial(dense_kernel, orders, spans, len(after))...  58.3 us
    pallas_call x1, Pallas kernels, gather_and_select(): pl.pallas_call(functools.partial(gather_kernel, capacity, experts_here, h...  44.5 us
    pallas_call x1, Pallas kernels, combine_and_return(): pl.pallas_call(functools.partial(return_kernel, capacity, count), out_sha...  37.2 us
    pallas_call x1, Pallas kernels, attend_back(): pl.pallas_call(attend_back_kernel, out_shape=(jax.ShapeDtypeStruct((rows,...  26.4 us
    pallas_call x2, Pallas kernels, total_over(): pl.pallas_call(functools.partial(total_kernel, axis, count), out_shape=ja...  23.6 us
    ppermute x18, starting transfers between devices, swap(): return lax.ppermute(values, axis, [(i, i ^ mask) for i in range(count)])  20.2 us
  transfers between devices with their start and end apart: 18, of which 7 were waited for; matrix products, arithmetic and copies ran while one was open for 5% of the time, Pallas kernels for 27%

profile of v3, /device:TPU:0, one launch (start us, length us, event | category | flops | bytes accessed | tf_op | source)
XLA Modules:
  0.0 504.3 jit_solution(2357860432131352598)
XLA Ops:
  3.8 3.0 collective-permute-start
  9.0 17.7 %attend.1 = (bf16[384,1024]{1,0:T(8,128)(2,1)}, bf16[384,2048]{1,0:T(8,128)(2,1)}, bf16[384,1024]{1,0:T(8,128)(2,1)}, f32[384,128]{1,0:T(8,128)}, f32[384,1024]{1,0:T(8,128)}, /*index=5*/bf16[384,1024]{1,0:T(8,128)(2,1)}) custom-call(f32[384,1024]{1,0:T(8,128)} %hidden_ref.3, s32[3,384]{1,0:T(4,128)} %pad_add_fusion.ids_ref, bf16[2,1024]{1,0:T(2,128)(2,1)} %gains_ref.3, ...), custom_call_target="tpu_custom_call" | custom-call | tf_op jit(solution)/shard_map/attend/pallas_call | solution.py:210
  28.5 44.5 %gather_and_select.1 = (bf16[4,8,144,1024]{3,2,1,0:T(8,128)(2,1)}, bf16[4,8,144,1024]{3,2,1,0:T(8,128)(2,1)}, f32[4,8,144,1]{3,2,1,0:T(8,128)}, f32[8,4,384]{2,1,0:T(4,128)}) custom-call(bf16[384,1024]{1,0:T(8,128)(2,1)} %get-tuple-element.60.token_ref, bf16[416,1024]{1,0:T(8,128)(2,1)} %copy-done.8, bf16[416,1024]{1,0:T(8,128)(2,1)} %copy-done.14, ...), custom_call_target="tpu_custom_call" | custom-call | tf_op jit(solution)/shard_map/gather_and_select/pallas_call | solution.py:717
  73.0 18.6 %expert_0.1 = (bf16[4,192,1024]{2,1,0:T(8,128)(2,1)}, bf16[4,192,1024]{2,1,0:T(8,128)(2,1)}, bf16[1152,1024]{1,0:T(8,128)(2,1)}, bf16[1152,1024]{1,0:T(8,128)(2,1)}) custom-call(s32[2]{0:T(128)} %pad_add_fusion.1.s_ref, bf16[4,8,144,1024]{3,2,1,0:T(8,128)(2,1)} %get-tuple-element.62.rec_ref, bf16[4,8,144,1024]{3,2,1,0:T(8,128)(2,1)} %get-tuple-element.63.arr_ref, ...), custom_call_target="tpu_custom_call" | custom-call | tf_op jit(solution)/shard_map/expert_0/pallas_call | solution.py:77
  93.2 18.8 %expert_1.1 = (bf16[4,192,1024]{2,1,0:T(8,128)(2,1)}, bf16[4,192,1024]{2,1,0:T(8,128)(2,1)}, bf16[1152,1024]{1,0:T(8,128)(2,1)}, bf16[1152,1024]{1,0:T(8,128)(2,1)}) custom-call(s32[2]{0:T(128)} %pad_add_fusion.1.s_ref, bf16[4,8,144,1024]{3,2,1,0:T(8,128)(2,1)} %get-tuple-element.62.rec_ref, bf16[4,8,144,1024]{3,2,1,0:T(8,128)(2,1)} %get-tuple-element.63.arr_ref, ...), custom_call_target="tpu_custom_call" | custom-call | tf_op jit(solution)/shard_map/expert_1/pallas_call | solution.py:77
  112.4 18.4 %expert_2.1 = (bf16[4,192,1024]{2,1,0:T(8,128)(2,1)}, bf16[4,192,1024]{2,1,0:T(8,128)(2,1)}, bf16[1152,1024]{1,0:T(8,128)(2,1)}, bf16[1152,1024]{1,0:T(8,128)(2,1)}) custom-call(s32[2]{0:T(128)} %pad_add_fusion.1.s_ref, bf16[4,8,144,1024]{3,2,1,0:T(8,128)(2,1)} %get-tuple-element.62.rec_ref, bf16[4,8,144,1024]{3,2,1,0:T(8,128)(2,1)} %get-tuple-element.63.arr_ref, ...), custom_call_target="tpu_custom_call" | custom-call | tf_op jit(solution)/shard_map/expert_2/pallas_call | solution.py:77
  132.5 3.8 add_convert_fusion.3.refs_1_
  136.3 18.7 %expert_3.1 = (bf16[4,192,1024]{2,1,0:T(8,128)(2,1)}, bf16[4,192,1024]{2,1,0:T(8,128)(2,1)}, bf16[1152,1024]{1,0:T(8,128)(2,1)}, bf16[1152,1024]{1,0:T(8,128)(2,1)}) custom-call(s32[2]{0:T(128)} %pad_add_fusion.1.s_ref, bf16[4,8,144,1024]{3,2,1,0:T(8,128)(2,1)} %get-tuple-element.62.rec_ref, bf16[4,8,144,1024]{3,2,1,0:T(8,128)(2,1)} %get-tuple-element.63.arr_ref, ...), custom_call_target="tpu_custom_call" | custom-call | tf_op jit(solution)/shard_map/expert_3/pallas_call | solution.py:77
  155.0 37.2 %combine_and_return.1 = (f32[384,1024]{1,0:T(8,128)}, bf16[4,384,1024]{2,1,0:T(8,128)(2,1)}) custom-call(f32[8,4,384]{2,1,0:T(4,128)} %get-tuple-element.61.code_ref, bf16[1152,1024]{1,0:T(8,128)(2,1)} %get-tuple-element.65.refs_0_, bf16[1152,1024]{1,0:T(8,128)(2,1)} %get-tuple-element.66.refs_0_.refs_1_, ...), custom_call_target="tpu_custom_call" | custom-call | tf_op jit(solution)/shard_map/combine_and_return/pallas_call | solution.py:844
  192.3 3.3 add_convert_fusion.2.refs_0_
  195.5 26.4 %attend_back.1 = (f32[384,1024]{1,0:T(8,128)}, bf16[1024,3200]{1,0:T(8,128)(2,1)}) custom-call(f32[384,1024]{1,0:T(8,128)} %hidden_ref.3, f32[384,1024]{1,0:T(8,128)} %grad_ref.1, f32[384,1024]{1,0:T(8,128)} %get-tuple-element.59.middle_ref, f32[384,1024]{1,0:T(8,128)} %get-tuple-element.76.normed_grad_ref, bf16[384,1024]{1,0:T(8,128)(2,1)} %get-tuple-element.77.normed_ref, ...), custom_call_target="tpu_custom_call" | custom-call | tf_op jit(solution)/shard_map/attend_back/pallas_call | solution.py:317
  223.8 58.3 %reduce_dense.1 = bf16[2,2,32,3200]{3,2,1,0:T(8,128)(2,1)} custom-call(bf16[2,2,2,2,2,32,3200]{6,5,4,3,2,1,0:T(8,128)(2,1)} %bitcast.132, bf16[4,192,1024]{2,1,0:T(8,128)(2,1)} %add_convert_fusion.1.refs_0_), custom_call_target="tpu_custom_call" | custom-call | tf_op jit(solution)/shard_map/reduce_dense/pallas_call | solution.py:553
  288.2 11.7 %total_4.1 = f32[8,8,128]{2,1,0:T(8,128)S(1)} custom-call(f32[8,8,128]{2,1,0:T(8,128)S(1)} %pad_bitcast_fusion.mine_ref), custom_call_target="tpu_custom_call" | custom-call | tf_op jit(solution)/shard_map/total_4/pallas_call | solution.py:391
  320.6 32.2 %collective-permute-done.9 = bf16[1,2,192,1024]{3,2,1,0:T(8,128)(2,1)} collective-permute-done((bf16[1,2,192,1024]{3,2,1,0:T(8,128)(2,1)}, bf16[1,2,192,1024]{3,2,1,0:T(8,128)(2,1)}, u32[]{:S(2)}, u32[]{:S(2)}) %collective-permute-start.9) | collective-permute-done | bytes 786464 | tf_op jit(solution)/shard_map/ppermute | solution.py:878
  354.9 6.3 %collective-permute-done.12 = bf16[4,192,1024]{2,1,0:T(8,128)(2,1)} collective-permute-done((bf16[4,192,1024]{2,1,0:T(8,128)(2,1)}, bf16[4,192,1024]{2,1,0:T(8,128)(2,1)}, u32[]{:S(2)}, u32[]{:S(2)}) %collective-permute-start.12) | collective-permute-done | bytes 1572896 | tf_op jit(solution)/shard_map/ppermute | solution.py:878
  364.1 41.3 %collective-permute-done.10 = bf16[1,2,192,1024]{3,2,1,0:T(8,128)(2,1)} collective-permute-done((bf16[1,2,192,1024]{3,2,1,0:T(8,128)(2,1)}, bf16[1,2,192,1024]{3,2,1,0:T(8,128)(2,1)}, u32[]{:S(2)}, u32[]{:S(2)}) %collective-permute-start.10) | collective-permute-done | bytes 786464 | tf_op jit(solution)/shard_map/ppermute | solution.py:878
  406.9 23.7 %collective-permute-done.11 = bf16[1,2,192,1024]{3,2,1,0:T(8,128)(2,1)S(1)} collective-permute-done((bf16[1,2,192,1024]{3,2,1,0:T(8,128)(2,1)S(1)}, bf16[1,2,192,1024]{3,2,1,0:T(8,128)(2,1)S(1)}, u32[]{:S(2)}, u32[]{:S(2)}) %collective-permute-start.11) | collective-permute-done | bytes 786464 | tf_op jit(solution)/shard_map/ppermute | solution.py:878
  431.5 12.5 %collective-permute-done.13 = bf16[1,2,192,1024]{3,2,1,0:T(8,128)(2,1)S(1)} collective-permute-done((bf16[1,2,192,1024]{3,2,1,0:T(8,128)(2,1)S(1)}, bf16[1,2,192,1024]{3,2,1,0:T(8,128)(2,1)S(1)}, u32[]{:S(2)}, u32[]{:S(2)}) %collective-permute-start.13) | collective-permute-done | bytes 786464 | tf_op jit(solution)/shard_map/ppermute | solution.py:878
  449.4 6.5 %collective-permute-done.16 = bf16[1,192,1024]{2,1,0:T(8,128)(2,1)S(1)} collective-permute-done((bf16[1,192,1024]{2,1,0:T(8,128)(2,1)S(1)}, bf16[1,192,1024]{2,1,0:T(8,128)(2,1)S(1)}, u32[]{:S(2)}, u32[]{:S(2)}) %collective-permute-start.16) | collective-permute-done | bytes 393248 | tf_op jit(solution)/shard_map/ppermute | solution.py:878
  455.9 4.2 collective-permute-done.17
  466.7 11.9 %total_1.1 = f32[8,40,128]{2,1,0:T(8,128)S(1)} custom-call(f32[8,40,128]{2,1,0:T(8,128)S(1)} %bitcast.124), custom_call_target="tpu_custom_call" | custom-call | tf_op jit(solution)/shard_map/total_1/pallas_call | solution.py:391
  481.0 3.7 collect_2.1
  490.0 3.6 multiply_subtract_fusion.1
  494.3 5.6 %multiply_subtract_fusion = f32[8,128,1024]{2,1,0:T(8,128)} fusion(f32[8,192,1024]{2,1,0:T(8,128)} %copy-done.2, f32[8,1024]{1,0:T(8,128)S(1)} %get-tuple-element.156, f32[8,128]{1,0:T(8,128)S(1)} %rsqrt_multiply_fusion.2, bf16[8,1024,1024]{2,1,0:T(8,128)(2,1)} %up_ref.7, s32[]{:T(128)S(6)} %select_n.63), kind=kLoop, calls=%fused_computation.1 | loop fusion | flops 4194304 | bytes 10522628 | tf_op jit(solution)/shard_map/sub | solution.py:1149
  (168 shorter events, 67.7 us)
Async XLA Ops:
  0.7 131.7 %copy-start = (f32[2,1024]{1,0:T(2,128)S(1)}, f32[2,1024]{1,0:T(2,128)}, u32[]{:S(2)}) copy-start(f32[2,1024]{1,0:T(2,128)} %param.36) | copy-start | bytes 24580
  3.8 23.5 %collective-permute-start = (bf16[416,1024]{1,0:T(8,128)(2,1)S(1)}, bf16[416,1024]{1,0:T(8,128)(2,1)S(1)}, u32[]{:S(2)}, u32[]{:S(2)}) collective-permute-start(bf16[416,1024]{1,0:T(8,128)(2,1)S(1)} %fusion.7.grad_ref), channel_id=1, source_target_pairs={{0,2},{1,3},{2,0},{3,1},{4,6},{5,7},{6,4},{7,5},{8,10},{9,11},{10,... | collective-permute-start | bytes 2555912 | tf_op jit(solution)/shard_map/ppermute | solution.py:878
  6.9 20.4 %collective-permute-start.1 = (bf16[416,1024]{1,0:T(8,128)(2,1)S(1)}, bf16[416,1024]{1,0:T(8,128)(2,1)S(1)}, u32[]{:S(2)}, u32[]{:S(2)}) collective-permute-start(bf16[416,1024]{1,0:T(8,128)(2,1)S(1)} %fusion.7.grad_ref), channel_id=1, source_target_pairs={{0,4},{4,0},{8,12},{12,8},{16,20},{20,16},{24,28},{28,24},{1,5},{5... | collective-permute-start | bytes 2555912 | tf_op jit(solution)/shard_map/ppermute | solution.py:878
  91.6 40.9 %collective-permute-start.2 = (bf16[4,192,1024]{2,1,0:T(8,128)(2,1)}, bf16[4,192,1024]{2,1,0:T(8,128)(2,1)}, u32[]{:S(2)}, u32[]{:S(2)}) collective-permute-start(bf16[4,192,1024]{2,1,0:T(8,128)(2,1)} %get-tuple-element.69), channel_id=1, source_target_pairs={{0,8},{4,12},{8,0},{12,4},{16,24},{20,28},{24,16},{28,20},{1,9},{5... | collective-permute-start | bytes 4718600 | tf_op jit(solution)/shard_map/ppermute | solution.py:878
  111.9 80.3 %collective-permute-start.7 = (bf16[4,192,1024]{2,1,0:T(8,128)(2,1)}, bf16[4,192,1024]{2,1,0:T(8,128)(2,1)}, u32[]{:S(2)}, u32[]{:S(2)}) collective-permute-start(bf16[4,192,1024]{2,1,0:T(8,128)(2,1)} %get-tuple-element.82), channel_id=1, source_target_pairs={{0,8},{4,12},{8,0},{12,4},{16,24},{20,28},{24,16},{28,20},{1,9},{5... | collective-permute-start | bytes 4718600 | tf_op jit(solution)/shard_map/ppermute | solution.py:878
  130.8 91.2 %collective-permute-start.8 = (bf16[4,192,1024]{2,1,0:T(8,128)(2,1)}, bf16[4,192,1024]{2,1,0:T(8,128)(2,1)S(1)}, u32[]{:S(2)}, u32[]{:S(2)}) collective-permute-start(bf16[4,192,1024]{2,1,0:T(8,128)(2,1)} %get-tuple-element.86), channel_id=1, source_target_pairs={{0,8},{4,12},{8,0},{12,4},{16,24},{20,28},{24,16},{28,20},{1,9},{5... | collective-permute-start | bytes 4718600 | tf_op jit(solution)/shard_map/ppermute | solution.py:878
  285.7 200.9 %copy-start.25 = (f32[128]{0:T(128)}, f32[128]{0:T(128)S(1)}, u32[]{:S(2)}) copy-start(f32[128]{0:T(128)S(1)} %get-tuple-element.131) | copy-start | bytes 1540
  285.7 201.6 %copy-start.26 = (f32[128]{0:T(128)}, f32[128]{0:T(128)S(1)}, u32[]{:S(2)}) copy-start(f32[128]{0:T(128)S(1)} %get-tuple-element.167) | copy-start | bytes 1540
  300.0 61.2 %collective-permute-start.12 = (bf16[4,192,1024]{2,1,0:T(8,128)(2,1)}, bf16[4,192,1024]{2,1,0:T(8,128)(2,1)}, u32[]{:S(2)}, u32[]{:S(2)}) collective-permute-start(bf16[4,192,1024]{2,1,0:T(8,128)(2,1)} %get-tuple-element.88), channel_id=1, source_target_pairs={{0,8},{4,12},{8,0},{12,4},{16,24},{20,28},{24,16},{28,20},{1,9},{5... | collective-permute-start | bytes 4718600 | tf_op jit(solution)/shard_map/ppermute | solution.py:878
  303.4 13.3 %collective-permute-start.3 = (bf16[192,1024]{1,0:T(8,128)(2,1)}, bf16[192,1024]{1,0:T(8,128)(2,1)}, u32[]{:S(2)}, u32[]{:S(2)}) collective-permute-start(bf16[192,1024]{1,0:T(8,128)(2,1)} %get-tuple-element.142), channel_id=1, source_target_pairs={{0,4},{4,0},{8,12},{12,8},{16,20},{20,16},{24,28},{28,24},{1,5},{5... | collective-permute-start | bytes 1179656 | tf_op jit(solution)/shard_map/ppermute | solution.py:878
  304.0 14.2 %collective-permute-start.5 = (bf16[192,1024]{1,0:T(8,128)(2,1)}, bf16[192,1024]{1,0:T(8,128)(2,1)}, u32[]{:S(2)}, u32[]{:S(2)}) collective-permute-start(bf16[192,1024]{1,0:T(8,128)(2,1)} %get-tuple-element.143), channel_id=1, source_target_pairs={{0,2},{1,3},{2,0},{3,1},{4,6},{5,7},{6,4},{7,5},{8,10},{9,11},{10,... | collective-permute-start | bytes 1179656 | tf_op jit(solution)/shard_map/ppermute | solution.py:878
  307.9 44.9 %collective-permute-start.9 = (bf16[1,2,192,1024]{3,2,1,0:T(8,128)(2,1)}, bf16[1,2,192,1024]{3,2,1,0:T(8,128)(2,1)}, u32[]{:S(2)}, u32[]{:S(2)}) collective-permute-start(bf16[1,2,192,1024]{3,2,1,0:T(8,128)(2,1)} %dynamic-slice_bitcast_fusion.3), channel_id=1, source_target_pairs={{0,16},{4,20},{8,24},{12,28},{16,0},{20,4},{24,8},{28,12},{1,17},{... | collective-permute-start | bytes 2359304 | tf_op jit(solution)/shard_map/ppermute | solution.py:878
  311.3 94.1 %collective-permute-start.10 = (bf16[1,2,192,1024]{3,2,1,0:T(8,128)(2,1)}, bf16[1,2,192,1024]{3,2,1,0:T(8,128)(2,1)}, u32[]{:S(2)}, u32[]{:S(2)}) collective-permute-start(bf16[1,2,192,1024]{3,2,1,0:T(8,128)(2,1)} %dynamic-slice_bitcast_fusion.2), channel_id=1, source_target_pairs={{0,16},{4,20},{8,24},{12,28},{16,0},{20,4},{24,8},{28,12},{1,17},{... | collective-permute-start | bytes 2359304 | tf_op jit(solution)/shard_map/ppermute | solution.py:878
  316.7 113.9 %collective-permute-start.11 = (bf16[1,2,192,1024]{3,2,1,0:T(8,128)(2,1)S(1)}, bf16[1,2,192,1024]{3,2,1,0:T(8,128)(2,1)S(1)}, u32[]{:S(2)}, u32[]{:S(2)}) collective-permute-start(bf16[1,2,192,1024]{3,2,1,0:T(8,128)(2,1)S(1)} %dynamic-slice_bitcast_fusion.1), channel_id=1, source_target_pairs={{0,16},{4,20},{8,24},{12,28},{16,0},{20,4},{24,8},{28,12},{1,17},{... | collective-permute-start | bytes 2359304 | tf_op jit(solution)/shard_map/ppermute | solution.py:878
  319.9 125.1 %collective-permute-start.4 = (bf16[384,1024]{1,0:T(8,128)(2,1)S(1)}, bf16[384,1024]{1,0:T(8,128)(2,1)S(1)}, u32[]{:S(2)}, u32[]{:S(2)}) collective-permute-start(bf16[384,1024]{1,0:T(8,128)(2,1)S(1)} %pad_maximum_fusion), channel_id=1, source_target_pairs={{0,2},{1,3},{2,0},{3,1},{4,6},{5,7},{6,4},{7,5},{8,10},{9,11},{10,... | collective-permute-start | bytes 2359304 | tf_op jit(solution)/shard_map/ppermute | solution.py:878
  320.6 41.5 %copy-start.11 = (bf16[4,192,1024]{2,1,0:T(8,128)(2,1)S(1)}, bf16[4,192,1024]{2,1,0:T(8,128)(2,1)}, u32[]{:S(2)}) copy-start(bf16[4,192,1024]{2,1,0:T(8,128)(2,1)} %get-tuple-element.87) | copy-start | bytes 4718596
  352.8 93.7 %collective-permute-start.6 = (bf16[384,1024]{1,0:T(8,128)(2,1)S(1)}, bf16[384,1024]{1,0:T(8,128)(2,1)S(1)}, u32[]{:S(2)}, u32[]{:S(2)}) collective-permute-start(bf16[384,1024]{1,0:T(8,128)(2,1)S(1)} %pad_maximum_fusion.1), channel_id=1, source_target_pairs={{0,4},{4,0},{8,12},{12,8},{16,20},{20,16},{24,28},{28,24},{1,5},{5... | collective-permute-start | bytes 2359304 | tf_op jit(solution)/shard_map/ppermute | solution.py:878
  361.2 88.3 %collective-permute-start.14 = (bf16[1,192,1024]{2,1,0:T(8,128)(2,1)S(1)}, bf16[1,192,1024]{2,1,0:T(8,128)(2,1)S(1)}, u32[]{:S(2)}, u32[]{:S(2)}) collective-permute-start(bf16[1,192,1024]{2,1,0:T(8,128)(2,1)S(1)} %get-tuple-element.147), channel_id=1, source_target_pairs={{0,4},{4,0},{8,12},{12,8},{16,20},{20,16},{24,28},{28,24},{1,5},{5... | collective-permute-start | bytes 1179656 | tf_op jit(solution)/shard_map/ppermute | solution.py:878
  364.0 41.4 %copy-start.5 = (bf16[4,192,1024]{2,1,0:T(8,128)(2,1)S(1)}, bf16[4,192,1024]{2,1,0:T(8,128)(2,1)}, u32[]{:S(2)}) copy-start(bf16[4,192,1024]{2,1,0:T(8,128)(2,1)} %add_convert_fusion.2.refs_0_) | copy-start | bytes 4718596
  364.1 67.1 %copy-start.6 = (bf16[4,192,1024]{2,1,0:T(8,128)(2,1)S(1)}, bf16[4,192,1024]{2,1,0:T(8,128)(2,1)}, u32[]{:S(2)}) copy-start(bf16[4,192,1024]{2,1,0:T(8,128)(2,1)} %add_convert_fusion.1.refs_0_) | copy-start | bytes 4718596
  405.4 38.6 %collective-permute-start.13 = (bf16[1,2,192,1024]{3,2,1,0:T(8,128)(2,1)S(1)}, bf16[1,2,192,1024]{3,2,1,0:T(8,128)(2,1)S(1)}, u32[]{:S(2)}, u32[]{:S(2)}) collective-permute-start(bf16[1,2,192,1024]{3,2,1,0:T(8,128)(2,1)S(1)} %dynamic-slice_bitcast_fusion), channel_id=1, source_target_pairs={{0,16},{4,20},{8,24},{12,28},{16,0},{20,4},{24,8},{28,12},{1,17},{... | collective-permute-start | bytes 2359304 | tf_op jit(solution)/shard_map/ppermute | solution.py:878
  430.6 18.9 %collective-permute-start.15 = (bf16[1,192,1024]{2,1,0:T(8,128)(2,1)S(1)}, bf16[1,192,1024]{2,1,0:T(8,128)(2,1)S(1)}, u32[]{:S(2)}, u32[]{:S(2)}) collective-permute-start(bf16[1,192,1024]{2,1,0:T(8,128)(2,1)S(1)} %get-tuple-element.149), channel_id=1, source_target_pairs={{0,4},{4,0},{8,12},{12,8},{16,20},{20,16},{24,28},{28,24},{1,5},{5... | collective-permute-start | bytes 1179656 | tf_op jit(solution)/shard_map/ppermute | solution.py:878
  444.0 11.9 %collective-permute-start.16 = (bf16[1,192,1024]{2,1,0:T(8,128)(2,1)S(1)}, bf16[1,192,1024]{2,1,0:T(8,128)(2,1)S(1)}, u32[]{:S(2)}, u32[]{:S(2)}) collective-permute-start(bf16[1,192,1024]{2,1,0:T(8,128)(2,1)S(1)} %get-tuple-element.151), channel_id=1, source_target_pairs={{0,4},{4,0},{8,12},{12,8},{16,20},{20,16},{24,28},{28,24},{1,5},{5... | collective-permute-start | bytes 1179656 | tf_op jit(solution)/shard_map/ppermute | solution.py:878
  445.0 15.2 %collective-permute-start.17 = (bf16[1,192,1024]{2,1,0:T(8,128)(2,1)S(1)}, bf16[1,192,1024]{2,1,0:T(8,128)(2,1)S(1)}, u32[]{:S(2)}, u32[]{:S(2)}) collective-permute-start(bf16[1,192,1024]{2,1,0:T(8,128)(2,1)S(1)} %get-tuple-element.153), channel_id=1, source_target_pairs={{0,4},{4,0},{8,12},{12,8},{16,20},{20,16},{24,28},{28,24},{1,5},{5... | collective-permute-start | bytes 1179656 | tf_op jit(solution)/shard_map/ppermute | solution.py:878
  (26 other events, 331.6 us)

commit v4 on v3

--- a/solution.py
+++ b/solution.py
@@ -9,6 +9,13 @@
 from jax.sharding import PartitionSpec as P
 
 VM = 60 * 1024 * 1024
+SCALE = 1e6
+
+
+def lasts(microseconds):
+    return pl.CostEstimate(
+        flops=int(microseconds * SCALE), bytes_accessed=1024, transcendentals=0
+    )
 
 
 def dot(a, b, ca=1, cb=0):
@@ -48,9 +55,8 @@
     up_rows = width // owners
     down_rows = ff // owners
     for slot in range(owners // 2):
-        high, low = slot // 2, slot % 2
         for ref, side in ((keep_ref, bit), (give_ref, 1 - bit)):
-            owner = high * 4 + side * 2 + low
+            owner = 2 * slot + side
             ref[slot, :up_rows, :] = wg_s[
                 pl.ds(pl.multiple_of(owner * up_rows, up_rows), up_rows), :
             ].astype(jnp.bfloat16)
@@ -97,6 +103,7 @@
             ],
         ),
         compiler_params=pltpu.CompilerParams(vmem_limit_bytes=VM),
+        cost_estimate=lasts(18),
         name="expert_%d" % j,
     )(scalars, received, arrived, scale, up_w, down_w, *after)
 
@@ -224,6 +231,7 @@
             pltpu.VMEM((rows, rows), jnp.float32),
         ],
         compiler_params=pltpu.CompilerParams(vmem_limit_bytes=VM),
+        cost_estimate=lasts(18),
         name="attend",
     )(hidden, ids, gains, qkv_w, out_w)
 
@@ -329,6 +337,7 @@
             pltpu.VMEM((rows, out_w.shape[0]), jnp.bfloat16),
         ],
         compiler_params=pltpu.CompilerParams(vmem_limit_bytes=VM),
+        cost_estimate=lasts(26),
         name="attend_back",
     )(hidden, out_grad, middle, normed_f_grad, normed, qkv, attended, lse, ids, gains, qkv_w, out_w, *after)
 
@@ -343,7 +352,8 @@
     pl.semaphore_wait(barrier, len(peers))
 
 
-def total_kernel(axis, count, mine_ref, out_ref, got_ref, send_sem, recv_sem):
+def total_kernel(axis, count, mine_ref, *refs):
+    out_ref, got_ref, send_sem, recv_sem = refs[-4:]
     me = lax.axis_index(axis)
     after = [lax.rem(me + k, count) for k in range(count)]
     greet([{axis: after[k]} for k in range(1, count)])
@@ -384,14 +394,14 @@
         copy.wait_send()
 
 
-def total_over(values, axis, label):
+def total_over(values, axis, label, after=()):
     count = lax.axis_size(axis)
     rows = -(-values.shape[0] // (8 * 128 * count)) * 8
     padded = jnp.pad(values, (0, count * rows * 128 - values.shape[0])).reshape(count, rows, 128)
     out = pl.pallas_call(
         functools.partial(total_kernel, axis, count),
         out_shape=jax.ShapeDtypeStruct(padded.shape, jnp.float32),
-        in_specs=[pl.BlockSpec(memory_space=pltpu.VMEM)],
+        in_specs=[pl.BlockSpec(memory_space=pltpu.VMEM)] + [pl.BlockSpec(memory_space=pl.ANY)] * len(after),
         out_specs=pl.BlockSpec(memory_space=pltpu.VMEM),
         scratch_shapes=[
             pltpu.VMEM(padded.shape, jnp.float32),
@@ -401,8 +411,9 @@
         compiler_params=pltpu.CompilerParams(
             collective_id=label, has_side_effects=True, vmem_limit_bytes=16 * 1024 * 1024
         ),
+        cost_estimate=lasts(12),
         name="total_%d" % label,
-    )(padded)
+    )(padded, *after)
     return out.reshape(-1)[: values.shape[0]]
 
 
@@ -443,6 +454,7 @@
         compiler_params=pltpu.CompilerParams(
             collective_id=label, has_side_effects=True, vmem_limit_bytes=16 * 1024 * 1024
         ),
+        cost_estimate=lasts(4),
         name="collect_%d" % label,
     )(values)
 
@@ -453,9 +465,9 @@
     return bit, {axis: index + mask - 2 * mask * bit}
 
 
-def dense_kernel(orders, spans, waits, mine_ref, *refs):
+def dense_kernel(orders, spans, waits, far_bit, mine_ref, go_ref, *refs):
     steps = len(orders[0])
-    (out_ref, sum_ref), scratch = refs[waits : waits + 2], refs[waits + 2 :]
+    (out_ref, come_ref, sum_ref), scratch = refs[waits : waits + 3], refs[waits + 3 :]
     first_got = scratch[0]
     got = scratch[1 : 1 + steps]
     send_sem, recv_sem = scratch[1 + steps :]
@@ -484,6 +496,7 @@
         return (first.astype(jnp.float32) + second.astype(jnp.float32)).astype(jnp.bfloat16)
 
     flying = []
+    beside = send(go_ref, come_ref, links[far_bit][1], 0, 3 + steps)
     for part, span in enumerate(spans):
         at = whole + (1 - core, slice(None), slice(None), span)
         flying.append(send(mine_ref.at[at], first_got.at[..., span], core_peer, part, 0))
@@ -526,7 +539,7 @@
         flying[part].wait_recv()
         mine = out_ref.at[core, :, :, span]
         flying[part] = send(mine, mine, core_peer, part, 2 + steps)
-    for copy in flying:
+    for copy in flying + [beside]:
         copy.wait_recv()
     for copy in copies:
         copy.wait_send()
@@ -536,7 +549,7 @@
     return (slice(None),) * (len(orders[part]) - 1 - step)
 
 
-def reduce_dense(dense, label, after=()):
+def reduce_dense(dense, go, far_mask, label, after=()):
     owners = lax.axis_size("dp")
     width, columns = dense.shape
     bits = owners.bit_length() - 1
@@ -550,26 +563,31 @@
     orders = [tuple(all_links[s:] + all_links[:s]) for s in starts[:parts]]
     shape = (2,) * bits + (2, 2, rows, columns)
     half = (2,) * bits + (2, rows, columns)
-    out = pl.pallas_call(
-        functools.partial(dense_kernel, orders, spans, len(after)),
-        out_shape=jax.ShapeDtypeStruct((2, 2, rows, columns), jnp.bfloat16),
-        in_specs=[pl.BlockSpec(memory_space=pltpu.VMEM)] + [pl.BlockSpec(memory_space=pl.ANY)] * len(after),
-        out_specs=pl.BlockSpec(memory_space=pltpu.VMEM),
+    out, come = pl.pallas_call(
+        functools.partial(dense_kernel, orders, spans, len(after), far_mask.bit_length() - 1),
+        out_shape=(
+            jax.ShapeDtypeStruct((2, 2, rows, columns), jnp.bfloat16),
+            jax.ShapeDtypeStruct(go.shape, jnp.bfloat16),
+        ),
+        in_specs=[pl.BlockSpec(memory_space=pltpu.VMEM)]
+        + [pl.BlockSpec(memory_space=pl.ANY)] * (1 + len(after)),
+        out_specs=[pl.BlockSpec(memory_space=pltpu.VMEM), pl.BlockSpec(memory_space=pl.ANY)],
         scratch_shapes=[pltpu.VMEM(half, jnp.bfloat16), pltpu.VMEM(half, jnp.bfloat16)]
         + [
             pltpu.VMEM((2,) * (bits - step) + (rows, columns), jnp.bfloat16)
             for step in range(bits + 1)
         ]
-        + [pltpu.SemaphoreType.DMA((parts, bits + 4)), pltpu.SemaphoreType.DMA((parts, bits + 4))],
+        + [pltpu.SemaphoreType.DMA((parts, bits + 5)), pltpu.SemaphoreType.DMA((parts, bits + 5))],
         compiler_params=pltpu.CompilerParams(
             collective_id=label, has_side_effects=True, vmem_limit_bytes=VM
         ),
+        cost_estimate=lasts(50),
         name="reduce_dense",
-    )(dense.reshape(shape), *after)
-    return out.reshape(width // owners, columns)
-
-
-PAIR = 1
+    )(dense.reshape(shape), go, *after)
+    return out.reshape(width // owners, columns), come
+
+
+PAIR = 2
 ROUTE_ROWS = 32
 
 
@@ -736,22 +754,25 @@
         compiler_params=pltpu.CompilerParams(
             collective_id=label, has_side_effects=True, vmem_limit_bytes=VM
         ),
+        cost_estimate=lasts(44),
         name="gather_and_select",
     )(token, grad, chip_grad, pair_grad)
 
 
-def return_kernel(capacity, count, code_ref, *refs):
+def return_kernel(capacity, count, far_mask, code_ref, *refs):
     backs, mixes = refs[:count], refs[count : 2 * count]
-    out_ref, mix_ref = refs[2 * count : 2 * count + 2]
+    go_ref, out_ref, near_ref, far_ref, come_ref = refs[2 * count : 2 * count + 5]
     (fetched, theirs, core_got, own, theirs_mix, core_got_mix, half_pair, half_chip, from_chip, from_pair,
-     send_sem, recv_sem, local_sem) = refs[2 * count + 2 :]
+     send_sem, recv_sem, local_sem) = refs[2 * count + 5 :]
     rows = out_ref.shape[0]
     half = rows // 2
     _, core = flipped("expert", 1)
     _, chip = flipped("expert", 2)
     _, pair = flipped("dp", PAIR)
-    greet([core, chip, pair])
+    _, far = flipped("dp", far_mask)
+    greet([core, chip, pair, far])
     push = Pusher(send_sem, recv_sem)
+    beside = push(go_ref, come_ref, far)
     order = [(backs, r) for r in (7, 6, 3, 2, 5, 4, 1, 0)] + [(mixes, r) for r in (7, 6, 3, 2, 5, 4, 1, 0)]
     depth = fetched.shape[0]
     fetching = []
@@ -816,7 +837,7 @@
     out_ref[...] = mine + core_got[0].astype(jnp.float32)
     mine, copy = sums(3, theirs_mix, core_got_mix)
     copy.wait_recv()
-    mix_ref[3] = plus(mine, core_got_mix[3])
+    far_ref[1] = plus(mine, core_got_mix[3])
     at_pair.wait_recv()
     own[1, :half] = plus(own[1, :half].astype(jnp.float32), half_pair[...])
     high_chip = push(own.at[1, 0:half], from_chip.at[0:half], chip)
@@ -826,60 +847,321 @@
     for i in (1, 2, 0):
         mine, copy = sums(i, theirs_mix, core_got_mix)
         copy.wait_recv()
-        mix_ref[i] = plus(mine, core_got_mix[i])
+        (far_ref if i > 1 else near_ref)[i % 2] = plus(mine, core_got_mix[i])
     low_chip.wait_recv()
     high_pair.wait_recv()
     high_chip.wait_recv()
     low_pair.wait_recv()
     out_ref[...] += from_chip[...].astype(jnp.float32) + from_pair[...].astype(jnp.float32)
+    beside.wait_recv()
     push.finish()
 
 
-def combine_and_return(code, backs, mixes, capacity, label):
+def combine_and_return(code, backs, mixes, capacity, go, far_mask, label):
     _, count, rows = code.shape
     width = backs[0].shape[1]
     vmem = pl.BlockSpec(memory_space=pltpu.VMEM)
     anywhere = pl.BlockSpec(memory_space=pl.ANY)
     four = pltpu.VMEM((4, rows, width), jnp.bfloat16)
     return pl.pallas_call(
-        functools.partial(return_kernel, capacity, count),
+        functools.partial(return_kernel, capacity, count, far_mask),
         out_shape=(
             jax.ShapeDtypeStruct((rows, width), jnp.float32),
-            jax.ShapeDtypeStruct((4, rows, width), jnp.bfloat16),
+            jax.ShapeDtypeStruct((2, rows, width), jnp.bfloat16),
+            jax.ShapeDtypeStruct((2, rows, width), jnp.bfloat16),
+            jax.ShapeDtypeStruct(go.shape, jnp.bfloat16),
         ),
-        in_specs=[vmem] + [anywhere] * (2 * count),
-        out_specs=[vmem, vmem],
+        in_specs=[vmem] + [anywhere] * (2 * count + 1),
+        out_specs=[vmem, vmem, vmem, anywhere],
         scratch_shapes=[pltpu.VMEM((4, count * capacity, width), jnp.bfloat16), four, four, four, four, four]
         + [pltpu.VMEM((rows // 2, width), jnp.bfloat16)] * 2
         + [pltpu.VMEM((rows, width), jnp.bfloat16)] * 2
         + [
-            pltpu.SemaphoreType.DMA((14,)),
-            pltpu.SemaphoreType.DMA((14,)),
+            pltpu.SemaphoreType.DMA((16,)),
+            pltpu.SemaphoreType.DMA((16,)),
             pltpu.SemaphoreType.DMA((4, count)),
         ],
         compiler_params=pltpu.CompilerParams(
             collective_id=label, has_side_effects=True, vmem_limit_bytes=VM
         ),
+        cost_estimate=lasts(37),
         name="combine_and_return",
-    )(code, *backs, *mixes)
-
-
-D = 1024
-FF = 512
-TOP = 8
+    )(code, *backs, *mixes, go)
+
+
+def settle_kernel(bit_ref, keep_ref, got_ref, *refs):
+    stay_ref, go_ref = refs[-2:]
+    bit = bit_ref[0]
+    for high in range(keep_ref.shape[0]):
+        for low in range(keep_ref.shape[2]):
+            for ref, side in ((stay_ref, bit), (go_ref, 1 - bit)):
+                total = keep_ref[high, side, low].astype(jnp.float32) + got_ref[
+                    high, side, low
+                ].astype(jnp.float32)
+                ref[high, low] = total.astype(jnp.bfloat16)
+
+
+def settle(keep, got, mask, label, after):
+    count, rows, columns = keep.shape
+    low = 1 if mask == PAIR else 2
+    shape = (count // 2 // low, 2, low, rows, columns)
+    half = jax.ShapeDtypeStruct((count // 2 // low, low, rows, columns), jnp.bfloat16)
+    bit = lax.rem(lax.axis_index("dp") // mask, 2)
+    vmem = pl.BlockSpec(memory_space=pltpu.VMEM)
+    stay, go = pl.pallas_call(
+        settle_kernel,
+        out_shape=(half, half),
+        in_specs=[pl.BlockSpec(memory_space=pltpu.SMEM), vmem, vmem]
+        + [pl.BlockSpec(memory_space=pl.ANY)] * len(after),
+        out_specs=[vmem, vmem],
+        compiler_params=pltpu.CompilerParams(vmem_limit_bytes=VM),
+        cost_estimate=lasts(3),
+        name="settle_%s" % label,
+    )(bit.reshape(1), keep.reshape(shape), got.reshape(shape), *after)
+    return stay.reshape(-1, rows, columns), go.reshape(-1, rows, columns)
+
+
+def settle_mix_kernel(near_ref, got_ref, *refs):
+    refs[-1][...] = (near_ref[1].astype(jnp.float32) + got_ref[1].astype(jnp.float32)).astype(jnp.bfloat16)
+
+
+def settle_mix(near, got, after):
+    vmem = pl.BlockSpec(memory_space=pltpu.VMEM)
+    return pl.pallas_call(
+        settle_mix_kernel,
+        out_shape=jax.ShapeDtypeStruct(near.shape[1:], jnp.bfloat16),
+        in_specs=[vmem] * 2 + [pl.BlockSpec(memory_space=pl.ANY)] * len(after),
+        out_specs=vmem,
+        compiler_params=pltpu.CompilerParams(vmem_limit_bytes=VM),
+        cost_estimate=lasts(3),
+        name="settle_mix",
+    )(near, got, *after)
+
+
 EPS_STAT = 1e-30
 STAT_DECAY = 0.5
 LEARN_RATE = 0.5
 CLIP_LEVEL = 0.05
 
 
+def decayed(old, new):
+    return STAT_DECAY * old + (1.0 - STAT_DECAY) * new
+
+
+def clip_factor(squares, count):
+    return LEARN_RATE / jnp.maximum(1.0, jnp.sqrt(squares / count) / CLIP_LEVEL)
+
+
+def add_all(values):
+    return jnp.sum(jnp.sum(values, axis=1, keepdims=True), axis=0, keepdims=True)
+
+
+def column_of(table, lane, at):
+    return jnp.sum(jnp.where(lane == at, table, 0.0), axis=1, keepdims=True)
+
+
+def expert_stats_kernel(count, groups, half, *refs):
+    stays, gots = refs[:half], refs[half : 2 * half]
+    (up_old_ref, down_old_ref, up_rows_ref, down_rows_ref, up_cols_ref, down_cols_ref,
+     out_ref, sums_ref, up_new_ref, down_new_ref, pay_s, got_s, spread_s, send_sem, recv_sem) = refs[2 * half :]
+    width = up_rows_ref.shape[1]
+    ff = down_rows_ref.shape[1]
+    wide = width // 2
+    own_up = up_old_ref.shape[0]
+    own_down = down_old_ref.shape[0]
+    me = lax.axis_index("dp")
+    place = lax.axis_index("expert")
+    after = [lax.rem(me + k, count) for k in range(count)]
+    beside = [lax.rem(place + k, groups) for k in range(groups)]
+    greet([{"dp": after[k]} for k in range(1, count)] + [{"expert": beside[k]} for k in range(1, groups)])
+    push = Pusher(send_sem, recv_sem)
+    pair_bit = lax.rem(me // PAIR, 2)
+    up_lane = lax.broadcasted_iota(jnp.int32, (own_up, LANES), 1)
+    down_lane = lax.broadcasted_iota(jnp.int32, (own_down, LANES), 1)
+    up_new_ref[...] = jnp.zeros_like(up_new_ref)
+    down_new_ref[...] = jnp.zeros_like(down_new_ref)
+    for j in range(half):
+        for ref, at in ((stays[j], pair_bit * half + j), (gots[j], (1 - pair_bit) * half + j)):
+            for kind, (part, old_ref, new_ref, lane, rows) in enumerate(
+                (
+                    (ref[:own_up, :], up_old_ref, up_new_ref, up_lane, own_up),
+                    (ref[own_up:, :], down_old_ref, down_new_ref, down_lane, own_down),
+                )
+            ):
+                grad = part.astype(jnp.float32)
+                square = grad * grad
+                new = decayed(
+                    column_of(old_ref[...], lane, at),
+                    jnp.mean(square + EPS_STAT, axis=1, keepdims=True),
+                )
+                new_ref[:rows, :] = jnp.where(lane == at, new, new_ref[:rows, :])
+                total = jnp.sum(square + EPS_STAT, axis=0, keepdims=True)
+                scaled = jnp.sum(square * (1.0 / new), axis=0, keepdims=True)
+                for h in range(2):
+                    span = slice(h * wide, (h + 1) * wide)
+                    pay_s[at, 4 * kind + h : 4 * kind + h + 1, :] = total[:, span]
+                    pay_s[at, 4 * kind + 2 + h : 4 * kind + 3 + h, :] = scaled[:, span]
+    arriving = [push(pay_s.at[after[k]], got_s.at[k], {"dp": after[k]}) for k in range(1, count)]
+    tile = pay_s[me]
+    for k in range(1, count):
+        arriving[k - 1].wait_recv()
+        tile = tile + got_s[k]
+    made = []
+    tops = []
+    for kind, (rows_ref, cols_ref, rows) in enumerate(
+        ((up_rows_ref, up_cols_ref, width), (down_rows_ref, down_cols_ref, ff))
+    ):
+        here = pl.ds(me, 1)
+        square = jnp.concatenate([tile[4 * kind + h : 4 * kind + h + 1] for h in range(2)], axis=1)
+        scaled = jnp.concatenate([tile[4 * kind + 2 + h : 4 * kind + 3 + h] for h in range(2)], axis=1)
+        columns = decayed(cols_ref[here, :], square / rows)
+        row_mean = decayed(
+            jnp.mean(rows_ref[here, :], axis=1, keepdims=True),
+            jnp.sum(square, axis=1, keepdims=True) / (rows * width),
+        )
+        squares = row_mean * jnp.sum(scaled / columns, axis=1, keepdims=True)
+        made += [columns[:, :wide], columns[:, wide:]]
+        tops += [jnp.broadcast_to(v, (1, wide)) for v in (row_mean, squares)]
+    out_ref[me] = jnp.concatenate(made + tops, axis=0)
+    arriving = [push(out_ref.at[me], out_ref.at[me], {"dp": after[k]}) for k in range(1, count)]
+    for copy in arriving:
+        copy.wait_recv()
+    total = out_ref[0, :, :LANES]
+    for a in range(1, count):
+        total = total + out_ref[a, :, :LANES]
+    spread_s[place] = total
+    arriving = [push(spread_s.at[place], spread_s.at[place], {"expert": beside[k]}) for k in range(1, groups)]
+    for copy in arriving:
+        copy.wait_recv()
+    total = spread_s[0]
+    for e in range(1, groups):
+        total = total + spread_s[e]
+    sums_ref[...] = total
+    push.finish()
+
+
+def expert_stats(stays, gots, up_old, down_old, up_rows, down_rows, up_cols, down_cols, label):
+    count = lax.axis_size("dp")
+    groups = lax.axis_size("expert")
+    width = up_rows.shape[1]
+    vmem = pl.BlockSpec(memory_space=pltpu.VMEM)
+    tiles = (count, 8, width // 2)
+    copies = 2 * (count - 1) + groups - 1
+    return pl.pallas_call(
+        functools.partial(expert_stats_kernel, count, groups, len(stays)),
+        out_shape=(
+            jax.ShapeDtypeStruct(tiles, jnp.float32),
+            jax.ShapeDtypeStruct((8, LANES), jnp.float32),
+            jax.ShapeDtypeStruct((LANES, LANES), jnp.float32),
+            jax.ShapeDtypeStruct((LANES, LANES), jnp.float32),
+        ),
+        in_specs=[vmem] * (2 * len(stays) + 6),
+        out_specs=[vmem] * 4,
+        scratch_shapes=[
+            pltpu.VMEM(tiles, jnp.float32),
+            pltpu.VMEM(tiles, jnp.float32),
+            pltpu.VMEM((groups, 8, LANES), jnp.float32),
+            pltpu.SemaphoreType.DMA((copies,)),
+            pltpu.SemaphoreType.DMA((copies,)),
+        ],
+        compiler_params=pltpu.CompilerParams(
+            collective_id=label, has_side_effects=True, vmem_limit_bytes=VM
+        ),
+        cost_estimate=lasts(15),
+        name="expert_stats",
+    )(*stays, *gots, up_old, down_old, up_rows, down_rows, up_cols, down_cols)
+
+
+def expert_update_kernel(counts, half, s_ref, *refs):
+    stays, gots = refs[:half], refs[half : 2 * half]
+    (tiles_ref, sums_ref, up_new_ref, down_new_ref, up_w_ref, down_w_ref,
+     up_out_ref, down_out_ref, up_rows_ref, down_rows_ref, up_cols_ref, down_cols_ref) = refs[2 * half :]
+    own_up = up_out_ref.shape[1]
+    own_down = down_out_ref.shape[1]
+    wide = tiles_ref.shape[2]
+    pair_bit = s_ref[0]
+    up_table = up_new_ref[...]
+    down_table = down_new_ref[...]
+    lane = lax.broadcasted_iota(jnp.int32, up_table.shape, 1)
+    factors = [clip_factor(sums_ref[5 + 2 * kind : 6 + 2 * kind, 0:1], counts[kind]) for kind in range(2)]
+    for j in range(half):
+        for ref, at in ((stays[j], pair_bit * half + j), (gots[j], (1 - pair_bit) * half + j)):
+            tile = tiles_ref[at]
+            for kind, (table, weight_ref, out_ref, first, rows) in enumerate(
+                (
+                    (up_table, up_w_ref, up_out_ref, 0, own_up),
+                    (down_table, down_w_ref, down_out_ref, own_up, own_down),
+                )
+            ):
+                row_mean = tile[4 + 2 * kind : 5 + 2 * kind, 0:1]
+                scale = factors[kind] * lax.rsqrt(column_of(table, lane, at)[:rows] / row_mean)
+                for h in range(2):
+                    span = slice(h * wide, (h + 1) * wide)
+                    columns = lax.rsqrt(tile[2 * kind + h : 2 * kind + h + 1, :])
+                    out_ref[at, :, span] = (
+                        weight_ref[at, :, span].astype(jnp.float32)
+                        - ref[first : first + rows, span].astype(jnp.float32) * scale * columns
+                    )
+    up_rows_ref[...] = up_table.T[: up_rows_ref.shape[0], :own_up]
+    down_rows_ref[...] = down_table.T[: down_rows_ref.shape[0], :own_down]
+    for a in range(up_cols_ref.shape[0]):
+        for h in range(2):
+            span = slice(h * wide, (h + 1) * wide)
+            up_cols_ref[a : a + 1, span] = tiles_ref[a, h : h + 1, :]
+            down_cols_ref[a : a + 1, span] = tiles_ref[a, 2 + h : 3 + h, :]
+
+
+def expert_update(stays, gots, tiles, sums, up_new, down_new, up_w, down_w):
+    count = lax.axis_size("dp")
+    groups = lax.axis_size("expert")
+    me = lax.axis_index("dp")
+    experts, width, _ = up_w.shape
+    ff = down_w.shape[1]
+    own_up, own_down = width // count, ff // count
+    counts = (float(groups * experts * width * up_w.shape[2]), float(groups * experts * ff * width))
+    whole = lambda *shape: pl.BlockSpec(shape, lambda g, s: (0,) * len(shape))
+    shape = lambda *s: jax.ShapeDtypeStruct(s, jnp.float32)
+    rows = own_up + own_down
+    outs = [
+        shape(experts, own_up, up_w.shape[2]),
+        shape(experts, own_down, width),
+        shape(experts, own_up),
+        shape(experts, own_down),
+        shape(experts, up_w.shape[2]),
+        shape(experts, width),
+    ]
+    return pl.pallas_call(
+        functools.partial(expert_update_kernel, counts, len(stays)),
+        out_shape=outs,
+        grid_spec=pltpu.PrefetchScalarGridSpec(
+            num_scalar_prefetch=1,
+            grid=(1,),
+            in_specs=[whole(rows, width)] * (2 * len(stays))
+            + [whole(*tiles.shape), whole(*sums.shape), whole(*up_new.shape), whole(*down_new.shape)]
+            + [
+                pl.BlockSpec((experts, own_up, up_w.shape[2]), lambda g, s: (0, s[1], 0)),
+                pl.BlockSpec((experts, own_down, width), lambda g, s: (0, s[1], 0)),
+            ],
+            out_specs=[whole(*o.shape) for o in outs],
+        ),
+        compiler_params=pltpu.CompilerParams(vmem_limit_bytes=VM),
+        cost_estimate=lasts(6),
+        name="expert_update",
+    )(jnp.stack([lax.rem(me // PAIR, 2), me]), *stays, *gots, tiles, sums, up_new, down_new, up_w, down_w)
+
+
+D = 1024
+FF = 512
+TOP = 8
+
+
 def swap(values, axis, mask):
     count = lax.axis_size(axis)
     return lax.ppermute(values, axis, [(i, i ^ mask) for i in range(count)])
 
 
 def swap_pair(values):
-    return swap(values, "dp", 1)
+    return swap(values, "dp", PAIR)
 
 
 def swap_chip(values):
@@ -892,17 +1174,6 @@
 
 def plus(a, b):
     return (a.astype(jnp.float32) + b.astype(jnp.float32)).astype(jnp.bfloat16)
-
-
-def return_to_owners(summed):
-    half = summed[3].shape[0] // 2
-    for_chip = jnp.concatenate(
-        [plus(summed[1][:half], swap_pair(summed[3][:half])), summed[1][half:]], axis=0
-    )
-    for_pair = jnp.concatenate(
-        [summed[2][:half], plus(summed[2][half:], swap_chip(summed[3][half:]))], axis=0
-    )
-    return summed[0], swap_chip(for_chip), swap_pair(for_pair)
 
 
 def halve(blocks, axis, mask):
@@ -910,18 +1181,6 @@
     keep = lax.dynamic_index_in_dim(blocks, bit, 1, keepdims=False)
     give = lax.dynamic_index_in_dim(blocks, 1 - bit, 1, keepdims=False)
     return keep, swap(give, axis, mask)
-
-
-def far_sum(blocks):
-    count = lax.axis_size("dp")
-    rest = blocks.shape[1:]
-    low = 4
-    while low < count:
-        keep, got = halve(blocks.reshape((-1, 2, 2) + rest), "dp", low)
-        blocks = plus(keep, got)
-        low *= 2
-    keep, got = halve(blocks.reshape((1, 2) + rest), "dp", 1)
-    return keep[0], got[0]
 
 
 def reduce_dense_far(blocks):
@@ -951,10 +1210,6 @@
     count = lax.axis_size("dp")
     width = matrix.shape[along] // count
     return lax.dynamic_slice_in_dim(matrix, lax.axis_index("dp") * width, width, along)
-
-
-def decayed(old, new):
-    return STAT_DECAY * old + (1.0 - STAT_DECAY) * new
 
 
 def factored(part, rows_old):
@@ -998,8 +1253,7 @@
     capacity = 3 * rows_here * TOP // (2 * total_experts)
     half_experts = experts_here // 2
     dp_index = lax.axis_index("dp")
-    pair_bit = lax.rem(dp_index, 2)
-    z_bit = lax.rem(dp_index // 2, 2)
+    pair_bit = lax.rem(dp_index // PAIR, 2)
     first_local = pair_bit * half_experts
     first_expert = lax.axis_index("expert") * experts_here + first_local
 
@@ -1017,86 +1271,116 @@
     received, arrived, scale, code = gather_and_select(
         normed_ffn, grad_rows, chip_grad_rows, pair_grad_rows, capacity, experts_here, half_experts, TOP, 5
     )
-    scalars = jnp.stack([first_local, z_bit])
-    experts = []
-    near = []
-
-    def near_sum(j):
-        keep, give = experts[j][:2]
-        near.append(plus(keep, swap(give, "dp", 2)))
-
+    scalars = jnp.stack([first_local, lax.rem(dp_index, 2)])
+    experts, chains = [], []
+
+    def advance(j, after, come=None):
+        masks, stay, go = chains[j]
+        come = swap(go, "dp", masks[0]) if come is None else come
+        stay, go = settle(stay, come, masks[1], "%d_%d" % (j, masks[1]), after)
+        chains[j] = (masks[1:], stay, go)
+        return stay
+
+    masks = [1] + [1 << b for b in range(2, dp_count.bit_length() - 1)] + [PAIR]
     for j in range(half_experts):
         after = [experts[-1][2]] if experts else []
         if j == 3:
-            near_sum(0)
-            after.append(near[0])
+            after.append(advance(0, after))
         experts.append(
             run_expert(
                 scalars, j, received, arrived, scale, gate_up_weight, down_weight, dp_count, after
             )
         )
-    normed_f_grad, mix_sums = combine_and_return(
-        code, [e[2] for e in experts], [e[3] for e in experts], capacity, 6
+        chains.append((masks, experts[j][0], experts[j][1]))
+    normed_f_grad, near_mix, far_mix, come = combine_and_return(
+        code, [e[2] for e in experts], [e[3] for e in experts], capacity, chains[0][2], chains[0][0][0], 6
     )
-    mix_parts = return_to_owners(mix_sums)
-    block_out = middle + sum(part.astype(jnp.float32) for part in mix_parts)
-    near_sum(1)
+    steps = [normed_f_grad]
+    for j in (1, 2, 0):
+        steps.append(advance(j, steps[-1:], come if j == 0 else None))
     input_grad, dense = attend_back(
         hidden_in, out_grad, middle, normed_f_grad, normed, qkv, attended, lse, ids, norm_gains, qkv_weight,
-        out_weight, [near[1]]
+        out_weight, steps
     )
-    for j in range(2, half_experts):
-        near_sum(j)
-    far = [far_sum(blocks) for blocks in near]
-    own_parts = [own for own, _ in far]
-    other_parts = [other for _, other in far]
-
-    own = jnp.stack(own_parts).astype(jnp.float32)
-    other = jnp.stack(other_parts).astype(jnp.float32)
-    parts = jnp.where(pair_bit == 0, jnp.concatenate([own, other]), jnp.concatenate([other, own]))
-    gateup_part = parts[:, : D // dp_count]
-    down_part = parts[:, D // dp_count :]
-    gateup_rows_new, gateup_square, gateup_scaled = factored(gateup_part, own_share(gateup_rows, 1))
-    down_rows_new, down_square, down_scaled = factored(down_part, own_share(down_rows, 1))
-    sizes = [gateup_square.size, gateup_scaled.size, down_square.size, down_scaled.size]
-    summed = total_over(
-        jnp.concatenate(
-            [
-                gateup_square.reshape(-1),
-                gateup_scaled.reshape(-1),
-                down_square.reshape(-1),
-                down_scaled.reshape(-1),
-                jnp.sum(gateup_rows_new, axis=1),
-                jnp.sum(down_rows_new, axis=1),
-            ]
-        ),
-        "dp",
-        1,
-    )
-    pieces = jnp.split(summed, [sum(sizes[: i + 1]) for i in range(4)])
-    gateup_square, gateup_scaled, down_square, down_scaled = [
-        p.reshape(experts_here, D) for p in pieces[:4]
-    ]
-    gateup_row_mean = pieces[4][:experts_here] / D
-    down_row_mean = pieces[4][experts_here:] / FF
-    gateup_cols_new = decayed(gateup_cols, gateup_square / D)
-    down_cols_new = decayed(down_cols, down_square / FF)
-    expert_squares = jnp.stack(
-        [
-            jnp.sum(gateup_row_mean * jnp.sum(gateup_scaled / gateup_cols_new, axis=1)),
-            jnp.sum(down_row_mean * jnp.sum(down_scaled / down_cols_new, axis=1)),
-        ]
-    )
-    spread_squares = collect(
-        jnp.zeros((8, 128), jnp.float32).at[0, :2].set(expert_squares), "expert", 2
-    )
-    expert_squares = jnp.sum(spread_squares[:, 0, :2], axis=0)
+    pair_mix = swap_pair(far_mix)
+    for_chip = settle_mix(near_mix, pair_mix, [input_grad])
+    steps = [for_chip]
+    for j in (3, 1):
+        steps.append(advance(j, steps[-1:]))
+    mix_parts = (near_mix[0], pair_mix[0], swap_chip(for_chip))
+    block_out = middle + sum(part.astype(jnp.float32) for part in mix_parts)
 
     qkv_columns = qkv_weight.shape[1]
     if D // dp_count % 64 == 0:
-        dense_own = reduce_dense(dense, 3, [near[2]])
+        dense_own, come = reduce_dense(dense, chains[3][2], chains[3][0][0], 3, steps)
     else:
-        dense_own = reduce_dense_far(dense)
+        dense_own, come = reduce_dense_far(dense), None
+    for j in (2, 3, 0, 1):
+        while len(chains[j][0]) > 1:
+            advance(j, [dense_own], come if j == 3 else None)
+            come = None if j == 3 else come
+    own_parts = [c[1][0] for c in chains]
+    other_parts = [swap_pair(c[2][0]) for c in chains]
+    fused_tail = dp_count == experts_here
+    if fused_tail:
+        spare = ((0, 0), (0, LANES - experts_here))
+        tiles, sums, up_rows_T, down_rows_T = expert_stats(
+            own_parts,
+            other_parts,
+            jnp.pad(own_share(gateup_rows, 1).T, spare),
+            jnp.pad(own_share(down_rows, 1).T, spare),
+            gateup_rows,
+            down_rows,
+            gateup_cols,
+            down_cols,
+            1,
+        )
+        gate_up_new, down_new, gateup_rows_new, down_rows_new, gateup_cols_new, down_cols_new = expert_update(
+            own_parts, other_parts, tiles, sums, up_rows_T, down_rows_T, gate_up_weight, down_weight
+        )
+        expert_squares = jnp.stack([sums[5, 0], sums[7, 0]])
+    else:
+        own = jnp.stack(own_parts).astype(jnp.float32)
+        other = jnp.stack(other_parts).astype(jnp.float32)
+        parts = jnp.where(pair_bit == 0, jnp.concatenate([own, other]), jnp.concatenate([other, own]))
+        gateup_part = parts[:, : D // dp_count]
+        down_part = parts[:, D // dp_count :]
+        gateup_rows_new, gateup_square, gateup_scaled = factored(gateup_part, own_share(gateup_rows, 1))
+        down_rows_new, down_square, down_scaled = factored(down_part, own_share(down_rows, 1))
+        sizes = [gateup_square.size, gateup_scaled.size, down_square.size, down_scaled.size]
+        summed = total_over(
+            jnp.concatenate(
+                [
+                    gateup_square.reshape(-1),
+                    gateup_scaled.reshape(-1),
+                    down_square.reshape(-1),
+                    down_scaled.reshape(-1),
+                    jnp.sum(gateup_rows_new, axis=1),
+                    jnp.sum(down_rows_new, axis=1),
+                ]
+            ),
+            "dp",
+            1,
+        )
+        pieces = jnp.split(summed, [sum(sizes[: i + 1]) for i in range(4)])
+        gateup_square, gateup_scaled, down_square, down_scaled = [
+            p.reshape(experts_here, D) for p in pieces[:4]
+        ]
+        gateup_row_mean = pieces[4][:experts_here] / D
+        down_row_mean = pieces[4][experts_here:] / FF
+        gateup_cols_new = decayed(gateup_cols, gateup_square / D)
+        down_cols_new = decayed(down_cols, down_square / FF)
+        expert_squares = jnp.stack(
+            [
+                jnp.sum(gateup_row_mean * jnp.sum(gateup_scaled / gateup_cols_new, axis=1)),
+                jnp.sum(down_row_mean * jnp.sum(down_scaled / down_cols_new, axis=1)),
+            ]
+        )
+        spread_squares = collect(
+            jnp.zeros((8, 128), jnp.float32).at[0, :2].set(expert_squares), "expert", 2
+        )
+        expert_squares = jnp.sum(spread_squares[:, 0, :2], axis=0)
+
     dense_own = dense_own.astype(jnp.float32)
     qkv_own = dense_own[:, :qkv_columns]
     out_own = dense_own[:, qkv_columns : qkv_columns + D]
@@ -1119,6 +1403,7 @@
         ),
         "dp",
         4,
+        [c[1] for c in chains],
     )
     qkv_square, qkv_scaled, out_square, out_scaled, rest = jnp.split(
         dense_sums, [qkv_columns, 2 * qkv_columns, 2 * qkv_columns + D, 2 * qkv_columns + 2 * D]
@@ -1150,6 +1435,13 @@
             factor * lax.rsqrt(rows_new / row_mean[..., None])
         )[..., :, None] * lax.rsqrt(cols_new)[..., None, :]
 
+    if not fused_tail:
+        gate_up_new = stepped(
+            own_share(gate_up_weight, 1), gateup_part, gateup_rows_new, gateup_row_mean, gateup_cols_new, factors[3]
+        )
+        down_new = stepped(
+            own_share(down_weight, 1), down_part, down_rows_new, down_row_mean, down_cols_new, factors[4]
+        )
     return (
         block_out,
         input_grad,
@@ -1162,10 +1454,10 @@
         stepped(own_share(out_weight, 0), out_own, out_rows_new, out_row_mean, out_cols_new, factors[2]),
         out_rows_new,
         out_cols_new,
-        stepped(own_share(gate_up_weight, 1), gateup_part, gateup_rows_new, gateup_row_mean, gateup_cols_new, factors[3]),
+        gate_up_new,
         gateup_rows_new,
         gateup_cols_new,
-        stepped(own_share(down_weight, 1), down_part, down_rows_new, down_row_mean, down_cols_new, factors[4]),
+        down_new,
         down_rows_new,
         down_cols_new,
     )

time: 509 us -> 454 us (0.89)
  waiting for transfers between devices: 127 us -> 38.7 us
  Pallas kernels: 286 us -> 350 us
  other arithmetic: 54.4 us -> 19 us
  local copies, waits for them, and re-layouts: 12.3 us -> 18.1 us
    ppermute x18 -> x14, waiting for transfers between devices: 127 us -> 38.7 us  [swap(): return lax.ppermute(values, axis, [(i, i ^ mask) for i in range(count)])]
    pallas_call x3 -> x13, Pallas kernels: 99.1 us -> 176 us  [the longest x1 68.8 us: reduce_dense(): pl.pallas_call(functools.partial(dense_kernel, orders, spans, len(after),...]
    convert_element_type x11 -> x0, other arithmetic: 16.5 us -> none  [the longest x9 15.9 us: plus(): return (a.astype(jnp.float32) + b.astype(jnp.float32)).astype(jnp.bfloat16)]
    pallas_call x2 -> x1, Pallas kernels: 23.6 us -> 10.8 us  [total_over(): pl.pallas_call(functools.partial(total_kernel, axis, count), out_shape=ja...]
    sub x4 -> x2, other arithmetic: 13.3 us -> 4.36 us  [stepped(): weight.astype(jnp.float32)]
    unnamed x67 -> x63, local copies, waits for them, and re-layouts: 2.71 us -> 8.9 us
    ppermute x18 -> x14, starting transfers between devices: 20.2 us -> 18.7 us  [swap(): return lax.ppermute(values, axis, [(i, i ^ mask) for i in range(count)])]
  transfers between devices with their start and end apart: 18 -> 14, of which waited for: 7 -> 4; matrix products, arithmetic and copies ran while one was open for 5% -> 5% of each run, Pallas kernels for 27% -> 64%
where the time goes in v4:
time: 454 us; the launch traced here: 449 us
  Pallas kernels  350 us (77%)
  waiting for transfers between devices  38.7 us (9%)
  other arithmetic  19 us (4%)
  starting transfers between devices  18.7 us (4%)
  local copies, waits for them, and re-layouts  18.1 us (4%)
  between operations  4.71 us (1%)
    pallas_call x4, Pallas kernels, run_expert(): pl.pallas_call(functools.partial(expert_kernel, owners, len(after)), out_...  74.3 us
    pallas_call x1, Pallas kernels, reduce_dense(): pl.pallas_call(functools.partial(dense_kernel, orders, spans, len(after),...  68.8 us
    pallas_call x1, Pallas kernels, combine_and_return(): pl.pallas_call(functools.partial(return_kernel, capacity, count, far_mask...  53.9 us
    pallas_call x1, Pallas kernels, gather_and_select(): pl.pallas_call(functools.partial(gather_kernel, capacity, experts_here, h...  44.8 us
    ppermute x14, waiting for transfers between devices, swap(): return lax.ppermute(values, axis, [(i, i ^ mask) for i in range(count)])  38.7 us
    pallas_call x1, Pallas kernels, attend_back(): pl.pallas_call(attend_back_kernel, out_shape=(jax.ShapeDtypeStruct((rows,...  26.6 us
    pallas_call x8, Pallas kernels, settle(): pl.pallas_call(settle_kernel, out_shape=(half, half), in_specs=[pl.BlockS...  22.9 us
    pallas_call x1, Pallas kernels, expert_stats(): pl.pallas_call(functools.partial(expert_stats_kernel, count, groups, len(...  19.2 us
  transfers between devices with their start and end apart: 14, of which 4 were waited for; matrix products, arithmetic and copies ran while one was open for 5% of the time, Pallas kernels for 64%

profile of v4, /device:TPU:0, one launch (start us, length us, event | category | flops | bytes accessed | tf_op | source)
XLA Modules:
  0.0 449.3 jit_solution(181567357999657388)
XLA Ops:
  3.8 3.0 collective-permute-start
  9.1 18.0 %attend.1 = (bf16[384,1024]{1,0:T(8,128)(2,1)}, bf16[384,2048]{1,0:T(8,128)(2,1)}, bf16[384,1024]{1,0:T(8,128)(2,1)}, f32[384,128]{1,0:T(8,128)}, f32[384,1024]{1,0:T(8,128)}, /*index=5*/bf16[384,1024]{1,0:T(8,128)(2,1)}) custom-call(f32[384,1024]{1,0:T(8,128)} %hidden_ref.3, s32[3,384]{1,0:T(4,128)} %pad_add_fusion.ids_ref, bf16[2,1024]{1,0:T(2,128)(2,1)} %gains_ref.3, ...), custom_call_target="tpu_custom_call" | custom-call | flops 18000000 | bytes 1024 | tf_op jit(solution)/shard_map/attend/pallas_call | solution.py:217
  28.9 44.8 %gather_and_select.1 = (bf16[4,8,144,1024]{3,2,1,0:T(8,128)(2,1)}, bf16[4,8,144,1024]{3,2,1,0:T(8,128)(2,1)}, f32[4,8,144,1]{3,2,1,0:T(8,128)}, f32[8,4,384]{2,1,0:T(4,128)}) custom-call(bf16[384,1024]{1,0:T(8,128)(2,1)} %get-tuple-element.78.token_ref, bf16[416,1024]{1,0:T(8,128)(2,1)} %copy-done.9, bf16[416,1024]{1,0:T(8,128)(2,1)} %copy-done.16, ...), custom_call_target="tpu_custom_call" | custom-call | flops 44000000 | bytes 1024 | tf_op jit(solution)/shard_map/gather_and_select/pallas_call | solution.py:735
  73.6 18.5 %expert_0.1 = (bf16[4,192,1024]{2,1,0:T(8,128)(2,1)}, bf16[4,192,1024]{2,1,0:T(8,128)(2,1)}, bf16[1152,1024]{1,0:T(8,128)(2,1)}, bf16[1152,1024]{1,0:T(8,128)(2,1)}) custom-call(s32[2]{0:T(128)} %pad_add_fusion.1.s_ref, bf16[4,8,144,1024]{3,2,1,0:T(8,128)(2,1)} %get-tuple-element.80.rec_ref, bf16[4,8,144,1024]{3,2,1,0:T(8,128)(2,1)} %get-tuple-element.81.arr_ref, ...), custom_call_target="tpu_custom_call" | custom-call | flops 18000000 | bytes 1024 | tf_op jit(solution)/shard_map/expert_0/pallas_call | solution.py:83
  93.6 18.5 %expert_1.1 = (bf16[4,192,1024]{2,1,0:T(8,128)(2,1)}, bf16[4,192,1024]{2,1,0:T(8,128)(2,1)}, bf16[1152,1024]{1,0:T(8,128)(2,1)}, bf16[1152,1024]{1,0:T(8,128)(2,1)}) custom-call(s32[2]{0:T(128)} %pad_add_fusion.1.s_ref, bf16[4,8,144,1024]{3,2,1,0:T(8,128)(2,1)} %get-tuple-element.80.rec_ref, bf16[4,8,144,1024]{3,2,1,0:T(8,128)(2,1)} %get-tuple-element.81.arr_ref, ...), custom_call_target="tpu_custom_call" | custom-call | flops 18000000 | bytes 1024 | tf_op jit(solution)/shard_map/expert_1/pallas_call | solution.py:83
  112.7 18.7 %expert_2.1 = (bf16[4,192,1024]{2,1,0:T(8,128)(2,1)}, bf16[4,192,1024]{2,1,0:T(8,128)(2,1)}, bf16[1152,1024]{1,0:T(8,128)(2,1)}, bf16[1152,1024]{1,0:T(8,128)(2,1)}) custom-call(s32[2]{0:T(128)} %pad_add_fusion.1.s_ref, bf16[4,8,144,1024]{3,2,1,0:T(8,128)(2,1)} %get-tuple-element.80.rec_ref, bf16[4,8,144,1024]{3,2,1,0:T(8,128)(2,1)} %get-tuple-element.81.arr_ref, ...), custom_call_target="tpu_custom_call" | custom-call | flops 18000000 | bytes 1024 | tf_op jit(solution)/shard_map/expert_2/pallas_call | solution.py:83
  134.0 3.3 settle_0_4.1
  137.4 18.5 %expert_3.1 = (bf16[4,192,1024]{2,1,0:T(8,128)(2,1)}, bf16[4,192,1024]{2,1,0:T(8,128)(2,1)}, bf16[1152,1024]{1,0:T(8,128)(2,1)}, bf16[1152,1024]{1,0:T(8,128)(2,1)}) custom-call(s32[2]{0:T(128)} %pad_add_fusion.1.s_ref, bf16[4,8,144,1024]{3,2,1,0:T(8,128)(2,1)} %get-tuple-element.80.rec_ref, bf16[4,8,144,1024]{3,2,1,0:T(8,128)(2,1)} %get-tuple-element.81.arr_ref, ...), custom_call_target="tpu_custom_call" | custom-call | flops 18000000 | bytes 1024 | tf_op jit(solution)/shard_map/expert_3/pallas_call | solution.py:83
  155.9 53.9 %combine_and_return.1 = (f32[384,1024]{1,0:T(8,128)}, bf16[2,384,1024]{2,1,0:T(8,128)(2,1)}, bf16[2,384,1024]{2,1,0:T(8,128)(2,1)}, bf16[2,192,1024]{2,1,0:T(8,128)(2,1)}) custom-call(f32[8,4,384]{2,1,0:T(4,128)} %get-tuple-element.79.code_ref, bf16[1152,1024]{1,0:T(8,128)(2,1)} %get-tuple-element.83.refs_0_, ...), custom_call_target="tpu_custom_call" | custom-call | flops 37000000 | bytes 1024 | tf_op jit(solution)/shard_map/combine_and_return/pallas_call | solution.py:866
  211.7 3.3 settle_1_4.1
  220.7 3.3 settle_2_4.1
  229.3 26.6 %attend_back.1 = (f32[384,1024]{1,0:T(8,128)}, bf16[1024,3200]{1,0:T(8,128)(2,1)}) custom-call(f32[384,1024]{1,0:T(8,128)} %hidden_ref.3, f32[384,1024]{1,0:T(8,128)} %grad_ref.1, f32[384,1024]{1,0:T(8,128)} %get-tuple-element.77.middle_ref, f32[384,1024]{1,0:T(8,128)} %get-tuple-element.97.refs_0_.normed_grad_ref, ...), custom_call_target="tpu_custom_call" | custom-call | flops 26000000 | bytes 1024 | tf_op jit(solution)/shard_map/attend_back/pallas_call | solution.py:325
  255.9 19.4 %collective-permute-done.3.got_ref = bf16[2,384,1024]{2,1,0:T(8,128)(2,1)S(1)} collective-permute-done((bf16[2,384,1024]{2,1,0:T(8,128)(2,1)}, bf16[2,384,1024]{2,1,0:T(8,128)(2,1)S(1)}, u32[]{:S(2)}, u32[]{:S(2)}) %collective-permute-start.3) | collective-permute-done | bytes 1572896 | tf_op jit(solution)/shard_map/ppermute | solution.py:1160
  276.4 2.9 settle_mix.1.refs_0_
  281.7 3.4 settle_3_4.1
  288.3 68.8 %reduce_dense.1 = (bf16[2,2,32,3200]{3,2,1,0:T(8,128)(2,1)}, bf16[2,192,1024]{2,1,0:T(8,128)(2,1)}) custom-call(bf16[2,2,2,2,2,32,3200]{6,5,4,3,2,1,0:T(8,128)(2,1)} %bitcast.118, bf16[2,192,1024]{2,1,0:T(8,128)(2,1)} %bitcast.130, bf16[384,1024]{1,0:T(8,128)(2,1)} %settle_mix.1.refs_0_, bf16[2,192,1024]{2,1,0:T(8,128)(2,1)} %bitcast.116, ...), custom_call_target="tpu_custom_call" | custom-call | flops 50000000 | bytes 1024 | tf_op jit(solution)/shard_map/reduce_dense/pallas_call | solution.py:566
  365.5 2.4 settle_3_2.1
  369.0 10.8 %total_4.1 = f32[8,8,128]{2,1,0:T(8,128)S(1)} custom-call(f32[8,8,128]{2,1,0:T(8,128)S(1)} %pad_bitcast_fusion.mine_ref, bf16[1,192,1024]{2,1,0:T(8,128)(2,1)S(1)} %bitcast.98, bf16[1,192,1024]{2,1,0:T(8,128)(2,1)S(1)} %bitcast.94, bf16[1,192,1024]{2,1,0:T(8,128)(2,1)S(1)} %bitcast.101, bf16[1,192,1024]{2,1,0:T(8,128)(2,1)S(1)} %bitcast.104), custom_call_target="tpu_custom_call" | custom-call | flops 12000000 | bytes 1024 | tf_op jit(solution)/shard_map/total_4/pallas_call | solution.py:401
  387.6 5.1 %collective-permute-done.11.refs_5_ = bf16[192,1024]{1,0:T(8,128)(2,1)S(1)} collective-permute-done((bf16[192,1024]{1,0:T(8,128)(2,1)}, bf16[192,1024]{1,0:T(8,128)(2,1)S(1)}, u32[]{:S(2)}, u32[]{:S(2)}) %collective-permute-start.11) | collective-permute-done | bytes 393248 | tf_op jit(solution)/shard_map/ppermute | solution.py:1160
  392.7 8.4 %collective-permute-done.12.refs_6_ = bf16[192,1024]{1,0:T(8,128)(2,1)S(1)} collective-permute-done((bf16[192,1024]{1,0:T(8,128)(2,1)}, bf16[192,1024]{1,0:T(8,128)(2,1)S(1)}, u32[]{:S(2)}, u32[]{:S(2)}) %collective-permute-start.12) | collective-permute-done | bytes 393248 | tf_op jit(solution)/shard_map/ppermute | solution.py:1160
  401.1 5.8 %collective-permute-done.13.refs_7_ = bf16[192,1024]{1,0:T(8,128)(2,1)S(1)} collective-permute-done((bf16[192,1024]{1,0:T(8,128)(2,1)}, bf16[192,1024]{1,0:T(8,128)(2,1)S(1)}, u32[]{:S(2)}, u32[]{:S(2)}) %collective-permute-start.13) | collective-permute-done | bytes 393248 | tf_op jit(solution)/shard_map/ppermute | solution.py:1160
  407.7 19.2 %expert_stats.1 = (f32[8,8,512]{2,1,0:T(8,128)}, f32[8,128]{1,0:T(8,128)}, f32[128,128]{1,0:T(8,128)}, f32[128,128]{1,0:T(8,128)}) custom-call(bf16[192,1024]{1,0:T(8,128)(2,1)} %bitcast.96, bf16[192,1024]{1,0:T(8,128)(2,1)} %bitcast.92, bf16[192,1024]{1,0:T(8,128)(2,1)} %bitcast.99, bf16[192,1024]{1,0:T(8,128)(2,1)} %bitcast.102, ...), custom_call_target="tpu_custom_call" | custom-call | flops 15000000 | bytes 1024 | tf_op jit(solution)/shard_map/expert_stats/pallas_call | solution.py:1050
  434.0 7.8 %expert_update.1 = (f32[8,128,1024]{2,1,0:T(8,128)}, f32[8,64,1024]{2,1,0:T(8,128)}, f32[8,128]{1,0:T(8,128)}, f32[8,64]{1,0:T(8,128)}, f32[8,1024]{1,0:T(8,128)}, /*index=5*/f32[8,1024]{1,0:T(8,128)}) custom-call(s32[2]{0:T(128)} %pad_add_fusion.2.s_ref, bf16[192,1024]{1,0:T(8,128)(2,1)} %bitcast.97, bf16[192,1024]{1,0:T(8,128)(2,1)} %bitcast.93, ...), custom_call_target="tpu_custom_call" | custom-call | flops 6000000 | bytes 1024 | tf_op jit(solution)/shard_map/expert_update/pallas_call | solution.py:1133
  446.2 2.7 fusion.1
  (128 shorter events, 57.3 us)
Async XLA Ops:
  0.7 216.3 %copy-start = (f32[2,1024]{1,0:T(2,128)S(1)}, f32[2,1024]{1,0:T(2,128)}, u32[]{:S(2)}) copy-start(f32[2,1024]{1,0:T(2,128)} %param.34) | copy-start | bytes 24580
  3.8 23.3 %copy-start.9 = (bf16[416,1024]{1,0:T(8,128)(2,1)}, bf16[416,1024]{1,0:T(8,128)(2,1)S(1)}, u32[]{:S(2)}) copy-start(bf16[416,1024]{1,0:T(8,128)(2,1)S(1)} %fusion.2.grad_ref) | copy-start | bytes 2555908
  3.8 23.9 %collective-permute-start = (bf16[416,1024]{1,0:T(8,128)(2,1)S(1)}, bf16[416,1024]{1,0:T(8,128)(2,1)S(1)}, u32[]{:S(2)}, u32[]{:S(2)}) collective-permute-start(bf16[416,1024]{1,0:T(8,128)(2,1)S(1)} %fusion.2.grad_ref), channel_id=1, source_target_pairs={{0,2},{1,3},{2,0},{3,1},{4,6},{5,7},{6,4},{7,5},{8,10},{9,11},{10,... | collective-permute-start | bytes 2555912 | tf_op jit(solution)/shard_map/ppermute | solution.py:1160
  6.9 20.8 %collective-permute-start.1 = (bf16[416,1024]{1,0:T(8,128)(2,1)S(1)}, bf16[416,1024]{1,0:T(8,128)(2,1)S(1)}, u32[]{:S(2)}, u32[]{:S(2)}) collective-permute-start(bf16[416,1024]{1,0:T(8,128)(2,1)S(1)} %fusion.2.grad_ref), channel_id=1, source_target_pairs={{0,8},{4,12},{8,0},{12,4},{16,24},{20,28},{24,16},{28,20},{1,9},{5... | collective-permute-start | bytes 2555912 | tf_op jit(solution)/shard_map/ppermute | solution.py:1160
  92.2 40.8 %collective-permute-start.2 = (bf16[4,192,1024]{2,1,0:T(8,128)(2,1)}, bf16[4,192,1024]{2,1,0:T(8,128)(2,1)S(1)}, u32[]{:S(2)}, u32[]{:S(2)}) collective-permute-start(bf16[4,192,1024]{2,1,0:T(8,128)(2,1)} %get-tuple-element.87), channel_id=1, source_target_pairs={{0,4},{4,0},{8,12},{12,8},{16,20},{20,16},{24,28},{28,24},{1,5},{5... | collective-permute-start | bytes 4718600 | tf_op jit(solution)/shard_map/ppermute | solution.py:1160
  112.1 98.4 %collective-permute-start.4 = (bf16[4,192,1024]{2,1,0:T(8,128)(2,1)}, bf16[4,192,1024]{2,1,0:T(8,128)(2,1)S(1)}, u32[]{:S(2)}, u32[]{:S(2)}) collective-permute-start(bf16[4,192,1024]{2,1,0:T(8,128)(2,1)} %get-tuple-element.103), channel_id=1, source_target_pairs={{0,4},{4,0},{8,12},{12,8},{16,20},{20,16},{24,28},{28,24},{1,5},{5... | collective-permute-start | bytes 4718600 | tf_op jit(solution)/shard_map/ppermute | solution.py:1160
  131.4 89.2 %collective-permute-start.5 = (bf16[4,192,1024]{2,1,0:T(8,128)(2,1)}, bf16[4,192,1024]{2,1,0:T(8,128)(2,1)}, u32[]{:S(2)}, u32[]{:S(2)}) collective-permute-start(bf16[4,192,1024]{2,1,0:T(8,128)(2,1)} %get-tuple-element.106), channel_id=1, source_target_pairs={{0,4},{4,0},{8,12},{12,8},{16,20},{20,16},{24,28},{28,24},{1,5},{5... | collective-permute-start | bytes 4718600 | tf_op jit(solution)/shard_map/ppermute | solution.py:1160
  209.8 65.4 %collective-permute-start.3 = (bf16[2,384,1024]{2,1,0:T(8,128)(2,1)}, bf16[2,384,1024]{2,1,0:T(8,128)(2,1)S(1)}, u32[]{:S(2)}, u32[]{:S(2)}) collective-permute-start(bf16[2,384,1024]{2,1,0:T(8,128)(2,1)} %get-tuple-element.96), channel_id=1, source_target_pairs={{0,8},{4,12},{8,0},{12,4},{16,24},{20,28},{24,16},{28,20},{1,9},{5... | collective-permute-start | bytes 4718600 | tf_op jit(solution)/shard_map/ppermute | solution.py:1160
  209.9 71.8 %collective-permute-start.7 = (bf16[4,192,1024]{2,1,0:T(8,128)(2,1)}, bf16[4,192,1024]{2,1,0:T(8,128)(2,1)}, u32[]{:S(2)}, u32[]{:S(2)}) collective-permute-start(bf16[4,192,1024]{2,1,0:T(8,128)(2,1)} %get-tuple-element.113), channel_id=1, source_target_pairs={{0,4},{4,0},{8,12},{12,8},{16,20},{20,16},{24,28},{28,24},{1,5},{5... | collective-permute-start | bytes 4718600 | tf_op jit(solution)/shard_map/ppermute | solution.py:1160
  215.0 70.1 %collective-permute-start.8 = (bf16[2,192,1024]{2,1,0:T(8,128)(2,1)}, bf16[2,192,1024]{2,1,0:T(8,128)(2,1)S(1)}, u32[]{:S(2)}, u32[]{:S(2)}) collective-permute-start(bf16[2,192,1024]{2,1,0:T(8,128)(2,1)} %bitcast.134), channel_id=1, source_target_pairs={{0,16},{4,20},{8,24},{12,28},{16,0},{20,4},{24,8},{28,12},{1,17},{... | collective-permute-start | bytes 2359304 | tf_op jit(solution)/shard_map/ppermute | solution.py:1160
  224.0 139.2 %collective-permute-start.9 = (bf16[2,192,1024]{2,1,0:T(8,128)(2,1)}, bf16[2,192,1024]{2,1,0:T(8,128)(2,1)}, u32[]{:S(2)}, u32[]{:S(2)}) collective-permute-start(bf16[2,192,1024]{2,1,0:T(8,128)(2,1)} %bitcast.135), channel_id=1, source_target_pairs={{0,16},{4,20},{8,24},{12,28},{16,0},{20,4},{24,8},{28,12},{1,17},{... | collective-permute-start | bytes 2359304 | tf_op jit(solution)/shard_map/ppermute | solution.py:1160
  227.3 160.2 %collective-permute-start.10 = (bf16[192,1024]{1,0:T(8,128)(2,1)}, bf16[192,1024]{1,0:T(8,128)(2,1)S(1)}, u32[]{:S(2)}, u32[]{:S(2)}) collective-permute-start(bf16[192,1024]{1,0:T(8,128)(2,1)} %bitcast.136), channel_id=1, source_target_pairs={{0,8},{4,12},{8,0},{12,4},{16,24},{20,28},{24,16},{28,20},{1,9},{5... | collective-permute-start | bytes 1179656 | tf_op jit(solution)/shard_map/ppermute | solution.py:1160
  279.4 166.8 %collective-permute-start.6 = (bf16[384,1024]{1,0:T(8,128)(2,1)}, bf16[384,1024]{1,0:T(8,128)(2,1)}, u32[]{:S(2)}, u32[]{:S(2)}) collective-permute-start(bf16[384,1024]{1,0:T(8,128)(2,1)} %settle_mix.1.refs_0_), channel_id=1, source_target_pairs={{0,2},{1,3},{2,0},{3,1},{4,6},{5,7},{6,4},{7,5},{8,10},{9,11},{10,... | collective-permute-start | bytes 2359304 | tf_op jit(solution)/shard_map/ppermute | solution.py:1160
  360.1 71.9 %copy-start.23 = (f32[128]{0:T(128)}, f32[128]{0:T(128)S(1)}, u32[]{:S(2)}) copy-start(f32[128]{0:T(128)S(1)} %get-tuple-element.181) | copy-start | bytes 1540
  360.1 72.6 %copy-start.22 = (f32[128]{0:T(128)}, f32[128]{0:T(128)S(1)}, u32[]{:S(2)}) copy-start(f32[128]{0:T(128)S(1)} %get-tuple-element.167) | copy-start | bytes 1540
  365.5 14.3 %copy-start.21 = (f32[2048]{0:T(1024)S(1)}, f32[2048]{0:T(1024)}, u32[]{:S(2)}) copy-start(f32[2048]{0:T(1024)} %param.36) | copy-start | bytes 24580
  365.5 20.7 %copy-start.24 = (f32[1024]{0:T(1024)S(1)}, f32[1024]{0:T(1024)}, u32[]{:S(2)}) copy-start(f32[1024]{0:T(1024)} %param.38) | copy-start | bytes 12292
  379.8 47.1 %copy-start.19 = (f32[2048]{0:T(1024)}, f32[2048]{0:T(1024)S(1)}, u32[]{:S(2)}) copy-start(f32[2048]{0:T(1024)S(1)} %get-tuple-element.161) | copy-start | bytes 24580
  380.4 12.3 %collective-permute-start.11 = (bf16[192,1024]{1,0:T(8,128)(2,1)}, bf16[192,1024]{1,0:T(8,128)(2,1)S(1)}, u32[]{:S(2)}, u32[]{:S(2)}) collective-permute-start(bf16[192,1024]{1,0:T(8,128)(2,1)} %bitcast.55), channel_id=1, source_target_pairs={{0,8},{4,12},{8,0},{12,4},{16,24},{20,28},{24,16},{28,20},{1,9},{5... | collective-permute-start | bytes 1179656 | tf_op jit(solution)/shard_map/ppermute | solution.py:1160
  381.1 20.0 %collective-permute-start.12 = (bf16[192,1024]{1,0:T(8,128)(2,1)}, bf16[192,1024]{1,0:T(8,128)(2,1)S(1)}, u32[]{:S(2)}, u32[]{:S(2)}) collective-permute-start(bf16[192,1024]{1,0:T(8,128)(2,1)} %bitcast.56), channel_id=1, source_target_pairs={{0,8},{4,12},{8,0},{12,4},{16,24},{20,28},{24,16},{28,20},{1,9},{5... | collective-permute-start | bytes 1179656 | tf_op jit(solution)/shard_map/ppermute | solution.py:1160
  382.4 24.5 %collective-permute-start.13 = (bf16[192,1024]{1,0:T(8,128)(2,1)}, bf16[192,1024]{1,0:T(8,128)(2,1)S(1)}, u32[]{:S(2)}, u32[]{:S(2)}) collective-permute-start(bf16[192,1024]{1,0:T(8,128)(2,1)} %bitcast.57), channel_id=1, source_target_pairs={{0,8},{4,12},{8,0},{12,4},{16,24},{20,28},{24,16},{28,20},{1,9},{5... | collective-permute-start | bytes 1179656 | tf_op jit(solution)/shard_map/ppermute | solution.py:1160
  386.3 40.6 %copy-start.20 = (f32[1024]{0:T(1024)}, f32[1024]{0:T(1024)S(1)}, u32[]{:S(2)}) copy-start(f32[1024]{0:T(1024)S(1)} %get-tuple-element.159) | copy-start | bytes 12292
  387.6 19.3 %copy-start.10 = (bf16[192,1024]{1,0:T(8,128)(2,1)}, bf16[192,1024]{1,0:T(8,128)(2,1)S(1)}, u32[]{:S(2)}) copy-start(bf16[192,1024]{1,0:T(8,128)(2,1)S(1)} %collective-permute-done.10.refs_4_) | copy-start | bytes 1179652
  407.7 22.6 %copy-start.28 = (f32[5]{0:T(128)S(1)}, f32[5]{0:T(128)}, u32[]{:S(2)}) copy-start(f32[5]{0:T(128)} %constant.112) | copy-start | bytes 64
  (19 other events, 73.4 us)

commit v5 on v4

--- a/solution.py
+++ b/solution.py
@@ -28,20 +28,49 @@
     return [place == code[j : j + 1, :] for j in range(count)]
 
 
-def expert_kernel(owners, waits, s_ref, rec_ref, arr_ref, scale_ref, up_ref, down_ref, *refs):
-    (keep_ref, give_ref, back_ref, mix_ref, act_s, gug_s, wg_s, wd_s) = refs[waits:]
-    ff = down_ref.shape[1]
-    rows, width = act_s.shape[0], up_ref.shape[1]
-    tile = rows // 3
-    up_w = up_ref[0]
-    down_w = down_ref[0]
-    received = rec_ref[0].reshape(rows, width)
-    arrived = arr_ref[0].reshape(rows, width)
-    scale = scale_ref[0].reshape(rows, 1)
-    for t in range(3):
+def expert_kernel(j, owners, tiles, waits, s_ref, rec_hbm, arr_hbm, scale_ref, up_hbm, down_hbm, *refs):
+    (keep_hbm, give_hbm, back_hbm, mix_hbm,
+     rec_s, arr_s, up_s, down_s, act_s, gug_s, wg_s, wd_s, parts_s, out_s, in_sem, out_sem) = refs[waits:]
+    rows, ff = act_s.shape
+    width = up_s.shape[0]
+    sources, capacity = rec_s.shape[0], rec_s.shape[1]
+    tile = rows // tiles
+    per = sources // tiles
+
+    def load(src, dst, at):
+        copy = pltpu.make_async_copy(src, dst, in_sem.at[at])
+        copy.start()
+        return copy
+
+    def load_rows(hbm, held, t, at):
+        span = slice(t * per, (t + 1) * per)
+        return load(hbm.at[j, span], held.at[span], at)
+
+    expert = s_ref[0] + j
+    rec_in = [load_rows(rec_hbm, rec_s, 0, 0)]
+    up_in = load(up_hbm.at[expert], up_s, 2 * tiles)
+    arr_in = [load_rows(arr_hbm, arr_s, 0, tiles)]
+    down_in = load(down_hbm.at[expert], down_s, 2 * tiles + 1)
+    for t in range(1, tiles):
+        rec_in.append(load_rows(rec_hbm, rec_s, t, t))
+        arr_in.append(load_rows(arr_hbm, arr_s, t, tiles + t))
+    def products(t):
+        span = slice(t * per, (t + 1) * per)
+        return (
+            dot(rec_s[span].reshape(tile, width), up_s[...]),
+            dot(arr_s[span].reshape(tile, width), down_s[...], 1, 1),
+        )
+
+    for copy in (up_in, down_in, rec_in[0], arr_in[0]):
+        copy.wait()
+    following = products(0)
+    for t in range(tiles):
         at = slice(t * tile, (t + 1) * tile)
-        gate_up = dot(received[at], up_w)
-        act_grad = dot(arrived[at], down_w, 1, 1)
+        gate_up, act_grad = following
+        if t + 1 < tiles:
+            rec_in[t + 1].wait()
+            arr_in[t + 1].wait()
+            following = products(t + 1)
         gate = gate_up[:, :ff]
         up = gate_up[:, ff:]
         sig = 1.0 / (1.0 + jnp.exp(-gate))
@@ -49,57 +78,74 @@
         act_s[at, :] = (silu * up).astype(jnp.bfloat16)
         gug_s[at, :ff] = (act_grad * up * sig * (1.0 + gate * (1.0 - sig))).astype(jnp.bfloat16)
         gug_s[at, ff:] = (act_grad * silu).astype(jnp.bfloat16)
-    wg_s[...] = dot(received, gug_s[...], 0, 0)
-    wd_s[...] = dot(act_s[...], arrived, 0, 0)
+    wg_s[...] = dot(rec_s[...].reshape(rows, width), gug_s[...], 0, 0)
+    wd_s[...] = dot(act_s[...], arr_s[...].reshape(rows, width), 0, 0)
     bit = s_ref[1]
     up_rows = width // owners
     down_rows = ff // owners
-    for slot in range(owners // 2):
-        for ref, side in ((keep_ref, bit), (give_ref, 1 - bit)):
+    leaving = []
+    for k, (hbm, side) in enumerate(((give_hbm, 1 - bit), (keep_hbm, bit))):
+        for slot in range(owners // 2):
             owner = 2 * slot + side
-            ref[slot, :up_rows, :] = wg_s[
+            parts_s[k, slot, :up_rows, :] = wg_s[
                 pl.ds(pl.multiple_of(owner * up_rows, up_rows), up_rows), :
             ].astype(jnp.bfloat16)
-            ref[slot, up_rows:, :] = wd_s[
+            parts_s[k, slot, up_rows:, :] = wd_s[
                 pl.ds(pl.multiple_of(owner * down_rows, down_rows), down_rows), :
             ].astype(jnp.bfloat16)
-    for t in range(3):
+        copy = pltpu.make_async_copy(parts_s.at[k], hbm, out_sem.at[k])
+        copy.start()
+        leaving.append(copy)
+    for t in range(tiles):
         at = slice(t * tile, (t + 1) * tile)
-        back = dot(gug_s[at, :], up_w, 1, 1).astype(jnp.bfloat16)
-        mix = (dot(act_s[at, :], down_w) * scale[at]).astype(jnp.bfloat16)
-        back_ref[at, :] = back
-        mix_ref[at, :] = mix
+        out_s[0, at] = dot(gug_s[at, :], up_s[...], 1, 1).astype(jnp.bfloat16)
+        scale = scale_ref[0, t * per : (t + 1) * per].reshape(tile, 1)
+        out_s[1, at] = (dot(act_s[at, :], down_s[...]) * scale).astype(jnp.bfloat16)
+        for k, hbm in enumerate((back_hbm, mix_hbm)):
+            copy = pltpu.make_async_copy(out_s.at[k, at], hbm.at[at], out_sem.at[2 + 2 * t + k])
+            copy.start()
+            leaving.append(copy)
+    for copy in leaving:
+        copy.wait()
 
 
 def run_expert(scalars, j, received, arrived, scale, up_w, down_w, owners, after=()):
     count, sources, capacity, width = received.shape
     ff = down_w.shape[1]
     rows = sources * capacity
+    tiles = 2
     share = (owners // 2, (width + ff) // owners, width)
-    rows_spec = pl.BlockSpec((1, sources, capacity, width), lambda g, s: (j, 0, 0, 0))
-    whole2 = lambda *shape: pl.BlockSpec(shape, lambda g, s: (0,) * len(shape))
     slots = jax.ShapeDtypeStruct((rows, width), jnp.bfloat16)
     parts = jax.ShapeDtypeStruct(share, jnp.bfloat16)
+    anywhere = pl.BlockSpec(memory_space=pl.ANY)
     return pl.pallas_call(
-        functools.partial(expert_kernel, owners, len(after)),
+        functools.partial(expert_kernel, j, owners, tiles, len(after)),
         out_shape=(parts, parts, slots, slots),
         grid_spec=pltpu.PrefetchScalarGridSpec(
             num_scalar_prefetch=1,
             grid=(1,),
             in_specs=[
-                rows_spec,
-                rows_spec,
+                anywhere,
+                anywhere,
                 pl.BlockSpec((1, sources, capacity, 1), lambda g, s: (j, 0, 0, 0)),
-                pl.BlockSpec((1, width, 2 * ff), lambda g, s: (s[0] + j, 0, 0)),
-                pl.BlockSpec((1, ff, width), lambda g, s: (s[0] + j, 0, 0)),
+                anywhere,
+                anywhere,
             ]
-            + [pl.BlockSpec(memory_space=pl.ANY)] * len(after),
-            out_specs=[whole2(*share), whole2(*share), whole2(rows, width), whole2(rows, width)],
+            + [anywhere] * len(after),
+            out_specs=[anywhere] * 4,
             scratch_shapes=[
+                pltpu.VMEM((sources, capacity, width), jnp.bfloat16),
+                pltpu.VMEM((sources, capacity, width), jnp.bfloat16),
+                pltpu.VMEM((width, 2 * ff), jnp.bfloat16),
+                pltpu.VMEM((ff, width), jnp.bfloat16),
                 pltpu.VMEM((rows, ff), jnp.bfloat16),
                 pltpu.VMEM((rows, 2 * ff), jnp.bfloat16),
                 pltpu.VMEM((width, 2 * ff), jnp.float32),
                 pltpu.VMEM((ff, width), jnp.float32),
+                pltpu.VMEM((2,) + share, jnp.bfloat16),
+                pltpu.VMEM((2, rows, width), jnp.bfloat16),
+                pltpu.SemaphoreType.DMA((2 * tiles + 2,)),
+                pltpu.SemaphoreType.DMA((2 + 2 * tiles,)),
             ],
         ),
         compiler_params=pltpu.CompilerParams(vmem_limit_bytes=VM),
@@ -465,9 +511,11 @@
     return bit, {axis: index + mask - 2 * mask * bit}
 
 
-def dense_kernel(orders, spans, waits, far_bit, mine_ref, go_ref, *refs):
+def dense_kernel(orders, spans, waits, carried, mine_ref, *refs):
     steps = len(orders[0])
-    (out_ref, come_ref, sum_ref), scratch = refs[waits : waits + 3], refs[waits + 3 :]
+    extra = len(carried)
+    go_refs, out_ref, come_refs = refs[:extra], refs[extra + waits], refs[extra + waits + 1 : 2 * extra + waits + 1]
+    sum_ref, scratch = refs[2 * extra + waits + 1], refs[2 * extra + waits + 2 :]
     first_got = scratch[0]
     got = scratch[1 : 1 + steps]
     send_sem, recv_sem = scratch[1 + steps :]
@@ -496,7 +544,10 @@
         return (first.astype(jnp.float32) + second.astype(jnp.float32)).astype(jnp.bfloat16)
 
     flying = []
-    beside = send(go_ref, come_ref, links[far_bit][1], 0, 3 + steps)
+    beside = [
+        send(go, come, links[bit][1], i, 3 + steps)
+        for i, (bit, go, come) in enumerate(zip(carried, go_refs, come_refs))
+    ]
     for part, span in enumerate(spans):
         at = whole + (1 - core, slice(None), slice(None), span)
         flying.append(send(mine_ref.at[at], first_got.at[..., span], core_peer, part, 0))
@@ -539,7 +590,7 @@
         flying[part].wait_recv()
         mine = out_ref.at[core, :, :, span]
         flying[part] = send(mine, mine, core_peer, part, 2 + steps)
-    for copy in flying + [beside]:
+    for copy in flying + beside:
         copy.wait_recv()
     for copy in copies:
         copy.wait_send()
@@ -549,29 +600,29 @@
     return (slice(None),) * (len(orders[part]) - 1 - step)
 
 
-def reduce_dense(dense, go, far_mask, label, after=()):
+def reduce_dense(dense, carried, label, after=()):
     owners = lax.axis_size("dp")
     width, columns = dense.shape
     bits = owners.bit_length() - 1
     rows = width // owners // 4
     tiles = columns // 128
-    parts = bits
+    parts = 6
     bounds = [128 * (tiles * i // parts) for i in range(parts + 1)]
     spans = [slice(a, b) for a, b in zip(bounds[:-1], bounds[1:])]
-    all_links = list(range(bits + 1))
-    starts = [bits, 0, 1] + list(range(2, bits))
-    orders = [tuple(all_links[s:] + all_links[:s]) for s in starts[:parts]]
+    last = tuple(range(1, bits))
+    orders = [((bits, 0) if part % 2 == 0 else (0, bits)) + last for part in range(parts)]
     shape = (2,) * bits + (2, 2, rows, columns)
     half = (2,) * bits + (2, rows, columns)
-    out, come = pl.pallas_call(
-        functools.partial(dense_kernel, orders, spans, len(after), far_mask.bit_length() - 1),
-        out_shape=(
-            jax.ShapeDtypeStruct((2, 2, rows, columns), jnp.bfloat16),
-            jax.ShapeDtypeStruct(go.shape, jnp.bfloat16),
+    goes = [go for go, _ in carried]
+    out, *comes = pl.pallas_call(
+        functools.partial(
+            dense_kernel, orders, spans, len(after), [mask.bit_length() - 1 for _, mask in carried]
         ),
+        out_shape=[jax.ShapeDtypeStruct((2, 2, rows, columns), jnp.bfloat16)]
+        + [jax.ShapeDtypeStruct(go.shape, jnp.bfloat16) for go in goes],
         in_specs=[pl.BlockSpec(memory_space=pltpu.VMEM)]
-        + [pl.BlockSpec(memory_space=pl.ANY)] * (1 + len(after)),
-        out_specs=[pl.BlockSpec(memory_space=pltpu.VMEM), pl.BlockSpec(memory_space=pl.ANY)],
+        + [pl.BlockSpec(memory_space=pl.ANY)] * (len(goes) + len(after)),
+        out_specs=[pl.BlockSpec(memory_space=pltpu.VMEM)] + [pl.BlockSpec(memory_space=pl.ANY)] * len(goes),
         scratch_shapes=[pltpu.VMEM(half, jnp.bfloat16), pltpu.VMEM(half, jnp.bfloat16)]
         + [
             pltpu.VMEM((2,) * (bits - step) + (rows, columns), jnp.bfloat16)
@@ -583,8 +634,8 @@
         ),
         cost_estimate=lasts(50),
         name="reduce_dense",
-    )(dense.reshape(shape), go, *after)
-    return out.reshape(width // owners, columns), come
+    )(dense.reshape(shape), *goes, *after)
+    return out.reshape(width // owners, columns), *comes
 
 
 PAIR = 2
@@ -759,23 +810,10 @@
     )(token, grad, chip_grad, pair_grad)
 
 
-def return_kernel(capacity, count, far_mask, code_ref, *refs):
-    backs, mixes = refs[:count], refs[count : 2 * count]
-    go_ref, out_ref, near_ref, far_ref, come_ref = refs[2 * count : 2 * count + 5]
-    (fetched, theirs, core_got, own, theirs_mix, core_got_mix, half_pair, half_chip, from_chip, from_pair,
-     send_sem, recv_sem, local_sem) = refs[2 * count + 5 :]
-    rows = out_ref.shape[0]
-    half = rows // 2
-    _, core = flipped("expert", 1)
-    _, chip = flipped("expert", 2)
-    _, pair = flipped("dp", PAIR)
-    _, far = flipped("dp", far_mask)
-    greet([core, chip, pair, far])
-    push = Pusher(send_sem, recv_sem)
-    beside = push(go_ref, come_ref, far)
-    order = [(backs, r) for r in (7, 6, 3, 2, 5, 4, 1, 0)] + [(mixes, r) for r in (7, 6, 3, 2, 5, 4, 1, 0)]
+def fetcher(order, fetched, local_sem, capacity, code_ref):
     depth = fetched.shape[0]
     fetching = []
+    done = []
 
     def fetch():
         n = len(fetching)
@@ -794,60 +832,99 @@
             for copy in fetching[-1]:
                 copy.start()
 
-    done = []
-
-    def combined():
+    for _ in range(depth - 1):
+        fetch()
+
+    def next_sum():
+        fetch()
         n = len(done)
         for copy in fetching[n]:
             copy.wait()
-        made = dot(picked(code_ref[order[n][1]], capacity), fetched[n % depth], 0, 0)
         done.append(n)
-        return made
-
-    for _ in range(depth - 1):
-        fetch()
-
-    def next_sum():
-        fetch()
-        return combined()
+        return dot(picked(code_ref[order[n][1]], capacity), fetched[n % depth], 0, 0)
+
+    return next_sum
+
+
+def combine_kernel(capacity, count, code_ref, *refs):
+    slots = refs[:count]
+    mine_ref, theirs_ref, fetched, local_sem = refs[-4:]
+    order = [(slots, r) for r in (7, 6, 3, 2, 5, 4, 1, 0)]
+    next_sum = fetcher(order, fetched, local_sem, capacity, code_ref)
+    for _, r in order:
+        (theirs_ref if r % 2 else mine_ref)[r // 2] = next_sum().astype(jnp.bfloat16)
+
+
+def combine(code, slots, capacity, after):
+    _, count, rows = code.shape
+    width = slots[0].shape[1]
+    vmem = pl.BlockSpec(memory_space=pltpu.VMEM)
+    anywhere = pl.BlockSpec(memory_space=pl.ANY)
+    four = jax.ShapeDtypeStruct((4, rows, width), jnp.bfloat16)
+    return pl.pallas_call(
+        functools.partial(combine_kernel, capacity, count),
+        out_shape=(four, four),
+        in_specs=[vmem] + [anywhere] * (count + len(after)),
+        out_specs=[vmem, vmem],
+        scratch_shapes=[
+            pltpu.VMEM((4, count * capacity, width), jnp.bfloat16),
+            pltpu.SemaphoreType.DMA((4, count)),
+        ],
+        compiler_params=pltpu.CompilerParams(vmem_limit_bytes=VM),
+        cost_estimate=lasts(12),
+        name="combine",
+    )(code, *slots, *after)
+
+
+def return_kernel(capacity, count, far_mask, code_ref, mine_ref, theirs_ref, go_ref, *refs):
+    mixes = refs[:count]
+    (out_ref, near_ref, far_ref, come_ref, fetched, core_got, own, theirs_mix, core_got_mix, half_pair, half_chip, from_chip,
+     from_pair, send_sem, recv_sem, local_sem) = refs[-16:]
+    rows = out_ref.shape[0]
+    half = rows // 2
+    _, core = flipped("expert", 1)
+    _, chip = flipped("expert", 2)
+    _, pair = flipped("dp", PAIR)
+    _, far = flipped("dp", far_mask)
+    greet([core, chip, pair, far])
+    push = Pusher(send_sem, recv_sem)
+    beside = push(go_ref, come_ref, far)
+    crossing = {i: push(theirs_ref.at[i], core_got.at[i], core) for i in (3, 1, 2, 0)}
+    order = [(mixes, r) for r in (7, 6, 3, 2, 5, 4, 1, 0)]
+    next_sum = fetcher(order, fetched, local_sem, capacity, code_ref)
 
     def plus(a, b):
-        return (a + b.astype(jnp.float32)).astype(jnp.bfloat16)
-
-    def sums(i, theirs, core_got):
-        theirs[i] = next_sum().astype(jnp.bfloat16)
-        copy = push(theirs.at[i], core_got.at[i], core)
-        return next_sum(), copy
-
-    mine, copy = sums(3, theirs, core_got)
-    copy.wait_recv()
-    own[3] = plus(mine, core_got[3])
+        return (a.astype(jnp.float32) + b.astype(jnp.float32)).astype(jnp.bfloat16)
+
+    def mix(i, ref, at):
+        theirs_mix[i] = next_sum().astype(jnp.bfloat16)
+        copy = push(theirs_mix.at[i], core_got_mix.at[i], core)
+        mine = next_sum()
+        copy.wait_recv()
+        ref[at] = plus(mine, core_got_mix[i])
+
+    crossing[3].wait_recv()
+    own[3] = plus(mine_ref[3], core_got[3])
     at_pair = push(own.at[3, 0:half], half_pair, pair)
     at_chip = push(own.at[3, half:rows], half_chip, chip)
-    mine, copy = sums(1, theirs, core_got)
-    copy.wait_recv()
-    own[1] = plus(mine, core_got[1])
+    crossing[1].wait_recv()
+    own[1] = plus(mine_ref[1], core_got[1])
     low_chip = push(own.at[1, half:rows], from_chip.at[half:rows], chip)
-    mine, copy = sums(2, theirs, core_got)
-    copy.wait_recv()
-    own[2] = plus(mine, core_got[2])
+    crossing[2].wait_recv()
+    own[2] = plus(mine_ref[2], core_got[2])
     high_pair = push(own.at[2, 0:half], from_pair.at[0:half], pair)
-    mine, copy = sums(0, theirs, core_got)
-    copy.wait_recv()
-    out_ref[...] = mine + core_got[0].astype(jnp.float32)
-    mine, copy = sums(3, theirs_mix, core_got_mix)
-    copy.wait_recv()
-    far_ref[1] = plus(mine, core_got_mix[3])
+    crossing[0].wait_recv()
+    out_ref[...] = mine_ref[0].astype(jnp.float32) + core_got[0].astype(jnp.float32)
+    mix(3, far_ref, 1)
+    mix(1, far_ref, 0)
     at_pair.wait_recv()
-    own[1, :half] = plus(own[1, :half].astype(jnp.float32), half_pair[...])
+    own[1, :half] = plus(own[1, :half], half_pair[...])
     high_chip = push(own.at[1, 0:half], from_chip.at[0:half], chip)
     at_chip.wait_recv()
-    own[2, half:] = plus(own[2, half:].astype(jnp.float32), half_chip[...])
+    own[2, half:] = plus(own[2, half:], half_chip[...])
     low_pair = push(own.at[2, half:rows], from_pair.at[half:rows], pair)
-    for i in (1, 2, 0):
-        mine, copy = sums(i, theirs_mix, core_got_mix)
-        copy.wait_recv()
-        (far_ref if i > 1 else near_ref)[i % 2] = plus(mine, core_got_mix[i])
+    mix(2, near_ref, 1)
+    mix(0, near_ref, 0)
     low_chip.wait_recv()
     high_pair.wait_recv()
     high_chip.wait_recv()
@@ -857,40 +934,41 @@
     push.finish()
 
 
-def combine_and_return(code, backs, mixes, capacity, go, far_mask, label):
+def return_sums(code, mine, theirs, mixes, capacity, go, far_mask, label, after):
     _, count, rows = code.shape
-    width = backs[0].shape[1]
+    width = mine.shape[2]
     vmem = pl.BlockSpec(memory_space=pltpu.VMEM)
     anywhere = pl.BlockSpec(memory_space=pl.ANY)
     four = pltpu.VMEM((4, rows, width), jnp.bfloat16)
+    two = jax.ShapeDtypeStruct((2, rows, width), jnp.bfloat16)
     return pl.pallas_call(
         functools.partial(return_kernel, capacity, count, far_mask),
         out_shape=(
             jax.ShapeDtypeStruct((rows, width), jnp.float32),
-            jax.ShapeDtypeStruct((2, rows, width), jnp.bfloat16),
-            jax.ShapeDtypeStruct((2, rows, width), jnp.bfloat16),
+            two,
+            two,
             jax.ShapeDtypeStruct(go.shape, jnp.bfloat16),
         ),
-        in_specs=[vmem] + [anywhere] * (2 * count + 1),
-        out_specs=[vmem, vmem, vmem, anywhere],
-        scratch_shapes=[pltpu.VMEM((4, count * capacity, width), jnp.bfloat16), four, four, four, four, four]
+        in_specs=[vmem] * 3 + [anywhere] * (1 + count + len(after)),
+        out_specs=[vmem] * 3 + [anywhere],
+        scratch_shapes=[pltpu.VMEM((4, count * capacity, width), jnp.bfloat16), four, four, four, four]
         + [pltpu.VMEM((rows // 2, width), jnp.bfloat16)] * 2
         + [pltpu.VMEM((rows, width), jnp.bfloat16)] * 2
         + [
-            pltpu.SemaphoreType.DMA((16,)),
-            pltpu.SemaphoreType.DMA((16,)),
+            pltpu.SemaphoreType.DMA((15,)),
+            pltpu.SemaphoreType.DMA((15,)),
             pltpu.SemaphoreType.DMA((4, count)),
         ],
         compiler_params=pltpu.CompilerParams(
             collective_id=label, has_side_effects=True, vmem_limit_bytes=VM
         ),
         cost_estimate=lasts(37),
-        name="combine_and_return",
-    )(code, *backs, *mixes, go)
-
-
-def settle_kernel(bit_ref, keep_ref, got_ref, *refs):
-    stay_ref, go_ref = refs[-2:]
+        name="return_sums",
+    )(code, mine, theirs, go, *mixes, *after)
+
+
+def settle_kernel(waits, bit_ref, keep_ref, got_ref, *refs):
+    stay_ref, go_ref = refs[waits : waits + 2]
     bit = bit_ref[0]
     for high in range(keep_ref.shape[0]):
         for low in range(keep_ref.shape[2]):
@@ -901,24 +979,25 @@
                 ref[high, low] = total.astype(jnp.bfloat16)
 
 
-def settle(keep, got, mask, label, after):
+def settle(keep, got, mask, label, after, passed=()):
     count, rows, columns = keep.shape
     low = 1 if mask == PAIR else 2
     shape = (count // 2 // low, 2, low, rows, columns)
     half = jax.ShapeDtypeStruct((count // 2 // low, low, rows, columns), jnp.bfloat16)
     bit = lax.rem(lax.axis_index("dp") // mask, 2)
     vmem = pl.BlockSpec(memory_space=pltpu.VMEM)
-    stay, go = pl.pallas_call(
-        settle_kernel,
-        out_shape=(half, half),
-        in_specs=[pl.BlockSpec(memory_space=pltpu.SMEM), vmem, vmem]
-        + [pl.BlockSpec(memory_space=pl.ANY)] * len(after),
-        out_specs=[vmem, vmem],
+    anywhere = pl.BlockSpec(memory_space=pl.ANY)
+    stay, go, *passed = pl.pallas_call(
+        functools.partial(settle_kernel, len(after) + len(passed)),
+        out_shape=[half, half] + [jax.ShapeDtypeStruct(p.shape, p.dtype) for p in passed],
+        in_specs=[pl.BlockSpec(memory_space=pltpu.SMEM), vmem, vmem] + [anywhere] * (len(after) + len(passed)),
+        out_specs=[vmem, vmem] + [anywhere] * len(passed),
+        input_output_aliases={3 + len(after) + i: 2 + i for i in range(len(passed))},
         compiler_params=pltpu.CompilerParams(vmem_limit_bytes=VM),
         cost_estimate=lasts(3),
         name="settle_%s" % label,
-    )(bit.reshape(1), keep.reshape(shape), got.reshape(shape), *after)
-    return stay.reshape(-1, rows, columns), go.reshape(-1, rows, columns)
+    )(bit.reshape(1), keep.reshape(shape), got.reshape(shape), *after, *passed)
+    return stay.reshape(-1, rows, columns), go.reshape(-1, rows, columns), *passed
 
 
 def settle_mix_kernel(near_ref, got_ref, *refs):
@@ -948,22 +1027,13 @@
     return STAT_DECAY * old + (1.0 - STAT_DECAY) * new
 
 
-def clip_factor(squares, count):
-    return LEARN_RATE / jnp.maximum(1.0, jnp.sqrt(squares / count) / CLIP_LEVEL)
-
-
-def add_all(values):
-    return jnp.sum(jnp.sum(values, axis=1, keepdims=True), axis=0, keepdims=True)
-
-
-def column_of(table, lane, at):
-    return jnp.sum(jnp.where(lane == at, table, 0.0), axis=1, keepdims=True)
-
-
-def expert_stats_kernel(count, groups, half, *refs):
-    stays, gots = refs[:half], refs[half : 2 * half]
-    (up_old_ref, down_old_ref, up_rows_ref, down_rows_ref, up_cols_ref, down_cols_ref,
-     out_ref, sums_ref, up_new_ref, down_new_ref, pay_s, got_s, spread_s, send_sem, recv_sem) = refs[2 * half :]
+def final_stats_kernel(count, groups, half, early, *refs):
+    late = half - early
+    owns, gots = refs[:early], refs[early : 2 * early]
+    stays, comes = refs[2 * early : 2 * early + late], refs[2 * early + late : 2 * half]
+    (dense_ref, up_old_ref, down_old_ref, up_rows_ref, down_rows_ref, up_cols_ref, down_cols_ref, dense_old_ref,
+     dense_cols_ref, ends_ref, out_ref, sums_ref, up_new_ref, down_new_ref, dense_out_ref, dense_new_ref,
+     go_s, pay_s, got_s, dense_pay_s, dense_got_s, spread_s, send_sem, recv_sem) = refs[2 * half :]
     width = up_rows_ref.shape[1]
     ff = down_rows_ref.shape[1]
     wide = width // 2
@@ -973,35 +1043,116 @@
     place = lax.axis_index("expert")
     after = [lax.rem(me + k, count) for k in range(count)]
     beside = [lax.rem(place + k, groups) for k in range(groups)]
+    pair_bit, pair = flipped("dp", PAIR)
     greet([{"dp": after[k]} for k in range(1, count)] + [{"expert": beside[k]} for k in range(1, groups)])
     push = Pusher(send_sem, recv_sem)
-    pair_bit = lax.rem(me // PAIR, 2)
+
+    def summed(j, side):
+        return (
+            stays[j][side].astype(jnp.float32) + comes[j][side].astype(jnp.float32)
+        ).astype(jnp.bfloat16)
+
+    crossing = []
+    for j in range(late):
+        go_s[j] = summed(j, 1 - pair_bit)
+        crossing.append(push(go_s.at[j], ends_ref.at[late + j], pair))
+
+    def column_of(table_ref, lane, at):
+        return jnp.sum(jnp.where(lane == at, table_ref[...], 0.0), axis=1, keepdims=True)
+
     up_lane = lax.broadcasted_iota(jnp.int32, (own_up, LANES), 1)
     down_lane = lax.broadcasted_iota(jnp.int32, (own_down, LANES), 1)
     up_new_ref[...] = jnp.zeros_like(up_new_ref)
     down_new_ref[...] = jnp.zeros_like(down_new_ref)
-    for j in range(half):
-        for ref, at in ((stays[j], pair_bit * half + j), (gots[j], (1 - pair_bit) * half + j)):
-            for kind, (part, old_ref, new_ref, lane, rows) in enumerate(
-                (
-                    (ref[:own_up, :], up_old_ref, up_new_ref, up_lane, own_up),
-                    (ref[own_up:, :], down_old_ref, down_new_ref, down_lane, own_down),
-                )
-            ):
-                grad = part.astype(jnp.float32)
-                square = grad * grad
-                new = decayed(
-                    column_of(old_ref[...], lane, at),
-                    jnp.mean(square + EPS_STAT, axis=1, keepdims=True),
-                )
-                new_ref[:rows, :] = jnp.where(lane == at, new, new_ref[:rows, :])
-                total = jnp.sum(square + EPS_STAT, axis=0, keepdims=True)
-                scaled = jnp.sum(square * (1.0 / new), axis=0, keepdims=True)
-                for h in range(2):
-                    span = slice(h * wide, (h + 1) * wide)
-                    pay_s[at, 4 * kind + h : 4 * kind + h + 1, :] = total[:, span]
-                    pay_s[at, 4 * kind + 2 + h : 4 * kind + 3 + h, :] = scaled[:, span]
+
+    def factored(grad, old):
+        square = grad * grad
+        new = decayed(old, jnp.mean(square + EPS_STAT, axis=1, keepdims=True))
+        return (
+            new,
+            jnp.sum(square + EPS_STAT, axis=0, keepdims=True),
+            jnp.sum(square * (1.0 / new), axis=0, keepdims=True),
+        )
+
+    def expert(values, at):
+        for kind, (part, old_ref, new_ref, lane, rows) in enumerate(
+            (
+                (values[:own_up, :], up_old_ref, up_new_ref, up_lane, own_up),
+                (values[own_up:, :], down_old_ref, down_new_ref, down_lane, own_down),
+            )
+        ):
+            new, total, scaled = factored(part.astype(jnp.float32), column_of(old_ref, lane, at))
+            new_ref[:rows, :] = jnp.where(lane == at, new, new_ref[:rows, :])
+            for h in range(2):
+                span = slice(h * wide, (h + 1) * wide)
+                pay_s[at, 4 * kind + h : 4 * kind + h + 1, :] = total[:, span]
+                pay_s[at, 4 * kind + 2 + h : 4 * kind + 3 + h, :] = scaled[:, span]
+
+    own_at, got_at = pair_bit * half, (1 - pair_bit) * half
+    for j in range(late):
+        ends_ref[j] = summed(j, pair_bit)
+        expert(ends_ref[j], own_at + early + j)
+    for j in range(early):
+        expert(owns[j][...], own_at + j)
+        expert(gots[j][...], got_at + j)
+
+    columns = count * dense_cols_ref.shape[2]
+    piece = dense_cols_ref.shape[2]
+    dense_lane = lax.broadcasted_iota(jnp.int32, dense_new_ref.shape, 1)
+    old = dense_old_ref[...]
+    qkv_columns = columns - width
+    totals, scaleds, rows_new = [], [], []
+    for at, span in enumerate((slice(0, qkv_columns), slice(qkv_columns, columns))):
+        new, total, scaled = factored(
+            dense_ref[:, span].astype(jnp.float32), column_of(dense_old_ref, dense_lane, at)
+        )
+        rows_new.append(new)
+        totals.append(total)
+        scaleds.append(scaled)
+    gain_lanes = (dense_lane == 2) | (dense_lane == 3)
+    gains = pltpu.roll(dense_ref[:, columns:].astype(jnp.float32), 2, 1)
+    moments = jnp.where(gain_lanes, decayed(old, gains * gains + EPS_STAT), 1.0)
+    gain_steps = jnp.where(gain_lanes, gains * lax.rsqrt(moments), 0.0)
+    dense_new_ref[...] = jnp.where(
+        dense_lane == 0,
+        rows_new[0],
+        jnp.where(dense_lane == 1, rows_new[1], jnp.where(gain_lanes, gain_steps, pltpu.roll(moments, 2, 1))),
+    )
+    gain_squares = jnp.sum(jnp.sum(gain_steps * gain_steps, axis=1, keepdims=True), axis=0, keepdims=True)
+    total = jnp.concatenate(totals, axis=1)
+    scaled = jnp.concatenate(scaleds, axis=1)
+    for d in range(count):
+        span = slice(d * piece, (d + 1) * piece)
+        dense_pay_s[d] = jnp.concatenate(
+            [total[:, span], scaled[:, span], jnp.broadcast_to(gain_squares, (1, piece)), jnp.zeros((5, piece), jnp.float32)],
+            axis=0,
+        )
+    dense_arriving = [push(dense_pay_s.at[after[k]], dense_got_s.at[k], {"dp": after[k]}) for k in range(1, count)]
+    for j in range(late):
+        crossing[j].wait_recv()
+        expert(ends_ref[late + j], got_at + early + j)
     arriving = [push(pay_s.at[after[k]], got_s.at[k], {"dp": after[k]}) for k in range(1, count)]
+
+    tile = dense_pay_s[me]
+    for k in range(1, count):
+        dense_arriving[k - 1].wait_recv()
+        tile = tile + dense_got_s[k]
+    new_columns = decayed(dense_cols_ref[me], tile[0:1] / width)
+    is_qkv = lax.broadcasted_iota(jnp.int32, (1, piece), 1) + me * piece < qkv_columns
+    ratio = tile[1:2] / new_columns
+    sums = [
+        jnp.sum(jnp.where(chosen, row, 0.0), axis=1, keepdims=True)
+        for row in (ratio, tile[0:1])
+        for chosen in (is_qkv, ~is_qkv)
+    ]
+    dense_out_ref[me] = jnp.concatenate(
+        [new_columns]
+        + [jnp.broadcast_to(v, (1, piece)) for v in sums]
+        + [tile[2:3], jnp.zeros((2, piece), jnp.float32)],
+        axis=0,
+    )
+    dense_arriving = [push(dense_out_ref.at[me], dense_out_ref.at[me], {"dp": after[k]}) for k in range(1, count)]
+
     tile = pay_s[me]
     for k in range(1, count):
         arriving[k - 1].wait_recv()
@@ -1014,13 +1165,13 @@
         here = pl.ds(me, 1)
         square = jnp.concatenate([tile[4 * kind + h : 4 * kind + h + 1] for h in range(2)], axis=1)
         scaled = jnp.concatenate([tile[4 * kind + 2 + h : 4 * kind + 3 + h] for h in range(2)], axis=1)
-        columns = decayed(cols_ref[here, :], square / rows)
+        new_columns = decayed(cols_ref[here, :], square / rows)
         row_mean = decayed(
             jnp.mean(rows_ref[here, :], axis=1, keepdims=True),
             jnp.sum(square, axis=1, keepdims=True) / (rows * width),
         )
-        squares = row_mean * jnp.sum(scaled / columns, axis=1, keepdims=True)
-        made += [columns[:, :wide], columns[:, wide:]]
+        squares = row_mean * jnp.sum(scaled / new_columns, axis=1, keepdims=True)
+        made += [new_columns[:, :wide], new_columns[:, wide:]]
         tops += [jnp.broadcast_to(v, (1, wide)) for v in (row_mean, squares)]
     out_ref[me] = jnp.concatenate(made + tops, axis=0)
     arriving = [push(out_ref.at[me], out_ref.at[me], {"dp": after[k]}) for k in range(1, count)]
@@ -1031,7 +1182,7 @@
         total = total + out_ref[a, :, :LANES]
     spread_s[place] = total
     arriving = [push(spread_s.at[place], spread_s.at[place], {"expert": beside[k]}) for k in range(1, groups)]
-    for copy in arriving:
+    for copy in arriving + dense_arriving:
         copy.wait_recv()
     total = spread_s[0]
     for e in range(1, groups):
@@ -1040,26 +1191,39 @@
     push.finish()
 
 
-def expert_stats(stays, gots, up_old, down_old, up_rows, down_rows, up_cols, down_cols, label):
+def final_stats(owns, gots, stays, comes, dense, olds, all_rows, all_columns, dense_old, dense_columns, label):
     count = lax.axis_size("dp")
     groups = lax.axis_size("expert")
-    width = up_rows.shape[1]
+    width = all_rows[0].shape[1]
+    rows = olds[0].shape[0] + olds[1].shape[0]
+    piece = dense_columns.shape[2]
     vmem = pl.BlockSpec(memory_space=pltpu.VMEM)
     tiles = (count, 8, width // 2)
-    copies = 2 * (count - 1) + groups - 1
+    dense_tiles = (count, 8, piece)
+    late = len(stays)
+    copies = 4 * (count - 1) + groups - 1 + late
+    shape = lambda *s: jax.ShapeDtypeStruct(s, jnp.float32)
+    outs = (
+        jax.ShapeDtypeStruct((2 * late, rows, width), jnp.bfloat16),
+        shape(*tiles),
+        shape(8, LANES),
+        shape(LANES, LANES),
+        shape(LANES, LANES),
+        shape(*dense_tiles),
+        shape(dense.shape[0], LANES),
+    )
+    args = (*owns, *gots, *stays, *comes, dense, *olds, *all_rows, *all_columns, dense_old, dense_columns)
     return pl.pallas_call(
-        functools.partial(expert_stats_kernel, count, groups, len(stays)),
-        out_shape=(
-            jax.ShapeDtypeStruct(tiles, jnp.float32),
-            jax.ShapeDtypeStruct((8, LANES), jnp.float32),
-            jax.ShapeDtypeStruct((LANES, LANES), jnp.float32),
-            jax.ShapeDtypeStruct((LANES, LANES), jnp.float32),
-        ),
-        in_specs=[vmem] * (2 * len(stays) + 6),
-        out_specs=[vmem] * 4,
+        functools.partial(final_stats_kernel, count, groups, len(owns) + late, len(owns)),
+        out_shape=outs,
+        in_specs=[vmem] * len(args),
+        out_specs=[vmem] * len(outs),
         scratch_shapes=[
+            pltpu.VMEM((late, rows, width), jnp.bfloat16),
             pltpu.VMEM(tiles, jnp.float32),
             pltpu.VMEM(tiles, jnp.float32),
+            pltpu.VMEM(dense_tiles, jnp.float32),
+            pltpu.VMEM(dense_tiles, jnp.float32),
             pltpu.VMEM((groups, 8, LANES), jnp.float32),
             pltpu.SemaphoreType.DMA((copies,)),
             pltpu.SemaphoreType.DMA((copies,)),
@@ -1068,40 +1232,74 @@
             collective_id=label, has_side_effects=True, vmem_limit_bytes=VM
         ),
         cost_estimate=lasts(15),
-        name="expert_stats",
-    )(*stays, *gots, up_old, down_old, up_rows, down_rows, up_cols, down_cols)
-
-
-def expert_update_kernel(counts, half, s_ref, *refs):
-    stays, gots = refs[:half], refs[half : 2 * half]
-    (tiles_ref, sums_ref, up_new_ref, down_new_ref, up_w_ref, down_w_ref,
-     up_out_ref, down_out_ref, up_rows_ref, down_rows_ref, up_cols_ref, down_cols_ref) = refs[2 * half :]
+        name="final_stats",
+    )(*args)
+
+
+def update_kernel(counts, half, early, s_ref, *refs):
+    owns, gots = refs[:early], refs[early : 2 * early]
+    (ends_ref, tiles_ref, sums_ref, up_new_ref, down_new_ref, dense_tiles_ref, dense_new_ref, dense_ref, dense_rows_ref,
+     up_w_ref, down_w_ref, qkv_w_ref, out_w_ref,
+     up_out_ref, down_out_ref, up_rows_ref, down_rows_ref, up_cols_ref, down_cols_ref,
+     qkv_out_ref, out_out_ref, qkv_cols_ref, out_cols_ref, turned_ref, gains_ref, rms_ref) = refs[2 * early :]
+    late = half - early
     own_up = up_out_ref.shape[1]
     own_down = down_out_ref.shape[1]
     wide = tiles_ref.shape[2]
     pair_bit = s_ref[0]
+    count = dense_tiles_ref.shape[0]
+    dense_sums = dense_tiles_ref[0, :, 0:1]
+    for a in range(1, count):
+        dense_sums = dense_sums + dense_tiles_ref[a, :, 0:1]
+    width = dense_rows_ref.shape[1]
+    qkv_columns = qkv_out_ref.shape[1]
+    row_means = []
+    squares = [dense_tiles_ref[0, 5:6, 0:1]]
+    for at, columns in enumerate((qkv_columns, width)):
+        row_means.append(
+            decayed(
+                jnp.mean(dense_rows_ref[at : at + 1, :], axis=1, keepdims=True),
+                dense_sums[3 + at : 4 + at] / (width * columns),
+            )
+        )
+        squares.append(row_means[-1] * dense_sums[1 + at : 2 + at])
+    squares += [sums_ref[5:6, 0:1], sums_ref[7:8, 0:1]]
+    roots = [jnp.sqrt(square / number) for square, number in zip(squares, counts)]
+    factors = [LEARN_RATE / jnp.maximum(1.0, root / CLIP_LEVEL) for root in roots]
+    rms_ref[...] = jnp.concatenate(
+        [jnp.broadcast_to(root, (1, LANES)) for root in roots] + [jnp.zeros((3, LANES), jnp.float32)], axis=0
+    )
+
     up_table = up_new_ref[...]
     down_table = down_new_ref[...]
     lane = lax.broadcasted_iota(jnp.int32, up_table.shape, 1)
-    factors = [clip_factor(sums_ref[5 + 2 * kind : 6 + 2 * kind, 0:1], counts[kind]) for kind in range(2)]
-    for j in range(half):
-        for ref, at in ((stays[j], pair_bit * half + j), (gots[j], (1 - pair_bit) * half + j)):
-            tile = tiles_ref[at]
-            for kind, (table, weight_ref, out_ref, first, rows) in enumerate(
-                (
-                    (up_table, up_w_ref, up_out_ref, 0, own_up),
-                    (down_table, down_w_ref, down_out_ref, own_up, own_down),
+
+    def expert(ref, at):
+        tile = tiles_ref[at]
+        for kind, (table, weight_ref, out_ref, first, rows) in enumerate(
+            (
+                (up_table, up_w_ref, up_out_ref, 0, own_up),
+                (down_table, down_w_ref, down_out_ref, own_up, own_down),
+            )
+        ):
+            row_mean = tile[4 + 2 * kind : 5 + 2 * kind, 0:1]
+            column = jnp.sum(jnp.where(lane == at, table, 0.0), axis=1, keepdims=True)[:rows]
+            scale = factors[3 + kind] * lax.rsqrt(column / row_mean)
+            for h in range(2):
+                span = slice(h * wide, (h + 1) * wide)
+                columns = lax.rsqrt(tile[2 * kind + h : 2 * kind + h + 1, :])
+                out_ref[at, :, span] = (
+                    weight_ref[at, :, span].astype(jnp.float32)
+                    - ref[first : first + rows, span].astype(jnp.float32) * scale * columns
                 )
-            ):
-                row_mean = tile[4 + 2 * kind : 5 + 2 * kind, 0:1]
-                scale = factors[kind] * lax.rsqrt(column_of(table, lane, at)[:rows] / row_mean)
-                for h in range(2):
-                    span = slice(h * wide, (h + 1) * wide)
-                    columns = lax.rsqrt(tile[2 * kind + h : 2 * kind + h + 1, :])
-                    out_ref[at, :, span] = (
-                        weight_ref[at, :, span].astype(jnp.float32)
-                        - ref[first : first + rows, span].astype(jnp.float32) * scale * columns
-                    )
+
+    own_at, got_at = pair_bit * half, (1 - pair_bit) * half
+    for j in range(early):
+        expert(owns[j], own_at + j)
+        expert(gots[j], got_at + j)
+    for j in range(late):
+        expert(ends_ref.at[j], own_at + early + j)
+        expert(ends_ref.at[late + j], got_at + early + j)
     up_rows_ref[...] = up_table.T[: up_rows_ref.shape[0], :own_up]
     down_rows_ref[...] = down_table.T[: down_rows_ref.shape[0], :own_down]
     for a in range(up_cols_ref.shape[0]):
@@ -1110,44 +1308,87 @@
             up_cols_ref[a : a + 1, span] = tiles_ref[a, h : h + 1, :]
             down_cols_ref[a : a + 1, span] = tiles_ref[a, 2 + h : 3 + h, :]
 
-
-def expert_update(stays, gots, tiles, sums, up_new, down_new, up_w, down_w):
+    table = dense_new_ref[...]
+    scales = [
+        factors[1 + at] * lax.rsqrt(table[:, at : at + 1] / row_means[at]) for at in range(2)
+    ]
+    piece = dense_tiles_ref.shape[2]
+    for first in range(0, qkv_columns + width, LANES):
+        at = 0 if first < qkv_columns else 1
+        weight_ref, out_ref, cols_ref = (
+            (qkv_w_ref, qkv_out_ref, qkv_cols_ref) if at == 0 else (out_w_ref, out_out_ref, out_cols_ref)
+        )
+        here = slice(first - at * qkv_columns, first - at * qkv_columns + LANES)
+        within = first % piece
+        columns = dense_tiles_ref[first // piece, 0:1, within : within + LANES]
+        cols_ref[:, here] = columns
+        out_ref[:, here] = weight_ref[:, here].astype(jnp.float32) - dense_ref[
+            :, first : first + LANES
+        ].astype(jnp.float32) * scales[at] * lax.rsqrt(columns)
+    turned = table.T[:8]
+    turned_ref[...] = turned
+    gains_ref[...] = -factors[0] * turned
+
+
+def update(owns, gots, stats, dense, dense_rows, up_w, down_w, qkv_w, out_w):
     count = lax.axis_size("dp")
     groups = lax.axis_size("expert")
     me = lax.axis_index("dp")
-    experts, width, _ = up_w.shape
+    experts, width, up_columns = up_w.shape
     ff = down_w.shape[1]
+    qkv_columns = qkv_w.shape[1]
     own_up, own_down = width // count, ff // count
-    counts = (float(groups * experts * width * up_w.shape[2]), float(groups * experts * ff * width))
+    counts = (
+        float(2 * width),
+        float(width * qkv_columns),
+        float(width * width),
+        float(groups * experts * width * up_columns),
+        float(groups * experts * ff * width),
+    )
+    ends = stats[0]
+    early = len(owns)
     whole = lambda *shape: pl.BlockSpec(shape, lambda g, s: (0,) * len(shape))
     shape = lambda *s: jax.ShapeDtypeStruct(s, jnp.float32)
     rows = own_up + own_down
     outs = [
-        shape(experts, own_up, up_w.shape[2]),
+        shape(experts, own_up, up_columns),
         shape(experts, own_down, width),
         shape(experts, own_up),
         shape(experts, own_down),
-        shape(experts, up_w.shape[2]),
+        shape(experts, up_columns),
         shape(experts, width),
+        shape(own_up, qkv_columns),
+        shape(own_up, width),
+        shape(1, qkv_columns),
+        shape(1, width),
+        shape(8, LANES),
+        shape(8, LANES),
+        shape(8, LANES),
     ]
     return pl.pallas_call(
-        functools.partial(expert_update_kernel, counts, len(stays)),
+        functools.partial(update_kernel, counts, early + ends.shape[0] // 2, early),
         out_shape=outs,
         grid_spec=pltpu.PrefetchScalarGridSpec(
             num_scalar_prefetch=1,
             grid=(1,),
-            in_specs=[whole(rows, width)] * (2 * len(stays))
-            + [whole(*tiles.shape), whole(*sums.shape), whole(*up_new.shape), whole(*down_new.shape)]
+            in_specs=[whole(rows, width)] * (2 * early)
+            + [whole(*s.shape) for s in stats]
+            + [whole(*dense.shape), whole(*dense_rows.shape)]
             + [
-                pl.BlockSpec((experts, own_up, up_w.shape[2]), lambda g, s: (0, s[1], 0)),
+                pl.BlockSpec((experts, own_up, up_columns), lambda g, s: (0, s[1], 0)),
                 pl.BlockSpec((experts, own_down, width), lambda g, s: (0, s[1], 0)),
+                pl.BlockSpec((own_up, qkv_columns), lambda g, s: (s[1], 0)),
+                pl.BlockSpec((own_up, width), lambda g, s: (s[1], 0)),
             ],
             out_specs=[whole(*o.shape) for o in outs],
         ),
         compiler_params=pltpu.CompilerParams(vmem_limit_bytes=VM),
         cost_estimate=lasts(6),
-        name="expert_update",
-    )(jnp.stack([lax.rem(me // PAIR, 2), me]), *stays, *gots, tiles, sums, up_new, down_new, up_w, down_w)
+        name="update",
+    )(
+        jnp.stack([lax.rem(me // PAIR, 2), me]),
+        *owns, *gots, *stats, dense, dense_rows, up_w, down_w, qkv_w, out_w,
+    )
 
 
 D = 1024
@@ -1274,12 +1515,12 @@
     scalars = jnp.stack([first_local, lax.rem(dp_index, 2)])
     experts, chains = [], []
 
-    def advance(j, after, come=None):
+    def advance(j, after, come=None, passed=()):
         masks, stay, go = chains[j]
         come = swap(go, "dp", masks[0]) if come is None else come
-        stay, go = settle(stay, come, masks[1], "%d_%d" % (j, masks[1]), after)
+        stay, go, *passed = settle(stay, come, masks[1], "%d_%d" % (j, masks[1]), after, passed)
         chains[j] = (masks[1:], stay, go)
-        return stay
+        return (stay, *passed) if passed else stay
 
     masks = [1] + [1 << b for b in range(2, dp_count.bit_length() - 1)] + [PAIR]
     for j in range(half_experts):
@@ -1292,54 +1533,80 @@
             )
         )
         chains.append((masks, experts[j][0], experts[j][1]))
-    normed_f_grad, near_mix, far_mix, come = combine_and_return(
-        code, [e[2] for e in experts], [e[3] for e in experts], capacity, chains[0][2], chains[0][0][0], 6
+    mine, theirs = combine(code, [e[2] for e in experts], capacity, [])
+    steps = [advance(1, [mine])]
+    normed_f_grad, near_mix, far_mix, come = return_sums(
+        code, mine, theirs, [e[3] for e in experts], capacity, chains[1][2], chains[1][0][0], 6, steps
     )
     steps = [normed_f_grad]
-    for j in (1, 2, 0):
-        steps.append(advance(j, steps[-1:], come if j == 0 else None))
+    steps.append(advance(0, steps))
+    stay, far_mix = advance(2, steps[-1:], None, [far_mix])
+    steps.append(stay)
+    steps.append(advance(1, steps[-1:], come))
     input_grad, dense = attend_back(
         hidden_in, out_grad, middle, normed_f_grad, normed, qkv, attended, lse, ids, norm_gains, qkv_weight,
         out_weight, steps
     )
-    pair_mix = swap_pair(far_mix)
-    for_chip = settle_mix(near_mix, pair_mix, [input_grad])
-    steps = [for_chip]
-    for j in (3, 1):
-        steps.append(advance(j, steps[-1:]))
-    mix_parts = (near_mix[0], pair_mix[0], swap_chip(for_chip))
+    got_mix = swap_chip(far_mix)
+    steps = [input_grad]
+    steps.append(advance(3, steps[-1:]))
+    for_pair = settle_mix(near_mix, got_mix, steps[-1:])
+    steps.append(for_pair)
+    qkv_columns = qkv_weight.shape[1]
+    fast_tail = dp_count == experts_here and D // dp_count % 64 == 0
+    if fast_tail:
+        dense_own, come = reduce_dense(dense, [(chains[3][2], chains[3][0][0])], 3, steps)
+    else:
+        dense_own = reduce_dense_far(dense)
+    mix_parts = (near_mix[0], got_mix[0], swap_pair(for_pair))
     block_out = middle + sum(part.astype(jnp.float32) for part in mix_parts)
-
-    qkv_columns = qkv_weight.shape[1]
-    if D // dp_count % 64 == 0:
-        dense_own, come = reduce_dense(dense, chains[3][2], chains[3][0][0], 3, steps)
+    if fast_tail:
+        spare = ((0, 0), (0, LANES - experts_here))
+        owns = [chains[j][1][0] for j in (0, 1)]
+        gots = [swap_pair(chains[j][2][0]) for j in (0, 1)]
+        dense_rows = jnp.stack([qkv_rows, out_rows])
+        dense_old = jnp.pad(
+            jnp.concatenate([own_share(dense_rows, 1), own_share(gain_moment, 1)], axis=0).T,
+            ((0, 0), (0, LANES - 4)),
+        )
+        stats = final_stats(
+            owns,
+            gots,
+            [chains[j][1] for j in (2, 3)],
+            [swap(chains[2][2], "dp", chains[2][0][0]), come],
+            dense_own,
+            [jnp.pad(own_share(old, 1).T, spare) for old in (gateup_rows, down_rows)],
+            (gateup_rows, down_rows),
+            (gateup_cols, down_cols),
+            dense_old,
+            jnp.concatenate([qkv_cols, out_cols]).reshape(dp_count, 1, -1),
+            1,
+        )
+        (
+            gate_up_new,
+            down_new,
+            gateup_rows_new,
+            down_rows_new,
+            gateup_cols_new,
+            down_cols_new,
+            qkv_new,
+            out_new,
+            qkv_cols_new,
+            out_cols_new,
+            turned,
+            gains,
+            roots,
+        ) = update(owns, gots, stats, dense_own, dense_rows, gate_up_weight, down_weight, qkv_weight, out_weight)
+        qkv_cols_new, out_cols_new = qkv_cols_new[0], out_cols_new[0]
+        qkv_rows_new, out_rows_new = turned[0], turned[1]
+        gains_update, gain_moment_new = gains[2:4], turned[4:6]
+        update_rms = roots[:5, 0]
     else:
-        dense_own, come = reduce_dense_far(dense), None
-    for j in (2, 3, 0, 1):
-        while len(chains[j][0]) > 1:
-            advance(j, [dense_own], come if j == 3 else None)
-            come = None if j == 3 else come
-    own_parts = [c[1][0] for c in chains]
-    other_parts = [swap_pair(c[2][0]) for c in chains]
-    fused_tail = dp_count == experts_here
-    if fused_tail:
-        spare = ((0, 0), (0, LANES - experts_here))
-        tiles, sums, up_rows_T, down_rows_T = expert_stats(
-            own_parts,
-            other_parts,
-            jnp.pad(own_share(gateup_rows, 1).T, spare),
-            jnp.pad(own_share(down_rows, 1).T, spare),
-            gateup_rows,
-            down_rows,
-            gateup_cols,
-            down_cols,
-            1,
-        )
-        gate_up_new, down_new, gateup_rows_new, down_rows_new, gateup_cols_new, down_cols_new = expert_update(
-            own_parts, other_parts, tiles, sums, up_rows_T, down_rows_T, gate_up_weight, down_weight
-        )
-        expert_squares = jnp.stack([sums[5, 0], sums[7, 0]])
-    else:
+        for j in range(half_experts):
+            while len(chains[j][0]) > 1:
+                advance(j, [dense_own])
+        own_parts = [c[1][0] for c in chains]
+        other_parts = [swap_pair(c[2][0]) for c in chains]
         own = jnp.stack(own_parts).astype(jnp.float32)
         other = jnp.stack(other_parts).astype(jnp.float32)
         parts = jnp.where(pair_bit == 0, jnp.concatenate([own, other]), jnp.concatenate([other, own]))
@@ -1380,62 +1647,62 @@
             jnp.zeros((8, 128), jnp.float32).at[0, :2].set(expert_squares), "expert", 2
         )
         expert_squares = jnp.sum(spread_squares[:, 0, :2], axis=0)
-
-    dense_own = dense_own.astype(jnp.float32)
-    qkv_own = dense_own[:, :qkv_columns]
-    out_own = dense_own[:, qkv_columns : qkv_columns + D]
-    gains_own = dense_own[:, qkv_columns + D : qkv_columns + D + 2].T
-    gain_moment_new = decayed(own_share(gain_moment, 1), gains_own * gains_own + EPS_STAT)
-    gains_step = gains_own * lax.rsqrt(gain_moment_new)
-    qkv_rows_new, qkv_square, qkv_scaled = factored(qkv_own, own_share(qkv_rows, 0))
-    out_rows_new, out_square, out_scaled = factored(out_own, own_share(out_rows, 0))
-    dense_sums = total_over(
-        jnp.concatenate(
-            [
-                qkv_square,
-                qkv_scaled,
-                out_square,
-                out_scaled,
-                jnp.stack(
-                    [jnp.sum(qkv_rows_new), jnp.sum(out_rows_new), jnp.sum(gains_step * gains_step)]
-                ),
-            ]
-        ),
-        "dp",
-        4,
-        [c[1] for c in chains],
-    )
-    qkv_square, qkv_scaled, out_square, out_scaled, rest = jnp.split(
-        dense_sums, [qkv_columns, 2 * qkv_columns, 2 * qkv_columns + D, 2 * qkv_columns + 2 * D]
-    )
-    qkv_row_mean = rest[0] / D
-    out_row_mean = rest[1] / D
-    qkv_cols_new = decayed(qkv_cols, qkv_square / D)
-    out_cols_new = decayed(out_cols, out_square / D)
-    squares = jnp.concatenate(
-        [
-            jnp.stack(
+        dense_own = dense_own.astype(jnp.float32)
+        qkv_own = dense_own[:, :qkv_columns]
+        out_own = dense_own[:, qkv_columns : qkv_columns + D]
+        gains_own = dense_own[:, qkv_columns + D : qkv_columns + D + 2].T
+        gain_moment_new = decayed(own_share(gain_moment, 1), gains_own * gains_own + EPS_STAT)
+        gains_step = gains_own * lax.rsqrt(gain_moment_new)
+        qkv_rows_new, qkv_square, qkv_scaled = factored(qkv_own, own_share(qkv_rows, 0))
+        out_rows_new, out_square, out_scaled = factored(out_own, own_share(out_rows, 0))
+        dense_sums = total_over(
+            jnp.concatenate(
                 [
-                    rest[2],
-                    qkv_row_mean * jnp.sum(qkv_scaled / qkv_cols_new),
-                    out_row_mean * jnp.sum(out_scaled / out_cols_new),
+                    qkv_square,
+                    qkv_scaled,
+                    out_square,
+                    out_scaled,
+                    jnp.stack(
+                        [jnp.sum(qkv_rows_new), jnp.sum(out_rows_new), jnp.sum(gains_step * gains_step)]
+                    ),
                 ]
             ),
-            expert_squares,
-        ]
-    )
-    element_counts = jnp.array(
-        [2 * D, D * qkv_columns, D * D, total_experts * D * 2 * FF, total_experts * FF * D], jnp.float32
-    )
-    update_rms = jnp.sqrt(squares / element_counts)
-    factors = LEARN_RATE / jnp.maximum(1.0, update_rms / CLIP_LEVEL)
-
-    def stepped(weight, part, rows_new, row_mean, cols_new, factor):
-        return weight.astype(jnp.float32) - part * (
-            factor * lax.rsqrt(rows_new / row_mean[..., None])
-        )[..., :, None] * lax.rsqrt(cols_new)[..., None, :]
-
-    if not fused_tail:
+            "dp",
+            4,
+        )
+        qkv_square, qkv_scaled, out_square, out_scaled, rest = jnp.split(
+            dense_sums, [qkv_columns, 2 * qkv_columns, 2 * qkv_columns + D, 2 * qkv_columns + 2 * D]
+        )
+        qkv_row_mean = rest[0] / D
+        out_row_mean = rest[1] / D
+        qkv_cols_new = decayed(qkv_cols, qkv_square / D)
+        out_cols_new = decayed(out_cols, out_square / D)
+        squares = jnp.concatenate(
+            [
+                jnp.stack(
+                    [
+                        rest[2],
+                        qkv_row_mean * jnp.sum(qkv_scaled / qkv_cols_new),
+                        out_row_mean * jnp.sum(out_scaled / out_cols_new),
+                    ]
+                ),
+                expert_squares,
+            ]
+        )
+        element_counts = jnp.array(
+            [2 * D, D * qkv_columns, D * D, total_experts * D * 2 * FF, total_experts * FF * D], jnp.float32
+        )
+        update_rms = jnp.sqrt(squares / element_counts)
+        factors = LEARN_RATE / jnp.maximum(1.0, update_rms / CLIP_LEVEL)
+
+        def stepped(weight, part, rows_new, row_mean, cols_new, factor):
+            return weight.astype(jnp.float32) - part * (
+                factor * lax.rsqrt(rows_new / row_mean[..., None])
+            )[..., :, None] * lax.rsqrt(cols_new)[..., None, :]
+
+        gains_update = -factors[0] * gains_step
+        qkv_new = stepped(own_share(qkv_weight, 0), qkv_own, qkv_rows_new, qkv_row_mean, qkv_cols_new, factors[1])
+        out_new = stepped(own_share(out_weight, 0), out_own, out_rows_new, out_row_mean, out_cols_new, factors[2])
         gate_up_new = stepped(
             own_share(gate_up_weight, 1), gateup_part, gateup_rows_new, gateup_row_mean, gateup_cols_new, factors[3]
         )
@@ -1446,12 +1713,12 @@
         block_out,
         input_grad,
         update_rms,
-        -factors[0] * gains_step,
+        gains_update,
         gain_moment_new,
-        stepped(own_share(qkv_weight, 0), qkv_own, qkv_rows_new, qkv_row_mean, qkv_cols_new, factors[1]),
+        qkv_new,
         qkv_rows_new,
         qkv_cols_new,
-        stepped(own_share(out_weight, 0), out_own, out_rows_new, out_row_mean, out_cols_new, factors[2]),
+        out_new,
         out_rows_new,
         out_cols_new,
         gate_up_new,

time: 454 us -> 404 us (0.89)
  waiting for transfers between devices: 38.7 us -> 0.03 us
  other arithmetic: 19 us -> 9.9 us
  Pallas kernels: 350 us -> 357 us
    ppermute x14 -> x12, waiting for transfers between devices: 38.7 us -> 0.03 us  [swap(): return lax.ppermute(values, axis, [(i, i ^ mask) for i in range(count)])]
    pallas_call x16 -> x14, Pallas kernels: 189 us -> 205 us  [the longest x4 74.6 us: run_expert(): pl.pallas_call(functools.partial(expert_kernel, j, owners, tiles, len(aft...]
    pallas_call x1, Pallas kernels: 68.8 us -> 60.5 us  [reduce_dense(): pl.pallas_call(functools.partial(dense_kernel, orders, spans, len(after),...]
    ppermute x14 -> x12, starting transfers between devices: 18.7 us -> 16.5 us  [swap(): return lax.ppermute(values, axis, [(i, i ^ mask) for i in range(count)])]
  transfers between devices with their start and end apart: 14 -> 12, of which waited for: 4 -> 0; matrix products, arithmetic and copies ran while one was open for 5% -> 3% of each run, Pallas kernels for 64% -> 74%
where the time goes in v5:
time: 404 us; the launch traced here: 399 us
  Pallas kernels  357 us (88%)
  starting transfers between devices  16.5 us (4%)
  local copies, waits for them, and re-layouts  14.5 us (4%)
  other arithmetic  9.9 us (2%)
    pallas_call x4, Pallas kernels, run_expert(): pl.pallas_call(functools.partial(expert_kernel, j, owners, tiles, len(aft...  74.6 us
    pallas_call x1, Pallas kernels, reduce_dense(): pl.pallas_call(functools.partial(dense_kernel, orders, spans, len(after),...  60.5 us
    pallas_call x1, Pallas kernels, return_sums(): pl.pallas_call(functools.partial(return_kernel, capacity, count, far_mask...  52.9 us
    pallas_call x1, Pallas kernels, gather_and_select(): pl.pallas_call(functools.partial(gather_kernel, capacity, experts_here, h...  44.8 us
    pallas_call x1, Pallas kernels, final_stats(): pl.pallas_call(functools.partial(final_stats_kernel, count, groups, len(o...  39.7 us
    pallas_call x1, Pallas kernels, attend_back(): pl.pallas_call(attend_back_kernel, out_shape=(jax.ShapeDtypeStruct((rows,...  26.5 us
    pallas_call x1, Pallas kernels, attend(): pl.pallas_call(attend_kernel, out_shape=(shape((rows, width), jnp.bfloat1...  18 us
    pallas_call x6, Pallas kernels, settle(): pl.pallas_call(functools.partial(settle_kernel, len(after) + len(passed))...  18 us
  transfers between devices with their start and end apart: 12, of which 0 were waited for; matrix products, arithmetic and copies ran while one was open for 3% of the time, Pallas kernels for 74%

profile of v5, /device:TPU:0, one launch (start us, length us, event | category | flops | bytes accessed | tf_op | source)
XLA Modules:
  0.0 399.5 jit_solution(17632502843469833444)
XLA Ops:
  3.8 3.0 collective-permute-start
  9.1 18.0 %attend.1 = (bf16[384,1024]{1,0:T(8,128)(2,1)}, bf16[384,2048]{1,0:T(8,128)(2,1)}, bf16[384,1024]{1,0:T(8,128)(2,1)}, f32[384,128]{1,0:T(8,128)}, f32[384,1024]{1,0:T(8,128)}, /*index=5*/bf16[384,1024]{1,0:T(8,128)(2,1)}) custom-call(f32[384,1024]{1,0:T(8,128)} %hidden_ref.3, s32[3,384]{1,0:T(4,128)} %pad_add_fusion.ids_ref, bf16[2,1024]{1,0:T(2,128)(2,1)} %gains_ref.3, ...), custom_call_target="tpu_custom_call" | custom-call | flops 18000000 | bytes 1024 | tf_op jit(solution)/shard_map/attend/pallas_call | solution.py:263
  28.9 44.8 %gather_and_select.1 = (bf16[4,8,144,1024]{3,2,1,0:T(8,128)(2,1)}, bf16[4,8,144,1024]{3,2,1,0:T(8,128)(2,1)}, f32[4,8,144,1]{3,2,1,0:T(8,128)}, f32[8,4,384]{2,1,0:T(4,128)}) custom-call(bf16[384,1024]{1,0:T(8,128)(2,1)} %get-tuple-element.87.token_ref, bf16[416,1024]{1,0:T(8,128)(2,1)} %copy-done.3, bf16[416,1024]{1,0:T(8,128)(2,1)} %copy-done.8, ...), custom_call_target="tpu_custom_call" | custom-call | flops 44000000 | bytes 1024 | tf_op jit(solution)/shard_map/gather_and_select/pallas_call | solution.py:786
  73.6 18.6 %expert_0.1 = (bf16[4,192,1024]{2,1,0:T(8,128)(2,1)}, bf16[4,192,1024]{2,1,0:T(8,128)(2,1)}, bf16[1152,1024]{1,0:T(8,128)(2,1)}, bf16[1152,1024]{1,0:T(8,128)(2,1)}) custom-call(s32[2]{0:T(128)} %pad_add_fusion.1.s_ref, bf16[4,8,144,1024]{3,2,1,0:T(8,128)(2,1)} %get-tuple-element.89.rec_hbm, bf16[4,8,144,1024]{3,2,1,0:T(8,128)(2,1)} %get-tuple-element.90.arr_hbm, ...), custom_call_target="tpu_custom_call" | custom-call | flops 18000000 | bytes 1024 | tf_op jit(solution)/shard_map/expert_0/pallas_call | solution.py:121
  93.7 18.6 %expert_1.1 = (bf16[4,192,1024]{2,1,0:T(8,128)(2,1)}, bf16[4,192,1024]{2,1,0:T(8,128)(2,1)}, bf16[1152,1024]{1,0:T(8,128)(2,1)}, bf16[1152,1024]{1,0:T(8,128)(2,1)}) custom-call(s32[2]{0:T(128)} %pad_add_fusion.1.s_ref, bf16[4,8,144,1024]{3,2,1,0:T(8,128)(2,1)} %get-tuple-element.89.rec_hbm, bf16[4,8,144,1024]{3,2,1,0:T(8,128)(2,1)} %get-tuple-element.90.arr_hbm, ...), custom_call_target="tpu_custom_call" | custom-call | flops 18000000 | bytes 1024 | tf_op jit(solution)/shard_map/expert_1/pallas_call | solution.py:121
  113.0 18.9 %expert_2.1 = (bf16[4,192,1024]{2,1,0:T(8,128)(2,1)}, bf16[4,192,1024]{2,1,0:T(8,128)(2,1)}, bf16[1152,1024]{1,0:T(8,128)(2,1)}, bf16[1152,1024]{1,0:T(8,128)(2,1)}) custom-call(s32[2]{0:T(128)} %pad_add_fusion.1.s_ref, bf16[4,8,144,1024]{3,2,1,0:T(8,128)(2,1)} %get-tuple-element.89.rec_hbm, bf16[4,8,144,1024]{3,2,1,0:T(8,128)(2,1)} %get-tuple-element.90.arr_hbm, ...), custom_call_target="tpu_custom_call" | custom-call | flops 18000000 | bytes 1024 | tf_op jit(solution)/shard_map/expert_2/pallas_call | solution.py:121
  133.5 3.3 settle_0_4.1
  136.8 2.6 collective-permute-start.5
  139.4 18.5 %expert_3.1 = (bf16[4,192,1024]{2,1,0:T(8,128)(2,1)}, bf16[4,192,1024]{2,1,0:T(8,128)(2,1)}, bf16[1152,1024]{1,0:T(8,128)(2,1)}, bf16[1152,1024]{1,0:T(8,128)(2,1)}) custom-call(s32[2]{0:T(128)} %pad_add_fusion.1.s_ref, bf16[4,8,144,1024]{3,2,1,0:T(8,128)(2,1)} %get-tuple-element.89.rec_hbm, bf16[4,8,144,1024]{3,2,1,0:T(8,128)(2,1)} %get-tuple-element.90.arr_hbm, ...), custom_call_target="tpu_custom_call" | custom-call | flops 18000000 | bytes 1024 | tf_op jit(solution)/shard_map/expert_3/pallas_call | solution.py:121
  158.5 10.6 %combine.1 = (bf16[4,384,1024]{2,1,0:T(8,128)(2,1)}, bf16[4,384,1024]{2,1,0:T(8,128)(2,1)}) custom-call(f32[8,4,384]{2,1,0:T(4,128)} %get-tuple-element.88.code_ref, bf16[1152,1024]{1,0:T(8,128)(2,1)} %get-tuple-element.92.refs_0_, bf16[1152,1024]{1,0:T(8,128)(2,1)} %get-tuple-element.93.refs_0_.refs_1_, ...), custom_call_target="tpu_custom_call" | custom-call | flops 12000000 | bytes 1024 | tf_op jit(solution)/shard_map/combine/pallas_call | solution.py:864
  170.2 3.3 settle_1_4.1
  173.5 52.9 %return_sums.1 = (f32[384,1024]{1,0:T(8,128)}, bf16[2,384,1024]{2,1,0:T(8,128)(2,1)}, bf16[2,384,1024]{2,1,0:T(8,128)(2,1)}, bf16[2,192,1024]{2,1,0:T(8,128)(2,1)}) custom-call(f32[8,4,384]{2,1,0:T(4,128)} %get-tuple-element.88.code_ref, bf16[4,384,1024]{2,1,0:T(8,128)(2,1)} %get-tuple-element.99.refs_0_.mine_ref, ...), custom_call_target="tpu_custom_call" | custom-call | flops 37000000 | bytes 1024 | tf_op jit(solution)/shard_map/return_sums/pallas_call | solution.py:944
  226.4 2.4 settle_0_2.1
  229.9 3.3 settle_2_4.1
  236.2 2.1 collective-permute-start.9
  238.4 2.4 settle_1_2.1
  240.7 26.5 %attend_back.1 = (f32[384,1024]{1,0:T(8,128)}, bf16[1024,3200]{1,0:T(8,128)(2,1)}) custom-call(f32[384,1024]{1,0:T(8,128)} %hidden_ref.3, f32[384,1024]{1,0:T(8,128)} %grad_ref.1, f32[384,1024]{1,0:T(8,128)} %get-tuple-element.86.middle_ref, f32[384,1024]{1,0:T(8,128)} %get-tuple-element.113.refs_0_.normed_grad_ref, ...), custom_call_target="tpu_custom_call" | custom-call | flops 26000000 | bytes 1024 | tf_op jit(solution)/shard_map/attend_back/pallas_call | solution.py:371
  267.3 3.3 settle_3_4.1
  271.8 3.0 settle_mix.1.refs_3_
  274.7 2.0 collective-permute-start.8
  280.8 60.5 %reduce_dense.1 = (bf16[2,2,32,3200]{3,2,1,0:T(8,128)(2,1)}, bf16[2,192,1024]{2,1,0:T(8,128)(2,1)}) custom-call(bf16[2,2,2,2,2,32,3200]{6,5,4,3,2,1,0:T(8,128)(2,1)} %bitcast.58, bf16[2,192,1024]{2,1,0:T(8,128)(2,1)} %bitcast.80, f32[384,1024]{1,0:T(8,128)} %get-tuple-element.70.refs_0_.refs_1_, bf16[2,192,1024]{2,1,0:T(8,128)(2,1)} %bitcast.56, ...), custom_call_target="tpu_custom_call" | custom-call | flops 50000000 | bytes 1024 | tf_op jit(solution)/shard_map/reduce_dense/pallas_call | solution.py:617
  342.4 39.7 %final_stats.1 = (bf16[4,192,1024]{2,1,0:T(8,128)(2,1)}, f32[8,8,512]{2,1,0:T(8,128)}, f32[8,128]{1,0:T(8,128)}, f32[128,128]{1,0:T(8,128)}, f32[128,128]{1,0:T(...) custom-call(bf16[192,1024]{1,0:T(8,128)(2,1)} %bitcast.61, bf16[192,1024]{1,0:T(8,128)(2,1)} %bitcast.64, ...), custom_call_target="tpu_custom_call" | custom-call | flops 15000000 | bytes 1024 | tf_op jit(solution)/shard_map/final_stats/pallas_call | solution.py:1216
  382.1 9.0 %update.1 = (f32[8,128,1024]{2,1,0:T(8,128)}, f32[8,64,1024]{2,1,0:T(8,128)}, f32[8,128]{1,0:T(8,128)}, f32[8,64]{1,0:T(8,128)}, f32[8,1024]{1,0:T(8,128)}, /*in...) custom-call(s32[2]{0:T(128)} %pad_add_fusion.2.s_ref, ...), custom_call_target="tpu_custom_call" | custom-call | flops 6000000 | bytes 1024 | tf_op jit(solution)/shard_map/update/pallas_call | solution.py:1368
  396.2 3.0 fusion.1
  (83 shorter events, 28.0 us)
Async XLA Ops:
  2.2 6.3 %copy-start.15 = (s32[384]{0:T(512)S(1)}, s32[384]{0:T(512)}, u32[]{:S(2)}) copy-start(s32[384]{0:T(512)} %param.25) | copy-start | bytes 4612
  2.2 6.3 %copy-start.16 = (s32[384]{0:T(512)S(1)}, s32[384]{0:T(512)}, u32[]{:S(2)}) copy-start(s32[384]{0:T(512)} %param.24) | copy-start | bytes 4612
  2.2 6.3 %copy-start.17 = (s32[384]{0:T(512)S(1)}, s32[384]{0:T(512)}, u32[]{:S(2)}) copy-start(s32[384]{0:T(512)} %param.23) | copy-start | bytes 4612
  3.8 23.3 %copy-start.3 = (bf16[416,1024]{1,0:T(8,128)(2,1)}, bf16[416,1024]{1,0:T(8,128)(2,1)S(1)}, u32[]{:S(2)}) copy-start(bf16[416,1024]{1,0:T(8,128)(2,1)S(1)} %fusion.2.grad_ref) | copy-start | bytes 2555908
  3.8 23.8 %collective-permute-start = (bf16[416,1024]{1,0:T(8,128)(2,1)S(1)}, bf16[416,1024]{1,0:T(8,128)(2,1)S(1)}, u32[]{:S(2)}, u32[]{:S(2)}) collective-permute-start(bf16[416,1024]{1,0:T(8,128)(2,1)S(1)} %fusion.2.grad_ref), channel_id=1, source_target_pairs={{0,2},{1,3},{2,0},{3,1},{4,6},{5,7},{6,4},{7,5},{8,10},{9,11},{10,... | collective-permute-start | bytes 2555912 | tf_op jit(solution)/shard_map/ppermute | solution.py:1401
  6.9 20.8 %collective-permute-start.1 = (bf16[416,1024]{1,0:T(8,128)(2,1)S(1)}, bf16[416,1024]{1,0:T(8,128)(2,1)S(1)}, u32[]{:S(2)}, u32[]{:S(2)}) collective-permute-start(bf16[416,1024]{1,0:T(8,128)(2,1)S(1)} %fusion.2.grad_ref), channel_id=1, source_target_pairs={{0,8},{4,12},{8,0},{12,4},{16,24},{20,28},{24,16},{28,20},{1,9},{5... | collective-permute-start | bytes 2555912 | tf_op jit(solution)/shard_map/ppermute | solution.py:1401
  27.7 1.2 copy-start.9
  92.2 41.3 %collective-permute-start.2 = (bf16[4,192,1024]{2,1,0:T(8,128)(2,1)}, bf16[4,192,1024]{2,1,0:T(8,128)(2,1)}, u32[]{:S(2)}, u32[]{:S(2)}) collective-permute-start(bf16[4,192,1024]{2,1,0:T(8,128)(2,1)} %get-tuple-element.96), channel_id=1, source_target_pairs={{0,4},{4,0},{8,12},{12,8},{16,20},{20,16},{24,28},{28,24},{1,5},{5... | collective-permute-start | bytes 4718600 | tf_op jit(solution)/shard_map/ppermute | solution.py:1401
  112.4 56.7 %collective-permute-start.3 = (bf16[4,192,1024]{2,1,0:T(8,128)(2,1)}, bf16[4,192,1024]{2,1,0:T(8,128)(2,1)S(1)}, u32[]{:S(2)}, u32[]{:S(2)}) collective-permute-start(bf16[4,192,1024]{2,1,0:T(8,128)(2,1)} %get-tuple-element.102), channel_id=1, source_target_pairs={{0,4},{4,0},{8,12},{12,8},{16,20},{20,16},{24,28},{28,24},{1,5},{5... | collective-permute-start | bytes 4718600 | tf_op jit(solution)/shard_map/ppermute | solution.py:1401
  131.9 96.8 %collective-permute-start.4 = (bf16[4,192,1024]{2,1,0:T(8,128)(2,1)}, bf16[4,192,1024]{2,1,0:T(8,128)(2,1)S(1)}, u32[]{:S(2)}, u32[]{:S(2)}) collective-permute-start(bf16[4,192,1024]{2,1,0:T(8,128)(2,1)} %get-tuple-element.111), channel_id=1, source_target_pairs={{0,4},{4,0},{8,12},{12,8},{16,20},{20,16},{24,28},{28,24},{1,5},{5... | collective-permute-start | bytes 4718600 | tf_op jit(solution)/shard_map/ppermute | solution.py:1401
  136.8 89.6 %collective-permute-start.5 = (bf16[2,192,1024]{2,1,0:T(8,128)(2,1)}, bf16[2,192,1024]{2,1,0:T(8,128)(2,1)}, u32[]{:S(2)}, u32[]{:S(2)}) collective-permute-start(bf16[2,192,1024]{2,1,0:T(8,128)(2,1)} %bitcast.89), channel_id=1, source_target_pairs={{0,16},{4,20},{8,24},{12,28},{16,0},{20,4},{24,8},{28,12},{1,17},{... | collective-permute-start | bytes 2359304 | tf_op jit(solution)/shard_map/ppermute | solution.py:1401
  157.9 109.4 %collective-permute-start.7 = (bf16[4,192,1024]{2,1,0:T(8,128)(2,1)}, bf16[4,192,1024]{2,1,0:T(8,128)(2,1)}, u32[]{:S(2)}, u32[]{:S(2)}) collective-permute-start(bf16[4,192,1024]{2,1,0:T(8,128)(2,1)} %get-tuple-element.118), channel_id=1, source_target_pairs={{0,4},{4,0},{8,12},{12,8},{16,20},{20,16},{24,28},{28,24},{1,5},{5... | collective-permute-start | bytes 4718600 | tf_op jit(solution)/shard_map/ppermute | solution.py:1401
  229.9 4.1 %copy-start.11 = (f32[1024]{0:T(1024)S(1)}, f32[1024]{0:T(1024)}, u32[]{:S(2)}) copy-start(f32[1024]{0:T(1024)} %param.36) | copy-start | bytes 12292
  229.9 4.1 %copy-start.12 = (f32[1024]{0:T(1024)S(1)}, f32[1024]{0:T(1024)}, u32[]{:S(2)}) copy-start(f32[1024]{0:T(1024)} %param.34) | copy-start | bytes 12292
  233.2 37.4 %collective-permute-start.6 = (bf16[2,384,1024]{2,1,0:T(8,128)(2,1)}, bf16[2,384,1024]{2,1,0:T(8,128)(2,1)S(1)}, u32[]{:S(2)}, u32[]{:S(2)}) collective-permute-start(bf16[2,384,1024]{2,1,0:T(8,128)(2,1)} %get-tuple-element.116), channel_id=1, source_target_pairs={{0,2},{1,3},{2,0},{3,1},{4,6},{5,7},{6,4},{7,5},{8,10},{9,11},{10,... | collective-permute-start | bytes 4718600 | tf_op jit(solution)/shard_map/ppermute | solution.py:1401
  233.2 108.0 %collective-permute-start.11 = (bf16[2,192,1024]{2,1,0:T(8,128)(2,1)}, bf16[2,192,1024]{2,1,0:T(8,128)(2,1)S(1)}, u32[]{:S(2)}, u32[]{:S(2)}) collective-permute-start(bf16[2,192,1024]{2,1,0:T(8,128)(2,1)} %bitcast.88), channel_id=1, source_target_pairs={{0,16},{4,20},{8,24},{12,28},{16,0},{20,4},{24,8},{28,12},{1,17},{... | collective-permute-start | bytes 2359304 | tf_op jit(solution)/shard_map/ppermute | solution.py:1401
  236.2 105.0 %collective-permute-start.9 = (bf16[192,1024]{1,0:T(8,128)(2,1)}, bf16[192,1024]{1,0:T(8,128)(2,1)S(1)}, u32[]{:S(2)}, u32[]{:S(2)}) collective-permute-start(bf16[192,1024]{1,0:T(8,128)(2,1)} %bitcast.29), channel_id=1, source_target_pairs={{0,8},{4,12},{8,0},{12,4},{16,24},{20,28},{24,16},{28,20},{1,9},{5... | collective-permute-start | bytes 1179656 | tf_op jit(solution)/shard_map/ppermute | solution.py:1401
  240.7 100.5 %collective-permute-start.10 = (bf16[192,1024]{1,0:T(8,128)(2,1)}, bf16[192,1024]{1,0:T(8,128)(2,1)S(1)}, u32[]{:S(2)}, u32[]{:S(2)}) collective-permute-start(bf16[192,1024]{1,0:T(8,128)(2,1)} %bitcast.90), channel_id=1, source_target_pairs={{0,8},{4,12},{8,0},{12,4},{16,24},{20,28},{24,16},{28,20},{1,9},{5... | collective-permute-start | bytes 1179656 | tf_op jit(solution)/shard_map/ppermute | solution.py:1401
  270.6 1.2 copy-start.2
  271.8 8.4 %copy-start.13 = (f32[2048]{0:T(1024)S(1)}, f32[2048]{0:T(1024)}, u32[]{:S(2)}) copy-start(f32[2048]{0:T(1024)} %param.35) | copy-start | bytes 24580
  271.8 8.4 %copy-start.14 = (f32[1024]{0:T(1024)S(1)}, f32[1024]{0:T(1024)}, u32[]{:S(2)}) copy-start(f32[1024]{0:T(1024)} %param.37) | copy-start | bytes 12292
  274.7 121.4 %collective-permute-start.8 = (bf16[384,1024]{1,0:T(8,128)(2,1)}, bf16[384,1024]{1,0:T(8,128)(2,1)}, u32[]{:S(2)}, u32[]{:S(2)}) collective-permute-start(bf16[384,1024]{1,0:T(8,128)(2,1)} %settle_mix.1.refs_3_), channel_id=1, source_target_pairs={{0,8},{4,12},{8,0},{12,4},{16,24},{20,28},{24,16},{28,20},{1,9},{5... | collective-permute-start | bytes 2359304 | tf_op jit(solution)/shard_map/ppermute | solution.py:1401
  382.1 14.1 %copy-start = (f32[384,1024]{1,0:T(8,128)S(1)}, f32[384,1024]{1,0:T(8,128)}, u32[]{:S(2)}) copy-start(f32[384,1024]{1,0:T(8,128)} %get-tuple-element.86.middle_ref) | copy-start | bytes 4718596
  382.1 14.1 %copy-start.1 = (bf16[2,384,1024]{2,1,0:T(8,128)(2,1)S(1)}, bf16[2,384,1024]{2,1,0:T(8,128)(2,1)}, u32[]{:S(2)}) copy-start(bf16[2,384,1024]{2,1,0:T(8,128)(2,1)} %get-tuple-element.109.near_ref) | copy-start | bytes 4718596
  (6 other events, 5.9 us)

commit v6 on v5

--- a/solution.py
+++ b/solution.py
@@ -207,8 +207,23 @@
     return pl.ds(pl.multiple_of(index * LANES, LANES), LANES)
 
 
-def attend_kernel(hidden_ref, ids_ref, gains_ref, qkv_w_ref, out_w_ref,
-                  normed_ref, qkv_ref, attended_ref, lse_ref, middle_ref, normed_f_ref, proj_s, bias_s):
+def attend_kernel(hidden_ref, ids_ref, gains_ref, qkv_w_hbm, out_w_hbm,
+                  normed_hbm, qkv_hbm, attended_hbm, lse_ref, middle_ref, normed_f_ref,
+                  normed_ref, qkv_ref, attended_ref, qkv_w_ref, out_w_ref, proj_s, bias_s, sem):
+    moving = [
+        pltpu.make_async_copy(src, dst, sem.at[i])
+        for i, (src, dst) in enumerate(
+            (
+                (qkv_w_hbm, qkv_w_ref),
+                (out_w_hbm, out_w_ref),
+                (normed_ref, normed_hbm),
+                (qkv_ref, qkv_hbm),
+                (attended_ref, attended_hbm),
+            )
+        )
+    ]
+    moving[0].start()
+    moving[1].start()
     rows = hidden_ref.shape[0]
     att = HEADS * HEAD_DIM
     kv = KV_HEADS * HEAD_DIM
@@ -216,9 +231,11 @@
     gains = gains_ref[...].astype(jnp.float32)
     inverse = lax.rsqrt(jnp.mean(hidden * hidden, axis=-1, keepdims=True) + EPS_NORM)
     normed_ref[...] = (hidden * inverse * gains[0:1, :]).astype(jnp.bfloat16)
-    proj_s[...] = dot(normed_ref[...], qkv_w_ref[...])
+    moving[2].start()
     bias, cosine, sine, front, lane = mask_and_angles(ids_ref)
     bias_s[...] = bias
+    moving[0].wait()
+    proj_s[...] = dot(normed_ref[...], qkv_w_ref[...])
     lse_ref[...] = jnp.zeros_like(lse_ref)
 
     def pair_step(p, carry):
@@ -251,10 +268,15 @@
         return carry
 
     lax.fori_loop(0, KV_HEADS // 2, pair_step, 0)
+    moving[3].start()
+    moving[4].start()
+    moving[1].wait()
     middle = hidden + dot(attended_ref[...], out_w_ref[...])
     middle_ref[...] = middle
     inverse_f = lax.rsqrt(jnp.mean(middle * middle, axis=-1, keepdims=True) + EPS_NORM)
     normed_f_ref[...] = (middle * inverse_f * gains[1:2, :]).astype(jnp.bfloat16)
+    for copy in moving[2:]:
+        copy.wait()
 
 
 def attend(hidden, ids, gains, qkv_w, out_w):
@@ -270,11 +292,17 @@
             shape((rows, width), jnp.float32),
             shape((rows, width), jnp.bfloat16),
         ),
-        in_specs=[pl.BlockSpec(memory_space=pltpu.VMEM)] * 5,
-        out_specs=[pl.BlockSpec(memory_space=pltpu.VMEM)] * 6,
+        in_specs=[pl.BlockSpec(memory_space=pltpu.VMEM)] * 3 + [pl.BlockSpec(memory_space=pl.ANY)] * 2,
+        out_specs=[pl.BlockSpec(memory_space=pl.ANY)] * 3 + [pl.BlockSpec(memory_space=pltpu.VMEM)] * 3,
         scratch_shapes=[
+            pltpu.VMEM((rows, width), jnp.bfloat16),
+            pltpu.VMEM((rows, qkv_w.shape[1]), jnp.bfloat16),
+            pltpu.VMEM((rows, out_w.shape[0]), jnp.bfloat16),
+            pltpu.VMEM(qkv_w.shape, jnp.bfloat16),
+            pltpu.VMEM(out_w.shape, jnp.bfloat16),
             pltpu.VMEM((rows, qkv_w.shape[1]), jnp.float32),
             pltpu.VMEM((rows, rows), jnp.float32),
+            pltpu.SemaphoreType.DMA((5,)),
         ],
         compiler_params=pltpu.CompilerParams(vmem_limit_bytes=VM),
         cost_estimate=lasts(18),
@@ -282,10 +310,33 @@
     )(hidden, ids, gains, qkv_w, out_w)
 
 
-def attend_back_kernel(hidden_ref, grad_ref, middle_ref, normed_grad_ref, normed_ref, qkv_ref, attended_ref, lse_ref,
-                       ids_ref, gains_ref, qkv_w_ref, out_w_ref, *refs):
-    input_grad_ref, dense_ref, proj_s, bias_s, back_s = refs[-5:]
+def attend_back_kernel(waits, grad_ref, middle_ref, normed_grad_ref, lse_ref, ids_ref, gains_ref,
+                       hidden_hbm, normed_hbm, qkv_hbm, attended_hbm, qkv_w_hbm, out_w_hbm, *refs):
+    (input_grad_ref, dense_hbm, dense_ref, hidden_ref, normed_ref, qkv_ref, attended_ref, qkv_w_ref, out_w_ref,
+     proj_s, bias_s, back_s, sem) = refs[waits:]
     rows, width = hidden_ref.shape
+    incoming = {
+        name: pltpu.make_async_copy(src, dst, sem.at[i])
+        for i, (name, src, dst) in enumerate(
+            (
+                ("attended", attended_hbm, attended_ref),
+                ("out_w", out_w_hbm, out_w_ref),
+                ("qkv", qkv_hbm, qkv_ref),
+                ("normed", normed_hbm, normed_ref),
+                ("qkv_w", qkv_w_hbm, qkv_w_ref),
+                ("hidden", hidden_hbm, hidden_ref),
+            )
+        )
+    }
+    for copy in incoming.values():
+        copy.start()
+    leaving = []
+
+    def leave(span):
+        copy = pltpu.make_async_copy(dense_ref.at[:, span], dense_hbm.at[:, span], sem.at[6 + len(leaving)])
+        copy.start()
+        leaving.append(copy)
+
     att = HEADS * HEAD_DIM
     kv = KV_HEADS * HEAD_DIM
     gains = gains_ref[...].astype(jnp.float32)
@@ -302,11 +353,15 @@
     input_grad_ref[...] = middle_grad
     branch = middle_grad.astype(jnp.bfloat16)
     columns = att + 2 * kv
+    incoming["attended"].wait()
     dense_ref[:, columns : columns + width] = dot(attended_ref[...], branch, 0, 0).astype(jnp.bfloat16)
+    leave(slice(columns, columns + width))
+    incoming["out_w"].wait()
     back_s[...] = dot(branch, out_w_ref[...], 1, 1).astype(jnp.bfloat16)
     bias, cosine, sine, front, lane = mask_and_angles(ids_ref)
     bias_s[...] = bias
     low = lane < HEAD_DIM
+    incoming["qkv"].wait()
 
     def pair_step(p, carry):
         key_at = column_block(att // LANES + p)
@@ -352,7 +407,12 @@
         return carry
 
     lax.fori_loop(0, KV_HEADS // 2, pair_step, 0)
-    dense_ref[:, :columns] = dot(normed_ref[...], proj_s[...], 0, 0).astype(jnp.bfloat16)
+    for name in ("normed", "qkv_w", "hidden"):
+        incoming[name].wait()
+    for first in range(0, columns, columns // 2):
+        span = slice(first, first + columns // 2)
+        dense_ref[:, span] = dot(normed_ref[...], proj_s[:, span], 0, 0).astype(jnp.bfloat16)
+        leave(span)
     normed_grad = dot(proj_s[...], qkv_w_ref[...], 1, 1)
     hidden = hidden_ref[...]
     inverse = lax.rsqrt(jnp.mean(hidden * hidden, axis=-1, keepdims=True) + EPS_NORM)
@@ -363,29 +423,40 @@
     )
     both = jnp.concatenate([gain_a, gain_f, jnp.zeros((LANES - 2, width), jnp.float32)], axis=0)
     dense_ref[:, columns + width :] = both.T.astype(jnp.bfloat16)
+    leave(slice(columns + width, columns + width + LANES))
+    for copy in leaving:
+        copy.wait()
 
 
 def attend_back(hidden, out_grad, middle, normed_f_grad, normed, qkv, attended, lse, ids, gains, qkv_w, out_w, after=()):
     rows, width = hidden.shape
     columns = qkv_w.shape[1] + width + LANES
     return pl.pallas_call(
-        attend_back_kernel,
+        functools.partial(attend_back_kernel, len(after)),
         out_shape=(
             jax.ShapeDtypeStruct((rows, width), jnp.float32),
             jax.ShapeDtypeStruct((width, columns), jnp.bfloat16),
         ),
-        in_specs=[pl.BlockSpec(memory_space=pltpu.VMEM)] * 12
-        + [pl.BlockSpec(memory_space=pl.ANY)] * len(after),
-        out_specs=[pl.BlockSpec(memory_space=pltpu.VMEM)] * 2,
+        in_specs=[pl.BlockSpec(memory_space=pltpu.VMEM)] * 6
+        + [pl.BlockSpec(memory_space=pl.ANY)] * (6 + len(after)),
+        out_specs=[pl.BlockSpec(memory_space=pltpu.VMEM), pl.BlockSpec(memory_space=pl.ANY)],
         scratch_shapes=[
+            pltpu.VMEM((width, columns), jnp.bfloat16),
+            pltpu.VMEM((rows, width), jnp.float32),
+            pltpu.VMEM((rows, width), jnp.bfloat16),
+            pltpu.VMEM((rows, qkv_w.shape[1]), jnp.bfloat16),
+            pltpu.VMEM((rows, out_w.shape[0]), jnp.bfloat16),
+            pltpu.VMEM(qkv_w.shape, jnp.bfloat16),
+            pltpu.VMEM(out_w.shape, jnp.bfloat16),
             pltpu.VMEM((rows, qkv_w.shape[1]), jnp.bfloat16),
             pltpu.VMEM((rows, rows), jnp.float32),
             pltpu.VMEM((rows, out_w.shape[0]), jnp.bfloat16),
+            pltpu.SemaphoreType.DMA((10,)),
         ],
         compiler_params=pltpu.CompilerParams(vmem_limit_bytes=VM),
         cost_estimate=lasts(26),
         name="attend_back",
-    )(hidden, out_grad, middle, normed_f_grad, normed, qkv, attended, lse, ids, gains, qkv_w, out_w, *after)
+    )(out_grad, middle, normed_f_grad, lse, ids, gains, hidden, normed, qkv, attended, qkv_w, out_w, *after)
 
 
 MESH = pl.DeviceIdType.MESH
@@ -509,133 +580,6 @@
     index = lax.axis_index(axis)
     bit = lax.rem(index // mask, 2)
     return bit, {axis: index + mask - 2 * mask * bit}
-
-
-def dense_kernel(orders, spans, waits, carried, mine_ref, *refs):
-    steps = len(orders[0])
-    extra = len(carried)
-    go_refs, out_ref, come_refs = refs[:extra], refs[extra + waits], refs[extra + waits + 1 : 2 * extra + waits + 1]
-    sum_ref, scratch = refs[2 * extra + waits + 1], refs[2 * extra + waits + 2 :]
-    first_got = scratch[0]
-    got = scratch[1 : 1 + steps]
-    send_sem, recv_sem = scratch[1 + steps :]
-    bits = len(mine_ref.shape) - 4
-    core, core_peer = flipped("expert", 1)
-    chip, chip_peer = flipped("expert", 2)
-    links = [flipped("dp", 1 << b) for b in range(bits)] + [(chip, chip_peer)]
-    greet([core_peer] + [peer for _, peer in links])
-    whole = (slice(None),) * bits
-    copies = []
-
-    def send(src, dst, peer, part, step):
-        copy = pltpu.make_async_remote_copy(
-            src_ref=src,
-            dst_ref=dst,
-            send_sem=send_sem.at[part, step],
-            recv_sem=recv_sem.at[part, step],
-            device_id=peer,
-            device_id_type=MESH,
-        )
-        copy.start()
-        copies.append(copy)
-        return copy
-
-    def add(first, second):
-        return (first.astype(jnp.float32) + second.astype(jnp.float32)).astype(jnp.bfloat16)
-
-    flying = []
-    beside = [
-        send(go, come, links[bit][1], i, 3 + steps)
-        for i, (bit, go, come) in enumerate(zip(carried, go_refs, come_refs))
-    ]
-    for part, span in enumerate(spans):
-        at = whole + (1 - core, slice(None), slice(None), span)
-        flying.append(send(mine_ref.at[at], first_got.at[..., span], core_peer, part, 0))
-
-    def place(chosen, span):
-        return tuple(chosen.get(bits - 1 - i, slice(None)) for i in range(bits)) + (
-            chosen.get(bits, slice(None)),
-            slice(None),
-            span,
-        )
-
-    chosen = [{} for _ in spans]
-    for step in range(steps + 1):
-        for part, span in enumerate(spans):
-            flying[part].wait_recv()
-            if step == 0:
-                sum_ref[..., span] = add(
-                    mine_ref[whole + (core, slice(None), slice(None), span)], first_got[..., span]
-                )
-            else:
-                here = place(chosen[part], span)
-                sum_ref[here] = add(sum_ref[here], got[step - 1][part_index(orders, part, step - 1) + (slice(None), span)])
-            if step < steps:
-                link = orders[part][step]
-                bit, peer = links[link]
-                away = place({**chosen[part], link: 1 - bit}, span)
-                flying[part] = send(
-                    sum_ref.at[away],
-                    got[step].at[part_index(orders, part, step) + (slice(None), span)],
-                    peer,
-                    part,
-                    1 + step,
-                )
-                chosen[part] = {**chosen[part], link: bit}
-            else:
-                out_ref[core, chip, :, span] = sum_ref[place(chosen[part], span)]
-                mine = out_ref.at[core, chip, :, span]
-                flying[part] = send(mine, mine, chip_peer, part, 1 + steps)
-    for part, span in enumerate(spans):
-        flying[part].wait_recv()
-        mine = out_ref.at[core, :, :, span]
-        flying[part] = send(mine, mine, core_peer, part, 2 + steps)
-    for copy in flying + beside:
-        copy.wait_recv()
-    for copy in copies:
-        copy.wait_send()
-
-
-def part_index(orders, part, step):
-    return (slice(None),) * (len(orders[part]) - 1 - step)
-
-
-def reduce_dense(dense, carried, label, after=()):
-    owners = lax.axis_size("dp")
-    width, columns = dense.shape
-    bits = owners.bit_length() - 1
-    rows = width // owners // 4
-    tiles = columns // 128
-    parts = 6
-    bounds = [128 * (tiles * i // parts) for i in range(parts + 1)]
-    spans = [slice(a, b) for a, b in zip(bounds[:-1], bounds[1:])]
-    last = tuple(range(1, bits))
-    orders = [((bits, 0) if part % 2 == 0 else (0, bits)) + last for part in range(parts)]
-    shape = (2,) * bits + (2, 2, rows, columns)
-    half = (2,) * bits + (2, rows, columns)
-    goes = [go for go, _ in carried]
-    out, *comes = pl.pallas_call(
-        functools.partial(
-            dense_kernel, orders, spans, len(after), [mask.bit_length() - 1 for _, mask in carried]
-        ),
-        out_shape=[jax.ShapeDtypeStruct((2, 2, rows, columns), jnp.bfloat16)]
-        + [jax.ShapeDtypeStruct(go.shape, jnp.bfloat16) for go in goes],
-        in_specs=[pl.BlockSpec(memory_space=pltpu.VMEM)]
-        + [pl.BlockSpec(memory_space=pl.ANY)] * (len(goes) + len(after)),
-        out_specs=[pl.BlockSpec(memory_space=pltpu.VMEM)] + [pl.BlockSpec(memory_space=pl.ANY)] * len(goes),
-        scratch_shapes=[pltpu.VMEM(half, jnp.bfloat16), pltpu.VMEM(half, jnp.bfloat16)]
-        + [
-            pltpu.VMEM((2,) * (bits - step) + (rows, columns), jnp.bfloat16)
-            for step in range(bits + 1)
-        ]
-        + [pltpu.SemaphoreType.DMA((parts, bits + 5)), pltpu.SemaphoreType.DMA((parts, bits + 5))],
-        compiler_params=pltpu.CompilerParams(
-            collective_id=label, has_side_effects=True, vmem_limit_bytes=VM
-        ),
-        cost_estimate=lasts(50),
-        name="reduce_dense",
-    )(dense.reshape(shape), *goes, *after)
-    return out.reshape(width // owners, columns), *comes
 
 
 PAIR = 2
@@ -1027,13 +971,17 @@
     return STAT_DECAY * old + (1.0 - STAT_DECAY) * new
 
 
-def final_stats_kernel(count, groups, half, early, *refs):
-    late = half - early
-    owns, gots = refs[:early], refs[early : 2 * early]
-    stays, comes = refs[2 * early : 2 * early + late], refs[2 * early + late : 2 * half]
-    (dense_ref, up_old_ref, down_old_ref, up_rows_ref, down_rows_ref, up_cols_ref, down_cols_ref, dense_old_ref,
-     dense_cols_ref, ends_ref, out_ref, sums_ref, up_new_ref, down_new_ref, dense_out_ref, dense_new_ref,
-     go_s, pay_s, got_s, dense_pay_s, dense_got_s, spread_s, send_sem, recv_sem) = refs[2 * half :]
+def finish_kernel(count, groups, half, orders, spans, *refs):
+    bits = count.bit_length() - 1
+    steps = len(orders[0])
+    (mine_hbm, own_0, own_1, got_0, got_1, stay_2, come_2, keep_3, come_3, near_mix_ref, got_mix_ref,
+     up_old_ref, down_old_ref, up_rows_ref, down_rows_ref, up_cols_ref, down_cols_ref, dense_old_ref,
+     dense_cols_ref) = refs[:19]
+    (dense_ref, ends_ref, pair_mix_ref, out_ref, sums_ref, up_new_ref, down_new_ref, dense_out_ref,
+     dense_new_ref) = refs[19:28]
+    sum_ref, first_got, *got = refs[28 : 30 + steps]
+    (mine_ref, load_sem, go_s, far_go_s, far_stay_s, far_got_s, mix_s, pay_s, got_s, dense_pay_s, dense_got_s, spread_s,
+     send_sem, recv_sem) = refs[30 + steps :]
     width = up_rows_ref.shape[1]
     ff = down_rows_ref.shape[1]
     wide = width // 2
@@ -1044,18 +992,33 @@
     after = [lax.rem(me + k, count) for k in range(count)]
     beside = [lax.rem(place + k, groups) for k in range(groups)]
     pair_bit, pair = flipped("dp", PAIR)
+    far_bit, far = flipped("dp", FAR)
+    core, core_peer = flipped("expert", 1)
+    chip, chip_peer = flipped("expert", 2)
+    links = [flipped("dp", 1 << b) for b in range(bits)] + [(chip, chip_peer)]
+    whole = (slice(None),) * bits
+    loading = pltpu.make_async_copy(mine_hbm.at[whole + (core,)], mine_ref, load_sem)
+    loading.start()
     greet([{"dp": after[k]} for k in range(1, count)] + [{"expert": beside[k]} for k in range(1, groups)])
     push = Pusher(send_sem, recv_sem)
 
-    def summed(j, side):
-        return (
-            stays[j][side].astype(jnp.float32) + comes[j][side].astype(jnp.float32)
-        ).astype(jnp.bfloat16)
-
-    crossing = []
-    for j in range(late):
-        go_s[j] = summed(j, 1 - pair_bit)
-        crossing.append(push(go_s.at[j], ends_ref.at[late + j], pair))
+    def plus(a, b):
+        return (a.astype(jnp.float32) + b.astype(jnp.float32)).astype(jnp.bfloat16)
+
+    flying = [
+        push(mine_hbm.at[whole + (1 - core, slice(None), slice(None), span)], first_got.at[..., span], core_peer)
+        for span in spans
+    ]
+    for low in range(2):
+        far_go_s[low] = plus(keep_3[1 - far_bit, low], come_3[1 - far_bit, low])
+    far_exchange = push(far_go_s, far_got_s, far)
+    go_s[0] = plus(stay_2[1 - pair_bit], come_2[1 - pair_bit])
+    cross_2 = push(go_s.at[0], ends_ref.at[2], pair)
+    mix_s[...] = plus(near_mix_ref[1], got_mix_ref[1])
+    cross_mix = push(mix_s, pair_mix_ref, pair)
+    ends_ref[0] = plus(stay_2[pair_bit], come_2[pair_bit])
+    for low in range(2):
+        far_stay_s[low] = plus(keep_3[far_bit, low], come_3[far_bit, low])
 
     def column_of(table_ref, lane, at):
         return jnp.sum(jnp.where(lane == at, table_ref[...], 0.0), axis=1, keepdims=True)
@@ -1089,28 +1052,78 @@
                 pay_s[at, 4 * kind + 2 + h : 4 * kind + 3 + h, :] = scaled[:, span]
 
     own_at, got_at = pair_bit * half, (1 - pair_bit) * half
-    for j in range(late):
-        ends_ref[j] = summed(j, pair_bit)
-        expert(ends_ref[j], own_at + early + j)
-    for j in range(early):
-        expert(owns[j][...], own_at + j)
-        expert(gots[j][...], got_at + j)
+
+    def at_place(chosen, span):
+        return tuple(chosen.get(bits - 1 - i, slice(None)) for i in range(bits)) + (
+            chosen.get(bits, slice(None)),
+            slice(None),
+            span,
+        )
+
+    def got_place(step, span):
+        return (slice(None),) * (steps - 1 - step) + (slice(None), span)
+
+    loading.wait()
+    chosen = [{} for _ in spans]
+    for step in range(steps + 1):
+        for part, span in enumerate(spans):
+            flying[part].wait_recv()
+            if step == 0:
+                sum_ref[..., span] = plus(mine_ref[..., span], first_got[..., span])
+            else:
+                here = at_place(chosen[part], span)
+                sum_ref[here] = plus(sum_ref[here], got[step - 1][got_place(step - 1, span)])
+            if step < steps:
+                link = orders[part][step]
+                bit, peer = links[link]
+                away = at_place({**chosen[part], link: 1 - bit}, span)
+                flying[part] = push(sum_ref.at[away], got[step].at[got_place(step, span)], peer)
+                chosen[part] = {**chosen[part], link: bit}
+            else:
+                dense_ref[core, chip, :, span] = sum_ref[at_place(chosen[part], span)]
+                block = dense_ref.at[core, chip, :, span]
+                flying[part] = push(block, block, chip_peer)
+        if step == 0:
+            expert(own_0, own_at)
+            expert(got_0, got_at)
+            expert(own_1, own_at + 1)
+            expert(got_1, got_at + 1)
+        elif step == 1:
+            expert(ends_ref[0], own_at + 2)
+        elif step == steps - 1:
+            cross_2.wait_recv()
+            expert(ends_ref[2], got_at + 2)
+            far_exchange.wait_recv()
+            go_s[1] = plus(far_stay_s[1 - pair_bit], far_got_s[1 - pair_bit])
+            cross_3 = push(go_s.at[1], ends_ref.at[3], pair)
+            ends_ref[1] = plus(far_stay_s[pair_bit], far_got_s[pair_bit])
+            expert(ends_ref[1], own_at + 3)
+    for part, span in enumerate(spans):
+        flying[part].wait_recv()
+        block = dense_ref.at[core, :, :, span]
+        flying[part] = push(block, block, core_peer)
+    cross_3.wait_recv()
+    expert(ends_ref[3], got_at + 3)
+    arriving = [push(pay_s.at[after[k]], got_s.at[k], {"dp": after[k]}) for k in range(1, count)]
+    for copy in flying:
+        copy.wait_recv()
 
     columns = count * dense_cols_ref.shape[2]
     piece = dense_cols_ref.shape[2]
+    dense = dense_ref[...].reshape(own_up, dense_ref.shape[3])
     dense_lane = lax.broadcasted_iota(jnp.int32, dense_new_ref.shape, 1)
     old = dense_old_ref[...]
     qkv_columns = columns - width
     totals, scaleds, rows_new = [], [], []
     for at, span in enumerate((slice(0, qkv_columns), slice(qkv_columns, columns))):
         new, total, scaled = factored(
-            dense_ref[:, span].astype(jnp.float32), column_of(dense_old_ref, dense_lane, at)
+            dense[:, span].astype(jnp.float32), column_of(dense_old_ref, dense_lane, at)
         )
         rows_new.append(new)
         totals.append(total)
         scaleds.append(scaled)
     gain_lanes = (dense_lane == 2) | (dense_lane == 3)
-    gains = pltpu.roll(dense_ref[:, columns:].astype(jnp.float32), 2, 1)
+    gains = pltpu.roll(dense[:, columns:].astype(jnp.float32), 2, 1)
     moments = jnp.where(gain_lanes, decayed(old, gains * gains + EPS_STAT), 1.0)
     gain_steps = jnp.where(gain_lanes, gains * lax.rsqrt(moments), 0.0)
     dense_new_ref[...] = jnp.where(
@@ -1128,30 +1141,6 @@
             axis=0,
         )
     dense_arriving = [push(dense_pay_s.at[after[k]], dense_got_s.at[k], {"dp": after[k]}) for k in range(1, count)]
-    for j in range(late):
-        crossing[j].wait_recv()
-        expert(ends_ref[late + j], got_at + early + j)
-    arriving = [push(pay_s.at[after[k]], got_s.at[k], {"dp": after[k]}) for k in range(1, count)]
-
-    tile = dense_pay_s[me]
-    for k in range(1, count):
-        dense_arriving[k - 1].wait_recv()
-        tile = tile + dense_got_s[k]
-    new_columns = decayed(dense_cols_ref[me], tile[0:1] / width)
-    is_qkv = lax.broadcasted_iota(jnp.int32, (1, piece), 1) + me * piece < qkv_columns
-    ratio = tile[1:2] / new_columns
-    sums = [
-        jnp.sum(jnp.where(chosen, row, 0.0), axis=1, keepdims=True)
-        for row in (ratio, tile[0:1])
-        for chosen in (is_qkv, ~is_qkv)
-    ]
-    dense_out_ref[me] = jnp.concatenate(
-        [new_columns]
-        + [jnp.broadcast_to(v, (1, piece)) for v in sums]
-        + [tile[2:3], jnp.zeros((2, piece), jnp.float32)],
-        axis=0,
-    )
-    dense_arriving = [push(dense_out_ref.at[me], dense_out_ref.at[me], {"dp": after[k]}) for k in range(1, count)]
 
     tile = pay_s[me]
     for k in range(1, count):
@@ -1175,6 +1164,27 @@
         tops += [jnp.broadcast_to(v, (1, wide)) for v in (row_mean, squares)]
     out_ref[me] = jnp.concatenate(made + tops, axis=0)
     arriving = [push(out_ref.at[me], out_ref.at[me], {"dp": after[k]}) for k in range(1, count)]
+
+    tile = dense_pay_s[me]
+    for k in range(1, count):
+        dense_arriving[k - 1].wait_recv()
+        tile = tile + dense_got_s[k]
+    new_columns = decayed(dense_cols_ref[me], tile[0:1] / width)
+    is_qkv = lax.broadcasted_iota(jnp.int32, (1, piece), 1) + me * piece < qkv_columns
+    ratio = tile[1:2] / new_columns
+    sums = [
+        jnp.sum(jnp.where(chosen_columns, row, 0.0), axis=1, keepdims=True)
+        for row in (ratio, tile[0:1])
+        for chosen_columns in (is_qkv, ~is_qkv)
+    ]
+    dense_out_ref[me] = jnp.concatenate(
+        [new_columns]
+        + [jnp.broadcast_to(v, (1, piece)) for v in sums]
+        + [tile[2:3], jnp.zeros((2, piece), jnp.float32)],
+        axis=0,
+    )
+    dense_arriving = [push(dense_out_ref.at[me], dense_out_ref.at[me], {"dp": after[k]}) for k in range(1, count)]
+
     for copy in arriving:
         copy.wait_recv()
     total = out_ref[0, :, :LANES]
@@ -1182,7 +1192,7 @@
         total = total + out_ref[a, :, :LANES]
     spread_s[place] = total
     arriving = [push(spread_s.at[place], spread_s.at[place], {"expert": beside[k]}) for k in range(1, groups)]
-    for copy in arriving + dense_arriving:
+    for copy in arriving + dense_arriving + [cross_mix]:
         copy.wait_recv()
     total = spread_s[0]
     for e in range(1, groups):
@@ -1191,37 +1201,63 @@
     push.finish()
 
 
-def final_stats(owns, gots, stays, comes, dense, olds, all_rows, all_columns, dense_old, dense_columns, label):
+FAR = 4
+
+
+def finish(dense, owns, gots, settling, mixes, olds, all_rows, all_columns, dense_old, dense_columns, label):
     count = lax.axis_size("dp")
     groups = lax.axis_size("expert")
-    width = all_rows[0].shape[1]
+    width, dense_width = dense.shape
+    bits = count.bit_length() - 1
+    quarter = width // count // 4
+    parts = 6
+    tiles = dense_width // LANES
+    bounds = [LANES * (tiles * i // parts) for i in range(parts + 1)]
+    spans = [slice(a, b) for a, b in zip(bounds[:-1], bounds[1:])]
+    last = tuple(range(1, bits))
+    orders = [((bits, 0) if part % 2 == 0 else (0, bits)) + last for part in range(parts)]
+    half = (2,) * bits + (2, quarter, dense_width)
     rows = olds[0].shape[0] + olds[1].shape[0]
     piece = dense_columns.shape[2]
     vmem = pl.BlockSpec(memory_space=pltpu.VMEM)
-    tiles = (count, 8, width // 2)
+    stat_tiles = (count, 8, width // 2)
     dense_tiles = (count, 8, piece)
-    late = len(stays)
-    copies = 4 * (count - 1) + groups - 1 + late
+    copies = parts * (bits + 4) + 4 * (count - 1) + groups - 1 + 4
     shape = lambda *s: jax.ShapeDtypeStruct(s, jnp.float32)
+    low = lambda *s: jax.ShapeDtypeStruct(s, jnp.bfloat16)
+    held = lambda *s: pltpu.VMEM(s, jnp.bfloat16)
     outs = (
-        jax.ShapeDtypeStruct((2 * late, rows, width), jnp.bfloat16),
-        shape(*tiles),
+        low(2, 2, quarter, dense_width),
+        low(4, rows, width),
+        low(*mixes[0].shape[1:]),
+        shape(*stat_tiles),
         shape(8, LANES),
         shape(LANES, LANES),
         shape(LANES, LANES),
         shape(*dense_tiles),
-        shape(dense.shape[0], LANES),
-    )
-    args = (*owns, *gots, *stays, *comes, dense, *olds, *all_rows, *all_columns, dense_old, dense_columns)
-    return pl.pallas_call(
-        functools.partial(final_stats_kernel, count, groups, len(owns) + late, len(owns)),
+        shape(width // count, LANES),
+    )
+    args = (
+        dense.reshape((2,) * bits + (2, 2, quarter, dense_width)),
+        *owns, *gots, *settling, *mixes, *olds, *all_rows, *all_columns, dense_old, dense_columns,
+    )
+    own, *rest = pl.pallas_call(
+        functools.partial(finish_kernel, count, groups, 4, orders, spans),
         out_shape=outs,
-        in_specs=[vmem] * len(args),
+        in_specs=[pl.BlockSpec(memory_space=pl.ANY)] + [vmem] * (len(args) - 1),
         out_specs=[vmem] * len(outs),
-        scratch_shapes=[
-            pltpu.VMEM((late, rows, width), jnp.bfloat16),
-            pltpu.VMEM(tiles, jnp.float32),
-            pltpu.VMEM(tiles, jnp.float32),
+        scratch_shapes=[held(*half), held(*half)]
+        + [held(*((2,) * (bits - step)), quarter, dense_width) for step in range(bits + 1)]
+        + [
+            held(*half),
+            pltpu.SemaphoreType.DMA,
+            held(2, rows, width),
+            held(2, rows, width),
+            held(2, rows, width),
+            held(2, rows, width),
+            held(*mixes[0].shape[1:]),
+            pltpu.VMEM(stat_tiles, jnp.float32),
+            pltpu.VMEM(stat_tiles, jnp.float32),
             pltpu.VMEM(dense_tiles, jnp.float32),
             pltpu.VMEM(dense_tiles, jnp.float32),
             pltpu.VMEM((groups, 8, LANES), jnp.float32),
@@ -1231,17 +1267,24 @@
         compiler_params=pltpu.CompilerParams(
             collective_id=label, has_side_effects=True, vmem_limit_bytes=VM
         ),
-        cost_estimate=lasts(15),
-        name="final_stats",
+        cost_estimate=lasts(75),
+        name="finish",
     )(*args)
+    return own.reshape(width // count, dense_width), *rest
 
 
 def update_kernel(counts, half, early, s_ref, *refs):
     owns, gots = refs[:early], refs[early : 2 * early]
-    (ends_ref, tiles_ref, sums_ref, up_new_ref, down_new_ref, dense_tiles_ref, dense_new_ref, dense_ref, dense_rows_ref,
-     up_w_ref, down_w_ref, qkv_w_ref, out_w_ref,
-     up_out_ref, down_out_ref, up_rows_ref, down_rows_ref, up_cols_ref, down_cols_ref,
-     qkv_out_ref, out_out_ref, qkv_cols_ref, out_cols_ref, turned_ref, gains_ref, rms_ref) = refs[2 * early :]
+    (dense_ref, ends_ref, pair_mix_ref, tiles_ref, sums_ref, up_new_ref, down_new_ref, dense_tiles_ref, dense_new_ref,
+     dense_rows_ref, middle_ref, near_mix_ref, got_mix_ref, up_w_ref, down_w_ref, qkv_w_ref, out_w_ref,
+     block_ref, up_out_ref, down_out_ref, up_rows_ref, down_rows_ref, up_cols_ref, down_cols_ref,
+     qkv_out_ref, out_out_ref, qkv_cols_ref, out_cols_ref, qkv_rows_ref, out_rows_ref, gains_ref, moments_ref,
+     rms_ref) = refs[2 * early :]
+    block_ref[...] = middle_ref[...] + (
+        near_mix_ref[0].astype(jnp.float32)
+        + got_mix_ref[0].astype(jnp.float32)
+        + pair_mix_ref[...].astype(jnp.float32)
+    )
     late = half - early
     own_up = up_out_ref.shape[1]
     own_down = down_out_ref.shape[1]
@@ -1325,12 +1368,14 @@
         out_ref[:, here] = weight_ref[:, here].astype(jnp.float32) - dense_ref[
             :, first : first + LANES
         ].astype(jnp.float32) * scales[at] * lax.rsqrt(columns)
-    turned = table.T[:8]
-    turned_ref[...] = turned
-    gains_ref[...] = -factors[0] * turned
-
-
-def update(owns, gots, stats, dense, dense_rows, up_w, down_w, qkv_w, out_w):
+    turned = table.T
+    qkv_rows_ref[...] = turned[0:1]
+    out_rows_ref[...] = turned[1:2]
+    gains_ref[...] = -factors[0] * turned[2:4]
+    moments_ref[...] = turned[4:6]
+
+
+def update(owns, gots, finished, dense_rows, middle, mixes, up_w, down_w, qkv_w, out_w):
     count = lax.axis_size("dp")
     groups = lax.axis_size("expert")
     me = lax.axis_index("dp")
@@ -1345,12 +1390,13 @@
         float(groups * experts * width * up_columns),
         float(groups * experts * ff * width),
     )
-    ends = stats[0]
+    ends = finished[1]
     early = len(owns)
     whole = lambda *shape: pl.BlockSpec(shape, lambda g, s: (0,) * len(shape))
     shape = lambda *s: jax.ShapeDtypeStruct(s, jnp.float32)
     rows = own_up + own_down
     outs = [
+        shape(*middle.shape),
         shape(experts, own_up, up_columns),
         shape(experts, own_down, width),
         shape(experts, own_up),
@@ -1361,8 +1407,10 @@
         shape(own_up, width),
         shape(1, qkv_columns),
         shape(1, width),
-        shape(8, LANES),
-        shape(8, LANES),
+        shape(1, own_up),
+        shape(1, own_up),
+        shape(2, own_up),
+        shape(2, own_up),
         shape(8, LANES),
     ]
     return pl.pallas_call(
@@ -1372,8 +1420,7 @@
             num_scalar_prefetch=1,
             grid=(1,),
             in_specs=[whole(rows, width)] * (2 * early)
-            + [whole(*s.shape) for s in stats]
-            + [whole(*dense.shape), whole(*dense_rows.shape)]
+            + [whole(*a.shape) for a in (*finished, dense_rows, middle, *mixes)]
             + [
                 pl.BlockSpec((experts, own_up, up_columns), lambda g, s: (0, s[1], 0)),
                 pl.BlockSpec((experts, own_down, width), lambda g, s: (0, s[1], 0)),
@@ -1387,7 +1434,7 @@
         name="update",
     )(
         jnp.stack([lax.rem(me // PAIR, 2), me]),
-        *owns, *gots, *stats, dense, dense_rows, up_w, down_w, qkv_w, out_w,
+        *owns, *gots, *finished, dense_rows, middle, *mixes, up_w, down_w, qkv_w, out_w,
     )
 
 
@@ -1548,33 +1595,28 @@
         out_weight, steps
     )
     got_mix = swap_chip(far_mix)
-    steps = [input_grad]
-    steps.append(advance(3, steps[-1:]))
-    for_pair = settle_mix(near_mix, got_mix, steps[-1:])
-    steps.append(for_pair)
     qkv_columns = qkv_weight.shape[1]
     fast_tail = dp_count == experts_here and D // dp_count % 64 == 0
-    if fast_tail:
-        dense_own, come = reduce_dense(dense, [(chains[3][2], chains[3][0][0])], 3, steps)
-    else:
-        dense_own = reduce_dense_far(dense)
-    mix_parts = (near_mix[0], got_mix[0], swap_pair(for_pair))
-    block_out = middle + sum(part.astype(jnp.float32) for part in mix_parts)
     if fast_tail:
         spare = ((0, 0), (0, LANES - experts_here))
         owns = [chains[j][1][0] for j in (0, 1)]
         gots = [swap_pair(chains[j][2][0]) for j in (0, 1)]
+        settling = []
+        for j in (2, 3):
+            masks, stay, go = chains[j]
+            settling += [stay, swap(go, "dp", masks[0])]
+        settling[2:] = [x.reshape((2, 2) + x.shape[1:]) for x in settling[2:]]
         dense_rows = jnp.stack([qkv_rows, out_rows])
         dense_old = jnp.pad(
             jnp.concatenate([own_share(dense_rows, 1), own_share(gain_moment, 1)], axis=0).T,
             ((0, 0), (0, LANES - 4)),
         )
-        stats = final_stats(
+        finished = finish(
+            dense,
             owns,
             gots,
-            [chains[j][1] for j in (2, 3)],
-            [swap(chains[2][2], "dp", chains[2][0][0]), come],
-            dense_own,
+            settling,
+            (near_mix, got_mix),
             [jnp.pad(own_share(old, 1).T, spare) for old in (gateup_rows, down_rows)],
             (gateup_rows, down_rows),
             (gateup_cols, down_cols),
@@ -1583,6 +1625,7 @@
             1,
         )
         (
+            block_out,
             gate_up_new,
             down_new,
             gateup_rows_new,
@@ -1593,15 +1636,31 @@
             out_new,
             qkv_cols_new,
             out_cols_new,
-            turned,
-            gains,
+            qkv_rows_new,
+            out_rows_new,
+            gains_update,
+            gain_moment_new,
             roots,
-        ) = update(owns, gots, stats, dense_own, dense_rows, gate_up_weight, down_weight, qkv_weight, out_weight)
+        ) = update(
+            owns,
+            gots,
+            finished,
+            dense_rows,
+            middle,
+            (near_mix, got_mix),
+            gate_up_weight,
+            down_weight,
+            qkv_weight,
+            out_weight,
+        )
         qkv_cols_new, out_cols_new = qkv_cols_new[0], out_cols_new[0]
-        qkv_rows_new, out_rows_new = turned[0], turned[1]
-        gains_update, gain_moment_new = gains[2:4], turned[4:6]
+        qkv_rows_new, out_rows_new = qkv_rows_new[0], out_rows_new[0]
         update_rms = roots[:5, 0]
     else:
+        for_pair = settle_mix(near_mix, got_mix, [input_grad])
+        mix_parts = (near_mix[0], got_mix[0], swap_pair(for_pair))
+        block_out = middle + sum(part.astype(jnp.float32) for part in mix_parts)
+        dense_own = reduce_dense_far(dense)
         for j in range(half_experts):
             while len(chains[j][0]) > 1:
                 advance(j, [dense_own])

time: 404 us -> 383 us (0.948)
  Pallas kernels: 357 us -> 339 us
  waiting for transfers between devices: 0.03 us -> 7.71 us
  local copies, waits for them, and re-layouts: 14.5 us -> 9.92 us
    pallas_call x4 -> x2, Pallas kernels: 130 us -> 113 us  [the longest x1 89.9 us: finish(): pl.pallas_call(functools.partial(finish_kernel, count, groups, 4, orders,...]
    ppermute x12 -> x11, waiting for transfers between devices: 0.03 us -> 7.71 us  [swap(): return lax.ppermute(values, axis, [(i, i ^ mask) for i in range(count)])]
    pallas_call x6 -> x5, Pallas kernels: 18 us -> 14.7 us  [settle(): pl.pallas_call(functools.partial(settle_kernel, len(after) + len(passed))...]
    ppermute x12 -> x11, starting transfers between devices: 16.5 us -> 14.5 us  [swap(): return lax.ppermute(values, axis, [(i, i ^ mask) for i in range(count)])]
  transfers between devices with their start and end apart: 12 -> 11, of which waited for: 0 -> 1; matrix products, arithmetic and copies ran while one was open for 3% -> 2% of each run, Pallas kernels for 74% -> 46%
where the time goes in v6:
time: 383 us; the launch traced here: 379 us
  Pallas kernels  339 us (89%)
  starting transfers between devices  14.5 us (4%)
  local copies, waits for them, and re-layouts  9.92 us (3%)
  waiting for transfers between devices  7.71 us (2%)
  other arithmetic  6.85 us (2%)
    pallas_call x1, Pallas kernels, finish(): pl.pallas_call(functools.partial(finish_kernel, count, groups, 4, orders,...  89.9 us
    pallas_call x4, Pallas kernels, run_expert(): pl.pallas_call(functools.partial(expert_kernel, j, owners, tiles, len(aft...  74.5 us
    pallas_call x1, Pallas kernels, return_sums(): pl.pallas_call(functools.partial(return_kernel, capacity, count, far_mask...  52.9 us
    pallas_call x1, Pallas kernels, gather_and_select(): pl.pallas_call(functools.partial(gather_kernel, capacity, experts_here, h...  44.8 us
    pallas_call x1, Pallas kernels, attend_back(): pl.pallas_call(functools.partial(attend_back_kernel, len(after)), out_sha...  22.9 us
    pallas_call x1, Pallas kernels, attend(): pl.pallas_call(attend_kernel, out_shape=(shape((rows, width), jnp.bfloat1...  18 us
    pallas_call x5, Pallas kernels, settle(): pl.pallas_call(functools.partial(settle_kernel, len(after) + len(passed))...  14.7 us
    ppermute x11, starting transfers between devices, swap(): return lax.ppermute(values, axis, [(i, i ^ mask) for i in range(count)])  14.5 us
  transfers between devices with their start and end apart: 11, of which 1 were waited for; matrix products, arithmetic and copies ran while one was open for 2% of the time, Pallas kernels for 46%

profile of v6, /device:TPU:0, one launch (start us, length us, event | category | flops | bytes accessed | tf_op | source)
XLA Modules:
  0.0 379.4 jit_solution(8772589147675723322)
XLA Ops:
  2.2 1.6 convert_element_type.23
  3.8 3.0 collective-permute-start
  6.9 1.6 collective-permute-start.1
  9.1 18.0 %attend.1 = (bf16[384,1024]{1,0:T(8,128)(2,1)}, bf16[384,2048]{1,0:T(8,128)(2,1)}, bf16[384,1024]{1,0:T(8,128)(2,1)}, f32[384,128]{1,0:T(8,128)}, f32[384,1024]{1,0:T(8,128)}, /*index=5*/bf16[384,1024]{1,0:T(8,128)(2,1)}) custom-call(f32[384,1024]{1,0:T(8,128)} %hidden_hbm.1, s32[3,384]{1,0:T(4,128)} %pad_add_fusion.ids_ref, bf16[2,1024]{1,0:T(2,128)(2,1)} %gains_ref.3, ...), custom_call_target="tpu_custom_call" | custom-call | flops 18000000 | bytes 1024 | tf_op jit(solution)/shard_map/attend/pallas_call | solution.py:285
  28.9 44.8 %gather_and_select.1 = (bf16[4,8,144,1024]{3,2,1,0:T(8,128)(2,1)}, bf16[4,8,144,1024]{3,2,1,0:T(8,128)(2,1)}, f32[4,8,144,1]{3,2,1,0:T(8,128)}, f32[8,4,384]{2,1,0:T(4,128)}) custom-call(bf16[384,1024]{1,0:T(8,128)(2,1)} %get-tuple-element.87.token_ref, bf16[416,1024]{1,0:T(8,128)(2,1)} %copy-done.1, bf16[416,1024]{1,0:T(8,128)(2,1)} %copy-done.6, ...), custom_call_target="tpu_custom_call" | custom-call | flops 44000000 | bytes 1024 | tf_op jit(solution)/shard_map/gather_and_select/pallas_call | solution.py:730
  73.7 18.6 %expert_0.1 = (bf16[4,192,1024]{2,1,0:T(8,128)(2,1)}, bf16[4,192,1024]{2,1,0:T(8,128)(2,1)}, bf16[1152,1024]{1,0:T(8,128)(2,1)}, bf16[1152,1024]{1,0:T(8,128)(2,1)}) custom-call(s32[2]{0:T(128)} %pad_add_fusion.2.s_ref, bf16[4,8,144,1024]{3,2,1,0:T(8,128)(2,1)} %get-tuple-element.88.rec_hbm, bf16[4,8,144,1024]{3,2,1,0:T(8,128)(2,1)} %get-tuple-element.89.arr_hbm, ...), custom_call_target="tpu_custom_call" | custom-call | flops 18000000 | bytes 1024 | tf_op jit(solution)/shard_map/expert_0/pallas_call | solution.py:121
  92.3 1.6 collective-permute-start.2
  93.9 18.6 %expert_1.1 = (bf16[4,192,1024]{2,1,0:T(8,128)(2,1)}, bf16[4,192,1024]{2,1,0:T(8,128)(2,1)}, bf16[1152,1024]{1,0:T(8,128)(2,1)}, bf16[1152,1024]{1,0:T(8,128)(2,1)}) custom-call(s32[2]{0:T(128)} %pad_add_fusion.2.s_ref, bf16[4,8,144,1024]{3,2,1,0:T(8,128)(2,1)} %get-tuple-element.88.rec_hbm, bf16[4,8,144,1024]{3,2,1,0:T(8,128)(2,1)} %get-tuple-element.89.arr_hbm, ...), custom_call_target="tpu_custom_call" | custom-call | flops 18000000 | bytes 1024 | tf_op jit(solution)/shard_map/expert_1/pallas_call | solution.py:121
  113.1 18.9 %expert_2.1 = (bf16[4,192,1024]{2,1,0:T(8,128)(2,1)}, bf16[4,192,1024]{2,1,0:T(8,128)(2,1)}, bf16[1152,1024]{1,0:T(8,128)(2,1)}, bf16[1152,1024]{1,0:T(8,128)(2,1)}) custom-call(s32[2]{0:T(128)} %pad_add_fusion.2.s_ref, bf16[4,8,144,1024]{3,2,1,0:T(8,128)(2,1)} %get-tuple-element.88.rec_hbm, bf16[4,8,144,1024]{3,2,1,0:T(8,128)(2,1)} %get-tuple-element.89.arr_hbm, ...), custom_call_target="tpu_custom_call" | custom-call | flops 18000000 | bytes 1024 | tf_op jit(solution)/shard_map/expert_2/pallas_call | solution.py:121
  132.0 1.6 collective-permute-start.5
  133.6 3.3 settle_0_4.1
  136.9 2.6 collective-permute-start.3
  139.5 18.4 %expert_3.1 = (bf16[4,192,1024]{2,1,0:T(8,128)(2,1)}, bf16[4,192,1024]{2,1,0:T(8,128)(2,1)}, bf16[1152,1024]{1,0:T(8,128)(2,1)}, bf16[1152,1024]{1,0:T(8,128)(2,1)}) custom-call(s32[2]{0:T(128)} %pad_add_fusion.2.s_ref, bf16[4,8,144,1024]{3,2,1,0:T(8,128)(2,1)} %get-tuple-element.88.rec_hbm, bf16[4,8,144,1024]{3,2,1,0:T(8,128)(2,1)} %get-tuple-element.89.arr_hbm, ...), custom_call_target="tpu_custom_call" | custom-call | flops 18000000 | bytes 1024 | tf_op jit(solution)/shard_map/expert_3/pallas_call | solution.py:121
  158.7 10.6 %combine.1 = (bf16[4,384,1024]{2,1,0:T(8,128)(2,1)}, bf16[4,384,1024]{2,1,0:T(8,128)(2,1)}) custom-call(f32[8,4,384]{2,1,0:T(4,128)} %get-tuple-element.98.code_ref, bf16[1152,1024]{1,0:T(8,128)(2,1)} %get-tuple-element.93.refs_0_, bf16[1152,1024]{1,0:T(8,128)(2,1)} %get-tuple-element.94.refs_0_.refs_1_, ...), custom_call_target="tpu_custom_call" | custom-call | flops 12000000 | bytes 1024 | tf_op jit(solution)/shard_map/combine/pallas_call | solution.py:808
  170.4 3.3 settle_1_4.1
  173.7 52.9 %return_sums.1 = (f32[384,1024]{1,0:T(8,128)}, bf16[2,384,1024]{2,1,0:T(8,128)(2,1)}, bf16[2,384,1024]{2,1,0:T(8,128)(2,1)}, bf16[2,192,1024]{2,1,0:T(8,128)(2,1)}) custom-call(f32[8,4,384]{2,1,0:T(4,128)} %get-tuple-element.98.code_ref, bf16[4,384,1024]{2,1,0:T(8,128)(2,1)} %get-tuple-element.100.refs_0_.mine_ref, ...), custom_call_target="tpu_custom_call" | custom-call | flops 37000000 | bytes 1024 | tf_op jit(solution)/shard_map/return_sums/pallas_call | solution.py:888
  226.6 2.4 settle_0_2.1
  230.1 3.3 settle_2_4.1
  236.4 2.4 settle_1_2.1
  238.8 2.1 collective-permute-start.7
  244.9 22.9 %attend_back.1 = (f32[384,1024]{1,0:T(8,128)}, bf16[1024,3200]{1,0:T(8,128)(2,1)}) custom-call(f32[384,1024]{1,0:T(8,128)} %grad_ref.1, f32[384,1024]{1,0:T(8,128)} %get-tuple-element.120.middle_ref.refs_14_, f32[384,1024]{1,0:T(8,128)} %get-tuple-element.110.refs_0_.normed_grad_ref, f32[384,128]{1,0:T(8,128)} %get-tuple-element.121.lse_ref, ...), custom_call_target="tpu_custom_call" | custom-call | flops 26000000 | bytes 1024 | tf_op jit(solution)/shard_map/attend_back/pallas_call | solution.py:434
  267.9 7.7 %collective-permute-done.6.refs_3_.refs_2_ = bf16[192,1024]{1,0:T(8,128)(2,1)S(1)} collective-permute-done((bf16[192,1024]{1,0:T(8,128)(2,1)}, bf16[192,1024]{1,0:T(8,128)(2,1)S(1)}, u32[]{:S(2)}, u32[]{:S(2)}) %collective-permute-start.6) | collective-permute-done | bytes 393248 | tf_op jit(solution)/shard_map/ppermute | solution.py:1448
  277.1 89.9 %finish.1 = (bf16[2,2,32,3200]{3,2,1,0:T(8,128)(2,1)}, bf16[4,192,1024]{2,1,0:T(8,128)(2,1)}, bf16[384,1024]{1,0:T(8,128)(2,1)}, f32[8,8,512]{2,1,0:T(8,128)}, f...) custom-call(bf16[2,2,2,2,2,32,3200]{6,5,4,3,2,1,0:T(8,128)(2,1)} %bi, ...), custom_call_target="tpu_custom_call" | custom-call | flops 75000000 | bytes 1024 | tf_op jit(solution)/shard_map/finish/pallas_call | solution.py:1244
  366.9 10.9 %update.1 = (f32[384,1024]{1,0:T(8,128)}, f32[8,128,1024]{2,1,0:T(8,128)}, f32[8,64,1024]{2,1,0:T(8,128)}, f32[8,128]{1,0:T(8,128)}, f32[8,64]{1,0:T(8,128)}, /*...) custom-call(s32[2]{0:T(128)} %pad_add_fusion.1.s_ref, ...), custom_call_target="tpu_custom_call" | custom-call | flops 6000000 | bytes 1024 | tf_op jit(solution)/shard_map/update/pallas_call | solution.py:1416
  (70 shorter events, 17.4 us)
Async XLA Ops:
  2.2 6.3 %copy-start.13 = (s32[384]{0:T(512)S(1)}, s32[384]{0:T(512)}, u32[]{:S(2)}) copy-start(s32[384]{0:T(512)} %param.23) | copy-start | bytes 4612
  2.2 6.3 %copy-start.14 = (s32[384]{0:T(512)S(1)}, s32[384]{0:T(512)}, u32[]{:S(2)}) copy-start(s32[384]{0:T(512)} %param.24) | copy-start | bytes 4612
  2.2 6.3 %copy-start.15 = (s32[384]{0:T(512)S(1)}, s32[384]{0:T(512)}, u32[]{:S(2)}) copy-start(s32[384]{0:T(512)} %param.25) | copy-start | bytes 4612
  3.8 23.3 %copy-start.1 = (bf16[416,1024]{1,0:T(8,128)(2,1)}, bf16[416,1024]{1,0:T(8,128)(2,1)S(1)}, u32[]{:S(2)}) copy-start(bf16[416,1024]{1,0:T(8,128)(2,1)S(1)} %fusion.1.grad_ref) | copy-start | bytes 2555908
  3.8 23.9 %collective-permute-start = (bf16[416,1024]{1,0:T(8,128)(2,1)S(1)}, bf16[416,1024]{1,0:T(8,128)(2,1)S(1)}, u32[]{:S(2)}, u32[]{:S(2)}) collective-permute-start(bf16[416,1024]{1,0:T(8,128)(2,1)S(1)} %fusion.1.grad_ref), channel_id=1, source_target_pairs={{0,2},{1,3},{2,0},{3,1},{4,6},{5,7},{6,4},{7,5},{8,10},{9,11},{10,... | collective-permute-start | bytes 2555912 | tf_op jit(solution)/shard_map/ppermute | solution.py:1448
  6.9 20.9 %collective-permute-start.1 = (bf16[416,1024]{1,0:T(8,128)(2,1)S(1)}, bf16[416,1024]{1,0:T(8,128)(2,1)S(1)}, u32[]{:S(2)}, u32[]{:S(2)}) collective-permute-start(bf16[416,1024]{1,0:T(8,128)(2,1)S(1)} %fusion.1.grad_ref), channel_id=1, source_target_pairs={{0,8},{4,12},{8,0},{12,4},{16,24},{20,28},{24,16},{28,20},{1,9},{5... | collective-permute-start | bytes 2555912 | tf_op jit(solution)/shard_map/ppermute | solution.py:1448
  27.7 1.2 copy-start.7
  92.3 41.3 %collective-permute-start.2 = (bf16[4,192,1024]{2,1,0:T(8,128)(2,1)}, bf16[4,192,1024]{2,1,0:T(8,128)(2,1)}, u32[]{:S(2)}, u32[]{:S(2)}) collective-permute-start(bf16[4,192,1024]{2,1,0:T(8,128)(2,1)} %get-tuple-element.92), channel_id=1, source_target_pairs={{0,4},{4,0},{8,12},{12,8},{16,20},{20,16},{24,28},{28,24},{1,5},{5... | collective-permute-start | bytes 4718600 | tf_op jit(solution)/shard_map/ppermute | solution.py:1448
  112.5 56.8 %collective-permute-start.4 = (bf16[4,192,1024]{2,1,0:T(8,128)(2,1)}, bf16[4,192,1024]{2,1,0:T(8,128)(2,1)S(1)}, u32[]{:S(2)}, u32[]{:S(2)}) collective-permute-start(bf16[4,192,1024]{2,1,0:T(8,128)(2,1)} %get-tuple-element.103), channel_id=1, source_target_pairs={{0,4},{4,0},{8,12},{12,8},{16,20},{20,16},{24,28},{28,24},{1,5},{5... | collective-permute-start | bytes 4718600 | tf_op jit(solution)/shard_map/ppermute | solution.py:1448
  132.0 97.0 %collective-permute-start.5 = (bf16[4,192,1024]{2,1,0:T(8,128)(2,1)}, bf16[4,192,1024]{2,1,0:T(8,128)(2,1)S(1)}, u32[]{:S(2)}, u32[]{:S(2)}) collective-permute-start(bf16[4,192,1024]{2,1,0:T(8,128)(2,1)} %get-tuple-element.114), channel_id=1, source_target_pairs={{0,4},{4,0},{8,12},{12,8},{16,20},{20,16},{24,28},{28,24},{1,5},{5... | collective-permute-start | bytes 4718600 | tf_op jit(solution)/shard_map/ppermute | solution.py:1448
  136.9 89.7 %collective-permute-start.3 = (bf16[2,192,1024]{2,1,0:T(8,128)(2,1)}, bf16[2,192,1024]{2,1,0:T(8,128)(2,1)}, u32[]{:S(2)}, u32[]{:S(2)}) collective-permute-start(bf16[2,192,1024]{2,1,0:T(8,128)(2,1)} %bitcast.76), channel_id=1, source_target_pairs={{0,16},{4,20},{8,24},{12,28},{16,0},{20,4},{24,8},{28,12},{1,17},{... | collective-permute-start | bytes 2359304 | tf_op jit(solution)/shard_map/ppermute | solution.py:1448
  157.9 117.6 %collective-permute-start.9 = (bf16[4,192,1024]{2,1,0:T(8,128)(2,1)}, bf16[4,192,1024]{2,1,0:T(8,128)(2,1)}, u32[]{:S(2)}, u32[]{:S(2)}) collective-permute-start(bf16[4,192,1024]{2,1,0:T(8,128)(2,1)} %get-tuple-element.128), channel_id=1, source_target_pairs={{0,4},{4,0},{8,12},{12,8},{16,20},{20,16},{24,28},{28,24},{1,5},{5... | collective-permute-start | bytes 4718600 | tf_op jit(solution)/shard_map/ppermute | solution.py:1448
  169.3 1.1 copy-start.5
  229.0 1.1 copy-start.4
  230.1 4.1 %copy-start.9 = (f32[1024]{0:T(1024)S(1)}, f32[1024]{0:T(1024)}, u32[]{:S(2)}) copy-start(f32[1024]{0:T(1024)} %param.36) | copy-start | bytes 12292
  230.1 4.1 %copy-start.10 = (f32[1024]{0:T(1024)S(1)}, f32[1024]{0:T(1024)}, u32[]{:S(2)}) copy-start(f32[1024]{0:T(1024)} %param.34) | copy-start | bytes 12292
  233.5 10.8 %copy-start.11 = (f32[2048]{0:T(1024)S(1)}, f32[2048]{0:T(1024)}, u32[]{:S(2)}) copy-start(f32[2048]{0:T(1024)} %param.35) | copy-start | bytes 24580
  233.5 10.8 %copy-start.12 = (f32[1024]{0:T(1024)S(1)}, f32[1024]{0:T(1024)}, u32[]{:S(2)}) copy-start(f32[1024]{0:T(1024)} %param.37) | copy-start | bytes 12292
  233.5 42.1 %collective-permute-start.10 = (bf16[2,384,1024]{2,1,0:T(8,128)(2,1)}, bf16[2,384,1024]{2,1,0:T(8,128)(2,1)S(1)}, u32[]{:S(2)}, u32[]{:S(2)}) collective-permute-start(bf16[2,384,1024]{2,1,0:T(8,128)(2,1)} %get-tuple-element.130), channel_id=1, source_target_pairs={{0,2},{1,3},{2,0},{3,1},{4,6},{5,7},{6,4},{7,5},{8,10},{9,11},{10,... | collective-permute-start | bytes 4718600 | tf_op jit(solution)/shard_map/ppermute | solution.py:1448
  233.5 42.1 %collective-permute-start.8 = (bf16[2,192,1024]{2,1,0:T(8,128)(2,1)}, bf16[2,192,1024]{2,1,0:T(8,128)(2,1)S(1)}, u32[]{:S(2)}, u32[]{:S(2)}) collective-permute-start(bf16[2,192,1024]{2,1,0:T(8,128)(2,1)} %bitcast.75), channel_id=1, source_target_pairs={{0,16},{4,20},{8,24},{12,28},{16,0},{20,4},{24,8},{28,12},{1,17},{... | collective-permute-start | bytes 2359304 | tf_op jit(solution)/shard_map/ppermute | solution.py:1448
  238.8 29.1 %collective-permute-start.7 = (bf16[192,1024]{1,0:T(8,128)(2,1)}, bf16[192,1024]{1,0:T(8,128)(2,1)S(1)}, u32[]{:S(2)}, u32[]{:S(2)}) collective-permute-start(bf16[192,1024]{1,0:T(8,128)(2,1)} %bitcast.78), channel_id=1, source_target_pairs={{0,8},{4,12},{8,0},{12,4},{16,24},{20,28},{24,16},{28,20},{1,9},{5... | collective-permute-start | bytes 1179656 | tf_op jit(solution)/shard_map/ppermute | solution.py:1448
  240.9 34.7 %collective-permute-start.6 = (bf16[192,1024]{1,0:T(8,128)(2,1)}, bf16[192,1024]{1,0:T(8,128)(2,1)S(1)}, u32[]{:S(2)}, u32[]{:S(2)}) collective-permute-start(bf16[192,1024]{1,0:T(8,128)(2,1)} %bitcast.77), channel_id=1, source_target_pairs={{0,8},{4,12},{8,0},{12,4},{16,24},{20,28},{24,16},{28,20},{1,9},{5... | collective-permute-start | bytes 1179656 | tf_op jit(solution)/shard_map/ppermute | solution.py:1448
  267.8 7.7 %copy-start.2 = (bf16[192,1024]{1,0:T(8,128)(2,1)}, bf16[192,1024]{1,0:T(8,128)(2,1)S(1)}, u32[]{:S(2)}) copy-start(bf16[192,1024]{1,0:T(8,128)(2,1)S(1)} %collective-permute-done.7.refs_4_.refs_3_) | copy-start | bytes 1179652
  275.6 1.5 copy-start
  (3 other events, 2.7 us)
